TPU v7x, 32 devices: a whole 2x2x4 slice. The times are simulated.
32 devices in a mesh: region: 2 (over x), member: 16 (over z, y, core).
Axes of the slice: x: 2, y: 2, z: 4, core: 2. Of those that a mesh axis runs over, the one named last changes fastest.
Arguments:
- analyses: bfloat16 [16, 1024, 1024], P('member', 'region'), may hold values from -6 to 6
- owners: int32 [4], replicated, may hold values from 0 to 15, as said below
- noise: bfloat16 [16, 1024, 1024], P('member', 'region'), may hold values from -24 to 24
- targets: bfloat16 [1024, 1024], P(('region', 'member')), may hold values from -6 to 6
- area_weight: float32 [1024], P(('region', 'member')), may hold values from 0.025 to 1.5
- enc_weight: bfloat16 [1024, 1024], replicated, may hold values from -0.1875 to 0.1875
- sample_inlet_matrix: bfloat16 [1024, 2048], replicated, may hold values from -0.1875 to 0.1875
- sample_outlet_matrix: bfloat16 [2048, 1024], replicated, may hold values from -0.125 to 0.125
Outputs:
- member_grad: bfloat16 [16, 1024, 1024], P('member', 'region')
- energy: float32 [1024], P(('region', 'member'))
Inputs may be any that keep to these rules, and one draw needn't show every extreme that they name: `owners`: 4 distinct member indices, entry b naming the control member of block b; member 0 and member 16 - 1 are always among them.
All inputs are finite; a program needn't handle non-finite values.
Results may differ from a plain program's by a relative error of at most 0.005.
Values may be sent and summed in bfloat16 or wider, within the bound.
No kernel may reach another device: no remote copies, remote signals or barrier semaphores. Data moves between devices by JAX's collectives and lax.ppermute only.
A program may use at most 64 MiB of HBM per device.

v0:
```python
import jax
import jax.numpy as jnp
from jax import lax
from jax.sharding import PartitionSpec as P

epsilon = 1e-06


def from_root(value, axis, source):
    kept = jnp.where(lax.axis_index(axis) == source, value, 0).astype(value.dtype)
    return lax.psum(kept, axis)


def apply_model(sample_hidden_vectors, sample_inlet_matrix, sample_outlet_matrix):
    features = sample_hidden_vectors.shape[-1]
    flat = sample_hidden_vectors.reshape(-1, features)
    normed = (flat * lax.rsqrt(jnp.mean(flat * flat, axis=-1, keepdims=True) + epsilon)).astype(
        jnp.bfloat16
    )
    hidden = jax.nn.gelu(
        jnp.dot(normed, sample_inlet_matrix, preferred_element_type=jnp.float32)
    ).astype(jnp.bfloat16)
    output = flat + jnp.dot(hidden, sample_outlet_matrix, preferred_element_type=jnp.float32)
    return output.reshape(sample_hidden_vectors.shape).astype(jnp.bfloat16)


def spread_skill_loss(member_ensemble, targets, area_weight, coefficient_mean):
    members = member_ensemble.shape[0]
    features = member_ensemble.shape[2]
    values = member_ensemble.astype(jnp.float32)
    from_target = values - targets.astype(jnp.float32)[None]
    spread = jnp.sqrt(jnp.mean(from_target * from_target, axis=-1) + epsilon)
    inner = jnp.einsum(
        "mtd,jtd->tmj", member_ensemble, member_ensemble, preferred_element_type=jnp.float32
    )
    squares = jnp.diagonal(inner, axis1=1, axis2=2)
    pair_dist = jnp.sqrt(
        (squares[:, :, None] + squares[:, None, :] - 2.0 * inner) / features + epsilon
    )
    positions = jnp.arange(members)
    diagonal_mask = positions[:, None] == positions[None, :]
    pair_coeff = jnp.where(diagonal_mask[None], 0.0, 1.0 / pair_dist).astype(jnp.bfloat16)
    coeff_sum = jnp.sum(pair_coeff.astype(jnp.float32), axis=-1)
    combined = jnp.einsum(
        "tmj,jtd->mtd", pair_coeff, member_ensemble, preferred_element_type=jnp.float32
    )
    weight_scale = area_weight / coefficient_mean
    gradient = weight_scale[None, :, None] * (
        from_target / spread[:, :, None]
        - (jnp.transpose(coeff_sum)[:, :, None] * values - combined) / members
    )
    energy = weight_scale * (
        jnp.mean(spread, axis=0) - jnp.sum(pair_dist, axis=(1, 2)) / (2.0 * members * members)
    )
    return (gradient.astype(jnp.bfloat16), energy)


def broadcast_latents(analyses, owners, enc_weight, member_index):
    region_rows = analyses.shape[1]
    blocks = owners.shape[0]
    block_rows = region_rows // blocks

    def encode_block(block_input):
        return jnp.dot(block_input, enc_weight, preferred_element_type=jnp.float32).astype(
            jnp.bfloat16
        )

    def skip_block(block_input):
        return jnp.zeros(block_input.shape, jnp.bfloat16)

    pieces = []
    for block_index in range(blocks):
        rows_here = analyses[0, block_index * block_rows : (block_index + 1) * block_rows]
        encoded = lax.cond(member_index == owners[block_index], encode_block, skip_block, rows_here)
        pieces.append(from_root(encoded, "member", owners[block_index]))
    latent_all = jnp.concatenate(pieces, axis=0)

    def latent_rows(first_row, row_count):
        return latent_all

    return latent_rows


def on_device(
    analyses,
    owners,
    noise,
    targets,
    area_weight,
    enc_weight,
    sample_inlet_matrix,
    sample_outlet_matrix,
):
    members = lax.axis_size("member")
    member_index = lax.axis_index("member")
    region_rows = analyses.shape[1]
    own_rows = region_rows // members
    weight_total = lax.psum(jnp.sum(area_weight), ("region", "member"))
    coefficient_mean = weight_total / (own_rows * members * lax.axis_size("region"))
    latent_rows = broadcast_latents(analyses, owners, enc_weight, member_index)
    latent = latent_rows(0, region_rows)
    sample_hidden_vectors = latent.astype(jnp.float32)[None] + noise.astype(jnp.float32)
    zone_prediction = apply_model(sample_hidden_vectors, sample_inlet_matrix, sample_outlet_matrix)
    member_ensemble = lax.all_to_all(
        zone_prediction, "member", split_axis=1, concat_axis=0, tiled=True
    )
    gradient, energy = spread_skill_loss(member_ensemble, targets, area_weight, coefficient_mean)
    member_grad = lax.all_to_all(gradient, "member", split_axis=0, concat_axis=1, tiled=True)
    return (member_grad, energy)


def solution(mesh):
    return jax.shard_map(
        on_device,
        mesh=mesh,
        in_specs=(
            P("member", "region", None),
            P(),
            P("member", "region", None),
            P(("region", "member"), None),
            P(("region", "member")),
            P(),
            P(),
            P(),
        ),
        out_specs=(P("member", "region", None), P(("region", "member"))),
        check_vma=False,
    )
```

profile of v0, /device:TPU:0, one launch (start us, length us, event | category | flops | bytes accessed | tf_op | source)
XLA Modules:
  0.0 228.9 jit_solution(9643908432099121467)
XLA Ops:
  7.2 0.0 all-reduce.3.cloned.1.call-start
  7.2 1.5 fusion.56
  11.3 0.9 select_bitcast_fusion.2
  12.2 2.1 conditional.6
  12.2 2.1 convolution_convert_fusion.2
  14.4 0.0 copy-start
  14.4 0.8 select_bitcast_fusion
  15.3 0.0 all-reduce.3.cloned.1.call-update
  15.3 96.0 %all-reduce.3.cloned.1.call-done = (bf16[1,128,1024]{2,1,0:T(8,128)(2,1)}, bf16[1,128,1024]{2,1,0:T(8,128)(2,1)}, bf16[1,128,1024]{2,1,0:T(8,128)(2,1)}, bf16[1,128,1024]{2,1,0:T(8,128)(2,1)}) async-done(((bf16[1,128,1024]{2,1,0:T(8,128)(2,1)}, bf16[1,128,1024]{2,1,0:T(8,128)(2,1)}, bf16[1,128,1024]{2,1,0:T(8,128)(2,1)}, bf16[1,128,1024]{2,1,0:T(8,128)(2,1)}), (bf16[1,128,1024]{2,1,0:T(8,128)(2,1)}, ...) | async-done | bytes 1048592 | tf_op jit(solution)/shard_map/psum | solution.py:11
  111.3 0.0 copy-start.1
  111.3 0.0 copy-start.2
  111.3 0.0 copy-start.3
  111.3 0.0 copy-start.4
  111.3 0.0 copy-done
  111.3 1.7 fusion.25
  113.0 0.0 copy-done.1
  113.0 0.0 copy-done.2
  113.0 0.0 copy-done.3
  113.0 0.0 copy-done.4
  113.1 8.1 %fusion.35 = bf16[1,512,1024]{2,1,0:T(8,128)(2,1)S(1)} fusion(bf16[2048,1024]{1,0:T(8,128)(2,1)} %param.23, bf16[1,512,1024]{2,1,0:T(8,128)(2,1)S(1)} %copy-done, bf16[1024,2048]{1,0:T(8,128)(2,1)} %param.22, f32[512]{0:T(512)S(1)} %add_rsqrt_fusion, bf16[1,128,1024]{2,1,0:T(8,128)(2,1)S(1)} %copy-done.1, bf16[1,128,1024]{2,1,0:T(8,128)(2,1)S(1)} %copy-done.2, ...), kind=kOutput, calls=%fused_computation.45 | convolution fusion | flops 4316987392 | bytes 11536384 | tf_op jit(solution)/shard_map/dot_general | solution.py:23
  121.2 1.6 copy.59
  122.8 0.5 broadcast.73
  123.3 7.0 %reduce.1 = bf16[512,1024]{1,0:T(8,128)(2,1)S(1)} reduce(bf16[512,1,1024]{2,1,0:T(2,128)(2,1)S(1)} %bitcast.73, bf16[]{:T(256)} %broadcast.73), dimensions={1}, to_apply=%bitcast.69.reduce_sub_computation | reduce | bytes 2097154
  130.3 0.0 copy-start.6
  130.3 0.0 copy-start.5
  130.3 1.6 reshape.119
  131.9 4.2 %all-to-all-start = ((bf16[16,2,16384]{2,1,0:T(2,128)(2,1)}), bf16[16,2,16384]{2,1,0:T(2,128)(2,1)S(1)}, u32[]{:S(2)}, u32[]{:S(2)}) async-start(bf16[16,2,16384]{2,1,0:T(2,128)(2,1)} %reshape.119), calls=%async_computation | async-start | bytes 2097152 | tf_op jit(solution)/shard_map/all_to_all | solution.py:104
  136.0 0.0 copy-done.6
  136.0 0.6 reduce_sum.54
  136.7 46.1 %psum.35 = f32[]{:T(128)} all-reduce(f32[]{:T(128)} %reduce_sum.54), channel_id=1, replica_groups=mesh['region'=2,'member'=16] {'region','member'}, use_global_device_ids=true, to_apply=%region_1.0 | all-reduce | flops 1 | bytes 8 | tf_op jit(solution)/shard_map/psum | solution.py:98
  182.8 0.0 copy-done.5
  183.5 0.0 all-to-all-done
  183.5 1.1 reshape.120
  184.6 0.2 sub.25.clone
  184.8 0.5 fusion.24
  185.3 0.1 sqrt.14
  185.4 0.1 copy.41
  185.5 0.7 fusion.46
  186.2 0.2 copy.44
  186.3 0.6 gather_fusion
  187.0 0.1 copy.45
  187.0 0.6 convert_reduce_fusion
  187.6 0.5 subtract_multiply_fusion
  188.1 2.1 fusion.32
  190.2 0.6 copy.49
  190.8 30.3 %all_to_all.24 = bf16[16,32,1024]{2,1,0:T(8,128)(2,1)S(1)} all-to-all(bf16[16,32,1024]{2,1,0:T(8,128)(2,1)S(1)} %copy.49), channel_id=1, replica_groups=mesh['region'=2,'member'=16] {'member'}, dimensions={0} | all-to-all | bytes 2097152 | tf_op jit(solution)/shard_map/all_to_all | solution.py:108
  221.0 1.0 copy.73
  (12 shorter events, 0.3 us)
Async XLA Ops:
  7.2 104.1 %all-reduce.3.cloned.1.call-start = ((), (), s32[]{:S(2)}) async-start(), calls=%async_computation.2 | async-start | bytes 2097152 | tf_op jit(solution)/shard_map/psum | solution.py:11
  14.4 97.0 %copy-start = (bf16[1,512,1024]{2,1,0:T(8,128)(2,1)S(1)}, bf16[1,512,1024]{2,1,0:T(8,128)(2,1)}, u32[]{:S(2)}) copy-start(bf16[1,512,1024]{2,1,0:T(8,128)(2,1)} %param.18) | copy-start | bytes 3145732
  111.3 1.7 copy-start.1
  111.3 1.7 copy-start.2
  111.3 1.7 copy-start.3
  111.3 1.7 copy-start.4
  130.3 5.8 %copy-start.6 = (f32[32]{0:T(128)S(1)}, f32[32]{0:T(128)}, u32[]{:S(2)}) copy-start(f32[32]{0:T(128)} %param.20) | copy-start | bytes 388
  130.3 52.5 %copy-start.5 = (bf16[32,1024]{1,0:T(8,128)(2,1)S(1)}, bf16[32,1024]{1,0:T(8,128)(2,1)}, u32[]{:S(2)}) copy-start(bf16[32,1024]{1,0:T(8,128)(2,1)} %param.19) | copy-start | bytes 196612
  131.9 51.6 %all-to-all-start = ((bf16[16,2,16384]{2,1,0:T(2,128)(2,1)}), bf16[16,2,16384]{2,1,0:T(2,128)(2,1)S(1)}, u32[]{:S(2)}, u32[]{:S(2)}) async-start(bf16[16,2,16384]{2,1,0:T(2,128)(2,1)} %reshape.119), calls=%async_computation | async-start | bytes 2097152 | tf_op jit(solution)/shard_map/all_to_all | solution.py:104
Sparse Core Ops, SparseCore 0:
  15.4 95.8 all-reduce.2
where the time goes:
time: 230 us; the launch traced here: 229 us
  waiting for transfers between devices  96 us (42%)
  blocking collectives  76.4 us (33%)
  between operations  17.4 us (8%)
  matrix products  13 us (6%)
  other arithmetic  12.6 us (5%)
  local copies, waits for them, and re-layouts  9.16 us (4%)
  starting transfers between devices  4.19 us (2%)
    psum x1, waiting for transfers between devices, from_root(): return lax.psum(kept, axis)  96 us
    psum x1, blocking collectives, on_device(): weight_total = lax.psum(jnp.sum(area_weight), ('region', 'member'))  46.1 us
    all_to_all x1, blocking collectives, on_device(): lax.all_to_all(gradient, 'member', split_axis=0, concat_axis=1, tiled=True)  30.3 us
    dot_general x1, matrix products, apply_model(): jnp.dot(hidden, sample_outlet_matrix, preferred_element_type=jnp.float32)  8.1 us
    unnamed x1, other arithmetic  6.96 us
  transfers between devices with their start and end apart: 2, of which 1 were waited for; matrix products, arithmetic and copies ran while one was open for 0% of the time, Pallas kernels for 0%

commit v1 on v0

v1 whole, which is shorter than its diff:
```python
import functools
import math

import jax
import jax.numpy as jnp
from jax import lax
from jax.experimental import pallas as pl
from jax.experimental.pallas import tpu as pltpu
from jax.sharding import PartitionSpec as P

EPSILON = 1e-06
TOKENS_AT_ONCE = 16
HIDDEN_PIECES = 4
BF16 = jnp.bfloat16
F32 = jnp.float32


def swap(value, axis, bit):
    size = lax.axis_size(axis)
    return lax.ppermute(value, axis, [(i, i ^ bit) for i in range(size)])


def bits_of(size):
    return [1 << i for i in range(size.bit_length() - 1)]


def control_rows(analyses, owners):
    members = lax.axis_size("member")
    me = lax.axis_index("member")
    _, rows, features = analyses.shape
    blocks = owners.shape[0]
    lanes = members // blocks
    own = rows // members
    my_lane, my_block = me % lanes, me // lanes
    block_here = jnp.sum(jnp.where(owners == me, jnp.arange(blocks, dtype=jnp.int32), 0))
    held = lax.dynamic_slice_in_dim(analyses[0], block_here * (rows // blocks), rows // blocks, 0)
    held = held.reshape(1, lanes, own, features)
    for bit in reversed(bits_of(lanes)):
        halves = held.reshape(held.shape[0], 2, held.shape[1] // 2, own, features)
        mine = (my_lane // bit) % 2
        keep = lax.dynamic_index_in_dim(halves, mine, 1, keepdims=False)
        give = lax.dynamic_index_in_dim(halves, 1 - mine, 1, keepdims=False)
        held = jnp.concatenate([keep, swap(give, "member", bit)], axis=0)
    held = held.reshape(lanes, own, features)
    picked = []
    for block in range(blocks):
        apart = (owners[block] % lanes) ^ my_lane
        place = jnp.int32(0)
        for step, bit in enumerate(reversed(bits_of(lanes))):
            place = place + ((apart // bit) % 2) * (1 << step)
        picked.append(lax.dynamic_index_in_dim(held, place, 0, keepdims=False))
    held = jnp.stack(picked, axis=0)
    owner_block = owners // lanes
    for bit in bits_of(blocks):
        halves = held.reshape(held.shape[0] // 2, 2, own, features)
        mine = (my_block // bit) % 2
        keep = lax.dynamic_index_in_dim(halves, mine, 1, keepdims=False)
        give = lax.dynamic_index_in_dim(halves, 1 - mine, 1, keepdims=False)
        got = swap(give, "member", bit * lanes)
        ids = jnp.arange(halves.shape[0], dtype=jnp.int32) * (2 * bit) + my_block % (2 * bit)
        from_there = ((owner_block[ids] ^ my_block) // bit) % 2 == 1
        held = jnp.where(from_there[:, None, None], got, keep)
    return held[0]


def total_weight(area_weight):
    total = jnp.full((8, 128), jnp.sum(area_weight), F32)
    for bit in bits_of(lax.axis_size("member")):
        total = total + swap(total, "member", bit)
    for bit in bits_of(lax.axis_size("region")):
        total = total + swap(total, "region", bit)
    return total


def network(noise, latent, hidden_piece, pieces):
    members, tokens, features = noise.shape
    states = (noise.astype(F32) + latent.astype(F32)[None]).reshape(members * tokens, features)
    mean = jnp.sum(states * states, axis=-1, keepdims=True) * (1.0 / features)
    normed = (states * lax.rsqrt(mean + EPSILON)).astype(BF16)
    total = states
    for piece in range(pieces):
        total = total + hidden_piece(normed, piece)
    return total.astype(BF16)


def score(forecast, targets, scale, members, tokens):
    rows, features = forecast.shape
    gram = lax.dot_general(
        forecast, forecast, (((1,), (1,)), ((), ())), preferred_element_type=F32
    )
    first = lax.broadcasted_iota(jnp.int32, (rows, rows), 0)
    second = lax.broadcasted_iota(jnp.int32, (rows, rows), 1)
    same_row = first == second
    same_token = (first % tokens) == (second % tokens)
    on_diagonal = jnp.where(same_row, gram, 0.0)
    down = jnp.sum(on_diagonal, axis=1, keepdims=True)
    across = jnp.sum(on_diagonal, axis=0, keepdims=True)
    squared = jnp.maximum((down + across - 2.0 * gram) * (1.0 / features), 0.0) + EPSILON
    inverse = lax.rsqrt(squared)
    pairs = jnp.where(same_token, squared * inverse, 0.0)
    coeff = jnp.where(same_token & ~same_row, inverse, 0.0).astype(BF16)
    coeff_sum = jnp.sum(coeff.astype(F32), axis=1, keepdims=True)
    combined = jnp.dot(coeff, forecast, preferred_element_type=F32)
    values = forecast.astype(F32)
    apart = (
        values.reshape(members, tokens, features) - targets.astype(F32)[None]
    )
    squares = jnp.sum(apart * apart, axis=-1, keepdims=True) * (1.0 / features) + EPSILON
    inverse_spread = lax.rsqrt(squares)
    from_others = (coeff_sum * values - combined).reshape(members, tokens, features)
    gradient = scale[None] * (apart * inverse_spread - from_others * (1.0 / members))
    spread = jnp.sum(squares * inverse_spread, axis=0) * (1.0 / members)
    pair_sum = jnp.sum(jnp.sum(pairs, axis=1, keepdims=True).reshape(members, tokens, 1), axis=0)
    energy = scale * (spread - pair_sum * (1.0 / (2.0 * members * members)))
    return gradient, energy


def member_kernel(
    token_count,
    noise_ref,
    latent_ref,
    targets_ref,
    weight_ref,
    total_ref,
    inlet_hbm,
    outlet_hbm,
    gradient_ref,
    energy_ref,
    inlet,
    outlet,
    in_sems,
    out_sems,
):
    members, tokens, features = noise_ref.shape
    piece_width = inlet.shape[1] // HIDDEN_PIECES
    first = pl.program_id(0) == 0

    def copies(piece):
        part = pl.ds(piece * piece_width, piece_width)
        return (
            pltpu.make_async_copy(inlet_hbm.at[:, part], inlet.at[:, part], in_sems.at[piece]),
            pltpu.make_async_copy(outlet_hbm.at[part, :], outlet.at[part, :], out_sems.at[piece]),
        )

    @pl.when(first)
    def _():
        for piece in range(HIDDEN_PIECES):
            for copy in copies(piece):
                copy.start()

    def hidden_piece(normed, piece):
        @pl.when(first)
        def _():
            for copy in copies(piece):
                copy.wait()

        part = pl.ds(piece * piece_width, piece_width)
        hidden = jax.nn.gelu(
            jnp.dot(normed, inlet[:, part], preferred_element_type=F32), approximate=True
        ).astype(BF16)
        return jnp.dot(hidden, outlet[part, :], preferred_element_type=F32)

    forecast = network(noise_ref[...], latent_ref[...], hidden_piece, HIDDEN_PIECES)
    scale = weight_ref[...] * token_count / total_ref[0:1, 0:1]
    gradient, energy = score(forecast, targets_ref[...], scale, members, tokens)
    gradient_ref[...] = gradient.astype(BF16)
    energy_ref[...] = energy


def scored(noise, latent, targets, area_weight, total, inlet, outlet, token_count):
    members, own, features = noise.shape
    hidden = inlet.shape[1]
    tokens = TOKENS_AT_ONCE
    flops = 2 * members * own * (2 * features * hidden + 2 * members * tokens * features)
    return pl.pallas_call(
        functools.partial(member_kernel, token_count),
        grid=(own // tokens,),
        in_specs=[
            pl.BlockSpec((members, tokens, features), lambda i: (0, i, 0)),
            pl.BlockSpec((tokens, features), lambda i: (i, 0)),
            pl.BlockSpec((tokens, features), lambda i: (i, 0)),
            pl.BlockSpec((tokens, 1), lambda i: (i, 0)),
            pl.BlockSpec((8, 128), lambda i: (0, 0)),
            pl.BlockSpec(memory_space=pl.ANY),
            pl.BlockSpec(memory_space=pl.ANY),
        ],
        out_specs=[
            pl.BlockSpec((members, tokens, features), lambda i: (0, i, 0)),
            pl.BlockSpec((tokens, 1), lambda i: (i, 0)),
        ],
        out_shape=[
            jax.ShapeDtypeStruct((members, own, features), BF16),
            jax.ShapeDtypeStruct((own, 1), F32),
        ],
        scratch_shapes=[
            pltpu.VMEM((features, hidden), BF16),
            pltpu.VMEM((hidden, features), BF16),
            pltpu.SemaphoreType.DMA((HIDDEN_PIECES,)),
            pltpu.SemaphoreType.DMA((HIDDEN_PIECES,)),
        ],
        compiler_params=pltpu.CompilerParams(vmem_limit_bytes=40 * 2**20),
        cost_estimate=pl.CostEstimate(
            flops=flops, bytes_accessed=4 * features * hidden, transcendentals=0
        ),
    )(noise, latent, targets, area_weight, total, inlet, outlet)


def on_device(
    analyses,
    owners,
    noise,
    targets,
    area_weight,
    enc_weight,
    sample_inlet_matrix,
    sample_outlet_matrix,
):
    members = lax.axis_size("member")
    _, region_rows, features = noise.shape
    own = region_rows // members
    here = lax.all_to_all(
        noise.reshape(members, own, features), "member", split_axis=0, concat_axis=0, tiled=True
    )
    total = total_weight(area_weight)
    control = control_rows(analyses, owners)
    latent = jnp.dot(control, enc_weight, preferred_element_type=F32).astype(BF16)
    gradient, energy = scored(
        here,
        latent,
        targets,
        area_weight[:, None],
        total,
        sample_inlet_matrix,
        sample_outlet_matrix,
        float(region_rows * lax.axis_size("region")),
    )
    back = lax.all_to_all(gradient, "member", split_axis=0, concat_axis=0, tiled=True)
    return back.reshape(1, region_rows, features), energy[:, 0]


def solution(mesh):
    return jax.shard_map(
        on_device,
        mesh=mesh,
        in_specs=(
            P("member", "region", None),
            P(),
            P("member", "region", None),
            P(("region", "member"), None),
            P(("region", "member")),
            P(),
            P(),
            P(),
        ),
        out_specs=(P("member", "region", None), P(("region", "member"))),
        check_vma=False,
    )
```

time: 230 us -> 94.5 us (0.41)
  blocking collectives: 76.4 us -> 0 us
  waiting for transfers between devices: 96 us -> 33.5 us
  starting transfers between devices: 4.19 us -> 22.3 us
  matrix products: 13 us -> 0.47 us
  Pallas kernels: 0 us -> 9.99 us
  between operations: 17.4 us -> 10.1 us
  other arithmetic: 12.6 us -> 5.38 us
    psum x1 -> x0, waiting for transfers between devices: 96 us -> none  [from_root(): return lax.psum(kept, axis)]
    psum x1 -> x0, blocking collectives: 46.1 us -> none  [on_device(): weight_total = lax.psum(jnp.sum(area_weight), ('region', 'member'))]
    all_to_all x1 -> x0, blocking collectives: 30.3 us -> none  [on_device(): lax.all_to_all(gradient, 'member', split_axis=0, concat_axis=1, tiled=True)]
    all_to_all x1 -> x2, waiting for transfers between devices: 0.01 us -> 22.3 us  [the longest x1 22.3 us: on_device(): lax.all_to_all(gradient, 'member', split_axis=0, concat_axis=0, tiled=True)]
    dot_general x4 -> x1, matrix products: 13 us -> 0.47 us  [on_device(): jnp.dot(control, enc_weight, preferred_element_type=F32).astype(BF16)]
    ppermute x0 -> x9, waiting for transfers between devices: none -> 11.3 us  [swap(): return lax.ppermute(value, axis, [(i, i ^ bit) for i in range(size)])]
    ppermute x0 -> x9, starting transfers between devices: none -> 11.1 us  [swap(): return lax.ppermute(value, axis, [(i, i ^ bit) for i in range(size)])]
    pallas_call x0 -> x1, Pallas kernels: none -> 9.99 us  [scored(): pl.pallas_call(functools.partial(member_kernel, token_count), grid=(own /...]
  transfers between devices with their start and end apart: 2 -> 11, of which waited for: 1 -> 6; matrix products, arithmetic and copies ran while one was open for 0% -> 12% of each run, Pallas kernels for 0% -> 0%
where the time goes in v1:
time: 94.5 us; the launch traced here: 92.9 us
  waiting for transfers between devices  33.5 us (35%)
  starting transfers between devices  22.3 us (24%)
  local copies, waits for them, and re-layouts  11.2 us (12%)
  between operations  10.1 us (11%)
  Pallas kernels  9.99 us (11%)
  other arithmetic  5.38 us (6%)
    all_to_all x1, waiting for transfers between devices, on_device(): lax.all_to_all(gradient, 'member', split_axis=0, concat_axis=0, tiled=True)  22.3 us
    ppermute x9, waiting for transfers between devices, swap(): return lax.ppermute(value, axis, [(i, i ^ bit) for i in range(size)])  11.3 us
    ppermute x9, starting transfers between devices, swap(): return lax.ppermute(value, axis, [(i, i ^ bit) for i in range(size)])  11.1 us
    pallas_call x1, Pallas kernels, scored(): pl.pallas_call(functools.partial(member_kernel, token_count), grid=(own /...  9.99 us
    all_to_all x1, starting transfers between devices, on_device(): lax.all_to_all(noise.reshape(members, own, features), 'member', split_axi...  7.53 us
    unnamed x15, local copies, waits for them, and re-layouts  6.33 us
    all_to_all x1, starting transfers between devices, on_device(): lax.all_to_all(gradient, 'member', split_axis=0, concat_axis=0, tiled=True)  3.66 us
  transfers between devices with their start and end apart: 11, of which 6 were waited for; matrix products, arithmetic and copies ran while one was open for 12% of the time, Pallas kernels for 0%

profile of v1, /device:TPU:0, one launch (start us, length us, event | category | flops | bytes accessed | tf_op | source)
XLA Modules:
  0.0 92.9 jit_solution(14754713309749911349)
XLA Ops:
  0.6 0.0 copy-start
  0.6 0.0 copy-start.6
  0.7 7.5 %all-to-all-start = ((bf16[16,32,1024]{2,1,0:T(8,128)(2,1)}), bf16[16,32,1024]{2,1,0:T(8,128)(2,1)S(1)}, u32[]{:S(2)}, u32[]{:S(2)}) async-start(bf16[16,32,1024]{2,1,0:T(8,128)(2,1)} %bitcast.39), calls=%async_computation | async-start | bytes 2097152 | tf_op jit(solution)/shard_map/all_to_all | solution.py:221
  8.2 0.7 reduce_sum.19
  8.9 0.7 broadcast_in_dim.37
  9.6 0.5 collective-permute-start.4
  10.1 0.6 and_select_fusion.1
  11.4 1.0 %constant_dynamic-slice_fusion.1 = bf16[1,128,1024]{2,1,0:T(8,128)(2,1)S(1)} fusion(bf16[1,512,1024]{2,1,0:T(8,128)(2,1)} %param.8, s32[]{:T(128)S(6)} %select_n.214), kind=kLoop, calls=%fused_computation.35 | loop fusion | bytes 524292 | tf_op jit(solution)/shard_map/dynamic_slice | solution.py:36
  12.4 1.7 %collective-permute-start = (bf16[1,2,32,1024]{3,2,1,0:T(8,128)(2,1)S(1)}, bf16[1,2,32,1024]{3,2,1,0:T(8,128)(2,1)S(1)}, u32[]{:S(2)}, u32[]{:S(2)}) collective-permute-start(bf16[1,2,32,1024]{3,2,1,0:T(8,128)(2,1)S(1)} %get-tuple-element.23), channel_id=1, source_target_pairs={{0,2},{1,3},{2,0},{3,1},{4,6},{5,7},{6,4},{7,5},{8,10},{9,11},{10,... | collective-permute-start | bytes 393224 | tf_op jit(solution)/shard_map/ppermute | solution.py:20
  14.1 0.7 fusion.19
  14.8 0.5 fusion.18
  23.2 0.6 pad_clamp_fusion
  23.8 1.1 %gather_fusion = s32[2]{0:T(128)} fusion(s32[4]{0:T(128)S(1)} %get-tuple-element.25, s32[1024]{0:T(1024)S(1)} %pad_clamp_fusion), kind=kCustom, calls=%fused_computation | custom fusion | bytes 24 | tf_op jit(solution)/shard_map/gather | solution.py:61
  25.0 0.0 collective-permute-done
  25.0 0.1 collective-permute-start.1
  25.1 0.7 fusion.15
  25.8 0.6 collective-permute-done.1
  26.4 0.1 fusion.5
  26.6 1.5 %collective-permute-start.2 = (bf16[2,32,1024]{2,1,0:T(8,128)(2,1)S(1)}, bf16[2,32,1024]{2,1,0:T(8,128)(2,1)S(1)}, u32[]{:S(2)}, u32[]{:S(2)}) collective-permute-start(bf16[2,32,1024]{2,1,0:T(8,128)(2,1)S(1)} %dynamic-slice_bitcast_fusion), channel_id=1, source_target_pairs={{0,4},{1,5},{2,6},{3,7},{4,0},{5,1},{6,2},{7,3},{8,12},{9,13},{10,... | collective-permute-start | bytes 393224 | tf_op jit(solution)/shard_map/ppermute | solution.py:20
  28.1 0.0 collective-permute-done.4
  28.1 0.7 broadcast_add_fusion
  28.8 0.6 collective-permute-start.5
  29.4 5.2 %collective-permute-done.2 = bf16[2,32,1024]{2,1,0:T(8,128)(2,1)S(1)} collective-permute-done((bf16[2,32,1024]{2,1,0:T(8,128)(2,1)S(1)}, bf16[2,32,1024]{2,1,0:T(8,128)(2,1)S(1)}, u32[]{:S(2)}, u32[]{:S(2)}) %collective-permute-start.2) | collective-permute-done | bytes 131104 | tf_op jit(solution)/shard_map/ppermute | solution.py:20
  34.6 0.1 bitcast_select_fusion
  34.7 1.8 %collective-permute-start.3 = (bf16[1,32,1024]{2,1,0:T(8,128)(2,1)S(1)}, bf16[1,32,1024]{2,1,0:T(8,128)(2,1)S(1)}, u32[]{:S(2)}, u32[]{:S(2)}) collective-permute-start(bf16[1,32,1024]{2,1,0:T(8,128)(2,1)S(1)} %constant_dynamic-slice_fusion), channel_id=1, source_target_pairs={{0,8},{1,9},{2,10},{3,11},{4,12},{5,13},{6,14},{7,15},{8,0},{9,1},... | collective-permute-start | bytes 196616 | tf_op jit(solution)/shard_map/ppermute | solution.py:20
  36.5 0.0 collective-permute-done.5
  36.5 0.7 fusion.21
  37.2 2.5 %collective-permute-start.6 = (f32[8,128]{1,0:T(8,128)S(1)}, f32[8,128]{1,0:T(8,128)S(1)}, u32[]{:S(2)}, u32[]{:S(2)}) collective-permute-start(f32[8,128]{1,0:T(8,128)S(1)} %fusion.21), channel_id=1, source_target_pairs={{0,4},{1,5},{2,6},{3,7},{4,0},{5,1},{6,2},{7,3},{8,12},{9,13},{10,... | collective-permute-start | bytes 12296 | tf_op jit(solution)/shard_map/ppermute | solution.py:20
  39.8 1.6 %collective-permute-done.6 = f32[8,128]{1,0:T(8,128)S(1)} collective-permute-done((f32[8,128]{1,0:T(8,128)S(1)}, f32[8,128]{1,0:T(8,128)S(1)}, u32[]{:S(2)}, u32[]{:S(2)}) %collective-permute-start.6) | collective-permute-done | bytes 4128 | tf_op jit(solution)/shard_map/ppermute | solution.py:20
  41.4 0.7 collective-permute-start.7
  42.1 3.8 %collective-permute-done.7 = f32[8,128]{1,0:T(8,128)S(1)} collective-permute-done((f32[8,128]{1,0:T(8,128)S(1)}, f32[8,128]{1,0:T(8,128)S(1)}, u32[]{:S(2)}, u32[]{:S(2)}) %collective-permute-start.7) | collective-permute-done | bytes 4128 | tf_op jit(solution)/shard_map/ppermute | solution.py:20
  45.9 1.5 %collective-permute-start.8 = (f32[8,128]{1,0:T(8,128)S(1)}, f32[8,128]{1,0:T(8,128)S(1)}, u32[]{:S(2)}, u32[]{:S(2)}) collective-permute-start(f32[8,128]{1,0:T(8,128)S(1)} %add.238), channel_id=1, source_target_pairs={{0,16},{16,0},{1,17},{17,1},{2,18},{18,2},{3,19},{19,3},{4,20},{20... | collective-permute-start | bytes 12296 | tf_op jit(solution)/shard_map/ppermute | solution.py:20
  47.4 0.6 dynamic-slice.11
  48.6 0.7 copy.11.weight_ref
  49.4 0.1 collective-permute-done.8
  49.5 0.0 collective-permute-done.3
  49.5 0.5 convolution_convert_fusion.latent_ref
  50.0 0.0 all-to-all-done.noise_ref
  50.0 0.0 copy-start.2
  50.0 2.2 %copy-done.2 = bf16[1024,2048]{1,0:T(8,128)(2,1)S(1)} copy-done((bf16[1024,2048]{1,0:T(8,128)(2,1)S(1)}, bf16[1024,2048]{1,0:T(8,128)(2,1)}, u32[]{:S(2)}) %copy-start.2) | copy-done | bytes 4194328
  52.2 2.2 %copy-done.3 = bf16[2048,1024]{1,0:T(8,128)(2,1)S(1)} copy-done((bf16[2048,1024]{1,0:T(8,128)(2,1)S(1)}, bf16[2048,1024]{1,0:T(8,128)(2,1)}, u32[]{:S(2)}) %copy-start.3) | copy-done | bytes 4194328
  54.4 10.0 %shard_map.95 = (bf16[16,32,1024]{2,1,0:T(8,128)(2,1)S(1)}, f32[32,1]{1,0:T(8,128)S(1)}) custom-call(bf16[16,32,1024]{2,1,0:T(8,128)(2,1)S(1)} %all-to-all-done.noise_ref, bf16[32,1024]{1,0:T(8,128)(2,1)S(1)} %convolution_convert_fusion.latent_ref, bf16[32,1024]{1,0:T(8,128)(2,1)S(1)} %copy-done.4, f32[32,1]{1,0:T(8,128)S(1)} %copy.11.weight_ref, ...), custom_call_target="tpu_custom_call" | custom-call | flops 4831838208 | bytes 8388608 | tf_op jit(solution)/shard_map/pallas_call | solution.py:175
  64.4 0.0 copy-start.1
  64.4 1.0 %copy-done.1 = bf16[16,32,1024]{2,1,0:T(8,128)(2,1)} copy-done((bf16[16,32,1024]{2,1,0:T(8,128)(2,1)}, bf16[16,32,1024]{2,1,0:T(8,128)(2,1)S(1)}, u32[]{:S(2)}) %copy-start.1) | copy-done | bytes 1048600
  65.3 3.7 %all-to-all-start.1 = ((bf16[16,32,1024]{2,1,0:T(8,128)(2,1)}), bf16[16,32,1024]{2,1,0:T(8,128)(2,1)S(1)}, u32[]{:S(2)}, u32[]{:S(2)}) async-start(bf16[16,32,1024]{2,1,0:T(8,128)(2,1)} %copy-done.1), calls=%async_computation.1 | async-start | bytes 2097152 | tf_op jit(solution)/shard_map/all_to_all | solution.py:237
  69.0 0.6 reduce
  69.6 22.3 %all-to-all-done.1 = bf16[16,32,1024]{2,1,0:T(8,128)(2,1)S(1)} async-done(((bf16[16,32,1024]{2,1,0:T(8,128)(2,1)}), bf16[16,32,1024]{2,1,0:T(8,128)(2,1)S(1)}, u32[]{:S(2)}, u32[]{:S(2)}) %all-to-all-start.1) | async-done | bytes 1048608 | tf_op jit(solution)/shard_map/all_to_all | solution.py:237
  91.9 1.0 %copy.13 = bf16[1,512,1024]{2,1,0:T(8,128)(2,1)} copy(bf16[1,512,1024]{2,1,0:T(8,128)(2,1)S(1)} %bitcast.35) | data formatting | bytes 2097152
  (15 shorter events, 0.1 us)
Async XLA Ops:
  0.6 48.9 %copy-start = (bf16[1024,1024]{1,0:T(8,128)(2,1)S(1)}, bf16[1024,1024]{1,0:T(8,128)(2,1)}, u32[]{:S(2)}) copy-start(bf16[1024,1024]{1,0:T(8,128)(2,1)} %param.13) | copy-start | bytes 6291460
  0.6 7.6 %copy-start.6 = (f32[32]{0:T(128)S(1)}, f32[32]{0:T(128)}, u32[]{:S(2)}) copy-start(f32[32]{0:T(128)} %param.12) | copy-start | bytes 388
  0.7 9.4 %copy-start.5 = (s32[4]{0:T(128)S(1)}, s32[4]{0:T(128)}, u32[]{:S(2)}) copy-start(s32[4]{0:T(128)} %param.9) | copy-start | bytes 52
  0.7 49.3 %all-to-all-start = ((bf16[16,32,1024]{2,1,0:T(8,128)(2,1)}), bf16[16,32,1024]{2,1,0:T(8,128)(2,1)S(1)}, u32[]{:S(2)}, u32[]{:S(2)}) async-start(bf16[16,32,1024]{2,1,0:T(8,128)(2,1)} %bitcast.39), calls=%async_computation | async-start | bytes 2097152 | tf_op jit(solution)/shard_map/all_to_all | solution.py:221
  9.6 18.5 %collective-permute-start.4 = (f32[8,128]{1,0:T(8,128)S(1)}, f32[8,128]{1,0:T(8,128)S(1)}, u32[]{:S(2)}, u32[]{:S(2)}) collective-permute-start(f32[8,128]{1,0:T(8,128)S(1)} %broadcast_in_dim.37), channel_id=1, source_target_pairs={{0,1},{1,0},{2,3},{3,2},{4,5},{5,4},{6,7},{7,6},{8,9},{9,8},{10,11... | collective-permute-start | bytes 12296 | tf_op jit(solution)/shard_map/ppermute | solution.py:20
  12.4 12.6 %collective-permute-start = (bf16[1,2,32,1024]{3,2,1,0:T(8,128)(2,1)S(1)}, bf16[1,2,32,1024]{3,2,1,0:T(8,128)(2,1)S(1)}, u32[]{:S(2)}, u32[]{:S(2)}) collective-permute-start(bf16[1,2,32,1024]{3,2,1,0:T(8,128)(2,1)S(1)} %get-tuple-element.23), channel_id=1, source_target_pairs={{0,2},{1,3},{2,0},{3,1},{4,6},{5,7},{6,4},{7,5},{8,10},{9,11},{10,... | collective-permute-start | bytes 393224 | tf_op jit(solution)/shard_map/ppermute | solution.py:20
  25.0 1.4 %collective-permute-start.1 = (bf16[2,1,32,1024]{3,2,1,0:T(8,128)(2,1)S(1)}, bf16[2,1,32,1024]{3,2,1,0:T(8,128)(2,1)S(1)}, u32[]{:S(2)}, u32[]{:S(2)}) collective-permute-start(bf16[2,1,32,1024]{3,2,1,0:T(8,128)(2,1)S(1)} %get-tuple-element.21), channel_id=1, source_target_pairs={{0,1},{1,0},{2,3},{3,2},{4,5},{5,4},{6,7},{7,6},{8,9},{9,8},{10,11... | collective-permute-start | bytes 393224 | tf_op jit(solution)/shard_map/ppermute | solution.py:20
  26.4 23.6 %copy-start.4 = (bf16[32,1024]{1,0:T(8,128)(2,1)S(1)}, bf16[32,1024]{1,0:T(8,128)(2,1)}, u32[]{:S(2)}) copy-start(bf16[32,1024]{1,0:T(8,128)(2,1)} %targets_ref.1) | copy-start | bytes 196612
  26.6 8.1 %collective-permute-start.2 = (bf16[2,32,1024]{2,1,0:T(8,128)(2,1)S(1)}, bf16[2,32,1024]{2,1,0:T(8,128)(2,1)S(1)}, u32[]{:S(2)}, u32[]{:S(2)}) collective-permute-start(bf16[2,32,1024]{2,1,0:T(8,128)(2,1)S(1)} %dynamic-slice_bitcast_fusion), channel_id=1, source_target_pairs={{0,4},{1,5},{2,6},{3,7},{4,0},{5,1},{6,2},{7,3},{8,12},{9,13},{10,... | collective-permute-start | bytes 393224 | tf_op jit(solution)/shard_map/ppermute | solution.py:20
  28.8 7.7 %collective-permute-start.5 = (f32[8,128]{1,0:T(8,128)S(1)}, f32[8,128]{1,0:T(8,128)S(1)}, u32[]{:S(2)}, u32[]{:S(2)}) collective-permute-start(f32[8,128]{1,0:T(8,128)S(1)} %broadcast_add_fusion), channel_id=1, source_target_pairs={{0,2},{1,3},{2,0},{3,1},{4,6},{5,7},{6,4},{7,5},{8,10},{9,11},{10,... | collective-permute-start | bytes 12296 | tf_op jit(solution)/shard_map/ppermute | solution.py:20
  34.7 14.7 %collective-permute-start.3 = (bf16[1,32,1024]{2,1,0:T(8,128)(2,1)S(1)}, bf16[1,32,1024]{2,1,0:T(8,128)(2,1)S(1)}, u32[]{:S(2)}, u32[]{:S(2)}) collective-permute-start(bf16[1,32,1024]{2,1,0:T(8,128)(2,1)S(1)} %constant_dynamic-slice_fusion), channel_id=1, source_target_pairs={{0,8},{1,9},{2,10},{3,11},{4,12},{5,13},{6,14},{7,15},{8,0},{9,1},... | collective-permute-start | bytes 196616 | tf_op jit(solution)/shard_map/ppermute | solution.py:20
  37.2 4.1 %collective-permute-start.6 = (f32[8,128]{1,0:T(8,128)S(1)}, f32[8,128]{1,0:T(8,128)S(1)}, u32[]{:S(2)}, u32[]{:S(2)}) collective-permute-start(f32[8,128]{1,0:T(8,128)S(1)} %fusion.21), channel_id=1, source_target_pairs={{0,4},{1,5},{2,6},{3,7},{4,0},{5,1},{6,2},{7,3},{8,12},{9,13},{10,... | collective-permute-start | bytes 12296 | tf_op jit(solution)/shard_map/ppermute | solution.py:20
  41.4 4.5 %collective-permute-start.7 = (f32[8,128]{1,0:T(8,128)S(1)}, f32[8,128]{1,0:T(8,128)S(1)}, u32[]{:S(2)}, u32[]{:S(2)}) collective-permute-start(f32[8,128]{1,0:T(8,128)S(1)} %add.237), channel_id=1, source_target_pairs={{0,8},{1,9},{2,10},{3,11},{4,12},{5,13},{6,14},{7,15},{8,0},{9,1},... | collective-permute-start | bytes 12296 | tf_op jit(solution)/shard_map/ppermute | solution.py:20
  45.9 3.6 %collective-permute-start.8 = (f32[8,128]{1,0:T(8,128)S(1)}, f32[8,128]{1,0:T(8,128)S(1)}, u32[]{:S(2)}, u32[]{:S(2)}) collective-permute-start(f32[8,128]{1,0:T(8,128)S(1)} %add.238), channel_id=1, source_target_pairs={{0,16},{16,0},{1,17},{17,1},{2,18},{18,2},{3,19},{19,3},{4,20},{20... | collective-permute-start | bytes 12296 | tf_op jit(solution)/shard_map/ppermute | solution.py:20
  50.0 2.2 %copy-start.2 = (bf16[1024,2048]{1,0:T(8,128)(2,1)S(1)}, bf16[1024,2048]{1,0:T(8,128)(2,1)}, u32[]{:S(2)}) copy-start(bf16[1024,2048]{1,0:T(8,128)(2,1)} %inlet_hbm.1) | copy-start | bytes 12582916
  52.2 2.2 %copy-start.3 = (bf16[2048,1024]{1,0:T(8,128)(2,1)S(1)}, bf16[2048,1024]{1,0:T(8,128)(2,1)}, u32[]{:S(2)}) copy-start(bf16[2048,1024]{1,0:T(8,128)(2,1)} %outlet_hbm.1) | copy-start | bytes 12582916
  64.4 1.0 %copy-start.1 = (bf16[16,32,1024]{2,1,0:T(8,128)(2,1)}, bf16[16,32,1024]{2,1,0:T(8,128)(2,1)S(1)}, u32[]{:S(2)}) copy-start(bf16[16,32,1024]{2,1,0:T(8,128)(2,1)S(1)} %get-tuple-element.4) | copy-start | bytes 3145732
  65.3 26.6 %all-to-all-start.1 = ((bf16[16,32,1024]{2,1,0:T(8,128)(2,1)}), bf16[16,32,1024]{2,1,0:T(8,128)(2,1)S(1)}, u32[]{:S(2)}, u32[]{:S(2)}) async-start(bf16[16,32,1024]{2,1,0:T(8,128)(2,1)} %copy-done.1), calls=%async_computation.1 | async-start | bytes 2097152 | tf_op jit(solution)/shard_map/all_to_all | solution.py:237

commit v2 on v1

v2 whole, which is shorter than its diff:
```python
import functools

import jax
import jax.numpy as jnp
from jax import lax
from jax.experimental import pallas as pl
from jax.experimental.pallas import tpu as pltpu
from jax.sharding import PartitionSpec as P

EPSILON = 1e-06
TOKENS_AT_ONCE = 16
HIDDEN_PIECES = 2
TAIL = 16
BF16 = jnp.bfloat16
F32 = jnp.float32

VMEM = pl.BlockSpec(memory_space=pltpu.VMEM)
SMEM = pl.BlockSpec(memory_space=pltpu.SMEM)
ANY = pl.BlockSpec(memory_space=pl.ANY)


def swap(value, axis, bit):
    size = lax.axis_size(axis)
    return lax.ppermute(value, axis, [(i, i ^ bit) for i in range(size)])


def local_call(kernel, out_shape, in_specs, flops=0, moved=0, scratch=(), limit=40):
    return pl.pallas_call(
        kernel,
        in_specs=in_specs,
        out_specs=[VMEM] * len(out_shape),
        out_shape=out_shape,
        scratch_shapes=list(scratch),
        compiler_params=pltpu.CompilerParams(vmem_limit_bytes=limit * 2**20),
        cost_estimate=pl.CostEstimate(flops=flops, bytes_accessed=moved, transcendentals=0),
    )


def weight_rows(total, features):
    high = total.astype(BF16).astype(F32)
    middle = (total - high).astype(BF16).astype(F32)
    low = total - high - middle
    row = lax.broadcasted_iota(jnp.int32, (TAIL, features), 0)
    picked = jnp.where(row == 0, high, jnp.where(row == 1, middle, jnp.where(row == 2, low, 0.0)))
    return picked.astype(BF16)


def weight_from(rows):
    return jnp.sum(rows[:, 0:128].astype(F32), axis=0, keepdims=True)[:, 0:1]


def lanes_kernel(lanes, owners, analyses, weight, *refs):
    outs, sems = refs[:lanes], refs[lanes]
    own = outs[0].shape[0] - TAIL
    features = outs[0].shape[1]
    me = lax.axis_index("member")
    lane = me % lanes
    block = jnp.int32(0)
    for b in range(owners.shape[0]):
        block = jnp.where(owners[b] == me, b, block)
    copies = []
    for k in range(lanes):
        start = pl.multiple_of((block * lanes + (lane ^ k)) * own, own)
        copies.append(
            pltpu.make_async_copy(
                analyses.at[0, pl.ds(start, own), :], outs[k].at[pl.ds(0, own), :], sems.at[k]
            )
        )
    for copy in copies:
        copy.start()
    total = jnp.sum(weight[...], axis=1, keepdims=True)
    rows = weight_rows(total, features)
    for k in range(lanes):
        outs[k][pl.ds(own, TAIL), :] = rows
    for copy in copies:
        copy.wait()


def blocks_kernel(lanes, blocks, owners, *refs):
    held, (keep, give, total_out) = refs[:lanes], refs[lanes:]
    own, features = keep.shape[1], keep.shape[2]
    me = lax.axis_index("member")
    lane, here = me % lanes, me // lanes

    def rows_of(block):
        place = (owners[block] % lanes) ^ lane
        rows = held[0][pl.ds(0, own), :]
        for k in range(1, lanes):
            rows = jnp.where(place == k, held[k][pl.ds(0, own), :], rows)
        return rows

    side = here % 2
    for j in range(blocks // 2):
        keep[j] = rows_of(2 * j + side)
        give[pl.ds(j * own, own), :] = rows_of(2 * j + 1 - side)
    total = weight_from(held[0][pl.ds(own, TAIL), :])
    for k in range(1, lanes):
        total = total + weight_from(held[k][pl.ds(own, TAIL), :])
    give[pl.ds(blocks // 2 * own, TAIL), :] = weight_rows(total, features)
    total_out[...] = jnp.broadcast_to(total, total_out.shape)


def merged(owners, lanes, here, bit, keep, got, j, own):
    block = j * (2 * bit) + here % (2 * bit)
    there = ((owners[block] // lanes) ^ here) // bit % 2
    return jnp.where(there == 1, got[pl.ds(j * own, own), :], keep[j])


def halve_kernel(lanes, bit, owners, keep, got, total, keep_out, give, total_out):
    count, own, features = keep.shape
    here = lax.axis_index("member") // lanes
    side = here // (2 * bit) % 2
    rows = [merged(owners, lanes, here, bit, keep, got, j, own) for j in range(count)]
    for j in range(count // 2):
        keep_out[j] = jnp.where(side == 1, rows[2 * j + 1], rows[2 * j])
        give[pl.ds(j * own, own), :] = jnp.where(side == 1, rows[2 * j], rows[2 * j + 1])
    summed = total[0:1, 0:1] + weight_from(got[pl.ds(count * own, TAIL), :])
    give[pl.ds(count // 2 * own, TAIL), :] = weight_rows(summed, features)
    total_out[...] = jnp.broadcast_to(summed, total_out.shape)


def column(row):
    size = row.shape[1]
    first = lax.broadcasted_iota(jnp.int32, (size, size), 0)
    second = lax.broadcasted_iota(jnp.int32, (size, size), 1)
    return jnp.sum(jnp.where(first == second, row, 0.0), axis=1, keepdims=True)


def encode_kernel(lanes, bit, count, owners, keep, got, total, weight, encoder, latent, scale):
    _, own, _ = keep.shape
    here = lax.axis_index("member") // lanes
    control = merged(owners, lanes, here, bit, keep, got, 0, own)
    latent[...] = jnp.dot(control, encoder[...], preferred_element_type=F32).astype(BF16)
    summed = total[0:1, 0:1] + weight_from(got[pl.ds(own, TAIL), :])
    scale[...] = column(weight[...]) * (count / summed)


def latent_and_scale(analyses, owners, weight, weight_across, encoder):
    members = lax.axis_size("member")
    _, rows, features = analyses.shape
    blocks = owners.shape[0]
    lanes, own = members // blocks, rows // members
    count = float(rows * lax.axis_size("region"))
    small = jax.ShapeDtypeStruct((8, 128), F32)

    def some(rows):
        return jax.ShapeDtypeStruct((rows, features), BF16)

    def kept(many):
        return jax.ShapeDtypeStruct((many, own, features), BF16)

    by_lane = local_call(
        functools.partial(lanes_kernel, lanes),
        [some(own + TAIL)] * lanes,
        [SMEM, ANY, VMEM],
        scratch=[pltpu.SemaphoreType.DMA((lanes,))],
        limit=8,
    )(owners, analyses, weight_across)
    by_lane = [by_lane[0]] + [swap(by_lane[k], "member", k) for k in range(1, lanes)]
    keep, give, total = local_call(
        functools.partial(blocks_kernel, lanes, blocks),
        [kept(blocks // 2), some(blocks // 2 * own + TAIL), small],
        [SMEM] + [VMEM] * lanes,
        limit=8,
    )(owners, *by_lane)
    bit = 1
    while 2 * bit < blocks:
        got = swap(give, "member", bit * lanes)
        many = keep.shape[0] // 2
        keep, give, total = local_call(
            functools.partial(halve_kernel, lanes, bit),
            [kept(many), some(many * own + TAIL), small],
            [SMEM] + [VMEM] * 3,
            limit=8,
        )(owners, keep, got, total)
        bit *= 2
    got = swap(give, "member", bit * lanes)
    return local_call(
        functools.partial(encode_kernel, lanes, bit, count),
        [some(own), jax.ShapeDtypeStruct((own, 1), F32)],
        [SMEM] + [VMEM] * 5,
        flops=2 * own * features * features,
        limit=8,
    )(owners, keep, got, total, weight, encoder)


def network(noise, latent, hidden_piece, pieces):
    members, tokens, features = noise.shape
    states = (noise.astype(F32) + latent.astype(F32)[None]).reshape(members * tokens, features)
    mean = jnp.sum(states * states, axis=-1, keepdims=True) * (1.0 / features)
    normed = (states * lax.rsqrt(mean + EPSILON)).astype(BF16)
    total = states
    for piece in range(pieces):
        total = total + hidden_piece(normed, piece)
    return total.astype(BF16)


def score(forecast, targets, scale, members, tokens):
    rows, features = forecast.shape
    gram = lax.dot_general(
        forecast, forecast, (((1,), (1,)), ((), ())), preferred_element_type=F32
    )
    first = lax.broadcasted_iota(jnp.int32, (rows, rows), 0)
    second = lax.broadcasted_iota(jnp.int32, (rows, rows), 1)
    same_row = first == second
    same_token = (first % tokens) == (second % tokens)
    on_diagonal = jnp.where(same_row, gram, 0.0)
    down = jnp.sum(on_diagonal, axis=1, keepdims=True)
    across = jnp.sum(on_diagonal, axis=0, keepdims=True)
    squared = jnp.maximum((down + across - 2.0 * gram) * (1.0 / features), 0.0) + EPSILON
    inverse = lax.rsqrt(squared)
    pairs = jnp.where(same_token, squared * inverse, 0.0)
    coeff = jnp.where(same_token & ~same_row, inverse, 0.0).astype(BF16)
    coeff_sum = jnp.sum(coeff.astype(F32), axis=1, keepdims=True)
    combined = jnp.dot(coeff, forecast, preferred_element_type=F32)
    values = forecast.astype(F32)
    apart = (
        values.reshape(members, tokens, features) - targets.astype(F32)[None]
    )
    squares = jnp.sum(apart * apart, axis=-1, keepdims=True) * (1.0 / features) + EPSILON
    inverse_spread = lax.rsqrt(squares)
    from_others = (coeff_sum * values - combined).reshape(members, tokens, features)
    gradient = scale[None] * (apart * inverse_spread - from_others * (1.0 / members))
    spread = jnp.sum(squares * inverse_spread, axis=0) * (1.0 / members)
    pair_sum = jnp.sum(jnp.sum(pairs, axis=1, keepdims=True).reshape(members, tokens, 1), axis=0)
    energy = scale * (spread - pair_sum * (1.0 / (2.0 * members * members)))
    return gradient, energy


def member_kernel(noise, latent, targets, scale, inlet, outlet, gradient_out, energy_out):
    members, own, features = noise.shape
    width = inlet.shape[1] // HIDDEN_PIECES

    def hidden_piece(normed, piece):
        part = slice(piece * width, (piece + 1) * width)
        hidden = jax.nn.gelu(
            jnp.dot(normed, inlet[:, part], preferred_element_type=F32), approximate=True
        ).astype(BF16)
        return jnp.dot(hidden, outlet[part, :], preferred_element_type=F32)

    forecast = network(noise[...], latent[...], hidden_piece, HIDDEN_PIECES)
    forecast = forecast.reshape(members, own, features)
    for first in range(0, own, TOKENS_AT_ONCE):
        here = slice(first, first + TOKENS_AT_ONCE)
        gradient, energy = score(
            forecast[:, here].reshape(members * TOKENS_AT_ONCE, features),
            targets[here, :],
            scale[here, :],
            members,
            TOKENS_AT_ONCE,
        )
        gradient_out[:, here, :] = gradient.astype(BF16)
        energy_out[here, :] = energy


def on_device(
    analyses,
    owners,
    noise,
    targets,
    area_weight,
    enc_weight,
    sample_inlet_matrix,
    sample_outlet_matrix,
):
    members = lax.axis_size("member")
    _, region_rows, features = noise.shape
    hidden = sample_inlet_matrix.shape[1]
    own = region_rows // members
    regions = lax.axis_size("region")
    weight_across = area_weight
    for bit in (1 << i for i in range(regions.bit_length() - 1)):
        weight_across = weight_across + swap(weight_across, "region", bit)
    here = lax.all_to_all(
        noise.reshape(members, own, features), "member", split_axis=0, concat_axis=0, tiled=True
    )
    latent, scale = latent_and_scale(
        analyses, owners, area_weight[None], weight_across[None], enc_weight
    )
    gradient, energy = local_call(
        member_kernel,
        [
            jax.ShapeDtypeStruct((members, own, features), BF16),
            jax.ShapeDtypeStruct((own, 1), F32),
        ],
        [VMEM] * 6,
        flops=4 * members * own * features * (hidden + members),
        moved=4 * features * hidden,
    )(here, latent, targets, scale, sample_inlet_matrix, sample_outlet_matrix)
    back = lax.all_to_all(gradient, "member", split_axis=0, concat_axis=0, tiled=True)
    return back.reshape(1, region_rows, features), energy[:, 0]


def solution(mesh):
    return jax.shard_map(
        on_device,
        mesh=mesh,
        in_specs=(
            P("member", "region", None),
            P(),
            P("member", "region", None),
            P(("region", "member"), None),
            P(("region", "member")),
            P(),
            P(),
            P(),
        ),
        out_specs=(P("member", "region", None), P(("region", "member"))),
        check_vma=False,
    )
```

time: 94.5 us -> 87.5 us (0.926)
  waiting for transfers between devices: 33.5 us -> 45.3 us
  between operations: 10.1 us -> 0.71 us
  other arithmetic: 5.38 us -> 1.29 us
  starting transfers between devices: 22.3 us -> 19.3 us
  local copies, waits for them, and re-layouts: 11.2 us -> 8.72 us
    ppermute x9 -> x6, waiting for transfers between devices: 11.3 us -> 22.9 us  [swap(): return lax.ppermute(value, axis, [(i, i ^ bit) for i in range(size)])]
    ppermute x9 -> x6, starting transfers between devices: 11.1 us -> 7.95 us  [swap(): return lax.ppermute(value, axis, [(i, i ^ bit) for i in range(size)])]
    unnamed x15, local copies, waits for them, and re-layouts: 6.33 us -> 8.72 us
    gather x2 -> x0, local copies, waits for them, and re-layouts: 1.72 us -> none  [control_rows(): from_there = (owner_block[ids] ^ my_block) // bit % 2 == 1]
    broadcast_in_dim x2 -> x0, local copies, waits for them, and re-layouts: 1.42 us -> none  [the longest x1 0.74 us: on_device(): area_weight[:, None]]
    add x5 -> x0, other arithmetic: 1.39 us -> none  [the longest x4 1.38 us: total_weight(): total = total + swap(total, 'member', bit)]
    select_n x3 -> x0, other arithmetic: 1.24 us -> none  [the longest x1 0.63 us: control_rows(): owner_block = owners // lanes]
    dynamic_slice x1 -> x0, local copies, waits for them, and re-layouts: 0.97 us -> none  [control_rows(): lax.dynamic_slice_in_dim(analyses[0], block_here * (rows // blocks), rows...]
  transfers between devices with their start and end apart: 11 -> 8, of which waited for: 6 -> 6; matrix products, arithmetic and copies ran while one was open for 12% -> 1% of each run, Pallas kernels for 0% -> 4%
where the time goes in v2:
time: 87.5 us; the launch traced here: 85.9 us
  waiting for transfers between devices  45.3 us (52%)
  starting transfers between devices  19.3 us (22%)
  Pallas kernels  10.6 us (12%)
  local copies, waits for them, and re-layouts  8.72 us (10%)
  other arithmetic  1.29 us (1%)
    ppermute x6, waiting for transfers between devices, swap(): return lax.ppermute(value, axis, [(i, i ^ bit) for i in range(size)])  22.9 us
    all_to_all x1, waiting for transfers between devices, on_device(): lax.all_to_all(gradient, 'member', split_axis=0, concat_axis=0, tiled=True)  22.3 us
    unnamed x15, local copies, waits for them, and re-layouts  8.72 us
    ppermute x6, starting transfers between devices, swap(): return lax.ppermute(value, axis, [(i, i ^ bit) for i in range(size)])  7.95 us
    all_to_all x1, starting transfers between devices, on_device(): lax.all_to_all(noise.reshape(members, own, features), 'member', split_axi...  7.53 us
    pallas_call x1, Pallas kernels, on_device(): local_call(member_kernel, [jax.ShapeDtypeStruct((members, own, features),...  7.34 us
    all_to_all x1, starting transfers between devices, on_device(): lax.all_to_all(gradient, 'member', split_axis=0, concat_axis=0, tiled=True)  3.85 us
  transfers between devices with their start and end apart: 8, of which 6 were waited for; matrix products, arithmetic and copies ran while one was open for 1% of the time, Pallas kernels for 4%

profile of v2, /device:TPU:0, one launch (start us, length us, event | category | flops | bytes accessed | tf_op | source)
XLA Modules:
  0.0 85.9 jit_solution(15737121918072197681)
XLA Ops:
  0.6 0.0 copy-start
  0.6 7.5 %all-to-all-start = ((bf16[16,32,1024]{2,1,0:T(8,128)(2,1)}), bf16[16,32,1024]{2,1,0:T(8,128)(2,1)S(1)}, u32[]{:S(2)}, u32[]{:S(2)}) async-start(bf16[16,32,1024]{2,1,0:T(8,128)(2,1)} %bitcast.7), calls=%async_computation | async-start | bytes 2097152 | tf_op jit(solution)/shard_map/all_to_all | solution.py:274
  8.2 1.6 %collective-permute-start = (f32[32]{0:T(128)}, f32[32]{0:T(128)S(1)}, u32[]{:S(2)}, u32[]{:S(2)}) collective-permute-start(f32[32]{0:T(128)} %param.12), channel_id=1, source_target_pairs={{0,16},{16,0},{1,17},{17,1},{2,18},{18,2},{3,19},{19,3},{4,20},{20... | collective-permute-start | bytes 392 | tf_op jit(solution)/shard_map/ppermute | solution.py:24
  9.7 2.2 %collective-permute-done = f32[32]{0:T(128)S(1)} collective-permute-done((f32[32]{0:T(128)}, f32[32]{0:T(128)S(1)}, u32[]{:S(2)}, u32[]{:S(2)}) %collective-permute-start) | collective-permute-done | bytes 160 | tf_op jit(solution)/shard_map/ppermute | solution.py:24
  11.9 0.7 add_bitcast_fusion.weight
  12.6 0.0 copy-start.1
  12.6 1.2 %copy-done.1 = bf16[1,512,1024]{2,1,0:T(8,128)(2,1)S(1)} copy-done((bf16[1,512,1024]{2,1,0:T(8,128)(2,1)S(1)}, bf16[1,512,1024]{2,1,0:T(8,128)(2,1)}, u32[]{:S(2)}) %copy-start.1) | copy-done | bytes 1048600
  13.8 0.0 copy-start.2
  13.8 0.7 copy-done.2
  14.5 1.0 %shard_map.95 = (bf16[48,1024]{1,0:T(8,128)(2,1)S(1)}, bf16[48,1024]{1,0:T(8,128)(2,1)S(1)}, bf16[48,1024]{1,0:T(8,128)(2,1)S(1)}, bf16[48,1024]{1,0:T(8,128)(2,1)S(1)}) custom-call(s32[4]{0:T(128)S(1)} %copy-done.2, bf16[1,512,1024]{2,1,0:T(8,128)(2,1)S(1)} %copy-done.1, f32[1,32]{1,0:T(1,128)S(1)} %add_bitcast_fusion.weight), custom_call_target="tpu_custom_call" | custom-call | tf_op jit(solution)/shard_map/pallas_call | solution.py:152
  15.5 0.1 collective-permute-start.1
  15.6 1.9 %collective-permute-start.2 = (bf16[48,1024]{1,0:T(8,128)(2,1)S(1)}, bf16[48,1024]{1,0:T(8,128)(2,1)S(1)}, u32[]{:S(2)}, u32[]{:S(2)}) collective-permute-start(bf16[48,1024]{1,0:T(8,128)(2,1)S(1)} %get-tuple-element.18), channel_id=1, source_target_pairs={{0,2},{1,3},{2,0},{3,1},{4,6},{5,7},{6,4},{7,5},{8,10},{9,11},{10,... | collective-permute-start | bytes 294920 | tf_op jit(solution)/shard_map/ppermute | solution.py:24
  17.5 0.1 collective-permute-start.3
  17.6 0.0 collective-permute-done.1.refs_1_
  17.6 5.6 %collective-permute-done.2.refs_2_ = bf16[48,1024]{1,0:T(8,128)(2,1)S(1)} collective-permute-done((bf16[48,1024]{1,0:T(8,128)(2,1)S(1)}, bf16[48,1024]{1,0:T(8,128)(2,1)S(1)}, u32[]{:S(2)}, u32[]{:S(2)}) %collective-permute-start.2) | collective-permute-done | bytes 98336 | tf_op jit(solution)/shard_map/ppermute | solution.py:24
  23.2 3.1 %collective-permute-done.3.refs_3_ = bf16[48,1024]{1,0:T(8,128)(2,1)S(1)} collective-permute-done((bf16[48,1024]{1,0:T(8,128)(2,1)S(1)}, bf16[48,1024]{1,0:T(8,128)(2,1)S(1)}, u32[]{:S(2)}, u32[]{:S(2)}) %collective-permute-start.3) | collective-permute-done | bytes 98336 | tf_op jit(solution)/shard_map/ppermute | solution.py:24
  26.3 0.6 shard_map.96
  26.9 2.3 %collective-permute-start.4 = (bf16[80,1024]{1,0:T(8,128)(2,1)S(1)}, bf16[80,1024]{1,0:T(8,128)(2,1)S(1)}, u32[]{:S(2)}, u32[]{:S(2)}) collective-permute-start(bf16[80,1024]{1,0:T(8,128)(2,1)S(1)} %get-tuple-element.21), channel_id=1, source_target_pairs={{0,4},{1,5},{2,6},{3,7},{4,0},{5,1},{6,2},{7,3},{8,12},{9,13},{10,... | collective-permute-start | bytes 491528 | tf_op jit(solution)/shard_map/ppermute | solution.py:24
  29.2 6.2 %collective-permute-done.4.got = bf16[80,1024]{1,0:T(8,128)(2,1)S(1)} collective-permute-done((bf16[80,1024]{1,0:T(8,128)(2,1)S(1)}, bf16[80,1024]{1,0:T(8,128)(2,1)S(1)}, u32[]{:S(2)}, u32[]{:S(2)}) %collective-permute-start.4) | collective-permute-done | bytes 163872 | tf_op jit(solution)/shard_map/ppermute | solution.py:24
  35.4 0.6 shard_map.97
  36.0 2.0 %collective-permute-start.5 = (bf16[48,1024]{1,0:T(8,128)(2,1)S(1)}, bf16[48,1024]{1,0:T(8,128)(2,1)S(1)}, u32[]{:S(2)}, u32[]{:S(2)}) collective-permute-start(bf16[48,1024]{1,0:T(8,128)(2,1)S(1)} %get-tuple-element.24), channel_id=1, source_target_pairs={{0,8},{1,9},{2,10},{3,11},{4,12},{5,13},{6,14},{7,15},{8,0},{9,1},... | collective-permute-start | bytes 294920 | tf_op jit(solution)/shard_map/ppermute | solution.py:24
  38.1 5.8 %collective-permute-done.5.got = bf16[48,1024]{1,0:T(8,128)(2,1)S(1)} collective-permute-done((bf16[48,1024]{1,0:T(8,128)(2,1)S(1)}, bf16[48,1024]{1,0:T(8,128)(2,1)S(1)}, u32[]{:S(2)}, u32[]{:S(2)}) %collective-permute-start.5) | collective-permute-done | bytes 98336 | tf_op jit(solution)/shard_map/ppermute | solution.py:24
  43.9 0.0 copy-done
  43.9 0.0 copy-start.3
  43.9 0.7 copy-done.3
  44.5 1.0 %shard_map.98 = (bf16[32,1024]{1,0:T(8,128)(2,1)S(1)}, f32[32,1]{1,0:T(8,128)S(1)}) custom-call(s32[4]{0:T(128)S(1)} %copy-done.2, bf16[1,32,1024]{2,1,0:T(8,128)(2,1)S(1)} %get-tuple-element.23.keep, bf16[48,1024]{1,0:T(8,128)(2,1)S(1)} %collective-permute-done.5.got, f32[8,128]{1,0:T(8,128)S(1)} %get-tuple-element.25.total, f32[1,32]{1,0:T(1,128)S(1)} %bitcast.5, ...), custom_call_target="tpu_custom_call" | custom-call | flops 67108864 | tf_op jit(solution)/shard_map/pallas_call | solution.py:178
  45.5 0.0 all-to-all-done.noise
  45.6 0.0 copy-start.4
  45.6 2.2 %copy-done.4 = bf16[1024,2048]{1,0:T(8,128)(2,1)S(1)} copy-done((bf16[1024,2048]{1,0:T(8,128)(2,1)S(1)}, bf16[1024,2048]{1,0:T(8,128)(2,1)}, u32[]{:S(2)}) %copy-start.4) | copy-done | bytes 4194328
  47.8 0.0 copy-start.5
  47.8 2.2 %copy-done.5 = bf16[2048,1024]{1,0:T(8,128)(2,1)S(1)} copy-done((bf16[2048,1024]{1,0:T(8,128)(2,1)S(1)}, bf16[2048,1024]{1,0:T(8,128)(2,1)}, u32[]{:S(2)}) %copy-start.5) | copy-done | bytes 4194328
  49.9 0.0 copy-start.6
  49.9 0.8 copy-done.6
  50.8 7.3 %shard_map.99 = (bf16[16,32,1024]{2,1,0:T(8,128)(2,1)}, f32[32,1]{1,0:T(8,128)S(1)}) custom-call(bf16[16,32,1024]{2,1,0:T(8,128)(2,1)S(1)} %all-to-all-done.noise, bf16[32,1024]{1,0:T(8,128)(2,1)S(1)} %get-tuple-element.26.latent, bf16[32,1024]{1,0:T(8,128)(2,1)S(1)} %copy-done.6, f32[32,1]{1,0:T(8,128)S(1)} %get-tuple-element.27.scale, ...), custom_call_target="tpu_custom_call" | custom-call | flops 4328521728 | bytes 8388608 | tf_op jit(solution)/shard_map/pallas_call | solution.py:280
  58.1 3.8 %all-to-all-start.1 = ((bf16[16,32,1024]{2,1,0:T(8,128)(2,1)}), bf16[16,32,1024]{2,1,0:T(8,128)(2,1)S(1)}, u32[]{:S(2)}, u32[]{:S(2)}) async-start(bf16[16,32,1024]{2,1,0:T(8,128)(2,1)} %get-tuple-element.28), calls=%async_computation.1 | async-start | bytes 2097152 | tf_op jit(solution)/shard_map/all_to_all | solution.py:290
  62.0 0.6 reduce
  62.6 22.3 %all-to-all-done.1 = bf16[16,32,1024]{2,1,0:T(8,128)(2,1)S(1)} async-done(((bf16[16,32,1024]{2,1,0:T(8,128)(2,1)}), bf16[16,32,1024]{2,1,0:T(8,128)(2,1)S(1)}, u32[]{:S(2)}, u32[]{:S(2)}) %all-to-all-start.1) | async-done | bytes 1048608 | tf_op jit(solution)/shard_map/all_to_all | solution.py:290
  84.9 1.0 %copy.11 = bf16[1,512,1024]{2,1,0:T(8,128)(2,1)} copy(bf16[1,512,1024]{2,1,0:T(8,128)(2,1)S(1)} %bitcast.6) | data formatting | bytes 2097152
Async XLA Ops:
  0.6 43.3 %copy-start = (bf16[1024,1024]{1,0:T(8,128)(2,1)S(1)}, bf16[1024,1024]{1,0:T(8,128)(2,1)}, u32[]{:S(2)}) copy-start(bf16[1024,1024]{1,0:T(8,128)(2,1)} %encoder.1) | copy-start | bytes 6291460
  0.6 44.9 %all-to-all-start = ((bf16[16,32,1024]{2,1,0:T(8,128)(2,1)}), bf16[16,32,1024]{2,1,0:T(8,128)(2,1)S(1)}, u32[]{:S(2)}, u32[]{:S(2)}) async-start(bf16[16,32,1024]{2,1,0:T(8,128)(2,1)} %bitcast.7), calls=%async_computation | async-start | bytes 2097152 | tf_op jit(solution)/shard_map/all_to_all | solution.py:274
  8.2 3.7 %collective-permute-start = (f32[32]{0:T(128)}, f32[32]{0:T(128)S(1)}, u32[]{:S(2)}, u32[]{:S(2)}) collective-permute-start(f32[32]{0:T(128)} %param.12), channel_id=1, source_target_pairs={{0,16},{16,0},{1,17},{17,1},{2,18},{18,2},{3,19},{19,3},{4,20},{20... | collective-permute-start | bytes 392 | tf_op jit(solution)/shard_map/ppermute | solution.py:24
  12.6 1.2 %copy-start.1 = (bf16[1,512,1024]{2,1,0:T(8,128)(2,1)S(1)}, bf16[1,512,1024]{2,1,0:T(8,128)(2,1)}, u32[]{:S(2)}) copy-start(bf16[1,512,1024]{2,1,0:T(8,128)(2,1)} %analyses.1) | copy-start | bytes 3145732
  13.8 0.7 copy-start.2
  15.5 2.1 %collective-permute-start.1 = (bf16[48,1024]{1,0:T(8,128)(2,1)S(1)}, bf16[48,1024]{1,0:T(8,128)(2,1)S(1)}, u32[]{:S(2)}, u32[]{:S(2)}) collective-permute-start(bf16[48,1024]{1,0:T(8,128)(2,1)S(1)} %get-tuple-element.17), channel_id=1, source_target_pairs={{0,1},{1,0},{2,3},{3,2},{4,5},{5,4},{6,7},{7,6},{8,9},{9,8},{10,11... | collective-permute-start | bytes 294920 | tf_op jit(solution)/shard_map/ppermute | solution.py:24
  15.6 7.6 %collective-permute-start.2 = (bf16[48,1024]{1,0:T(8,128)(2,1)S(1)}, bf16[48,1024]{1,0:T(8,128)(2,1)S(1)}, u32[]{:S(2)}, u32[]{:S(2)}) collective-permute-start(bf16[48,1024]{1,0:T(8,128)(2,1)S(1)} %get-tuple-element.18), channel_id=1, source_target_pairs={{0,2},{1,3},{2,0},{3,1},{4,6},{5,7},{6,4},{7,5},{8,10},{9,11},{10,... | collective-permute-start | bytes 294920 | tf_op jit(solution)/shard_map/ppermute | solution.py:24
  17.5 8.8 %collective-permute-start.3 = (bf16[48,1024]{1,0:T(8,128)(2,1)S(1)}, bf16[48,1024]{1,0:T(8,128)(2,1)S(1)}, u32[]{:S(2)}, u32[]{:S(2)}) collective-permute-start(bf16[48,1024]{1,0:T(8,128)(2,1)S(1)} %get-tuple-element.19), channel_id=1, source_target_pairs={{0,3},{1,2},{2,1},{3,0},{4,7},{5,6},{6,5},{7,4},{8,11},{9,10},{10,... | collective-permute-start | bytes 294920 | tf_op jit(solution)/shard_map/ppermute | solution.py:24
  26.9 8.5 %collective-permute-start.4 = (bf16[80,1024]{1,0:T(8,128)(2,1)S(1)}, bf16[80,1024]{1,0:T(8,128)(2,1)S(1)}, u32[]{:S(2)}, u32[]{:S(2)}) collective-permute-start(bf16[80,1024]{1,0:T(8,128)(2,1)S(1)} %get-tuple-element.21), channel_id=1, source_target_pairs={{0,4},{1,5},{2,6},{3,7},{4,0},{5,1},{6,2},{7,3},{8,12},{9,13},{10,... | collective-permute-start | bytes 491528 | tf_op jit(solution)/shard_map/ppermute | solution.py:24
  36.0 7.8 %collective-permute-start.5 = (bf16[48,1024]{1,0:T(8,128)(2,1)S(1)}, bf16[48,1024]{1,0:T(8,128)(2,1)S(1)}, u32[]{:S(2)}, u32[]{:S(2)}) collective-permute-start(bf16[48,1024]{1,0:T(8,128)(2,1)S(1)} %get-tuple-element.24), channel_id=1, source_target_pairs={{0,8},{1,9},{2,10},{3,11},{4,12},{5,13},{6,14},{7,15},{8,0},{9,1},... | collective-permute-start | bytes 294920 | tf_op jit(solution)/shard_map/ppermute | solution.py:24
  43.9 0.7 copy-start.3
  45.6 2.2 %copy-start.4 = (bf16[1024,2048]{1,0:T(8,128)(2,1)S(1)}, bf16[1024,2048]{1,0:T(8,128)(2,1)}, u32[]{:S(2)}) copy-start(bf16[1024,2048]{1,0:T(8,128)(2,1)} %inlet.1) | copy-start | bytes 12582916
  47.8 2.2 %copy-start.5 = (bf16[2048,1024]{1,0:T(8,128)(2,1)S(1)}, bf16[2048,1024]{1,0:T(8,128)(2,1)}, u32[]{:S(2)}) copy-start(bf16[2048,1024]{1,0:T(8,128)(2,1)} %outlet.1) | copy-start | bytes 12582916
  49.9 0.8 copy-start.6
  58.1 26.8 %all-to-all-start.1 = ((bf16[16,32,1024]{2,1,0:T(8,128)(2,1)}), bf16[16,32,1024]{2,1,0:T(8,128)(2,1)S(1)}, u32[]{:S(2)}, u32[]{:S(2)}) async-start(bf16[16,32,1024]{2,1,0:T(8,128)(2,1)} %get-tuple-element.28), calls=%async_computation.1 | async-start | bytes 2097152 | tf_op jit(solution)/shard_map/all_to_all | solution.py:290

commit v3 on v2

v3 whole, which is shorter than its diff:
```python
import functools

import jax
import jax.numpy as jnp
from jax import lax
from jax.experimental import pallas as pl
from jax.experimental.pallas import tpu as pltpu
from jax.sharding import PartitionSpec as P

EPSILON = 1e-06
TOKENS_AT_ONCE = 16
HIDDEN_PIECES = 4
NETWORK_LIMIT = 50
FIRST_LIMIT = 54
TAIL = 16
BF16 = jnp.bfloat16
F32 = jnp.float32

VMEM = pl.BlockSpec(memory_space=pltpu.VMEM)
SMEM = pl.BlockSpec(memory_space=pltpu.SMEM)
HBM = pl.BlockSpec(memory_space=pltpu.HBM)


def swap(value, axis, bit):
    size = lax.axis_size(axis)
    return lax.ppermute(value, axis, [(i, i ^ bit) for i in range(size)])


def transposed(value):
    return lax.all_to_all(value, "member", split_axis=0, concat_axis=0, tiled=True)


def local_call(kernel, out_shape, in_specs, flops=0, moved=0, scratch=(), limit=40):
    return pl.pallas_call(
        kernel,
        in_specs=in_specs,
        out_specs=[VMEM] * len(out_shape),
        out_shape=out_shape,
        scratch_shapes=list(scratch),
        compiler_params=pltpu.CompilerParams(vmem_limit_bytes=limit * 2**20),
        cost_estimate=pl.CostEstimate(flops=flops, bytes_accessed=moved, transcendentals=0),
    )


def weight_rows(total, features):
    high = total.astype(BF16).astype(F32)
    middle = (total - high).astype(BF16).astype(F32)
    low = total - high - middle
    row = lax.broadcasted_iota(jnp.int32, (TAIL, features), 0)
    picked = jnp.where(row == 0, high, jnp.where(row == 1, middle, jnp.where(row == 2, low, 0.0)))
    return picked.astype(BF16)


def weight_from(rows):
    return jnp.sum(rows[:, 0:128].astype(F32), axis=0, keepdims=True)[:, 0:1]


def first_kernel(lanes, chunks, owners, analyses, noise, weight, *refs):
    rows_out, noise_out = refs[:lanes], refs[lanes : lanes + chunks]
    row_sems, noise_sems = refs[lanes + chunks :]
    own, features = rows_out[0].shape[0] - TAIL, rows_out[0].shape[1]
    me = lax.axis_index("member")
    lane = me % lanes
    block = jnp.int32(0)
    for b in range(owners.shape[0]):
        block = jnp.where(owners[b] == me, b, block)
    copies = []
    for k in range(lanes):
        start = pl.multiple_of((block * lanes + (lane ^ k)) * own, own)
        copies.append(
            pltpu.make_async_copy(
                analyses.at[0, pl.ds(start, own), :],
                rows_out[k].at[pl.ds(0, own), :],
                row_sems.at[k],
            )
        )
    for i in range(chunks):
        tokens = noise_out[i].shape[1]
        copies.append(
            pltpu.make_async_copy(
                noise.at[:, pl.ds(i * tokens, tokens), :], noise_out[i], noise_sems.at[i]
            )
        )
    for copy in copies:
        copy.start()
    rows = weight_rows(jnp.sum(weight[...], axis=1, keepdims=True), features)
    for k in range(lanes):
        rows_out[k][pl.ds(own, TAIL), :] = rows
    for copy in copies:
        copy.wait()


def planes_kernel(lanes, owners, *refs):
    held, outs = refs[:lanes], refs[lanes:]
    own, features = outs[0].shape[0] - TAIL, outs[0].shape[1]
    me = lax.axis_index("member")
    lane, plane = me % lanes, me // lanes
    total = weight_from(held[0][pl.ds(own, TAIL), :])
    for k in range(1, lanes):
        total = total + weight_from(held[k][pl.ds(own, TAIL), :])
    tail = weight_rows(total, features)
    for j in range(len(outs)):
        place = (owners[plane ^ j] % lanes) ^ lane
        rows = held[0][pl.ds(0, own), :]
        for k in range(1, lanes):
            rows = jnp.where(place == k, held[k][pl.ds(0, own), :], rows)
        outs[j][pl.ds(0, own), :] = rows
        outs[j][pl.ds(own, TAIL), :] = tail


def encode_kernel(lanes, owners, encoder, *refs):
    held, (latent, total_out) = refs[:-2], refs[-2:]
    own = latent.shape[0]
    plane = lax.axis_index("member") // lanes
    place = (owners[plane] // lanes) ^ plane
    control = held[0][pl.ds(0, own), :]
    total = weight_from(held[0][pl.ds(own, TAIL), :])
    for k in range(1, len(held)):
        control = jnp.where(place == k, held[k][pl.ds(0, own), :], control)
        total = total + weight_from(held[k][pl.ds(own, TAIL), :])
    latent[...] = jnp.dot(control, encoder[...], preferred_element_type=F32).astype(BF16)
    total_out[...] = jnp.broadcast_to(total, total_out.shape)


def column(row):
    size = row.shape[1]
    first = lax.broadcasted_iota(jnp.int32, (size, size), 0)
    second = lax.broadcasted_iota(jnp.int32, (size, size), 1)
    return jnp.sum(jnp.where(first == second, row, 0.0), axis=1, keepdims=True)


def network(noise, latent, hidden_piece, pieces):
    members, tokens, features = noise.shape
    states = (noise.astype(F32) + latent.astype(F32)[None]).reshape(members * tokens, features)
    mean = jnp.sum(states * states, axis=-1, keepdims=True) * (1.0 / features)
    normed = (states * lax.rsqrt(mean + EPSILON)).astype(BF16)
    total = states
    for piece in range(pieces):
        total = total + hidden_piece(normed, piece)
    return total.astype(BF16)


def score(forecast, targets, scale, members, tokens):
    rows, features = forecast.shape
    gram = lax.dot_general(
        forecast, forecast, (((1,), (1,)), ((), ())), preferred_element_type=F32
    )
    first = lax.broadcasted_iota(jnp.int32, (rows, rows), 0)
    second = lax.broadcasted_iota(jnp.int32, (rows, rows), 1)
    same_row = first == second
    same_token = (first % tokens) == (second % tokens)
    on_diagonal = jnp.where(same_row, gram, 0.0)
    down = jnp.sum(on_diagonal, axis=1, keepdims=True)
    across = jnp.sum(on_diagonal, axis=0, keepdims=True)
    squared = jnp.maximum((down + across - 2.0 * gram) * (1.0 / features), 0.0) + EPSILON
    inverse = lax.rsqrt(squared)
    pairs = jnp.where(same_token, squared * inverse, 0.0)
    coeff = jnp.where(same_token & ~same_row, inverse, 0.0).astype(BF16)
    coeff_sum = jnp.sum(coeff.astype(F32), axis=1, keepdims=True)
    combined = jnp.dot(coeff, forecast, preferred_element_type=F32)
    values = forecast.astype(F32)
    apart = (
        values.reshape(members, tokens, features) - targets.astype(F32)[None]
    )
    squares = jnp.sum(apart * apart, axis=-1, keepdims=True) * (1.0 / features) + EPSILON
    inverse_spread = lax.rsqrt(squares)
    from_others = (coeff_sum * values - combined).reshape(members, tokens, features)
    gradient = scale[None] * (apart * inverse_spread - from_others * (1.0 / members))
    spread = jnp.sum(squares * inverse_spread, axis=0) * (1.0 / members)
    pair_sum = jnp.sum(jnp.sum(pairs, axis=1, keepdims=True).reshape(members, tokens, 1), axis=0)
    energy = scale * (spread - pair_sum * (1.0 / (2.0 * members * members)))
    return gradient, energy


def network_kernel(
    chunk, noise, latent, inlet_hbm, outlet_hbm, forecast_out, inlet, outlet, inlet_sems, outlet_sems
):
    members, tokens, features = noise.shape
    width = inlet.shape[1] // HIDDEN_PIECES
    copies = []
    for piece in range(HIDDEN_PIECES):
        part = pl.ds(piece * width, width)
        copies.append(
            (
                pltpu.make_async_copy(
                    inlet_hbm.at[:, part], inlet.at[:, part], inlet_sems.at[piece]
                ),
                pltpu.make_async_copy(
                    outlet_hbm.at[part, :], outlet.at[part, :], outlet_sems.at[piece]
                ),
            )
        )
    for into, out_of in copies:
        into.start()
        out_of.start()

    def hidden_piece(normed, piece):
        part = slice(piece * width, (piece + 1) * width)
        copies[piece][0].wait()
        hidden = jax.nn.gelu(
            jnp.dot(normed, inlet[:, part], preferred_element_type=F32), approximate=True
        ).astype(BF16)
        copies[piece][1].wait()
        return jnp.dot(hidden, outlet[part, :], preferred_element_type=F32)

    here = slice(chunk * tokens, (chunk + 1) * tokens)
    forecast_out[...] = network(noise[...], latent[here, :], hidden_piece, HIDDEN_PIECES)


def scored(chunk, members, count, forecast, targets, weight, total):
    tokens = forecast.shape[0] // members
    here = slice(chunk * tokens, (chunk + 1) * tokens)
    scale = column(weight[...])[here, :] * (count / total[0:1, 0:1])
    gradient, energy = score(forecast[...], targets[here, :], scale, members, tokens)
    return gradient.astype(BF16), energy


def whole_score_kernel(chunk, count, forecast, targets, weight, total, gradient_out, energy_out):
    gradient, energy = scored(
        chunk, gradient_out.shape[0], count, forecast, targets, weight, total
    )
    gradient_out[...] = gradient
    energy_out[...] = energy


def split_score_kernel(
    chunk, count, forecast, targets, weight, total, keep, give, energy_out, gradient
):
    values, energy = scored(chunk, gradient.shape[0], count, forecast, targets, weight, total)
    gradient[...] = values
    energy_out[...] = energy
    me = lax.axis_index("member")
    for k in range(keep.shape[0]):
        keep[k] = gradient[me ^ (2 * k)]
        give[k] = gradient[me ^ (2 * k + 1)]


def pack_kernel(keep, got, *outs):
    for k, out in enumerate(outs):
        out[0] = keep[k + 1]
        out[1] = got[k + 1]


def finish_kernel(chips, own, *refs):
    *inputs, result, sems = refs
    back = inputs[-1]
    tokens = back.shape[1]
    chunk = own // tokens - 1
    me = lax.axis_index("member")
    copies = []

    def put(source, device, chunk):
        start = pl.multiple_of(device * own + chunk * tokens, tokens)
        copies.append(
            pltpu.make_async_copy(
                source, result.at[0, pl.ds(start, tokens), :], sems.at[len(copies)]
            )
        )

    for device in range(back.shape[0]):
        put(back.at[device], device, chunk)
    if chunk:
        keep, got = inputs[:2]
        put(keep.at[0], me, 0)
        put(got.at[0], me ^ 1, 0)
        for k in range(1, chips):
            put(inputs[k + 1].at[0], me ^ (2 * k), 0)
            put(inputs[k + 1].at[1], me ^ (2 * k + 1), 0)
    for copy in copies:
        copy.start()
    for copy in copies:
        copy.wait()


def on_device(
    analyses,
    owners,
    noise,
    targets,
    area_weight,
    enc_weight,
    sample_inlet_matrix,
    sample_outlet_matrix,
):
    members = lax.axis_size("member")
    regions = lax.axis_size("region")
    _, region_rows, features = noise.shape
    hidden = sample_inlet_matrix.shape[1]
    blocks = owners.shape[0]
    lanes = members // blocks
    chips = members // 2
    own = region_rows // members
    chunks = min(2, own // TOKENS_AT_ONCE)
    tokens = own // chunks
    count = float(region_rows * regions)
    weight = area_weight[None]

    def rows(many):
        return jax.ShapeDtypeStruct((many, features), BF16)

    def stack(many):
        return jax.ShapeDtypeStruct((many, tokens, features), BF16)

    small = jax.ShapeDtypeStruct((8, 128), F32)
    energies = jax.ShapeDtypeStruct((tokens, 1), F32)

    first = local_call(
        functools.partial(first_kernel, lanes, chunks),
        [rows(own + TAIL)] * lanes + [stack(members)] * chunks,
        [SMEM, HBM, HBM, VMEM],
        scratch=[pltpu.SemaphoreType.DMA((lanes,)), pltpu.SemaphoreType.DMA((chunks,))],
        limit=FIRST_LIMIT,
    )(owners, analyses, noise.reshape(members, own, features), weight)
    by_lane = [first[0]] + [swap(first[k], "member", k) for k in range(1, lanes)]
    parts = list(first[lanes:])
    parts[0], *by_lane = lax.optimization_barrier((parts[0], *by_lane))
    noises = [transposed(parts[0])]
    planes = local_call(
        functools.partial(planes_kernel, lanes),
        [rows(own + TAIL)] * blocks,
        [SMEM] + [VMEM] * lanes,
        limit=8,
    )(owners, *by_lane)
    by_plane = [planes[0]] + [swap(planes[k], "member", k * lanes) for k in range(1, blocks)]
    latent, total = local_call(
        functools.partial(encode_kernel, lanes),
        [rows(own), small],
        [SMEM] + [VMEM] * (1 + blocks),
        flops=2 * own * features * features,
        limit=8,
    )(owners, enc_weight, *by_plane)
    for part in parts[1:]:
        noises[-1], latent, part = lax.optimization_barrier((noises[-1], latent, part))
        noises.append(transposed(part))
    for bit in (1 << i for i in range(regions.bit_length() - 1)):
        total = total + swap(total, "region", bit)

    def forecast_of(chunk):
        return local_call(
            functools.partial(network_kernel, chunk),
            [rows(members * tokens)],
            [VMEM, VMEM, HBM, HBM],
            flops=4 * members * tokens * features * hidden,
            scratch=[
                pltpu.VMEM((features, hidden), BF16),
                pltpu.VMEM((hidden, features), BF16),
                pltpu.SemaphoreType.DMA((HIDDEN_PIECES,)),
                pltpu.SemaphoreType.DMA((HIDDEN_PIECES,)),
            ],
            limit=NETWORK_LIMIT,
        )(noises[chunk], latent, sample_inlet_matrix, sample_outlet_matrix)[0]

    energy, returned = [], []
    flops = 4 * members * tokens * features * members * tokens
    for chunk in range(chunks - 1):
        keep, give, part = local_call(
            functools.partial(split_score_kernel, chunk, count),
            [stack(chips), stack(chips), energies],
            [VMEM] * 4,
            flops=flops,
            scratch=[pltpu.VMEM((members, tokens, features), BF16)],
            limit=24,
        )(forecast_of(chunk), targets, weight, total)
        energy.append(part)
        got = swap(give, "member", 1)
        packed = local_call(pack_kernel, [stack(2)] * (chips - 1), [VMEM] * 2, limit=8)(keep, got)
        noises[chunk + 1], packed = lax.optimization_barrier((noises[chunk + 1], packed))
        returned = [keep, got] + [
            swap(packed[k - 1], "member", 2 * k) for k in range(1, chips)
        ]
    gradient, part = local_call(
        functools.partial(whole_score_kernel, chunks - 1, count),
        [stack(members), energies],
        [VMEM] * 4,
        flops=flops,
        limit=24,
    )(forecast_of(chunks - 1), targets, weight, total)
    energy.append(part)
    gradient, *returned = lax.optimization_barrier((gradient, *returned))
    back = transposed(gradient)
    member_grad = pl.pallas_call(
        functools.partial(finish_kernel, chips, own),
        in_specs=[VMEM] * (len(returned) + 1),
        out_specs=HBM,
        out_shape=jax.ShapeDtypeStruct((1, region_rows, features), BF16),
        scratch_shapes=[pltpu.SemaphoreType.DMA((members * chunks,))],
        compiler_params=pltpu.CompilerParams(vmem_limit_bytes=8 * 2**20),
    )(*returned, back)
    return member_grad, jnp.concatenate(energy, axis=0)[:, 0]


def solution(mesh):
    return jax.shard_map(
        on_device,
        mesh=mesh,
        in_specs=(
            P("member", "region", None),
            P(),
            P("member", "region", None),
            P(("region", "member"), None),
            P(("region", "member")),
            P(),
            P(),
            P(),
        ),
        out_specs=(P("member", "region", None), P(("region", "member"))),
        check_vma=False,
    )
```

time: 87.5 us -> 99.5 us (1.14); the launches traced: 85.9 us -> 99 us
  starting transfers between devices: 19.3 us -> 35 us
  Pallas kernels: 10.6 us -> 20.3 us
  local copies, waits for them, and re-layouts: 8.72 us -> 1.71 us
  waiting for transfers between devices: 45.3 us -> 40.7 us
    ppermute x6 -> x15, starting transfers between devices: 7.95 us -> 20.4 us  [swap(): return lax.ppermute(value, axis, [(i, i ^ bit) for i in range(size)])]
    pallas_call x5 -> x9, Pallas kernels: 10.6 us -> 20.3 us  [the longest x2 11.1 us: forecast_of(): local_call(functools.partial(network_kernel, chunk), [rows(members * toke...]
    unnamed x15 -> x10, local copies, waits for them, and re-layouts: 8.72 us -> 1.55 us
    all_to_all x2 -> x3, waiting for transfers between devices: 22.3 us -> 16.2 us  [transposed(): lax.all_to_all(value, 'member', split_axis=0, concat_axis=0, tiled=True)]
    all_to_all x2 -> x3, starting transfers between devices: 11.4 us -> 14.6 us  [transposed(): lax.all_to_all(value, 'member', split_axis=0, concat_axis=0, tiled=True)]
    ppermute x6 -> x15, waiting for transfers between devices: 22.9 us -> 24.5 us  [swap(): return lax.ppermute(value, axis, [(i, i ^ bit) for i in range(size)])]
  transfers between devices with their start and end apart: 8 -> 18, of which waited for: 6 -> 8; matrix products, arithmetic and copies ran while one was open for 1% -> 1% of each run, Pallas kernels for 4% -> 16%
where the time goes in v3:
time: 99.5 us; the launch traced here: 99 us
  waiting for transfers between devices  40.7 us (41%)
  starting transfers between devices  35 us (35%)
  Pallas kernels  20.3 us (20%)
  local copies, waits for them, and re-layouts  1.71 us (2%)
    ppermute x15, waiting for transfers between devices, swap(): return lax.ppermute(value, axis, [(i, i ^ bit) for i in range(size)])  24.5 us
    ppermute x15, starting transfers between devices, swap(): return lax.ppermute(value, axis, [(i, i ^ bit) for i in range(size)])  20.4 us
    all_to_all x3, waiting for transfers between devices, transposed(): lax.all_to_all(value, 'member', split_axis=0, concat_axis=0, tiled=True)  16.2 us
    all_to_all x3, starting transfers between devices, transposed(): lax.all_to_all(value, 'member', split_axis=0, concat_axis=0, tiled=True)  14.6 us
    pallas_call x2, Pallas kernels, forecast_of(): local_call(functools.partial(network_kernel, chunk), [rows(members * toke...  11.1 us
    pallas_call x1, Pallas kernels, on_device(): local_call(functools.partial(first_kernel, lanes, chunks), [rows(own + TA...  3.34 us
  transfers between devices with their start and end apart: 18, of which 8 were waited for; matrix products, arithmetic and copies ran while one was open for 1% of the time, Pallas kernels for 16%

profile of v3, /device:TPU:0, one launch (start us, length us, event | category | flops | bytes accessed | tf_op | source)
XLA Modules:
  0.0 99.0 jit_solution(10451875730621115091)
XLA Ops:
  0.6 3.3 %shard_map.95 = (bf16[48,1024]{1,0:T(8,128)(2,1)}, bf16[48,1024]{1,0:T(8,128)(2,1)}, bf16[48,1024]{1,0:T(8,128)(2,1)}, bf16[48,1024]{1,0:T(8,128)(2,1)}, bf16[16...) custom-call(s32[4]{0:T(128)} %owners.5, bf16[1,512,1024]{2,1,0:T(8,128)(2,1)} %analyses.1, ...), custom_call_target="tpu_custom_call" | custom-call | tf_op jit(solution)/shard_map/pallas_call | solution.py:307
  4.0 0.5 collective-permute-start
  4.5 2.6 %collective-permute-start.1 = (bf16[48,1024]{1,0:T(8,128)(2,1)}, bf16[48,1024]{1,0:T(8,128)(2,1)S(1)}, u32[]{:S(2)}, u32[]{:S(2)}) collective-permute-start(bf16[48,1024]{1,0:T(8,128)(2,1)} %get-tuple-element.55), channel_id=1, source_target_pairs={{0,2},{1,3},{2,0},{3,1},{4,6},{5,7},{6,4},{7,5},{8,10},{9,11},{10,... | collective-permute-start | bytes 294920 | tf_op jit(solution)/shard_map/ppermute | solution.py:26
  7.1 0.1 collective-permute-start.2
  7.2 0.0 collective-permute-done.refs_1_
  7.2 3.8 %collective-permute-done.1.refs_2_ = bf16[48,1024]{1,0:T(8,128)(2,1)S(1)} collective-permute-done((bf16[48,1024]{1,0:T(8,128)(2,1)}, bf16[48,1024]{1,0:T(8,128)(2,1)S(1)}, u32[]{:S(2)}, u32[]{:S(2)}) %collective-permute-start.1) | collective-permute-done | bytes 98336 | tf_op jit(solution)/shard_map/ppermute | solution.py:26
  11.0 1.6 %collective-permute-done.2.refs_3_ = bf16[48,1024]{1,0:T(8,128)(2,1)S(1)} collective-permute-done((bf16[48,1024]{1,0:T(8,128)(2,1)}, bf16[48,1024]{1,0:T(8,128)(2,1)S(1)}, u32[]{:S(2)}, u32[]{:S(2)}) %collective-permute-start.2) | collective-permute-done | bytes 98336 | tf_op jit(solution)/shard_map/ppermute | solution.py:26
  12.5 6.0 %all-to-all-start = ((bf16[16,16,1024]{2,1,0:T(8,128)(2,1)}), bf16[16,16,1024]{2,1,0:T(8,128)(2,1)S(1)}, u32[]{:S(2)}, u32[]{:S(2)}) async-start(bf16[16,16,1024]{2,1,0:T(8,128)(2,1)} %get-tuple-element.57), calls=%async_computation | async-start | bytes 1048576 | tf_op jit(solution)/shard_map/all_to_all | solution.py:30
  18.5 0.9 copy-done.1
  19.4 0.7 copy-done.2
  20.1 0.6 shard_map.96
  20.7 2.0 %collective-permute-start.3 = (bf16[48,1024]{1,0:T(8,128)(2,1)S(1)}, bf16[48,1024]{1,0:T(8,128)(2,1)S(1)}, u32[]{:S(2)}, u32[]{:S(2)}) collective-permute-start(bf16[48,1024]{1,0:T(8,128)(2,1)S(1)} %get-tuple-element.63), channel_id=1, source_target_pairs={{0,4},{1,5},{2,6},{3,7},{4,0},{5,1},{6,2},{7,3},{8,12},{9,13},{10,... | collective-permute-start | bytes 294920 | tf_op jit(solution)/shard_map/ppermute | solution.py:26
  22.7 2.4 %collective-permute-start.4 = (bf16[48,1024]{1,0:T(8,128)(2,1)S(1)}, bf16[48,1024]{1,0:T(8,128)(2,1)S(1)}, u32[]{:S(2)}, u32[]{:S(2)}) collective-permute-start(bf16[48,1024]{1,0:T(8,128)(2,1)S(1)} %get-tuple-element.64), channel_id=1, source_target_pairs={{0,8},{1,9},{2,10},{3,11},{4,12},{5,13},{6,14},{7,15},{8,0},{9,1},... | collective-permute-start | bytes 294920 | tf_op jit(solution)/shard_map/ppermute | solution.py:26
  25.1 0.1 collective-permute-start.5
  25.2 5.9 %collective-permute-done.3.refs_1_ = bf16[48,1024]{1,0:T(8,128)(2,1)S(1)} collective-permute-done((bf16[48,1024]{1,0:T(8,128)(2,1)S(1)}, bf16[48,1024]{1,0:T(8,128)(2,1)S(1)}, u32[]{:S(2)}, u32[]{:S(2)}) %collective-permute-start.3) | collective-permute-done | bytes 98336 | tf_op jit(solution)/shard_map/ppermute | solution.py:26
  31.1 9.6 %collective-permute-done.4.refs_2_ = bf16[48,1024]{1,0:T(8,128)(2,1)S(1)} collective-permute-done((bf16[48,1024]{1,0:T(8,128)(2,1)S(1)}, bf16[48,1024]{1,0:T(8,128)(2,1)S(1)}, u32[]{:S(2)}, u32[]{:S(2)}) %collective-permute-start.4) | collective-permute-done | bytes 98336 | tf_op jit(solution)/shard_map/ppermute | solution.py:26
  40.6 0.0 collective-permute-done.5.refs_3_
  40.6 1.0 %shard_map.97 = (bf16[32,1024]{1,0:T(8,128)(2,1)S(1)}, f32[8,128]{1,0:T(8,128)S(1)}) custom-call(s32[4]{0:T(128)S(1)} %copy-done.2, bf16[1024,1024]{1,0:T(8,128)(2,1)S(1)} %copy-done, bf16[48,1024]{1,0:T(8,128)(2,1)S(1)} %get-tuple-element.62.refs_0_, bf16[48,1024]{1,0:T(8,128)(2,1)S(1)} %collective-permute-done.3.refs_1_, ...), custom_call_target="tpu_custom_call" | custom-call | flops 67108864 | tf_op jit(solution)/shard_map/pallas_call | solution.py:325
  41.6 0.0 all-to-all-done.noise
  41.6 4.5 %all-to-all-start.1 = ((bf16[16,16,1024]{2,1,0:T(8,128)(2,1)}), bf16[16,16,1024]{2,1,0:T(8,128)(2,1)S(1)}, u32[]{:S(2)}, u32[]{:S(2)}) async-start(bf16[16,16,1024]{2,1,0:T(8,128)(2,1)} %get-tuple-element.68), calls=%async_computation.1 | async-start | bytes 1048576 | tf_op jit(solution)/shard_map/all_to_all | solution.py:30
  46.1 1.6 %collective-permute-start.6 = (f32[8,128]{1,0:T(8,128)S(1)}, f32[8,128]{1,0:T(8,128)S(1)}, u32[]{:S(2)}, u32[]{:S(2)}) collective-permute-start(f32[8,128]{1,0:T(8,128)S(1)} %get-tuple-element.71), channel_id=1, source_target_pairs={{0,16},{16,0},{1,17},{17,1},{2,18},{18,2},{3,19},{19,3},{4,20},{20... | collective-permute-start | bytes 12296 | tf_op jit(solution)/shard_map/ppermute | solution.py:26
  47.7 2.1 %collective-permute-done.6 = f32[8,128]{1,0:T(8,128)S(1)} collective-permute-done((f32[8,128]{1,0:T(8,128)S(1)}, f32[8,128]{1,0:T(8,128)S(1)}, u32[]{:S(2)}, u32[]{:S(2)}) %collective-permute-start.6) | collective-permute-done | bytes 4128 | tf_op jit(solution)/shard_map/ppermute | solution.py:26
  49.8 5.6 %shard_map.98.forecast = bf16[256,1024]{1,0:T(8,128)(2,1)S(1)} custom-call(bf16[16,16,1024]{2,1,0:T(8,128)(2,1)S(1)} %all-to-all-done.noise, bf16[32,1024]{1,0:T(8,128)(2,1)S(1)} %get-tuple-element.70.latent, bf16[1024,2048]{1,0:T(8,128)(2,1)} %inlet_hbm.3, bf16[2048,1024]{1,0:T(8,128)(2,1)} %outlet_hbm.3), custom_call_target="tpu_custom_call" | custom-call | flops 2147483648 | tf_op jit(solution)/shard_map/pallas_call | solution.py:339
  55.4 1.1 %shard_map.99 = (bf16[8,16,1024]{2,1,0:T(8,128)(2,1)S(1)}, bf16[8,16,1024]{2,1,0:T(8,128)(2,1)S(1)}, f32[16,1]{1,0:T(8,128)S(1)}) custom-call(bf16[256,1024]{1,0:T(8,128)(2,1)S(1)} %shard_map.98.forecast, bf16[32,1024]{1,0:T(8,128)(2,1)S(1)} %copy-done.4, f32[1,32]{1,0:T(1,128)S(1)} %bitcast.5, f32[8,128]{1,0:T(8,128)S(1)} %add.3.total), custom_call_target="tpu_custom_call" | custom-call | flops 268435456 | tf_op jit(solution)/shard_map/pallas_call | solution.py:356
  56.5 0.1 collective-permute-start.7
  56.6 1.5 %collective-permute-done.7.got.refs_1_ = bf16[8,16,1024]{2,1,0:T(8,128)(2,1)S(1)} collective-permute-done((bf16[8,16,1024]{2,1,0:T(8,128)(2,1)S(1)}, bf16[8,16,1024]{2,1,0:T(8,128)(2,1)S(1)}, u32[]{:S(2)}, u32[]{:S(2)}) %collective-permute-start.7) | collective-permute-done | bytes 262176 | tf_op jit(solution)/shard_map/ppermute | solution.py:26
  58.1 2.5 %all-to-all-done.1.noise = bf16[16,16,1024]{2,1,0:T(8,128)(2,1)S(1)} async-done(((bf16[16,16,1024]{2,1,0:T(8,128)(2,1)}), bf16[16,16,1024]{2,1,0:T(8,128)(2,1)S(1)}, u32[]{:S(2)}, u32[]{:S(2)}) %all-to-all-start.1) | async-done | bytes 524320 | tf_op jit(solution)/shard_map/all_to_all | solution.py:30
  60.6 0.4 collective-permute-start.8
  61.0 2.0 %collective-permute-start.9 = (bf16[2,16,1024]{2,1,0:T(8,128)(2,1)S(1)}, bf16[2,16,1024]{2,1,0:T(8,128)(2,1)S(1)}, u32[]{:S(2)}, u32[]{:S(2)}) collective-permute-start(bf16[2,16,1024]{2,1,0:T(8,128)(2,1)S(1)} %get-tuple-element.84), channel_id=1, source_target_pairs={{0,4},{1,5},{2,6},{3,7},{4,0},{5,1},{6,2},{7,3},{8,12},{9,13},{10,... | collective-permute-start | bytes 196616 | tf_op jit(solution)/shard_map/ppermute | solution.py:26
  63.0 1.1 %collective-permute-start.10 = (bf16[2,16,1024]{2,1,0:T(8,128)(2,1)S(1)}, bf16[2,16,1024]{2,1,0:T(8,128)(2,1)S(1)}, u32[]{:S(2)}, u32[]{:S(2)}) collective-permute-start(bf16[2,16,1024]{2,1,0:T(8,128)(2,1)S(1)} %get-tuple-element.85), channel_id=1, source_target_pairs={{0,6},{1,7},{2,4},{3,5},{4,2},{5,3},{6,0},{7,1},{8,14},{9,15},{10,... | collective-permute-start | bytes 196616 | tf_op jit(solution)/shard_map/ppermute | solution.py:26
  64.1 2.3 %collective-permute-start.11 = (bf16[2,16,1024]{2,1,0:T(8,128)(2,1)S(1)}, bf16[2,16,1024]{2,1,0:T(8,128)(2,1)S(1)}, u32[]{:S(2)}, u32[]{:S(2)}) collective-permute-start(bf16[2,16,1024]{2,1,0:T(8,128)(2,1)S(1)} %get-tuple-element.86), channel_id=1, source_target_pairs={{0,8},{1,9},{2,10},{3,11},{4,12},{5,13},{6,14},{7,15},{8,0},{9,1},... | collective-permute-start | bytes 196616 | tf_op jit(solution)/shard_map/ppermute | solution.py:26
  66.3 0.5 collective-permute-start.12
  66.8 0.0 collective-permute-done.8.refs_2_
  66.9 2.9 %collective-permute-start.13 = (bf16[2,16,1024]{2,1,0:T(8,128)(2,1)S(1)}, bf16[2,16,1024]{2,1,0:T(8,128)(2,1)S(1)}, u32[]{:S(2)}, u32[]{:S(2)}) collective-permute-start(bf16[2,16,1024]{2,1,0:T(8,128)(2,1)S(1)} %get-tuple-element.88), channel_id=1, source_target_pairs={{0,12},{1,13},{2,14},{3,15},{4,8},{5,9},{6,10},{7,11},{8,4},{9,5},... | collective-permute-start | bytes 196616 | tf_op jit(solution)/shard_map/ppermute | solution.py:26
  69.7 0.0 collective-permute-done.9.refs_3_
  69.7 2.0 %collective-permute-start.14 = (bf16[2,16,1024]{2,1,0:T(8,128)(2,1)S(1)}, bf16[2,16,1024]{2,1,0:T(8,128)(2,1)S(1)}, u32[]{:S(2)}, u32[]{:S(2)}) collective-permute-start(bf16[2,16,1024]{2,1,0:T(8,128)(2,1)S(1)} %get-tuple-element.89), channel_id=1, source_target_pairs={{0,14},{1,15},{2,12},{3,13},{4,10},{5,11},{6,8},{7,9},{8,6},{9,7},... | collective-permute-start | bytes 196616 | tf_op jit(solution)/shard_map/ppermute | solution.py:26
  71.7 5.5 %shard_map.101.forecast = bf16[256,1024]{1,0:T(8,128)(2,1)S(1)} custom-call(bf16[16,16,1024]{2,1,0:T(8,128)(2,1)S(1)} %all-to-all-done.1.noise, bf16[32,1024]{1,0:T(8,128)(2,1)S(1)} %get-tuple-element.70.latent, bf16[1024,2048]{1,0:T(8,128)(2,1)} %inlet_hbm.3, bf16[2048,1024]{1,0:T(8,128)(2,1)} %outlet_hbm.3), custom_call_target="tpu_custom_call" | custom-call | flops 2147483648 | tf_op jit(solution)/shard_map/pallas_call | solution.py:339
  77.3 1.8 %shard_map.102 = (bf16[16,16,1024]{2,1,0:T(8,128)(2,1)}, f32[16,1]{1,0:T(8,128)S(1)}) custom-call(bf16[256,1024]{1,0:T(8,128)(2,1)S(1)} %shard_map.101.forecast, bf16[32,1024]{1,0:T(8,128)(2,1)S(1)} %copy-done.4, f32[1,32]{1,0:T(1,128)S(1)} %bitcast.6, f32[8,128]{1,0:T(8,128)S(1)} %add.3.total), custom_call_target="tpu_custom_call" | custom-call | flops 268435456 | tf_op jit(solution)/shard_map/pallas_call | solution.py:371
  79.1 0.0 collective-permute-done.10.refs_4_
  79.1 0.0 collective-permute-done.11.refs_5_
  79.1 0.0 collective-permute-done.12.refs_6_
  79.1 0.0 collective-permute-done.13.refs_7_
  79.2 4.1 %all-to-all-start.2 = ((bf16[16,16,1024]{2,1,0:T(8,128)(2,1)}), bf16[16,16,1024]{2,1,0:T(8,128)(2,1)S(1)}, u32[]{:S(2)}, u32[]{:S(2)}) async-start(bf16[16,16,1024]{2,1,0:T(8,128)(2,1)} %get-tuple-element.99), calls=%async_computation.2 | async-start | bytes 1048576 | tf_op jit(solution)/shard_map/all_to_all | solution.py:30
  83.3 0.1 copy.10
  83.4 0.1 copy.11
  83.4 0.6 maximum_bitcast_fusion
  84.0 13.7 %all-to-all-done.2.refs_9_ = bf16[16,16,1024]{2,1,0:T(8,128)(2,1)S(1)} async-done(((bf16[16,16,1024]{2,1,0:T(8,128)(2,1)}), bf16[16,16,1024]{2,1,0:T(8,128)(2,1)S(1)}, u32[]{:S(2)}, u32[]{:S(2)}) %all-to-all-start.2) | async-done | bytes 524320 | tf_op jit(solution)/shard_map/all_to_all | solution.py:30
  97.7 1.2 %shard_map.103 = bf16[1,512,1024]{2,1,0:T(8,128)(2,1)} custom-call(bf16[8,16,1024]{2,1,0:T(8,128)(2,1)S(1)} %get-tuple-element.90.keep.refs_0_, bf16[8,16,1024]{2,1,0:T(8,128)(2,1)S(1)} %collective-permute-done.7.got.refs_1_, bf16[2,16,1024]{2,1,0:T(8,128)(2,1)S(1)} %collective-permute-done.8.refs_2_, ...), custom_call_target="tpu_custom_call" | custom-call | tf_op jit(solution)/shard_map/pallas_call | solution.py:381
  (11 shorter events, 0.1 us)
Async XLA Ops:
  0.6 40.0 %copy-start = (bf16[1024,1024]{1,0:T(8,128)(2,1)S(1)}, bf16[1024,1024]{1,0:T(8,128)(2,1)}, u32[]{:S(2)}) copy-start(bf16[1024,1024]{1,0:T(8,128)(2,1)} %encoder.1) | copy-start | bytes 6291460
  4.0 3.2 %collective-permute-start = (bf16[48,1024]{1,0:T(8,128)(2,1)}, bf16[48,1024]{1,0:T(8,128)(2,1)S(1)}, u32[]{:S(2)}, u32[]{:S(2)}) collective-permute-start(bf16[48,1024]{1,0:T(8,128)(2,1)} %get-tuple-element.54), channel_id=1, source_target_pairs={{0,1},{1,0},{2,3},{3,2},{4,5},{5,4},{6,7},{7,6},{8,9},{9,8},{10,11... | collective-permute-start | bytes 294920 | tf_op jit(solution)/shard_map/ppermute | solution.py:26
  4.5 6.4 %collective-permute-start.1 = (bf16[48,1024]{1,0:T(8,128)(2,1)}, bf16[48,1024]{1,0:T(8,128)(2,1)S(1)}, u32[]{:S(2)}, u32[]{:S(2)}) collective-permute-start(bf16[48,1024]{1,0:T(8,128)(2,1)} %get-tuple-element.55), channel_id=1, source_target_pairs={{0,2},{1,3},{2,0},{3,1},{4,6},{5,7},{6,4},{7,5},{8,10},{9,11},{10,... | collective-permute-start | bytes 294920 | tf_op jit(solution)/shard_map/ppermute | solution.py:26
  7.1 5.4 %collective-permute-start.2 = (bf16[48,1024]{1,0:T(8,128)(2,1)}, bf16[48,1024]{1,0:T(8,128)(2,1)S(1)}, u32[]{:S(2)}, u32[]{:S(2)}) collective-permute-start(bf16[48,1024]{1,0:T(8,128)(2,1)} %get-tuple-element.56), channel_id=1, source_target_pairs={{0,3},{1,2},{2,1},{3,0},{4,7},{5,6},{6,5},{7,4},{8,11},{9,10},{10,... | collective-permute-start | bytes 294920 | tf_op jit(solution)/shard_map/ppermute | solution.py:26
  12.5 29.1 %all-to-all-start = ((bf16[16,16,1024]{2,1,0:T(8,128)(2,1)}), bf16[16,16,1024]{2,1,0:T(8,128)(2,1)S(1)}, u32[]{:S(2)}, u32[]{:S(2)}) async-start(bf16[16,16,1024]{2,1,0:T(8,128)(2,1)} %get-tuple-element.57), calls=%async_computation | async-start | bytes 1048576 | tf_op jit(solution)/shard_map/all_to_all | solution.py:30
  18.5 0.9 copy-start.1
  19.4 0.7 copy-start.2
  20.7 10.3 %collective-permute-start.3 = (bf16[48,1024]{1,0:T(8,128)(2,1)S(1)}, bf16[48,1024]{1,0:T(8,128)(2,1)S(1)}, u32[]{:S(2)}, u32[]{:S(2)}) collective-permute-start(bf16[48,1024]{1,0:T(8,128)(2,1)S(1)} %get-tuple-element.63), channel_id=1, source_target_pairs={{0,4},{1,5},{2,6},{3,7},{4,0},{5,1},{6,2},{7,3},{8,12},{9,13},{10,... | collective-permute-start | bytes 294920 | tf_op jit(solution)/shard_map/ppermute | solution.py:26
  22.7 17.9 %collective-permute-start.4 = (bf16[48,1024]{1,0:T(8,128)(2,1)S(1)}, bf16[48,1024]{1,0:T(8,128)(2,1)S(1)}, u32[]{:S(2)}, u32[]{:S(2)}) collective-permute-start(bf16[48,1024]{1,0:T(8,128)(2,1)S(1)} %get-tuple-element.64), channel_id=1, source_target_pairs={{0,8},{1,9},{2,10},{3,11},{4,12},{5,13},{6,14},{7,15},{8,0},{9,1},... | collective-permute-start | bytes 294920 | tf_op jit(solution)/shard_map/ppermute | solution.py:26
  25.1 15.5 %collective-permute-start.5 = (bf16[48,1024]{1,0:T(8,128)(2,1)S(1)}, bf16[48,1024]{1,0:T(8,128)(2,1)S(1)}, u32[]{:S(2)}, u32[]{:S(2)}) collective-permute-start(bf16[48,1024]{1,0:T(8,128)(2,1)S(1)} %get-tuple-element.65), channel_id=1, source_target_pairs={{0,12},{1,13},{2,14},{3,15},{4,8},{5,9},{6,10},{7,11},{8,4},{9,5},... | collective-permute-start | bytes 294920 | tf_op jit(solution)/shard_map/ppermute | solution.py:26
  41.6 19.0 %all-to-all-start.1 = ((bf16[16,16,1024]{2,1,0:T(8,128)(2,1)}), bf16[16,16,1024]{2,1,0:T(8,128)(2,1)S(1)}, u32[]{:S(2)}, u32[]{:S(2)}) async-start(bf16[16,16,1024]{2,1,0:T(8,128)(2,1)} %get-tuple-element.68), calls=%async_computation.1 | async-start | bytes 1048576 | tf_op jit(solution)/shard_map/all_to_all | solution.py:30
  46.1 3.7 %collective-permute-start.6 = (f32[8,128]{1,0:T(8,128)S(1)}, f32[8,128]{1,0:T(8,128)S(1)}, u32[]{:S(2)}, u32[]{:S(2)}) collective-permute-start(f32[8,128]{1,0:T(8,128)S(1)} %get-tuple-element.71), channel_id=1, source_target_pairs={{0,16},{16,0},{1,17},{17,1},{2,18},{18,2},{3,19},{19,3},{4,20},{20... | collective-permute-start | bytes 12296 | tf_op jit(solution)/shard_map/ppermute | solution.py:26
  49.8 5.6 %copy-start.3 = (f32[32]{0:T(128)S(1)}, f32[32]{0:T(128)}, u32[]{:S(2)}) copy-start(f32[32]{0:T(128)} %param.12) | copy-start | bytes 388
  49.8 5.6 %copy-start.4 = (bf16[32,1024]{1,0:T(8,128)(2,1)S(1)}, bf16[32,1024]{1,0:T(8,128)(2,1)}, u32[]{:S(2)}) copy-start(bf16[32,1024]{1,0:T(8,128)(2,1)} %targets.3) | copy-start | bytes 196612
  56.5 1.6 %collective-permute-start.7 = (bf16[8,16,1024]{2,1,0:T(8,128)(2,1)S(1)}, bf16[8,16,1024]{2,1,0:T(8,128)(2,1)S(1)}, u32[]{:S(2)}, u32[]{:S(2)}) collective-permute-start(bf16[8,16,1024]{2,1,0:T(8,128)(2,1)S(1)} %get-tuple-element.73), channel_id=1, source_target_pairs={{0,1},{1,0},{2,3},{3,2},{4,5},{5,4},{6,7},{7,6},{8,9},{9,8},{10,11... | collective-permute-start | bytes 786440 | tf_op jit(solution)/shard_map/ppermute | solution.py:26
  60.6 6.3 %collective-permute-start.8 = (bf16[2,16,1024]{2,1,0:T(8,128)(2,1)S(1)}, bf16[2,16,1024]{2,1,0:T(8,128)(2,1)S(1)}, u32[]{:S(2)}, u32[]{:S(2)}) collective-permute-start(bf16[2,16,1024]{2,1,0:T(8,128)(2,1)S(1)} %get-tuple-element.83), channel_id=1, source_target_pairs={{0,2},{1,3},{2,0},{3,1},{4,6},{5,7},{6,4},{7,5},{8,10},{9,11},{10,... | collective-permute-start | bytes 196616 | tf_op jit(solution)/shard_map/ppermute | solution.py:26
  61.0 8.7 %collective-permute-start.9 = (bf16[2,16,1024]{2,1,0:T(8,128)(2,1)S(1)}, bf16[2,16,1024]{2,1,0:T(8,128)(2,1)S(1)}, u32[]{:S(2)}, u32[]{:S(2)}) collective-permute-start(bf16[2,16,1024]{2,1,0:T(8,128)(2,1)S(1)} %get-tuple-element.84), channel_id=1, source_target_pairs={{0,4},{1,5},{2,6},{3,7},{4,0},{5,1},{6,2},{7,3},{8,12},{9,13},{10,... | collective-permute-start | bytes 196616 | tf_op jit(solution)/shard_map/ppermute | solution.py:26
  63.0 16.2 %collective-permute-start.10 = (bf16[2,16,1024]{2,1,0:T(8,128)(2,1)S(1)}, bf16[2,16,1024]{2,1,0:T(8,128)(2,1)S(1)}, u32[]{:S(2)}, u32[]{:S(2)}) collective-permute-start(bf16[2,16,1024]{2,1,0:T(8,128)(2,1)S(1)} %get-tuple-element.85), channel_id=1, source_target_pairs={{0,6},{1,7},{2,4},{3,5},{4,2},{5,3},{6,0},{7,1},{8,14},{9,15},{10,... | collective-permute-start | bytes 196616 | tf_op jit(solution)/shard_map/ppermute | solution.py:26
  64.1 15.0 %collective-permute-start.11 = (bf16[2,16,1024]{2,1,0:T(8,128)(2,1)S(1)}, bf16[2,16,1024]{2,1,0:T(8,128)(2,1)S(1)}, u32[]{:S(2)}, u32[]{:S(2)}) collective-permute-start(bf16[2,16,1024]{2,1,0:T(8,128)(2,1)S(1)} %get-tuple-element.86), channel_id=1, source_target_pairs={{0,8},{1,9},{2,10},{3,11},{4,12},{5,13},{6,14},{7,15},{8,0},{9,1},... | collective-permute-start | bytes 196616 | tf_op jit(solution)/shard_map/ppermute | solution.py:26
  66.3 12.8 %collective-permute-start.12 = (bf16[2,16,1024]{2,1,0:T(8,128)(2,1)S(1)}, bf16[2,16,1024]{2,1,0:T(8,128)(2,1)S(1)}, u32[]{:S(2)}, u32[]{:S(2)}) collective-permute-start(bf16[2,16,1024]{2,1,0:T(8,128)(2,1)S(1)} %get-tuple-element.87), channel_id=1, source_target_pairs={{0,10},{1,11},{2,8},{3,9},{4,14},{5,15},{6,12},{7,13},{8,2},{9,3},... | collective-permute-start | bytes 196616 | tf_op jit(solution)/shard_map/ppermute | solution.py:26
  66.9 12.3 %collective-permute-start.13 = (bf16[2,16,1024]{2,1,0:T(8,128)(2,1)S(1)}, bf16[2,16,1024]{2,1,0:T(8,128)(2,1)S(1)}, u32[]{:S(2)}, u32[]{:S(2)}) collective-permute-start(bf16[2,16,1024]{2,1,0:T(8,128)(2,1)S(1)} %get-tuple-element.88), channel_id=1, source_target_pairs={{0,12},{1,13},{2,14},{3,15},{4,8},{5,9},{6,10},{7,11},{8,4},{9,5},... | collective-permute-start | bytes 196616 | tf_op jit(solution)/shard_map/ppermute | solution.py:26
  69.7 9.4 %collective-permute-start.14 = (bf16[2,16,1024]{2,1,0:T(8,128)(2,1)S(1)}, bf16[2,16,1024]{2,1,0:T(8,128)(2,1)S(1)}, u32[]{:S(2)}, u32[]{:S(2)}) collective-permute-start(bf16[2,16,1024]{2,1,0:T(8,128)(2,1)S(1)} %get-tuple-element.89), channel_id=1, source_target_pairs={{0,14},{1,15},{2,12},{3,13},{4,10},{5,11},{6,8},{7,9},{8,6},{9,7},... | collective-permute-start | bytes 196616 | tf_op jit(solution)/shard_map/ppermute | solution.py:26
  79.2 18.6 %all-to-all-start.2 = ((bf16[16,16,1024]{2,1,0:T(8,128)(2,1)}), bf16[16,16,1024]{2,1,0:T(8,128)(2,1)S(1)}, u32[]{:S(2)}, u32[]{:S(2)}) async-start(bf16[16,16,1024]{2,1,0:T(8,128)(2,1)} %get-tuple-element.99), calls=%async_computation.2 | async-start | bytes 1048576 | tf_op jit(solution)/shard_map/all_to_all | solution.py:30

commit v4 on v2

v4 whole, which is shorter than its diff:
```python
import functools

import jax
import jax.numpy as jnp
from jax import lax
from jax.experimental import pallas as pl
from jax.experimental.pallas import tpu as pltpu
from jax.sharding import PartitionSpec as P

EPSILON = 1e-06
TOKENS_AT_ONCE = 16
HIDDEN_PIECES = 4
NETWORK_LIMIT = 50
ROWS_LIMIT = 53
BF16 = jnp.bfloat16
F32 = jnp.float32

VMEM = pl.BlockSpec(memory_space=pltpu.VMEM)
SMEM = pl.BlockSpec(memory_space=pltpu.SMEM)
HBM = pl.BlockSpec(memory_space=pltpu.HBM)


def swap(value, axis, bit):
    size = lax.axis_size(axis)
    return lax.ppermute(value, axis, [(i, i ^ bit) for i in range(size)])


def bits_of(size):
    return [1 << i for i in range(size.bit_length() - 1)]


def transposed(value):
    return lax.all_to_all(value, "member", split_axis=0, concat_axis=0, tiled=True)


def local_call(kernel, out_shape, in_specs, flops=0, moved=0, scratch=(), limit=40):
    return pl.pallas_call(
        kernel,
        in_specs=in_specs,
        out_specs=[VMEM] * len(out_shape),
        out_shape=out_shape,
        scratch_shapes=list(scratch),
        compiler_params=pltpu.CompilerParams(vmem_limit_bytes=limit * 2**20),
        cost_estimate=pl.CostEstimate(flops=flops, bytes_accessed=moved, transcendentals=0),
    )


def rows_kernel(lanes, owners, analyses, *refs):
    outs, sems = refs[:lanes], refs[lanes]
    own = outs[0].shape[0]
    me = lax.axis_index("member")
    lane = me % lanes
    block = jnp.int32(0)
    for b in range(owners.shape[0]):
        block = jnp.where(owners[b] == me, b, block)
    copies = []
    for k in range(lanes):
        start = pl.multiple_of((block * lanes + (lane ^ k)) * own, own)
        copies.append(
            pltpu.make_async_copy(analyses.at[0, pl.ds(start, own), :], outs[k], sems.at[k])
        )
    for copy in copies:
        copy.start()
    for copy in copies:
        copy.wait()


def blocks_kernel(lanes, owners, *refs):
    held, (keep, give) = refs[:lanes], refs[lanes:]
    me = lax.axis_index("member")
    lane, plane = me % lanes, me // lanes

    def rows_of(block):
        place = (owners[block] % lanes) ^ lane
        rows = held[0][...]
        for k in range(1, lanes):
            rows = jnp.where(place == k, held[k][...], rows)
        return rows

    side = plane % 2
    for j in range(keep.shape[0]):
        keep[j] = rows_of(2 * j + side)
        give[j] = rows_of(2 * j + 1 - side)


def merged(lanes, owners, plane, bit, keep, got, j):
    block = j * (2 * bit) + plane % (2 * bit)
    there = ((owners[block] // lanes) ^ plane) // bit % 2
    return jnp.where(there == 1, got[j], keep[j])


def halve_kernel(lanes, bit, owners, keep, got, keep_out, give):
    plane = lax.axis_index("member") // lanes
    side = plane // (2 * bit) % 2
    rows = [merged(lanes, owners, plane, bit, keep, got, j) for j in range(keep.shape[0])]
    for j in range(keep_out.shape[0]):
        keep_out[j] = jnp.where(side == 1, rows[2 * j + 1], rows[2 * j])
        give[j] = jnp.where(side == 1, rows[2 * j], rows[2 * j + 1])


def encode_kernel(lanes, bit, owners, keep, got, encoder, latent):
    plane = lax.axis_index("member") // lanes
    control = merged(lanes, owners, plane, bit, keep, got, 0)
    latent[...] = jnp.dot(control, encoder[...], preferred_element_type=F32).astype(BF16)


def latent_rows(analyses, owners, encoder):
    members = lax.axis_size("member")
    _, rows, features = analyses.shape
    blocks = owners.shape[0]
    lanes, own = members // blocks, rows // members

    def kept(many):
        return jax.ShapeDtypeStruct((many, own, features), BF16)

    row = jax.ShapeDtypeStruct((own, features), BF16)
    by_lane = local_call(
        functools.partial(rows_kernel, lanes),
        [row] * lanes,
        [SMEM, HBM],
        scratch=[pltpu.SemaphoreType.DMA((lanes,))],
        limit=ROWS_LIMIT,
    )(owners, analyses)
    by_lane = [by_lane[0]] + [swap(by_lane[k], "member", k) for k in range(1, lanes)]
    keep, give = local_call(
        functools.partial(blocks_kernel, lanes),
        [kept(blocks // 2)] * 2,
        [SMEM] + [VMEM] * lanes,
        limit=8,
    )(owners, *by_lane)
    bit = 1
    while 2 * bit < blocks:
        got = swap(give, "member", bit * lanes)
        keep, give = local_call(
            functools.partial(halve_kernel, lanes, bit),
            [kept(keep.shape[0] // 2)] * 2,
            [SMEM] + [VMEM] * 2,
            limit=8,
        )(owners, keep, got)
        bit *= 2
    got = swap(give, "member", bit * lanes)
    return local_call(
        functools.partial(encode_kernel, lanes, bit),
        [row],
        [SMEM] + [VMEM] * 3,
        flops=2 * own * features * features,
        limit=8,
    )(owners, keep, got, encoder)[0]


def column(row):
    size = row.shape[1]
    first = lax.broadcasted_iota(jnp.int32, (size, size), 0)
    second = lax.broadcasted_iota(jnp.int32, (size, size), 1)
    return jnp.sum(jnp.where(first == second, row, 0.0), axis=1, keepdims=True)


def network(noise, latent, hidden_piece, pieces):
    members, tokens, features = noise.shape
    states = (noise.astype(F32) + latent.astype(F32)[None]).reshape(members * tokens, features)
    mean = jnp.sum(states * states, axis=-1, keepdims=True) * (1.0 / features)
    normed = (states * lax.rsqrt(mean + EPSILON)).astype(BF16)
    total = states
    for piece in range(pieces):
        total = total + hidden_piece(normed, piece)
    return total.astype(BF16)


def score(forecast, targets, scale, members, tokens):
    rows, features = forecast.shape
    gram = lax.dot_general(
        forecast, forecast, (((1,), (1,)), ((), ())), preferred_element_type=F32
    )
    first = lax.broadcasted_iota(jnp.int32, (rows, rows), 0)
    second = lax.broadcasted_iota(jnp.int32, (rows, rows), 1)
    same_row = first == second
    same_token = (first % tokens) == (second % tokens)
    on_diagonal = jnp.where(same_row, gram, 0.0)
    down = jnp.sum(on_diagonal, axis=1, keepdims=True)
    across = jnp.sum(on_diagonal, axis=0, keepdims=True)
    squared = jnp.maximum((down + across - 2.0 * gram) * (1.0 / features), 0.0) + EPSILON
    inverse = lax.rsqrt(squared)
    pairs = jnp.where(same_token, squared * inverse, 0.0)
    coeff = jnp.where(same_token & ~same_row, inverse, 0.0).astype(BF16)
    coeff_sum = jnp.sum(coeff.astype(F32), axis=1, keepdims=True)
    combined = jnp.dot(coeff, forecast, preferred_element_type=F32)
    values = forecast.astype(F32)
    apart = (
        values.reshape(members, tokens, features) - targets.astype(F32)[None]
    )
    squares = jnp.sum(apart * apart, axis=-1, keepdims=True) * (1.0 / features) + EPSILON
    inverse_spread = lax.rsqrt(squares)
    from_others = (coeff_sum * values - combined).reshape(members, tokens, features)
    gradient = scale[None] * (apart * inverse_spread - from_others * (1.0 / members))
    spread = jnp.sum(squares * inverse_spread, axis=0) * (1.0 / members)
    pair_sum = jnp.sum(jnp.sum(pairs, axis=1, keepdims=True).reshape(members, tokens, 1), axis=0)
    energy = scale * (spread - pair_sum * (1.0 / (2.0 * members * members)))
    return gradient, energy


def member_kernel(
    noise,
    latent,
    targets,
    weight,
    inlet_hbm,
    outlet_hbm,
    gradient_out,
    energy_out,
    inlet,
    outlet,
    inlet_sems,
    outlet_sems,
):
    members, own, features = noise.shape
    width = inlet.shape[1] // HIDDEN_PIECES
    copies = []
    for piece in range(HIDDEN_PIECES):
        part = pl.ds(piece * width, width)
        copies.append(
            (
                pltpu.make_async_copy(
                    inlet_hbm.at[:, part], inlet.at[:, part], inlet_sems.at[piece]
                ),
                pltpu.make_async_copy(
                    outlet_hbm.at[part, :], outlet.at[part, :], outlet_sems.at[piece]
                ),
            )
        )
    for into, out_of in copies:
        into.start()
        out_of.start()

    def hidden_piece(normed, piece):
        part = slice(piece * width, (piece + 1) * width)
        copies[piece][0].wait()
        hidden = jax.nn.gelu(
            jnp.dot(normed, inlet[:, part], preferred_element_type=F32), approximate=True
        ).astype(BF16)
        copies[piece][1].wait()
        return jnp.dot(hidden, outlet[part, :], preferred_element_type=F32)

    forecast = network(noise[...], latent[...], hidden_piece, HIDDEN_PIECES)
    forecast = forecast.reshape(members, own, features)
    scale = column(weight[...])
    for first in range(0, own, TOKENS_AT_ONCE):
        here = slice(first, first + TOKENS_AT_ONCE)
        gradient, energy = score(
            forecast[:, here].reshape(members * TOKENS_AT_ONCE, features),
            targets[here, :],
            scale[here, :],
            members,
            TOKENS_AT_ONCE,
        )
        gradient_out[:, here, :] = gradient.astype(BF16)
        energy_out[here, :] = energy


def on_device(
    analyses,
    owners,
    noise,
    targets,
    area_weight,
    enc_weight,
    sample_inlet_matrix,
    sample_outlet_matrix,
):
    members, regions = lax.axis_size("member"), lax.axis_size("region")
    _, region_rows, features = noise.shape
    hidden = sample_inlet_matrix.shape[1]
    own = region_rows // members
    here = transposed(noise.reshape(members, own, features))
    latent = latent_rows(analyses, owners, enc_weight)
    gradient, energy = local_call(
        member_kernel,
        [
            jax.ShapeDtypeStruct((members, own, features), BF16),
            jax.ShapeDtypeStruct((own, 1), F32),
        ],
        [VMEM] * 4 + [HBM] * 2,
        flops=4 * members * own * features * (hidden + members),
        moved=4 * features * hidden,
        scratch=[
            pltpu.VMEM((features, hidden), BF16),
            pltpu.VMEM((hidden, features), BF16),
            pltpu.SemaphoreType.DMA((HIDDEN_PIECES,)),
            pltpu.SemaphoreType.DMA((HIDDEN_PIECES,)),
        ],
        limit=NETWORK_LIMIT,
    )(here, latent, targets, area_weight[None], sample_inlet_matrix, sample_outlet_matrix)
    gradient, total = lax.optimization_barrier((gradient, area_weight))
    back = transposed(gradient)
    for bit in bits_of(members):
        total = total + swap(total, "member", bit)
    for bit in bits_of(regions):
        total = total + swap(total, "region", bit)
    factor = float(region_rows * regions) / jnp.sum(total)
    member_grad = (back.astype(F32) * factor).astype(BF16).reshape(1, region_rows, features)
    return member_grad, energy[:, 0] * factor


def solution(mesh):
    return jax.shard_map(
        on_device,
        mesh=mesh,
        in_specs=(
            P("member", "region", None),
            P(),
            P("member", "region", None),
            P(("region", "member"), None),
            P(("region", "member")),
            P(),
            P(),
            P(),
        ),
        out_specs=(P("member", "region", None), P(("region", "member"))),
        check_vma=False,
    )
```

time: 87.5 us -> 89.1 us (1.018); the launches traced: 85.9 us -> 88.8 us
  starting transfers between devices: 19.3 us -> 29.5 us
  local copies, waits for them, and re-layouts: 8.72 us -> 0.02 us
  waiting for transfers between devices: 45.3 us -> 40.8 us
  Pallas kernels: 10.6 us -> 14.6 us
  other arithmetic: 1.29 us -> 2.43 us
    all_to_all x2, waiting for transfers between devices: 22.3 us -> 0.02 us  [transposed(): lax.all_to_all(value, 'member', split_axis=0, concat_axis=0, tiled=True)]
    ppermute x6 -> x10, waiting for transfers between devices: 22.9 us -> 40.8 us  [swap(): return lax.ppermute(value, axis, [(i, i ^ bit) for i in range(size)])]
    unnamed x15 -> x8, local copies, waits for them, and re-layouts: 8.72 us -> 0.02 us
    ppermute x6 -> x10, starting transfers between devices: 7.95 us -> 14.7 us  [swap(): return lax.ppermute(value, axis, [(i, i ^ bit) for i in range(size)])]
    pallas_call x1, Pallas kernels: 7.34 us -> 10.9 us  [on_device(): local_call(member_kernel, [jax.ShapeDtypeStruct((members, own, features),...]
    all_to_all x2, starting transfers between devices: 11.4 us -> 14.8 us  [transposed(): lax.all_to_all(value, 'member', split_axis=0, concat_axis=0, tiled=True)]
    convert_element_type x0 -> x1, other arithmetic: none -> 1.19 us  [on_device(): (back.astype(F32) * factor).astype(BF16).reshape(1, region_rows, features)]
  transfers between devices with their start and end apart: 8 -> 12, of which waited for: 6 -> 9; matrix products, arithmetic and copies ran while one was open for 1% -> 1% of each run, Pallas kernels for 4% -> 4%
where the time goes in v4:
time: 89.1 us; the launch traced here: 88.8 us
  waiting for transfers between devices  40.8 us (46%)
  starting transfers between devices  29.5 us (33%)
  Pallas kernels  14.6 us (16%)
  other arithmetic  2.43 us (3%)
  between operations  1.45 us (2%)
    ppermute x10, waiting for transfers between devices, swap(): return lax.ppermute(value, axis, [(i, i ^ bit) for i in range(size)])  40.8 us
    all_to_all x2, starting transfers between devices, transposed(): lax.all_to_all(value, 'member', split_axis=0, concat_axis=0, tiled=True)  14.8 us
    ppermute x10, starting transfers between devices, swap(): return lax.ppermute(value, axis, [(i, i ^ bit) for i in range(size)])  14.7 us
    pallas_call x1, Pallas kernels, on_device(): local_call(member_kernel, [jax.ShapeDtypeStruct((members, own, features),...  10.9 us
  transfers between devices with their start and end apart: 12, of which 9 were waited for; matrix products, arithmetic and copies ran while one was open for 1% of the time, Pallas kernels for 4%

profile of v4, /device:TPU:0, one launch (start us, length us, event | category | flops | bytes accessed | tf_op | source)
XLA Modules:
  0.0 88.8 jit_solution(8076478473916251125)
XLA Ops:
  0.6 0.0 copy-start.1
  0.6 0.0 copy-start
  0.6 7.5 %all-to-all-start = ((bf16[16,32,1024]{2,1,0:T(8,128)(2,1)}), bf16[16,32,1024]{2,1,0:T(8,128)(2,1)S(1)}, u32[]{:S(2)}, u32[]{:S(2)}) async-start(bf16[16,32,1024]{2,1,0:T(8,128)(2,1)} %bitcast.5), calls=%async_computation | async-start | bytes 2097152 | tf_op jit(solution)/shard_map/all_to_all | solution.py:33
  8.2 0.0 copy-done.1
  8.2 0.0 copy-start.2
  8.2 0.0 copy-start.3
  8.2 1.5 %shard_map.95 = (bf16[32,1024]{1,0:T(8,128)(2,1)S(1)}, bf16[32,1024]{1,0:T(8,128)(2,1)S(1)}, bf16[32,1024]{1,0:T(8,128)(2,1)S(1)}, bf16[32,1024]{1,0:T(8,128)(2,1)S(1)}) custom-call(s32[4]{0:T(128)S(1)} %copy-done.1, bf16[1,512,1024]{2,1,0:T(8,128)(2,1)} %analyses.1), custom_call_target="tpu_custom_call" | custom-call | tf_op jit(solution)/shard_map/pallas_call | solution.py:117
  9.8 0.5 collective-permute-start
  10.2 1.7 %collective-permute-start.1 = (bf16[32,1024]{1,0:T(8,128)(2,1)S(1)}, bf16[32,1024]{1,0:T(8,128)(2,1)S(1)}, u32[]{:S(2)}, u32[]{:S(2)}) collective-permute-start(bf16[32,1024]{1,0:T(8,128)(2,1)S(1)} %get-tuple-element.16), channel_id=1, source_target_pairs={{0,2},{1,3},{2,0},{3,1},{4,6},{5,7},{6,4},{7,5},{8,10},{9,11},{10,... | collective-permute-start | bytes 196616 | tf_op jit(solution)/shard_map/ppermute | solution.py:25
  11.9 0.0 collective-permute-start.2
  11.9 0.0 collective-permute-done.refs_1_
  11.9 7.9 %collective-permute-done.1.refs_2_ = bf16[32,1024]{1,0:T(8,128)(2,1)S(1)} collective-permute-done((bf16[32,1024]{1,0:T(8,128)(2,1)S(1)}, bf16[32,1024]{1,0:T(8,128)(2,1)S(1)}, u32[]{:S(2)}, u32[]{:S(2)}) %collective-permute-start.1) | collective-permute-done | bytes 65568 | tf_op jit(solution)/shard_map/ppermute | solution.py:25
  19.8 0.6 collective-permute-done.2.refs_3_
  20.4 0.6 shard_map.96
  21.0 0.1 collective-permute-start.3
  21.0 8.0 %collective-permute-done.3.got = bf16[2,32,1024]{2,1,0:T(8,128)(2,1)S(1)} collective-permute-done((bf16[2,32,1024]{2,1,0:T(8,128)(2,1)S(1)}, bf16[2,32,1024]{2,1,0:T(8,128)(2,1)S(1)}, u32[]{:S(2)}, u32[]{:S(2)}) %collective-permute-start.3) | collective-permute-done | bytes 131104 | tf_op jit(solution)/shard_map/ppermute | solution.py:25
  29.1 0.6 shard_map.97
  29.7 4.5 %collective-permute-start.4 = (bf16[1,32,1024]{2,1,0:T(8,128)(2,1)S(1)}, bf16[1,32,1024]{2,1,0:T(8,128)(2,1)S(1)}, u32[]{:S(2)}, u32[]{:S(2)}) collective-permute-start(bf16[1,32,1024]{2,1,0:T(8,128)(2,1)S(1)} %get-tuple-element.21), channel_id=1, source_target_pairs={{0,8},{1,9},{2,10},{3,11},{4,12},{5,13},{6,14},{7,15},{8,0},{9,1},... | collective-permute-start | bytes 196616 | tf_op jit(solution)/shard_map/ppermute | solution.py:25
  34.1 2.2 %collective-permute-done.4.got = bf16[1,32,1024]{2,1,0:T(8,128)(2,1)S(1)} collective-permute-done((bf16[1,32,1024]{2,1,0:T(8,128)(2,1)S(1)}, bf16[1,32,1024]{2,1,0:T(8,128)(2,1)S(1)}, u32[]{:S(2)}, u32[]{:S(2)}) %collective-permute-start.4) | collective-permute-done | bytes 65568 | tf_op jit(solution)/shard_map/ppermute | solution.py:25
  36.4 0.0 copy-done
  36.4 1.0 %shard_map.98.latent = bf16[32,1024]{1,0:T(8,128)(2,1)S(1)} custom-call(s32[4]{0:T(128)S(1)} %copy-done.1, bf16[1,32,1024]{2,1,0:T(8,128)(2,1)S(1)} %get-tuple-element.20.keep, bf16[1,32,1024]{2,1,0:T(8,128)(2,1)S(1)} %collective-permute-done.4.got, bf16[1024,1024]{1,0:T(8,128)(2,1)S(1)} %copy-done), custom_call_target="tpu_custom_call" | custom-call | flops 67108864 | tf_op jit(solution)/shard_map/pallas_call | solution.py:142
  37.4 0.0 all-to-all-done.noise
  37.4 0.0 copy-done.2
  37.4 0.0 copy-done.3
  37.4 10.9 %shard_map.99 = (bf16[16,32,1024]{2,1,0:T(8,128)(2,1)}, f32[32,1]{1,0:T(8,128)S(1)}) custom-call(bf16[16,32,1024]{2,1,0:T(8,128)(2,1)S(1)} %all-to-all-done.noise, bf16[32,1024]{1,0:T(8,128)(2,1)S(1)} %shard_map.98.latent, bf16[32,1024]{1,0:T(8,128)(2,1)S(1)} %copy-done.2, f32[1,32]{1,0:T(1,128)S(1)} %bitcast.3, bf16[1024,2048]{1,0:T(8,128)(2,1)} %inlet_hbm.1, ...), custom_call_target="tpu_custom_call" | custom-call | flops 4328521728 | bytes 8388608 | tf_op jit(solution)/shard_map/pallas_call | solution.py:275
  48.3 7.3 %all-to-all-start.1 = ((bf16[16,32,1024]{2,1,0:T(8,128)(2,1)}), bf16[16,32,1024]{2,1,0:T(8,128)(2,1)S(1)}, u32[]{:S(2)}, u32[]{:S(2)}) async-start(bf16[16,32,1024]{2,1,0:T(8,128)(2,1)} %get-tuple-element.23), calls=%async_computation.1 | async-start | bytes 2097152 | tf_op jit(solution)/shard_map/all_to_all | solution.py:33
  55.6 0.4 collective-permute-start.5
  56.0 0.8 collective-permute-done.5
  56.8 1.8 %collective-permute-start.6 = (f32[32]{0:T(128)S(1)}, f32[32]{0:T(128)S(1)}, u32[]{:S(2)}, u32[]{:S(2)}) collective-permute-start(f32[32]{0:T(128)S(1)} %add.15), channel_id=1, source_target_pairs={{0,2},{1,3},{2,0},{3,1},{4,6},{5,7},{6,4},{7,5},{8,10},{9,11},{10,... | collective-permute-start | bytes 392 | tf_op jit(solution)/shard_map/ppermute | solution.py:25
  58.7 5.2 %collective-permute-done.6 = f32[32]{0:T(128)S(1)} collective-permute-done((f32[32]{0:T(128)S(1)}, f32[32]{0:T(128)S(1)}, u32[]{:S(2)}, u32[]{:S(2)}) %collective-permute-start.6) | collective-permute-done | bytes 160 | tf_op jit(solution)/shard_map/ppermute | solution.py:25
  63.9 0.0 collective-permute-start.7
  63.9 9.9 %collective-permute-done.7 = f32[32]{0:T(128)S(1)} collective-permute-done((f32[32]{0:T(128)S(1)}, f32[32]{0:T(128)S(1)}, u32[]{:S(2)}, u32[]{:S(2)}) %collective-permute-start.7) | collective-permute-done | bytes 160 | tf_op jit(solution)/shard_map/ppermute | solution.py:25
  73.8 4.3 %collective-permute-start.8 = (f32[32]{0:T(128)S(1)}, f32[32]{0:T(128)S(1)}, u32[]{:S(2)}, u32[]{:S(2)}) collective-permute-start(f32[32]{0:T(128)S(1)} %add.17), channel_id=1, source_target_pairs={{0,8},{1,9},{2,10},{3,11},{4,12},{5,13},{6,14},{7,15},{8,0},{9,1},... | collective-permute-start | bytes 392 | tf_op jit(solution)/shard_map/ppermute | solution.py:25
  78.1 4.1 %collective-permute-done.8 = f32[32]{0:T(128)S(1)} collective-permute-done((f32[32]{0:T(128)S(1)}, f32[32]{0:T(128)S(1)}, u32[]{:S(2)}, u32[]{:S(2)}) %collective-permute-start.8) | collective-permute-done | bytes 160 | tf_op jit(solution)/shard_map/ppermute | solution.py:25
  82.1 1.5 %collective-permute-start.9 = (f32[32]{0:T(128)S(1)}, f32[32]{0:T(128)S(1)}, u32[]{:S(2)}, u32[]{:S(2)}) collective-permute-start(f32[32]{0:T(128)S(1)} %add.18), channel_id=1, source_target_pairs={{0,16},{16,0},{1,17},{17,1},{2,18},{18,2},{3,19},{19,3},{4,20},{20... | collective-permute-start | bytes 392 | tf_op jit(solution)/shard_map/ppermute | solution.py:25
  83.6 2.1 %collective-permute-done.9 = f32[32]{0:T(128)S(1)} collective-permute-done((f32[32]{0:T(128)S(1)}, f32[32]{0:T(128)S(1)}, u32[]{:S(2)}, u32[]{:S(2)}) %collective-permute-start.9) | collective-permute-done | bytes 160 | tf_op jit(solution)/shard_map/ppermute | solution.py:25
  85.7 0.6 add_reduce_fusion
  87.0 0.6 multiply_reduce_fusion
  87.6 0.0 all-to-all-done.1
  87.6 1.2 %multiply_convert_fusion = bf16[16,32,1024]{2,1,0:T(8,128)(2,1)} fusion(bf16[16,32,1024]{2,1,0:T(8,128)(2,1)S(1)} %all-to-all-done.1, f32[]{:T(128)S(6)} %div.3), kind=kLoop, calls=%fused_computation | loop fusion | flops 1572864 | bytes 2097156 | tf_op jit(solution)/shard_map/convert_element_type | solution.py:299
  (4 shorter events, 0.0 us)
Async XLA Ops:
  0.6 7.6 %copy-start.1 = (s32[4]{0:T(128)S(1)}, s32[4]{0:T(128)}, u32[]{:S(2)}) copy-start(s32[4]{0:T(128)} %owners.7) | copy-start | bytes 52
  0.6 35.8 %copy-start = (bf16[1024,1024]{1,0:T(8,128)(2,1)S(1)}, bf16[1024,1024]{1,0:T(8,128)(2,1)}, u32[]{:S(2)}) copy-start(bf16[1024,1024]{1,0:T(8,128)(2,1)} %encoder.1) | copy-start | bytes 6291460
  0.6 36.8 %all-to-all-start = ((bf16[16,32,1024]{2,1,0:T(8,128)(2,1)}), bf16[16,32,1024]{2,1,0:T(8,128)(2,1)S(1)}, u32[]{:S(2)}, u32[]{:S(2)}) async-start(bf16[16,32,1024]{2,1,0:T(8,128)(2,1)} %bitcast.5), calls=%async_computation | async-start | bytes 2097152 | tf_op jit(solution)/shard_map/all_to_all | solution.py:33
  8.2 29.2 %copy-start.2 = (bf16[32,1024]{1,0:T(8,128)(2,1)S(1)}, bf16[32,1024]{1,0:T(8,128)(2,1)}, u32[]{:S(2)}) copy-start(bf16[32,1024]{1,0:T(8,128)(2,1)} %targets.1) | copy-start | bytes 196612
  8.2 29.2 %copy-start.3 = (f32[32]{0:T(128)S(1)}, f32[32]{0:T(128)}, u32[]{:S(2)}) copy-start(f32[32]{0:T(128)} %param.12) | copy-start | bytes 388
  9.8 2.2 %collective-permute-start = (bf16[32,1024]{1,0:T(8,128)(2,1)S(1)}, bf16[32,1024]{1,0:T(8,128)(2,1)S(1)}, u32[]{:S(2)}, u32[]{:S(2)}) collective-permute-start(bf16[32,1024]{1,0:T(8,128)(2,1)S(1)} %get-tuple-element.15), channel_id=1, source_target_pairs={{0,1},{1,0},{2,3},{3,2},{4,5},{5,4},{6,7},{7,6},{8,9},{9,8},{10,11... | collective-permute-start | bytes 196616 | tf_op jit(solution)/shard_map/ppermute | solution.py:25
  10.2 9.6 %collective-permute-start.1 = (bf16[32,1024]{1,0:T(8,128)(2,1)S(1)}, bf16[32,1024]{1,0:T(8,128)(2,1)S(1)}, u32[]{:S(2)}, u32[]{:S(2)}) collective-permute-start(bf16[32,1024]{1,0:T(8,128)(2,1)S(1)} %get-tuple-element.16), channel_id=1, source_target_pairs={{0,2},{1,3},{2,0},{3,1},{4,6},{5,7},{6,4},{7,5},{8,10},{9,11},{10,... | collective-permute-start | bytes 196616 | tf_op jit(solution)/shard_map/ppermute | solution.py:25
  11.9 8.5 %collective-permute-start.2 = (bf16[32,1024]{1,0:T(8,128)(2,1)S(1)}, bf16[32,1024]{1,0:T(8,128)(2,1)S(1)}, u32[]{:S(2)}, u32[]{:S(2)}) collective-permute-start(bf16[32,1024]{1,0:T(8,128)(2,1)S(1)} %get-tuple-element.17), channel_id=1, source_target_pairs={{0,3},{1,2},{2,1},{3,0},{4,7},{5,6},{6,5},{7,4},{8,11},{9,10},{10,... | collective-permute-start | bytes 196616 | tf_op jit(solution)/shard_map/ppermute | solution.py:25
  21.0 8.1 %collective-permute-start.3 = (bf16[2,32,1024]{2,1,0:T(8,128)(2,1)S(1)}, bf16[2,32,1024]{2,1,0:T(8,128)(2,1)S(1)}, u32[]{:S(2)}, u32[]{:S(2)}) collective-permute-start(bf16[2,32,1024]{2,1,0:T(8,128)(2,1)S(1)} %get-tuple-element.19), channel_id=1, source_target_pairs={{0,4},{1,5},{2,6},{3,7},{4,0},{5,1},{6,2},{7,3},{8,12},{9,13},{10,... | collective-permute-start | bytes 393224 | tf_op jit(solution)/shard_map/ppermute | solution.py:25
  29.7 6.7 %collective-permute-start.4 = (bf16[1,32,1024]{2,1,0:T(8,128)(2,1)S(1)}, bf16[1,32,1024]{2,1,0:T(8,128)(2,1)S(1)}, u32[]{:S(2)}, u32[]{:S(2)}) collective-permute-start(bf16[1,32,1024]{2,1,0:T(8,128)(2,1)S(1)} %get-tuple-element.21), channel_id=1, source_target_pairs={{0,8},{1,9},{2,10},{3,11},{4,12},{5,13},{6,14},{7,15},{8,0},{9,1},... | collective-permute-start | bytes 196616 | tf_op jit(solution)/shard_map/ppermute | solution.py:25
  48.3 39.3 %all-to-all-start.1 = ((bf16[16,32,1024]{2,1,0:T(8,128)(2,1)}), bf16[16,32,1024]{2,1,0:T(8,128)(2,1)S(1)}, u32[]{:S(2)}, u32[]{:S(2)}) async-start(bf16[16,32,1024]{2,1,0:T(8,128)(2,1)} %get-tuple-element.23), calls=%async_computation.1 | async-start | bytes 2097152 | tf_op jit(solution)/shard_map/all_to_all | solution.py:33
  55.6 1.2 %collective-permute-start.5 = (f32[32]{0:T(128)S(1)}, f32[32]{0:T(128)S(1)}, u32[]{:S(2)}, u32[]{:S(2)}) collective-permute-start(f32[32]{0:T(128)S(1)} %copy-done.3), channel_id=1, source_target_pairs={{0,1},{1,0},{2,3},{3,2},{4,5},{5,4},{6,7},{7,6},{8,9},{9,8},{10,11... | collective-permute-start | bytes 392 | tf_op jit(solution)/shard_map/ppermute | solution.py:25
  56.8 7.0 %collective-permute-start.6 = (f32[32]{0:T(128)S(1)}, f32[32]{0:T(128)S(1)}, u32[]{:S(2)}, u32[]{:S(2)}) collective-permute-start(f32[32]{0:T(128)S(1)} %add.15), channel_id=1, source_target_pairs={{0,2},{1,3},{2,0},{3,1},{4,6},{5,7},{6,4},{7,5},{8,10},{9,11},{10,... | collective-permute-start | bytes 392 | tf_op jit(solution)/shard_map/ppermute | solution.py:25
  63.9 9.9 %collective-permute-start.7 = (f32[32]{0:T(128)S(1)}, f32[32]{0:T(128)S(1)}, u32[]{:S(2)}, u32[]{:S(2)}) collective-permute-start(f32[32]{0:T(128)S(1)} %add.16), channel_id=1, source_target_pairs={{0,4},{1,5},{2,6},{3,7},{4,0},{5,1},{6,2},{7,3},{8,12},{9,13},{10,... | collective-permute-start | bytes 392 | tf_op jit(solution)/shard_map/ppermute | solution.py:25
  73.8 8.4 %collective-permute-start.8 = (f32[32]{0:T(128)S(1)}, f32[32]{0:T(128)S(1)}, u32[]{:S(2)}, u32[]{:S(2)}) collective-permute-start(f32[32]{0:T(128)S(1)} %add.17), channel_id=1, source_target_pairs={{0,8},{1,9},{2,10},{3,11},{4,12},{5,13},{6,14},{7,15},{8,0},{9,1},... | collective-permute-start | bytes 392 | tf_op jit(solution)/shard_map/ppermute | solution.py:25
  82.1 3.5 %collective-permute-start.9 = (f32[32]{0:T(128)S(1)}, f32[32]{0:T(128)S(1)}, u32[]{:S(2)}, u32[]{:S(2)}) collective-permute-start(f32[32]{0:T(128)S(1)} %add.18), channel_id=1, source_target_pairs={{0,16},{16,0},{1,17},{17,1},{2,18},{18,2},{3,19},{19,3},{4,20},{20... | collective-permute-start | bytes 392 | tf_op jit(solution)/shard_map/ppermute | solution.py:25

commit v5 on v4

--- a/solution.py
+++ b/solution.py
@@ -104,7 +104,13 @@
     latent[...] = jnp.dot(control, encoder[...], preferred_element_type=F32).astype(BF16)
 
 
-def latent_rows(analyses, owners, encoder):
+def summed(value, axis, bits):
+    for bit in bits:
+        value = value + swap(value, axis, bit)
+    return value
+
+
+def latent_rows(analyses, owners, encoder, weight):
     members = lax.axis_size("member")
     _, rows, features = analyses.shape
     blocks = owners.shape[0]
@@ -131,6 +137,9 @@
     bit = 1
     while 2 * bit < blocks:
         got = swap(give, "member", bit * lanes)
+        if bit == 1:
+            weight = summed(weight, "region", bits_of(lax.axis_size("region")))
+            got, weight = lax.optimization_barrier((got, weight))
         keep, give = local_call(
             functools.partial(halve_kernel, lanes, bit),
             [kept(keep.shape[0] // 2)] * 2,
@@ -139,13 +148,16 @@
         )(owners, keep, got)
         bit *= 2
     got = swap(give, "member", bit * lanes)
-    return local_call(
+    weight = summed(weight, "member", [1])
+    got, weight = lax.optimization_barrier((got, weight))
+    latent = local_call(
         functools.partial(encode_kernel, lanes, bit),
         [row],
         [SMEM] + [VMEM] * 3,
         flops=2 * own * features * features,
         limit=8,
     )(owners, keep, got, encoder)[0]
+    return latent, weight
 
 
 def column(row):
@@ -227,13 +239,18 @@
                 ),
             )
         )
-    for into, out_of in copies:
-        into.start()
-        out_of.start()
+
+    def fetch(piece):
+        for copy in copies[piece]:
+            copy.start()
+
+    fetch(0)
 
     def hidden_piece(normed, piece):
         part = slice(piece * width, (piece + 1) * width)
         copies[piece][0].wait()
+        if piece + 1 < HIDDEN_PIECES:
+            fetch(piece + 1)
         hidden = jax.nn.gelu(
             jnp.dot(normed, inlet[:, part], preferred_element_type=F32), approximate=True
         ).astype(BF16)
@@ -271,7 +288,7 @@
     hidden = sample_inlet_matrix.shape[1]
     own = region_rows // members
     here = transposed(noise.reshape(members, own, features))
-    latent = latent_rows(analyses, owners, enc_weight)
+    latent, total = latent_rows(analyses, owners, enc_weight, area_weight)
     gradient, energy = local_call(
         member_kernel,
         [
@@ -289,12 +306,11 @@
         ],
         limit=NETWORK_LIMIT,
     )(here, latent, targets, area_weight[None], sample_inlet_matrix, sample_outlet_matrix)
-    gradient, total = lax.optimization_barrier((gradient, area_weight))
+    planes = members // owners.shape[0]
+    total = summed(total, "member", [bit for bit in bits_of(members) if 1 < bit < planes])
+    gradient, total = lax.optimization_barrier((gradient, total))
     back = transposed(gradient)
-    for bit in bits_of(members):
-        total = total + swap(total, "member", bit)
-    for bit in bits_of(regions):
-        total = total + swap(total, "region", bit)
+    total = summed(total, "member", [bit for bit in bits_of(members) if bit >= planes])
     factor = float(region_rows * regions) / jnp.sum(total)
     member_grad = (back.astype(F32) * factor).astype(BF16).reshape(1, region_rows, features)
     return member_grad, energy[:, 0] * factor

time: 89.1 us -> 87.9 us (0.987)
  waiting for transfers between devices: 40.8 us -> 38.5 us
  starting transfers between devices: 29.5 us -> 30.8 us
    ppermute x10, waiting for transfers between devices: 40.8 us -> 38.5 us  [swap(): return lax.ppermute(value, axis, [(i, i ^ bit) for i in range(size)])]
    ppermute x10, starting transfers between devices: 14.7 us -> 16 us  [swap(): return lax.ppermute(value, axis, [(i, i ^ bit) for i in range(size)])]
where the time goes in v5:
time: 87.9 us; the launch traced here: 87.5 us
  waiting for transfers between devices  38.5 us (44%)
  starting transfers between devices  30.8 us (35%)
  Pallas kernels  14.3 us (16%)
  other arithmetic  2.46 us (3%)
  between operations  1.44 us (2%)
    ppermute x10, waiting for transfers between devices, swap(): return lax.ppermute(value, axis, [(i, i ^ bit) for i in range(size)])  38.5 us
    ppermute x10, starting transfers between devices, swap(): return lax.ppermute(value, axis, [(i, i ^ bit) for i in range(size)])  16 us
    all_to_all x2, starting transfers between devices, transposed(): lax.all_to_all(value, 'member', split_axis=0, concat_axis=0, tiled=True)  14.8 us
    pallas_call x1, Pallas kernels, on_device(): local_call(member_kernel, [jax.ShapeDtypeStruct((members, own, features),...  10.6 us
  transfers between devices with their start and end apart: 12, of which 9 were waited for; matrix products, arithmetic and copies ran while one was open for 1% of the time, Pallas kernels for 4%

profile of v5, /device:TPU:0, one launch (start us, length us, event | category | flops | bytes accessed | tf_op | source)
XLA Modules:
  0.0 87.5 jit_solution(12766882987131835335)
XLA Ops:
  0.6 0.0 copy-start.1
  0.6 0.0 copy-start.3
  0.7 0.0 copy-start
  0.7 7.5 %all-to-all-start = ((bf16[16,32,1024]{2,1,0:T(8,128)(2,1)}), bf16[16,32,1024]{2,1,0:T(8,128)(2,1)S(1)}, u32[]{:S(2)}, u32[]{:S(2)}) async-start(bf16[16,32,1024]{2,1,0:T(8,128)(2,1)} %bitcast.5), calls=%async_computation | async-start | bytes 2097152 | tf_op jit(solution)/shard_map/all_to_all | solution.py:33
  8.2 0.0 copy-done.1
  8.2 0.0 copy-start.2
  8.2 1.5 %shard_map.95 = (bf16[32,1024]{1,0:T(8,128)(2,1)S(1)}, bf16[32,1024]{1,0:T(8,128)(2,1)S(1)}, bf16[32,1024]{1,0:T(8,128)(2,1)S(1)}, bf16[32,1024]{1,0:T(8,128)(2,1)S(1)}) custom-call(s32[4]{0:T(128)S(1)} %copy-done.1, bf16[1,512,1024]{2,1,0:T(8,128)(2,1)} %analyses.1), custom_call_target="tpu_custom_call" | custom-call | tf_op jit(solution)/shard_map/pallas_call | solution.py:123
  9.8 0.5 collective-permute-start
  10.2 1.7 %collective-permute-start.1 = (bf16[32,1024]{1,0:T(8,128)(2,1)S(1)}, bf16[32,1024]{1,0:T(8,128)(2,1)S(1)}, u32[]{:S(2)}, u32[]{:S(2)}) collective-permute-start(bf16[32,1024]{1,0:T(8,128)(2,1)S(1)} %get-tuple-element.20), channel_id=1, source_target_pairs={{0,2},{1,3},{2,0},{3,1},{4,6},{5,7},{6,4},{7,5},{8,10},{9,11},{10,... | collective-permute-start | bytes 196616 | tf_op jit(solution)/shard_map/ppermute | solution.py:25
  11.9 0.0 collective-permute-start.2
  11.9 0.0 collective-permute-done.refs_1_
  11.9 7.9 %collective-permute-done.1.refs_2_ = bf16[32,1024]{1,0:T(8,128)(2,1)S(1)} collective-permute-done((bf16[32,1024]{1,0:T(8,128)(2,1)S(1)}, bf16[32,1024]{1,0:T(8,128)(2,1)S(1)}, u32[]{:S(2)}, u32[]{:S(2)}) %collective-permute-start.1) | collective-permute-done | bytes 65568 | tf_op jit(solution)/shard_map/ppermute | solution.py:25
  19.8 0.6 collective-permute-done.2.refs_3_
  20.4 0.6 shard_map.96
  21.0 0.1 collective-permute-start.3
  21.1 0.0 copy-done.3
  21.1 1.6 %collective-permute-start.4 = (f32[32]{0:T(128)S(1)}, f32[32]{0:T(128)S(1)}, u32[]{:S(2)}, u32[]{:S(2)}) collective-permute-start(f32[32]{0:T(128)S(1)} %copy-done.3), channel_id=1, source_target_pairs={{0,16},{16,0},{1,17},{17,1},{2,18},{18,2},{3,19},{19,3},{4,20},{20... | collective-permute-start | bytes 392 | tf_op jit(solution)/shard_map/ppermute | solution.py:25
  22.6 2.0 %collective-permute-done.4 = f32[32]{0:T(128)S(1)} collective-permute-done((f32[32]{0:T(128)S(1)}, f32[32]{0:T(128)S(1)}, u32[]{:S(2)}, u32[]{:S(2)}) %collective-permute-start.4) | collective-permute-done | bytes 160 | tf_op jit(solution)/shard_map/ppermute | solution.py:25
  24.7 4.4 %collective-permute-done.3.got = bf16[2,32,1024]{2,1,0:T(8,128)(2,1)S(1)} collective-permute-done((bf16[2,32,1024]{2,1,0:T(8,128)(2,1)S(1)}, bf16[2,32,1024]{2,1,0:T(8,128)(2,1)S(1)}, u32[]{:S(2)}, u32[]{:S(2)}) %collective-permute-start.3) | collective-permute-done | bytes 131104 | tf_op jit(solution)/shard_map/ppermute | solution.py:25
  29.1 0.6 shard_map.97
  29.7 4.5 %collective-permute-start.5 = (bf16[1,32,1024]{2,1,0:T(8,128)(2,1)S(1)}, bf16[1,32,1024]{2,1,0:T(8,128)(2,1)S(1)}, u32[]{:S(2)}, u32[]{:S(2)}) collective-permute-start(bf16[1,32,1024]{2,1,0:T(8,128)(2,1)S(1)} %get-tuple-element.26), channel_id=1, source_target_pairs={{0,8},{1,9},{2,10},{3,11},{4,12},{5,13},{6,14},{7,15},{8,0},{9,1},... | collective-permute-start | bytes 196616 | tf_op jit(solution)/shard_map/ppermute | solution.py:25
  34.2 0.0 collective-permute-start.6
  34.2 1.1 %collective-permute-done.6 = f32[32]{0:T(128)S(1)} collective-permute-done((f32[32]{0:T(128)S(1)}, f32[32]{0:T(128)S(1)}, u32[]{:S(2)}, u32[]{:S(2)}) %collective-permute-start.6) | collective-permute-done | bytes 160 | tf_op jit(solution)/shard_map/ppermute | solution.py:25
  35.3 1.1 %collective-permute-done.5.got = bf16[1,32,1024]{2,1,0:T(8,128)(2,1)S(1)} collective-permute-done((bf16[1,32,1024]{2,1,0:T(8,128)(2,1)S(1)}, bf16[1,32,1024]{2,1,0:T(8,128)(2,1)S(1)}, u32[]{:S(2)}, u32[]{:S(2)}) %collective-permute-start.5) | collective-permute-done | bytes 65568 | tf_op jit(solution)/shard_map/ppermute | solution.py:25
  36.4 1.5 %collective-permute-start.7 = (f32[32]{0:T(128)S(1)}, f32[32]{0:T(128)S(1)}, u32[]{:S(2)}, u32[]{:S(2)}) collective-permute-start(f32[32]{0:T(128)S(1)} %add.16), channel_id=1, source_target_pairs={{0,2},{1,3},{2,0},{3,1},{4,6},{5,7},{6,4},{7,5},{8,10},{9,11},{10,... | collective-permute-start | bytes 392 | tf_op jit(solution)/shard_map/ppermute | solution.py:25
  37.9 0.0 copy-done
  37.9 1.0 %shard_map.98.latent = bf16[32,1024]{1,0:T(8,128)(2,1)S(1)} custom-call(s32[4]{0:T(128)S(1)} %copy-done.1, bf16[1,32,1024]{2,1,0:T(8,128)(2,1)S(1)} %get-tuple-element.25.keep, bf16[1,32,1024]{2,1,0:T(8,128)(2,1)S(1)} %collective-permute-done.5.got, bf16[1024,1024]{1,0:T(8,128)(2,1)S(1)} %copy-done), custom_call_target="tpu_custom_call" | custom-call | flops 67108864 | tf_op jit(solution)/shard_map/pallas_call | solution.py:153
  38.9 1.0 %collective-permute-done.7 = f32[32]{0:T(128)S(1)} collective-permute-done((f32[32]{0:T(128)S(1)}, f32[32]{0:T(128)S(1)}, u32[]{:S(2)}, u32[]{:S(2)}) %collective-permute-start.7) | collective-permute-done | bytes 160 | tf_op jit(solution)/shard_map/ppermute | solution.py:25
  39.9 0.0 all-to-all-done.noise
  40.0 0.0 copy-done.2
  40.0 10.6 %shard_map.99 = (bf16[16,32,1024]{2,1,0:T(8,128)(2,1)}, f32[32,1]{1,0:T(8,128)S(1)}) custom-call(bf16[16,32,1024]{2,1,0:T(8,128)(2,1)S(1)} %all-to-all-done.noise, bf16[32,1024]{1,0:T(8,128)(2,1)S(1)} %shard_map.98.latent, bf16[32,1024]{1,0:T(8,128)(2,1)S(1)} %copy-done.2, f32[1,32]{1,0:T(1,128)S(1)} %bitcast.3, bf16[1024,2048]{1,0:T(8,128)(2,1)} %inlet_hbm.1, ...), custom_call_target="tpu_custom_call" | custom-call | flops 4328521728 | bytes 8388608 | tf_op jit(solution)/shard_map/pallas_call | solution.py:292
  50.5 7.2 %all-to-all-start.1 = ((bf16[16,32,1024]{2,1,0:T(8,128)(2,1)}), bf16[16,32,1024]{2,1,0:T(8,128)(2,1)S(1)}, u32[]{:S(2)}, u32[]{:S(2)}) async-start(bf16[16,32,1024]{2,1,0:T(8,128)(2,1)} %get-tuple-element.31), calls=%async_computation.1 | async-start | bytes 2097152 | tf_op jit(solution)/shard_map/all_to_all | solution.py:33
  57.8 1.9 %collective-permute-start.8 = (f32[32]{0:T(128)S(1)}, f32[32]{0:T(128)S(1)}, u32[]{:S(2)}, u32[]{:S(2)}) collective-permute-start(f32[32]{0:T(128)S(1)} %add.17), channel_id=1, source_target_pairs={{0,4},{1,5},{2,6},{3,7},{4,0},{5,1},{6,2},{7,3},{8,12},{9,13},{10,... | collective-permute-start | bytes 392 | tf_op jit(solution)/shard_map/ppermute | solution.py:25
  59.7 16.2 %collective-permute-done.8 = f32[32]{0:T(128)S(1)} collective-permute-done((f32[32]{0:T(128)S(1)}, f32[32]{0:T(128)S(1)}, u32[]{:S(2)}, u32[]{:S(2)}) %collective-permute-start.8) | collective-permute-done | bytes 160 | tf_op jit(solution)/shard_map/ppermute | solution.py:25
  76.0 4.3 %collective-permute-start.9 = (f32[32]{0:T(128)S(1)}, f32[32]{0:T(128)S(1)}, u32[]{:S(2)}, u32[]{:S(2)}) collective-permute-start(f32[32]{0:T(128)S(1)} %add.18), channel_id=1, source_target_pairs={{0,8},{1,9},{2,10},{3,11},{4,12},{5,13},{6,14},{7,15},{8,0},{9,1},... | collective-permute-start | bytes 392 | tf_op jit(solution)/shard_map/ppermute | solution.py:25
  80.3 4.1 %collective-permute-done.9 = f32[32]{0:T(128)S(1)} collective-permute-done((f32[32]{0:T(128)S(1)}, f32[32]{0:T(128)S(1)}, u32[]{:S(2)}, u32[]{:S(2)}) %collective-permute-start.9) | collective-permute-done | bytes 160 | tf_op jit(solution)/shard_map/ppermute | solution.py:25
  84.3 0.6 add_reduce_fusion
  85.6 0.6 multiply_reduce_fusion
  86.3 0.0 all-to-all-done.1
  86.3 1.2 %multiply_convert_fusion = bf16[16,32,1024]{2,1,0:T(8,128)(2,1)} fusion(bf16[16,32,1024]{2,1,0:T(8,128)(2,1)S(1)} %all-to-all-done.1, f32[]{:T(128)S(6)} %div.3), kind=kLoop, calls=%fused_computation | loop fusion | flops 1572864 | bytes 2097156 | tf_op jit(solution)/shard_map/convert_element_type | solution.py:315
  (4 shorter events, 0.0 us)
Async XLA Ops:
  0.6 7.6 %copy-start.1 = (s32[4]{0:T(128)S(1)}, s32[4]{0:T(128)}, u32[]{:S(2)}) copy-start(s32[4]{0:T(128)} %owners.7) | copy-start | bytes 52
  0.6 20.4 %copy-start.3 = (f32[32]{0:T(128)S(1)}, f32[32]{0:T(128)}, u32[]{:S(2)}) copy-start(f32[32]{0:T(128)} %param.12) | copy-start | bytes 388
  0.7 37.3 %copy-start = (bf16[1024,1024]{1,0:T(8,128)(2,1)S(1)}, bf16[1024,1024]{1,0:T(8,128)(2,1)}, u32[]{:S(2)}) copy-start(bf16[1024,1024]{1,0:T(8,128)(2,1)} %encoder.1) | copy-start | bytes 6291460
  0.7 39.3 %all-to-all-start = ((bf16[16,32,1024]{2,1,0:T(8,128)(2,1)}), bf16[16,32,1024]{2,1,0:T(8,128)(2,1)S(1)}, u32[]{:S(2)}, u32[]{:S(2)}) async-start(bf16[16,32,1024]{2,1,0:T(8,128)(2,1)} %bitcast.5), calls=%async_computation | async-start | bytes 2097152 | tf_op jit(solution)/shard_map/all_to_all | solution.py:33
  8.2 31.7 %copy-start.2 = (bf16[32,1024]{1,0:T(8,128)(2,1)S(1)}, bf16[32,1024]{1,0:T(8,128)(2,1)}, u32[]{:S(2)}) copy-start(bf16[32,1024]{1,0:T(8,128)(2,1)} %targets.1) | copy-start | bytes 196612
  9.8 2.2 %collective-permute-start = (bf16[32,1024]{1,0:T(8,128)(2,1)S(1)}, bf16[32,1024]{1,0:T(8,128)(2,1)S(1)}, u32[]{:S(2)}, u32[]{:S(2)}) collective-permute-start(bf16[32,1024]{1,0:T(8,128)(2,1)S(1)} %get-tuple-element.19), channel_id=1, source_target_pairs={{0,1},{1,0},{2,3},{3,2},{4,5},{5,4},{6,7},{7,6},{8,9},{9,8},{10,11... | collective-permute-start | bytes 196616 | tf_op jit(solution)/shard_map/ppermute | solution.py:25
  10.2 9.6 %collective-permute-start.1 = (bf16[32,1024]{1,0:T(8,128)(2,1)S(1)}, bf16[32,1024]{1,0:T(8,128)(2,1)S(1)}, u32[]{:S(2)}, u32[]{:S(2)}) collective-permute-start(bf16[32,1024]{1,0:T(8,128)(2,1)S(1)} %get-tuple-element.20), channel_id=1, source_target_pairs={{0,2},{1,3},{2,0},{3,1},{4,6},{5,7},{6,4},{7,5},{8,10},{9,11},{10,... | collective-permute-start | bytes 196616 | tf_op jit(solution)/shard_map/ppermute | solution.py:25
  11.9 8.5 %collective-permute-start.2 = (bf16[32,1024]{1,0:T(8,128)(2,1)S(1)}, bf16[32,1024]{1,0:T(8,128)(2,1)S(1)}, u32[]{:S(2)}, u32[]{:S(2)}) collective-permute-start(bf16[32,1024]{1,0:T(8,128)(2,1)S(1)} %get-tuple-element.21), channel_id=1, source_target_pairs={{0,3},{1,2},{2,1},{3,0},{4,7},{5,6},{6,5},{7,4},{8,11},{9,10},{10,... | collective-permute-start | bytes 196616 | tf_op jit(solution)/shard_map/ppermute | solution.py:25
  21.0 8.1 %collective-permute-start.3 = (bf16[2,32,1024]{2,1,0:T(8,128)(2,1)S(1)}, bf16[2,32,1024]{2,1,0:T(8,128)(2,1)S(1)}, u32[]{:S(2)}, u32[]{:S(2)}) collective-permute-start(bf16[2,32,1024]{2,1,0:T(8,128)(2,1)S(1)} %get-tuple-element.23), channel_id=1, source_target_pairs={{0,4},{1,5},{2,6},{3,7},{4,0},{5,1},{6,2},{7,3},{8,12},{9,13},{10,... | collective-permute-start | bytes 393224 | tf_op jit(solution)/shard_map/ppermute | solution.py:25
  21.1 3.6 %collective-permute-start.4 = (f32[32]{0:T(128)S(1)}, f32[32]{0:T(128)S(1)}, u32[]{:S(2)}, u32[]{:S(2)}) collective-permute-start(f32[32]{0:T(128)S(1)} %copy-done.3), channel_id=1, source_target_pairs={{0,16},{16,0},{1,17},{17,1},{2,18},{18,2},{3,19},{19,3},{4,20},{20... | collective-permute-start | bytes 392 | tf_op jit(solution)/shard_map/ppermute | solution.py:25
  29.7 6.7 %collective-permute-start.5 = (bf16[1,32,1024]{2,1,0:T(8,128)(2,1)S(1)}, bf16[1,32,1024]{2,1,0:T(8,128)(2,1)S(1)}, u32[]{:S(2)}, u32[]{:S(2)}) collective-permute-start(bf16[1,32,1024]{2,1,0:T(8,128)(2,1)S(1)} %get-tuple-element.26), channel_id=1, source_target_pairs={{0,8},{1,9},{2,10},{3,11},{4,12},{5,13},{6,14},{7,15},{8,0},{9,1},... | collective-permute-start | bytes 196616 | tf_op jit(solution)/shard_map/ppermute | solution.py:25
  34.2 1.1 %collective-permute-start.6 = (f32[32]{0:T(128)S(1)}, f32[32]{0:T(128)S(1)}, u32[]{:S(2)}, u32[]{:S(2)}) collective-permute-start(f32[32]{0:T(128)S(1)} %add.15), channel_id=1, source_target_pairs={{0,1},{1,0},{2,3},{3,2},{4,5},{5,4},{6,7},{7,6},{8,9},{9,8},{10,11... | collective-permute-start | bytes 392 | tf_op jit(solution)/shard_map/ppermute | solution.py:25
  36.4 3.5 %collective-permute-start.7 = (f32[32]{0:T(128)S(1)}, f32[32]{0:T(128)S(1)}, u32[]{:S(2)}, u32[]{:S(2)}) collective-permute-start(f32[32]{0:T(128)S(1)} %add.16), channel_id=1, source_target_pairs={{0,2},{1,3},{2,0},{3,1},{4,6},{5,7},{6,4},{7,5},{8,10},{9,11},{10,... | collective-permute-start | bytes 392 | tf_op jit(solution)/shard_map/ppermute | solution.py:25
  50.5 35.7 %all-to-all-start.1 = ((bf16[16,32,1024]{2,1,0:T(8,128)(2,1)}), bf16[16,32,1024]{2,1,0:T(8,128)(2,1)S(1)}, u32[]{:S(2)}, u32[]{:S(2)}) async-start(bf16[16,32,1024]{2,1,0:T(8,128)(2,1)} %get-tuple-element.31), calls=%async_computation.1 | async-start | bytes 2097152 | tf_op jit(solution)/shard_map/all_to_all | solution.py:33
  57.8 18.2 %collective-permute-start.8 = (f32[32]{0:T(128)S(1)}, f32[32]{0:T(128)S(1)}, u32[]{:S(2)}, u32[]{:S(2)}) collective-permute-start(f32[32]{0:T(128)S(1)} %add.17), channel_id=1, source_target_pairs={{0,4},{1,5},{2,6},{3,7},{4,0},{5,1},{6,2},{7,3},{8,12},{9,13},{10,... | collective-permute-start | bytes 392 | tf_op jit(solution)/shard_map/ppermute | solution.py:25
  76.0 8.4 %collective-permute-start.9 = (f32[32]{0:T(128)S(1)}, f32[32]{0:T(128)S(1)}, u32[]{:S(2)}, u32[]{:S(2)}) collective-permute-start(f32[32]{0:T(128)S(1)} %add.18), channel_id=1, source_target_pairs={{0,8},{1,9},{2,10},{3,11},{4,12},{5,13},{6,14},{7,15},{8,0},{9,1},... | collective-permute-start | bytes 392 | tf_op jit(solution)/shard_map/ppermute | solution.py:25

commit v6 on v4

--- a/solution.py
+++ b/solution.py
@@ -9,9 +9,10 @@
 
 EPSILON = 1e-06
 TOKENS_AT_ONCE = 16
-HIDDEN_PIECES = 4
+HIDDEN_PIECES = 2
+INLET_PARTS = 2
+ROWS_LIMIT = 53
 NETWORK_LIMIT = 50
-ROWS_LIMIT = 53
 BF16 = jnp.bfloat16
 F32 = jnp.float32
 
@@ -45,15 +46,17 @@
     )
 
 
-def rows_kernel(lanes, owners, analyses, *refs):
-    outs, sems = refs[:lanes], refs[lanes]
+def rows_kernel(lanes, owners, analyses, weight, *refs):
+    *outs, weight_out, sems = refs
     own = outs[0].shape[0]
     me = lax.axis_index("member")
     lane = me % lanes
     block = jnp.int32(0)
     for b in range(owners.shape[0]):
         block = jnp.where(owners[b] == me, b, block)
-    copies = []
+    copies = [
+        pltpu.make_async_copy(weight, weight_out, sems.at[lanes]),
+    ]
     for k in range(lanes):
         start = pl.multiple_of((block * lanes + (lane ^ k)) * own, own)
         copies.append(
@@ -66,7 +69,8 @@
 
 
 def blocks_kernel(lanes, owners, *refs):
-    held, (keep, give) = refs[:lanes], refs[lanes:]
+    held, (weight, across, keep, give, weight_out) = refs[:lanes], refs[lanes:]
+    weight_out[...] = weight[...] + across[...]
     me = lax.axis_index("member")
     lane, plane = me % lanes, me // lanes
 
@@ -89,7 +93,9 @@
     return jnp.where(there == 1, got[j], keep[j])
 
 
-def halve_kernel(lanes, bit, owners, keep, got, keep_out, give):
+def halve_kernel(lanes, bit, owners, keep, got, *refs):
+    *weights, keep_out, give, weight_out = refs
+    weight_out[...] = sum((ref[...] for ref in weights[1:]), weights[0][...])
     plane = lax.axis_index("member") // lanes
     side = plane // (2 * bit) % 2
     rows = [merged(lanes, owners, plane, bit, keep, got, j) for j in range(keep.shape[0])]
@@ -98,54 +104,66 @@
         give[j] = jnp.where(side == 1, rows[2 * j], rows[2 * j + 1])
 
 
-def encode_kernel(lanes, bit, owners, keep, got, encoder, latent):
+def encode_kernel(lanes, bit, count, owners, keep, got, encoder, weight, *refs):
+    *weights, latent, scale = refs
     plane = lax.axis_index("member") // lanes
     control = merged(lanes, owners, plane, bit, keep, got, 0)
     latent[...] = jnp.dot(control, encoder[...], preferred_element_type=F32).astype(BF16)
-
-
-def latent_rows(analyses, owners, encoder):
-    members = lax.axis_size("member")
+    total = jnp.sum(sum((ref[...] for ref in weights[1:]), weights[0][...]), keepdims=True)
+    scale[...] = weight[...] * (count / total)
+
+
+def prepared(analyses, owners, encoder, area_weight):
+    members, regions = lax.axis_size("member"), lax.axis_size("region")
     _, rows, features = analyses.shape
     blocks = owners.shape[0]
     lanes, own = members // blocks, rows // members
+    row = jax.ShapeDtypeStruct((own, features), BF16)
+    line = jax.ShapeDtypeStruct((1, own), F32)
 
     def kept(many):
         return jax.ShapeDtypeStruct((many, own, features), BF16)
 
-    row = jax.ShapeDtypeStruct((own, features), BF16)
-    by_lane = local_call(
+    *by_lane, own_weight = local_call(
         functools.partial(rows_kernel, lanes),
-        [row] * lanes,
-        [SMEM, HBM],
-        scratch=[pltpu.SemaphoreType.DMA((lanes,))],
+        [row] * lanes + [line],
+        [SMEM] + [HBM] * 2,
+        scratch=[pltpu.SemaphoreType.DMA((lanes + 1,))],
         limit=ROWS_LIMIT,
-    )(owners, analyses)
+    )(owners, analyses, area_weight[None])
     by_lane = [by_lane[0]] + [swap(by_lane[k], "member", k) for k in range(1, lanes)]
-    keep, give = local_call(
+    weight = own_weight
+    for bit in bits_of(regions)[:-1]:
+        weight = weight + swap(weight, "region", bit)
+    across = swap(weight, "region", regions // 2)
+    keep, give, weight = local_call(
         functools.partial(blocks_kernel, lanes),
-        [kept(blocks // 2)] * 2,
-        [SMEM] + [VMEM] * lanes,
+        [kept(blocks // 2)] * 2 + [line],
+        [SMEM] + [VMEM] * (lanes + 2),
         limit=8,
-    )(owners, *by_lane)
+    )(owners, *by_lane, weight, across)
+    weights = [weight] + [swap(weight, "member", k) for k in range(1, lanes)]
     bit = 1
     while 2 * bit < blocks:
         got = swap(give, "member", bit * lanes)
-        keep, give = local_call(
+        keep, give, weight = local_call(
             functools.partial(halve_kernel, lanes, bit),
-            [kept(keep.shape[0] // 2)] * 2,
-            [SMEM] + [VMEM] * 2,
+            [kept(keep.shape[0] // 2)] * 2 + [line],
+            [SMEM] + [VMEM] * (2 + len(weights)),
             limit=8,
-        )(owners, keep, got)
+        )(owners, keep, got, *weights)
+        weights = [weight]
         bit *= 2
     got = swap(give, "member", bit * lanes)
-    return local_call(
-        functools.partial(encode_kernel, lanes, bit),
-        [row],
-        [SMEM] + [VMEM] * 3,
+    weights = [weight] + [swap(weight, "member", k * lanes) for k in range(1, blocks)]
+    latent, scale = local_call(
+        functools.partial(encode_kernel, lanes, bit, float(rows * regions)),
+        [row, line],
+        [SMEM] + [VMEM] * (4 + len(weights)),
         flops=2 * own * features * features,
         limit=8,
-    )(owners, keep, got, encoder)[0]
+    )(owners, keep, got, encoder, own_weight, *weights)
+    return latent, scale
 
 
 def column(row):
@@ -201,54 +219,64 @@
 def member_kernel(
     noise,
     latent,
-    targets,
-    weight,
+    scale,
+    targets_hbm,
     inlet_hbm,
     outlet_hbm,
     gradient_out,
     energy_out,
+    targets,
     inlet,
     outlet,
-    inlet_sems,
-    outlet_sems,
+    hidden,
+    sems,
 ):
     members, own, features = noise.shape
     width = inlet.shape[1] // HIDDEN_PIECES
+    part = width // INLET_PARTS
     copies = []
     for piece in range(HIDDEN_PIECES):
-        part = pl.ds(piece * width, width)
-        copies.append(
-            (
-                pltpu.make_async_copy(
-                    inlet_hbm.at[:, part], inlet.at[:, part], inlet_sems.at[piece]
-                ),
-                pltpu.make_async_copy(
-                    outlet_hbm.at[part, :], outlet.at[part, :], outlet_sems.at[piece]
-                ),
-            )
-        )
-    for into, out_of in copies:
-        into.start()
-        out_of.start()
+        for i in range(INLET_PARTS):
+            columns = pl.ds(piece * width + i * part, part)
+            copies.append((inlet_hbm.at[:, columns], inlet.at[:, columns]))
+        rows = pl.ds(piece * width, width)
+        copies.append((outlet_hbm.at[rows, :], outlet.at[rows, :]))
+    copies = [
+        pltpu.make_async_copy(source, target, sems.at[i])
+        for i, (source, target) in enumerate(copies)
+    ]
+
+    def arrived(i):
+        copies[i].wait()
+        if i + 2 < len(copies):
+            copies[i + 2].start()
+
+    aside = pltpu.make_async_copy(targets_hbm, targets, sems.at[len(copies)])
+    for copy in (*copies[:2], aside):
+        copy.start()
 
     def hidden_piece(normed, piece):
-        part = slice(piece * width, (piece + 1) * width)
-        copies[piece][0].wait()
-        hidden = jax.nn.gelu(
-            jnp.dot(normed, inlet[:, part], preferred_element_type=F32), approximate=True
-        ).astype(BF16)
-        copies[piece][1].wait()
-        return jnp.dot(hidden, outlet[part, :], preferred_element_type=F32)
+        for i in range(INLET_PARTS):
+            arrived(piece * (INLET_PARTS + 1) + i)
+            first = piece * width + i * part
+            hidden[:, i * part : (i + 1) * part] = jax.nn.gelu(
+                jnp.dot(normed, inlet[:, first : first + part], preferred_element_type=F32),
+                approximate=True,
+            ).astype(BF16)
+        arrived(piece * (INLET_PARTS + 1) + INLET_PARTS)
+        rows = slice(piece * width, (piece + 1) * width)
+        return jnp.dot(hidden[...], outlet[rows, :], preferred_element_type=F32)
 
     forecast = network(noise[...], latent[...], hidden_piece, HIDDEN_PIECES)
     forecast = forecast.reshape(members, own, features)
-    scale = column(weight[...])
+    aside.wait()
+    scales = column(scale[...])
     for first in range(0, own, TOKENS_AT_ONCE):
         here = slice(first, first + TOKENS_AT_ONCE)
         gradient, energy = score(
             forecast[:, here].reshape(members * TOKENS_AT_ONCE, features),
             targets[here, :],
-            scale[here, :],
+            scales[here, :],
             members,
             TOKENS_AT_ONCE,
         )
@@ -271,33 +299,27 @@
     hidden = sample_inlet_matrix.shape[1]
     own = region_rows // members
     here = transposed(noise.reshape(members, own, features))
-    latent = latent_rows(analyses, owners, enc_weight)
+    latent, scale = prepared(analyses, owners, enc_weight, area_weight)
     gradient, energy = local_call(
         member_kernel,
         [
             jax.ShapeDtypeStruct((members, own, features), BF16),
             jax.ShapeDtypeStruct((own, 1), F32),
         ],
-        [VMEM] * 4 + [HBM] * 2,
+        [VMEM] * 3 + [HBM] * 3,
         flops=4 * members * own * features * (hidden + members),
         moved=4 * features * hidden,
         scratch=[
+            pltpu.VMEM((own, features), BF16),
             pltpu.VMEM((features, hidden), BF16),
             pltpu.VMEM((hidden, features), BF16),
-            pltpu.SemaphoreType.DMA((HIDDEN_PIECES,)),
-            pltpu.SemaphoreType.DMA((HIDDEN_PIECES,)),
+            pltpu.VMEM((members * own, hidden // HIDDEN_PIECES), BF16),
+            pltpu.SemaphoreType.DMA((HIDDEN_PIECES * (INLET_PARTS + 1) + 1,)),
         ],
         limit=NETWORK_LIMIT,
-    )(here, latent, targets, area_weight[None], sample_inlet_matrix, sample_outlet_matrix)
-    gradient, total = lax.optimization_barrier((gradient, area_weight))
+    )(here, latent, scale, targets, sample_inlet_matrix, sample_outlet_matrix)
     back = transposed(gradient)
-    for bit in bits_of(members):
-        total = total + swap(total, "member", bit)
-    for bit in bits_of(regions):
-        total = total + swap(total, "region", bit)
-    factor = float(region_rows * regions) / jnp.sum(total)
-    member_grad = (back.astype(F32) * factor).astype(BF16).reshape(1, region_rows, features)
-    return member_grad, energy[:, 0] * factor
+    return back.reshape(1, region_rows, features), energy[:, 0]
 
 
 def solution(mesh):

time: 89.1 us -> 83.7 us (0.939); the launches traced: 88.8 us -> 82.2 us
  waiting for transfers between devices: 40.8 us -> 36.3 us
  local copies, waits for them, and re-layouts: 0.02 us -> 3.11 us
  starting transfers between devices: 29.5 us -> 27.5 us
  other arithmetic: 2.43 us -> 0.63 us
    ppermute x10 -> x12, waiting for transfers between devices: 40.8 us -> 14 us  [swap(): return lax.ppermute(value, axis, [(i, i ^ bit) for i in range(size)])]
    all_to_all x2, waiting for transfers between devices: 0.02 us -> 22.3 us  [transposed(): lax.all_to_all(value, 'member', split_axis=0, concat_axis=0, tiled=True)]
    all_to_all x2, starting transfers between devices: 14.8 us -> 11.2 us  [transposed(): lax.all_to_all(value, 'member', split_axis=0, concat_axis=0, tiled=True)]
    unnamed x8 -> x9, local copies, waits for them, and re-layouts: 0.02 us -> 3.11 us
    ppermute x10 -> x12, starting transfers between devices: 14.7 us -> 16.3 us  [swap(): return lax.ppermute(value, axis, [(i, i ^ bit) for i in range(size)])]
    convert_element_type x1 -> x0, other arithmetic: 1.19 us -> none  [on_device(): (back.astype(F32) * factor).astype(BF16).reshape(1, region_rows, features)]
  transfers between devices with their start and end apart: 12 -> 14, of which waited for: 9 -> 10; matrix products, arithmetic and copies ran while one was open for 1% -> 1% of each run, Pallas kernels for 4% -> 5%
where the time goes in v6:
time: 83.7 us; the launch traced here: 82.2 us
  waiting for transfers between devices  36.3 us (43%)
  starting transfers between devices  27.5 us (33%)
  Pallas kernels  13.8 us (16%)
  local copies, waits for them, and re-layouts  3.11 us (4%)
    all_to_all x2, waiting for transfers between devices, transposed(): lax.all_to_all(value, 'member', split_axis=0, concat_axis=0, tiled=True)  22.3 us
    ppermute x12, starting transfers between devices, swap(): return lax.ppermute(value, axis, [(i, i ^ bit) for i in range(size)])  16.3 us
    ppermute x12, waiting for transfers between devices, swap(): return lax.ppermute(value, axis, [(i, i ^ bit) for i in range(size)])  14 us
    all_to_all x2, starting transfers between devices, transposed(): lax.all_to_all(value, 'member', split_axis=0, concat_axis=0, tiled=True)  11.2 us
    pallas_call x1, Pallas kernels, on_device(): local_call(member_kernel, [jax.ShapeDtypeStruct((members, own, features),...  10.1 us
    unnamed x9, local copies, waits for them, and re-layouts  3.11 us
  transfers between devices with their start and end apart: 14, of which 10 were waited for; matrix products, arithmetic and copies ran while one was open for 1% of the time, Pallas kernels for 5%

profile of v6, /device:TPU:0, one launch (start us, length us, event | category | flops | bytes accessed | tf_op | source)
XLA Modules:
  0.0 82.2 jit_solution(18152755128809260671)
XLA Ops:
  0.6 0.0 copy-start
  0.6 7.5 %all-to-all-start = ((bf16[16,32,1024]{2,1,0:T(8,128)(2,1)}), bf16[16,32,1024]{2,1,0:T(8,128)(2,1)S(1)}, u32[]{:S(2)}, u32[]{:S(2)}) async-start(bf16[16,32,1024]{2,1,0:T(8,128)(2,1)} %bitcast.5), calls=%async_computation | async-start | bytes 2097152 | tf_op jit(solution)/shard_map/all_to_all | solution.py:34
  8.2 0.0 copy-start.1
  8.2 0.6 copy-done.1
  8.8 0.0 copy-start.2
  8.8 0.7 copy-done.2
  9.5 1.5 %shard_map.95 = (bf16[32,1024]{1,0:T(8,128)(2,1)S(1)}, bf16[32,1024]{1,0:T(8,128)(2,1)S(1)}, bf16[32,1024]{1,0:T(8,128)(2,1)S(1)}, bf16[32,1024]{1,0:T(8,128)(2,1)S(1)}, f32[1,32]{1,0:T(1,128)S(1)}) custom-call(s32[4]{0:T(128)S(1)} %copy-done.1, bf16[1,512,1024]{2,1,0:T(8,128)(2,1)} %analyses.1, f32[1,32]{1,0:T(1,128)S(1)} %bitcast.3), custom_call_target="tpu_custom_call" | custom-call | tf_op jit(solution)/shard_map/pallas_call | solution.py:127
  11.0 0.5 collective-permute-start
  11.5 1.7 %collective-permute-start.1 = (bf16[32,1024]{1,0:T(8,128)(2,1)S(1)}, bf16[32,1024]{1,0:T(8,128)(2,1)S(1)}, u32[]{:S(2)}, u32[]{:S(2)}) collective-permute-start(bf16[32,1024]{1,0:T(8,128)(2,1)S(1)} %get-tuple-element.19), channel_id=1, source_target_pairs={{0,2},{1,3},{2,0},{3,1},{4,6},{5,7},{6,4},{7,5},{8,10},{9,11},{10,... | collective-permute-start | bytes 196616 | tf_op jit(solution)/shard_map/ppermute | solution.py:26
  13.2 0.0 collective-permute-start.2
  13.2 1.5 %collective-permute-start.3 = (f32[1,32]{1,0:T(1,128)S(1)}, f32[1,32]{1,0:T(1,128)S(1)}, u32[]{:S(2)}, u32[]{:S(2)}) collective-permute-start(f32[1,32]{1,0:T(1,128)S(1)} %get-tuple-element.21.refs_4_.weight), channel_id=1, source_target_pairs={{0,16},{16,0},{1,17},{17,1},{2,18},{18,2},{3,19},{19,3},{4,20},{20... | collective-permute-start | bytes 392 | tf_op jit(solution)/shard_map/ppermute | solution.py:26
  14.7 2.0 %collective-permute-done.3.refs_5_ = f32[1,32]{1,0:T(1,128)S(1)} collective-permute-done((f32[1,32]{1,0:T(1,128)S(1)}, f32[1,32]{1,0:T(1,128)S(1)}, u32[]{:S(2)}, u32[]{:S(2)}) %collective-permute-start.3) | collective-permute-done | bytes 160 | tf_op jit(solution)/shard_map/ppermute | solution.py:26
  16.7 0.0 collective-permute-done.refs_1_
  16.7 3.0 %collective-permute-done.1.refs_2_ = bf16[32,1024]{1,0:T(8,128)(2,1)S(1)} collective-permute-done((bf16[32,1024]{1,0:T(8,128)(2,1)S(1)}, bf16[32,1024]{1,0:T(8,128)(2,1)S(1)}, u32[]{:S(2)}, u32[]{:S(2)}) %collective-permute-start.1) | collective-permute-done | bytes 65568 | tf_op jit(solution)/shard_map/ppermute | solution.py:26
  19.8 1.0 %collective-permute-done.2.refs_3_ = bf16[32,1024]{1,0:T(8,128)(2,1)S(1)} collective-permute-done((bf16[32,1024]{1,0:T(8,128)(2,1)S(1)}, bf16[32,1024]{1,0:T(8,128)(2,1)S(1)}, u32[]{:S(2)}, u32[]{:S(2)}) %collective-permute-start.2) | collective-permute-done | bytes 65568 | tf_op jit(solution)/shard_map/ppermute | solution.py:26
  20.8 0.6 shard_map.96
  21.4 0.1 collective-permute-start.4
  21.4 2.3 %collective-permute-start.7 = (f32[1,32]{1,0:T(1,128)S(1)}, f32[1,32]{1,0:T(1,128)S(1)}, u32[]{:S(2)}, u32[]{:S(2)}) collective-permute-start(f32[1,32]{1,0:T(1,128)S(1)} %get-tuple-element.24.refs_0_), channel_id=1, source_target_pairs={{0,3},{1,2},{2,1},{3,0},{4,7},{5,6},{6,5},{7,4},{8,11},{9,10},{10,... | collective-permute-start | bytes 392 | tf_op jit(solution)/shard_map/ppermute | solution.py:26
  23.7 0.9 %collective-permute-start.6 = (f32[1,32]{1,0:T(1,128)S(1)}, f32[1,32]{1,0:T(1,128)S(1)}, u32[]{:S(2)}, u32[]{:S(2)}) collective-permute-start(f32[1,32]{1,0:T(1,128)S(1)} %get-tuple-element.24.refs_0_), channel_id=1, source_target_pairs={{0,2},{1,3},{2,0},{3,1},{4,6},{5,7},{6,4},{7,5},{8,10},{9,11},{10,... | collective-permute-start | bytes 392 | tf_op jit(solution)/shard_map/ppermute | solution.py:26
  24.6 0.0 collective-permute-start.5
  24.6 0.4 collective-permute-done.7.refs_3_
  25.0 2.2 %collective-permute-done.6.refs_2_ = f32[1,32]{1,0:T(1,128)S(1)} collective-permute-done((f32[1,32]{1,0:T(1,128)S(1)}, f32[1,32]{1,0:T(1,128)S(1)}, u32[]{:S(2)}, u32[]{:S(2)}) %collective-permute-start.6) | collective-permute-done | bytes 160 | tf_op jit(solution)/shard_map/ppermute | solution.py:26
  27.3 0.0 collective-permute-done.5.refs_1_
  27.3 1.8 %collective-permute-done.4.got = bf16[2,32,1024]{2,1,0:T(8,128)(2,1)S(1)} collective-permute-done((bf16[2,32,1024]{2,1,0:T(8,128)(2,1)S(1)}, bf16[2,32,1024]{2,1,0:T(8,128)(2,1)S(1)}, u32[]{:S(2)}, u32[]{:S(2)}) %collective-permute-start.4) | collective-permute-done | bytes 131104 | tf_op jit(solution)/shard_map/ppermute | solution.py:26
  29.1 0.6 shard_map.97
  29.7 4.5 %collective-permute-start.8 = (bf16[1,32,1024]{2,1,0:T(8,128)(2,1)S(1)}, bf16[1,32,1024]{2,1,0:T(8,128)(2,1)S(1)}, u32[]{:S(2)}, u32[]{:S(2)}) collective-permute-start(bf16[1,32,1024]{2,1,0:T(8,128)(2,1)S(1)} %get-tuple-element.26), channel_id=1, source_target_pairs={{0,8},{1,9},{2,10},{3,11},{4,12},{5,13},{6,14},{7,15},{8,0},{9,1},... | collective-permute-start | bytes 196616 | tf_op jit(solution)/shard_map/ppermute | solution.py:26
  34.1 3.0 %collective-permute-start.11 = (f32[1,32]{1,0:T(1,128)S(1)}, f32[1,32]{1,0:T(1,128)S(1)}, u32[]{:S(2)}, u32[]{:S(2)}) collective-permute-start(f32[1,32]{1,0:T(1,128)S(1)} %get-tuple-element.27.refs_0_), channel_id=1, source_target_pairs={{0,12},{1,13},{2,14},{3,15},{4,8},{5,9},{6,10},{7,11},{8,4},{9,5},... | collective-permute-start | bytes 392 | tf_op jit(solution)/shard_map/ppermute | solution.py:26
  37.1 1.9 %collective-permute-start.10 = (f32[1,32]{1,0:T(1,128)S(1)}, f32[1,32]{1,0:T(1,128)S(1)}, u32[]{:S(2)}, u32[]{:S(2)}) collective-permute-start(f32[1,32]{1,0:T(1,128)S(1)} %get-tuple-element.27.refs_0_), channel_id=1, source_target_pairs={{0,8},{1,9},{2,10},{3,11},{4,12},{5,13},{6,14},{7,15},{8,0},{9,1},... | collective-permute-start | bytes 392 | tf_op jit(solution)/shard_map/ppermute | solution.py:26
  39.1 0.0 collective-permute-start.9
  39.1 0.4 collective-permute-done.11.refs_3_
  39.5 2.1 %collective-permute-done.10.refs_2_ = f32[1,32]{1,0:T(1,128)S(1)} collective-permute-done((f32[1,32]{1,0:T(1,128)S(1)}, f32[1,32]{1,0:T(1,128)S(1)}, u32[]{:S(2)}, u32[]{:S(2)}) %collective-permute-start.10) | collective-permute-done | bytes 160 | tf_op jit(solution)/shard_map/ppermute | solution.py:26
  41.6 1.0 %collective-permute-done.9.refs_1_ = f32[1,32]{1,0:T(1,128)S(1)} collective-permute-done((f32[1,32]{1,0:T(1,128)S(1)}, f32[1,32]{1,0:T(1,128)S(1)}, u32[]{:S(2)}, u32[]{:S(2)}) %collective-permute-start.9) | collective-permute-done | bytes 160 | tf_op jit(solution)/shard_map/ppermute | solution.py:26
  42.6 0.0 collective-permute-done.8.got
  42.6 0.0 copy-done
  42.6 1.0 %shard_map.98 = (bf16[32,1024]{1,0:T(8,128)(2,1)S(1)}, f32[1,32]{1,0:T(1,128)S(1)}) custom-call(s32[4]{0:T(128)S(1)} %copy-done.1, bf16[1,32,1024]{2,1,0:T(8,128)(2,1)S(1)} %get-tuple-element.25.keep, bf16[1,32,1024]{2,1,0:T(8,128)(2,1)S(1)} %collective-permute-done.8.got, bf16[1024,1024]{1,0:T(8,128)(2,1)S(1)} %copy-done, ...), custom_call_target="tpu_custom_call" | custom-call | flops 67108864 | tf_op jit(solution)/shard_map/pallas_call | solution.py:159
  43.7 0.0 all-to-all-done.noise
  43.7 0.0 copy-start.3
  43.7 0.8 %copy-done.3 = bf16[32,1024]{1,0:T(8,128)(2,1)S(1)} copy-done((bf16[32,1024]{1,0:T(8,128)(2,1)S(1)}, bf16[32,1024]{1,0:T(8,128)(2,1)}, u32[]{:S(2)}) %copy-start.3) | copy-done | bytes 65560
  44.5 10.1 %shard_map.99 = (bf16[16,32,1024]{2,1,0:T(8,128)(2,1)}, f32[32,1]{1,0:T(8,128)S(1)}) custom-call(bf16[16,32,1024]{2,1,0:T(8,128)(2,1)S(1)} %all-to-all-done.noise, bf16[32,1024]{1,0:T(8,128)(2,1)S(1)} %get-tuple-element.28.latent, f32[1,32]{1,0:T(1,128)S(1)} %get-tuple-element.29.scale, bf16[32,1024]{1,0:T(8,128)(2,1)S(1)} %copy-done.3, ...), custom_call_target="tpu_custom_call" | custom-call | flops 4328521728 | bytes 8388608 | tf_op jit(solution)/shard_map/pallas_call | solution.py:303
  54.6 3.7 %all-to-all-start.1 = ((bf16[16,32,1024]{2,1,0:T(8,128)(2,1)}), bf16[16,32,1024]{2,1,0:T(8,128)(2,1)S(1)}, u32[]{:S(2)}, u32[]{:S(2)}) async-start(bf16[16,32,1024]{2,1,0:T(8,128)(2,1)} %get-tuple-element.30), calls=%async_computation.1 | async-start | bytes 2097152 | tf_op jit(solution)/shard_map/all_to_all | solution.py:34
  58.3 0.6 reduce
  58.9 22.3 %all-to-all-done.1 = bf16[16,32,1024]{2,1,0:T(8,128)(2,1)S(1)} async-done(((bf16[16,32,1024]{2,1,0:T(8,128)(2,1)}), bf16[16,32,1024]{2,1,0:T(8,128)(2,1)S(1)}, u32[]{:S(2)}, u32[]{:S(2)}) %all-to-all-start.1) | async-done | bytes 1048608 | tf_op jit(solution)/shard_map/all_to_all | solution.py:34
  81.2 1.0 %copy.11 = bf16[1,512,1024]{2,1,0:T(8,128)(2,1)} copy(bf16[1,512,1024]{2,1,0:T(8,128)(2,1)S(1)} %bitcast.4) | data formatting | bytes 2097152
Async XLA Ops:
  0.6 42.0 %copy-start = (bf16[1024,1024]{1,0:T(8,128)(2,1)S(1)}, bf16[1024,1024]{1,0:T(8,128)(2,1)}, u32[]{:S(2)}) copy-start(bf16[1024,1024]{1,0:T(8,128)(2,1)} %encoder.1) | copy-start | bytes 6291460
  0.6 43.0 %all-to-all-start = ((bf16[16,32,1024]{2,1,0:T(8,128)(2,1)}), bf16[16,32,1024]{2,1,0:T(8,128)(2,1)S(1)}, u32[]{:S(2)}, u32[]{:S(2)}) async-start(bf16[16,32,1024]{2,1,0:T(8,128)(2,1)} %bitcast.5), calls=%async_computation | async-start | bytes 2097152 | tf_op jit(solution)/shard_map/all_to_all | solution.py:34
  8.2 0.7 copy-start.1
  8.8 0.7 copy-start.2
  11.0 5.7 %collective-permute-start = (bf16[32,1024]{1,0:T(8,128)(2,1)S(1)}, bf16[32,1024]{1,0:T(8,128)(2,1)S(1)}, u32[]{:S(2)}, u32[]{:S(2)}) collective-permute-start(bf16[32,1024]{1,0:T(8,128)(2,1)S(1)} %get-tuple-element.18), channel_id=1, source_target_pairs={{0,1},{1,0},{2,3},{3,2},{4,5},{5,4},{6,7},{7,6},{8,9},{9,8},{10,11... | collective-permute-start | bytes 196616 | tf_op jit(solution)/shard_map/ppermute | solution.py:26
  11.5 8.3 %collective-permute-start.1 = (bf16[32,1024]{1,0:T(8,128)(2,1)S(1)}, bf16[32,1024]{1,0:T(8,128)(2,1)S(1)}, u32[]{:S(2)}, u32[]{:S(2)}) collective-permute-start(bf16[32,1024]{1,0:T(8,128)(2,1)S(1)} %get-tuple-element.19), channel_id=1, source_target_pairs={{0,2},{1,3},{2,0},{3,1},{4,6},{5,7},{6,4},{7,5},{8,10},{9,11},{10,... | collective-permute-start | bytes 196616 | tf_op jit(solution)/shard_map/ppermute | solution.py:26
  13.2 7.6 %collective-permute-start.2 = (bf16[32,1024]{1,0:T(8,128)(2,1)S(1)}, bf16[32,1024]{1,0:T(8,128)(2,1)S(1)}, u32[]{:S(2)}, u32[]{:S(2)}) collective-permute-start(bf16[32,1024]{1,0:T(8,128)(2,1)S(1)} %get-tuple-element.20), channel_id=1, source_target_pairs={{0,3},{1,2},{2,1},{3,0},{4,7},{5,6},{6,5},{7,4},{8,11},{9,10},{10,... | collective-permute-start | bytes 196616 | tf_op jit(solution)/shard_map/ppermute | solution.py:26
  13.2 3.5 %collective-permute-start.3 = (f32[1,32]{1,0:T(1,128)S(1)}, f32[1,32]{1,0:T(1,128)S(1)}, u32[]{:S(2)}, u32[]{:S(2)}) collective-permute-start(f32[1,32]{1,0:T(1,128)S(1)} %get-tuple-element.21.refs_4_.weight), channel_id=1, source_target_pairs={{0,16},{16,0},{1,17},{17,1},{2,18},{18,2},{3,19},{19,3},{4,20},{20... | collective-permute-start | bytes 392 | tf_op jit(solution)/shard_map/ppermute | solution.py:26
  21.4 7.7 %collective-permute-start.4 = (bf16[2,32,1024]{2,1,0:T(8,128)(2,1)S(1)}, bf16[2,32,1024]{2,1,0:T(8,128)(2,1)S(1)}, u32[]{:S(2)}, u32[]{:S(2)}) collective-permute-start(bf16[2,32,1024]{2,1,0:T(8,128)(2,1)S(1)} %get-tuple-element.23), channel_id=1, source_target_pairs={{0,4},{1,5},{2,6},{3,7},{4,0},{5,1},{6,2},{7,3},{8,12},{9,13},{10,... | collective-permute-start | bytes 393224 | tf_op jit(solution)/shard_map/ppermute | solution.py:26
  21.4 3.6 %collective-permute-start.7 = (f32[1,32]{1,0:T(1,128)S(1)}, f32[1,32]{1,0:T(1,128)S(1)}, u32[]{:S(2)}, u32[]{:S(2)}) collective-permute-start(f32[1,32]{1,0:T(1,128)S(1)} %get-tuple-element.24.refs_0_), channel_id=1, source_target_pairs={{0,3},{1,2},{2,1},{3,0},{4,7},{5,6},{6,5},{7,4},{8,11},{9,10},{10,... | collective-permute-start | bytes 392 | tf_op jit(solution)/shard_map/ppermute | solution.py:26
  23.7 3.5 %collective-permute-start.6 = (f32[1,32]{1,0:T(1,128)S(1)}, f32[1,32]{1,0:T(1,128)S(1)}, u32[]{:S(2)}, u32[]{:S(2)}) collective-permute-start(f32[1,32]{1,0:T(1,128)S(1)} %get-tuple-element.24.refs_0_), channel_id=1, source_target_pairs={{0,2},{1,3},{2,0},{3,1},{4,6},{5,7},{6,4},{7,5},{8,10},{9,11},{10,... | collective-permute-start | bytes 392 | tf_op jit(solution)/shard_map/ppermute | solution.py:26
  24.6 2.6 %collective-permute-start.5 = (f32[1,32]{1,0:T(1,128)S(1)}, f32[1,32]{1,0:T(1,128)S(1)}, u32[]{:S(2)}, u32[]{:S(2)}) collective-permute-start(f32[1,32]{1,0:T(1,128)S(1)} %get-tuple-element.24.refs_0_), channel_id=1, source_target_pairs={{0,1},{1,0},{2,3},{3,2},{4,5},{5,4},{6,7},{7,6},{8,9},{9,8},{10,11... | collective-permute-start | bytes 392 | tf_op jit(solution)/shard_map/ppermute | solution.py:26
  29.7 13.0 %collective-permute-start.8 = (bf16[1,32,1024]{2,1,0:T(8,128)(2,1)S(1)}, bf16[1,32,1024]{2,1,0:T(8,128)(2,1)S(1)}, u32[]{:S(2)}, u32[]{:S(2)}) collective-permute-start(bf16[1,32,1024]{2,1,0:T(8,128)(2,1)S(1)} %get-tuple-element.26), channel_id=1, source_target_pairs={{0,8},{1,9},{2,10},{3,11},{4,12},{5,13},{6,14},{7,15},{8,0},{9,1},... | collective-permute-start | bytes 196616 | tf_op jit(solution)/shard_map/ppermute | solution.py:26
  34.1 5.3 %collective-permute-start.11 = (f32[1,32]{1,0:T(1,128)S(1)}, f32[1,32]{1,0:T(1,128)S(1)}, u32[]{:S(2)}, u32[]{:S(2)}) collective-permute-start(f32[1,32]{1,0:T(1,128)S(1)} %get-tuple-element.27.refs_0_), channel_id=1, source_target_pairs={{0,12},{1,13},{2,14},{3,15},{4,8},{5,9},{6,10},{7,11},{8,4},{9,5},... | collective-permute-start | bytes 392 | tf_op jit(solution)/shard_map/ppermute | solution.py:26
  37.1 4.4 %collective-permute-start.10 = (f32[1,32]{1,0:T(1,128)S(1)}, f32[1,32]{1,0:T(1,128)S(1)}, u32[]{:S(2)}, u32[]{:S(2)}) collective-permute-start(f32[1,32]{1,0:T(1,128)S(1)} %get-tuple-element.27.refs_0_), channel_id=1, source_target_pairs={{0,8},{1,9},{2,10},{3,11},{4,12},{5,13},{6,14},{7,15},{8,0},{9,1},... | collective-permute-start | bytes 392 | tf_op jit(solution)/shard_map/ppermute | solution.py:26
  39.1 3.5 %collective-permute-start.9 = (f32[1,32]{1,0:T(1,128)S(1)}, f32[1,32]{1,0:T(1,128)S(1)}, u32[]{:S(2)}, u32[]{:S(2)}) collective-permute-start(f32[1,32]{1,0:T(1,128)S(1)} %get-tuple-element.27.refs_0_), channel_id=1, source_target_pairs={{0,4},{1,5},{2,6},{3,7},{4,0},{5,1},{6,2},{7,3},{8,12},{9,13},{10,... | collective-permute-start | bytes 392 | tf_op jit(solution)/shard_map/ppermute | solution.py:26
  43.7 0.8 %copy-start.3 = (bf16[32,1024]{1,0:T(8,128)(2,1)S(1)}, bf16[32,1024]{1,0:T(8,128)(2,1)}, u32[]{:S(2)}) copy-start(bf16[32,1024]{1,0:T(8,128)(2,1)} %targets_hbm.1) | copy-start | bytes 196612
  54.6 26.6 %all-to-all-start.1 = ((bf16[16,32,1024]{2,1,0:T(8,128)(2,1)}), bf16[16,32,1024]{2,1,0:T(8,128)(2,1)S(1)}, u32[]{:S(2)}, u32[]{:S(2)}) async-start(bf16[16,32,1024]{2,1,0:T(8,128)(2,1)} %get-tuple-element.30), calls=%async_computation.1 | async-start | bytes 2097152 | tf_op jit(solution)/shard_map/all_to_all | solution.py:34

commit v7 on v6

--- a/solution.py
+++ b/solution.py
@@ -9,6 +9,7 @@
 
 EPSILON = 1e-06
 TOKENS_AT_ONCE = 16
+TAIL = 16
 HIDDEN_PIECES = 2
 INLET_PARTS = 2
 ROWS_LIMIT = 53
@@ -87,6 +88,19 @@
         give[j] = rows_of(2 * j + 1 - side)
 
 
+def weight_rows(total, features):
+    high = total.astype(BF16).astype(F32)
+    middle = (total - high).astype(BF16).astype(F32)
+    low = total - high - middle
+    row = lax.broadcasted_iota(jnp.int32, (TAIL, features), 0)
+    picked = jnp.where(row == 0, high, jnp.where(row == 1, middle, jnp.where(row == 2, low, 0.0)))
+    return picked.astype(BF16)
+
+
+def weight_from(rows):
+    return jnp.sum(rows[:, 0:128].astype(F32), axis=0, keepdims=True)
+
+
 def merged(lanes, owners, plane, bit, keep, got, j):
     block = j * (2 * bit) + plane % (2 * bit)
     there = ((owners[block] // lanes) ^ plane) // bit % 2
@@ -95,22 +109,25 @@
 
 def halve_kernel(lanes, bit, owners, keep, got, *refs):
     *weights, keep_out, give, weight_out = refs
-    weight_out[...] = sum((ref[...] for ref in weights[1:]), weights[0][...])
+    own, features = keep.shape[1], keep.shape[2]
+    total = jnp.sum(sum((ref[...] for ref in weights[1:]), weights[0][...]), keepdims=True)
+    weight_out[...] = jnp.broadcast_to(total, weight_out.shape)
     plane = lax.axis_index("member") // lanes
     side = plane // (2 * bit) % 2
     rows = [merged(lanes, owners, plane, bit, keep, got, j) for j in range(keep.shape[0])]
     for j in range(keep_out.shape[0]):
         keep_out[j] = jnp.where(side == 1, rows[2 * j + 1], rows[2 * j])
-        give[j] = jnp.where(side == 1, rows[2 * j], rows[2 * j + 1])
-
-
-def encode_kernel(lanes, bit, count, owners, keep, got, encoder, weight, *refs):
-    *weights, latent, scale = refs
+        give[pl.ds(j * own, own), :] = jnp.where(side == 1, rows[2 * j], rows[2 * j + 1])
+    give[pl.ds(keep_out.shape[0] * own, TAIL), :] = weight_rows(total, features)
+
+
+def encode_kernel(lanes, bit, owners, keep, got, encoder, total, latent, total_out):
+    own = latent.shape[0]
     plane = lax.axis_index("member") // lanes
-    control = merged(lanes, owners, plane, bit, keep, got, 0)
+    rows = [got[pl.ds(0, own), :]]
+    control = merged(lanes, owners, plane, bit, keep, rows, 0)
     latent[...] = jnp.dot(control, encoder[...], preferred_element_type=F32).astype(BF16)
-    total = jnp.sum(sum((ref[...] for ref in weights[1:]), weights[0][...]), keepdims=True)
-    scale[...] = weight[...] * (count / total)
+    total_out[...] = total[...] + weight_from(got[pl.ds(own, TAIL), :])
 
 
 def prepared(analyses, owners, encoder, area_weight):
@@ -143,27 +160,23 @@
         limit=8,
     )(owners, *by_lane, weight, across)
     weights = [weight] + [swap(weight, "member", k) for k in range(1, lanes)]
-    bit = 1
-    while 2 * bit < blocks:
-        got = swap(give, "member", bit * lanes)
-        keep, give, weight = local_call(
-            functools.partial(halve_kernel, lanes, bit),
-            [kept(keep.shape[0] // 2)] * 2 + [line],
-            [SMEM] + [VMEM] * (2 + len(weights)),
-            limit=8,
-        )(owners, keep, got, *weights)
-        weights = [weight]
-        bit *= 2
-    got = swap(give, "member", bit * lanes)
-    weights = [weight] + [swap(weight, "member", k * lanes) for k in range(1, blocks)]
-    latent, scale = local_call(
-        functools.partial(encode_kernel, lanes, bit, float(rows * regions)),
-        [row, line],
-        [SMEM] + [VMEM] * (4 + len(weights)),
+    got = swap(give, "member", lanes)
+    small = jax.ShapeDtypeStruct((8, 128), F32)
+    keep, give, total = local_call(
+        functools.partial(halve_kernel, lanes, 1),
+        [kept(1), jax.ShapeDtypeStruct((own + TAIL, features), BF16), small],
+        [SMEM] + [VMEM] * (2 + len(weights)),
+        limit=8,
+    )(owners, keep, got, *weights)
+    got = swap(give, "member", 2 * lanes)
+    latent, total = local_call(
+        functools.partial(encode_kernel, lanes, 2),
+        [row, small],
+        [SMEM] + [VMEM] * 4,
         flops=2 * own * features * features,
         limit=8,
-    )(owners, keep, got, encoder, own_weight, *weights)
-    return latent, scale
+    )(owners, keep, got, encoder, total)
+    return latent, own_weight, total, swap(total, "member", lanes)
 
 
 def column(row):
@@ -219,7 +232,7 @@
 def member_kernel(
     noise,
     latent,
-    scale,
+    weight,
     targets_hbm,
     inlet_hbm,
     outlet_hbm,
@@ -270,7 +283,7 @@
     forecast = network(noise[...], latent[...], hidden_piece, HIDDEN_PIECES)
     forecast = forecast.reshape(members, own, features)
     aside.wait()
-    scales = column(scale[...])
+    scales = column(weight[...])
     for first in range(0, own, TOKENS_AT_ONCE):
         here = slice(first, first + TOKENS_AT_ONCE)
         gradient, energy = score(
@@ -299,7 +312,7 @@
     hidden = sample_inlet_matrix.shape[1]
     own = region_rows // members
     here = transposed(noise.reshape(members, own, features))
-    latent, scale = prepared(analyses, owners, enc_weight, area_weight)
+    latent, weight, total, across = prepared(analyses, owners, enc_weight, area_weight)
     gradient, energy = local_call(
         member_kernel,
         [
@@ -317,9 +330,12 @@
             pltpu.SemaphoreType.DMA((HIDDEN_PIECES * (INLET_PARTS + 1) + 1,)),
         ],
         limit=NETWORK_LIMIT,
-    )(here, latent, scale, targets, sample_inlet_matrix, sample_outlet_matrix)
+    )(here, latent, weight, targets, sample_inlet_matrix, sample_outlet_matrix)
+    gradient, across = lax.optimization_barrier((gradient, across))
     back = transposed(gradient)
-    return back.reshape(1, region_rows, features), energy[:, 0]
+    factor = float(region_rows * regions) / (total[0, 0] + across[0, 0])
+    member_grad = (back.astype(F32) * factor).astype(BF16).reshape(1, region_rows, features)
+    return member_grad, energy[:, 0] * factor
 
 
 def solution(mesh):

time: 83.7 us -> 82.1 us (0.981)
  local copies, waits for them, and re-layouts: 3.11 us -> 1.04 us
  waiting for transfers between devices: 36.3 us -> 34.8 us
  between operations: 0.73 us -> 2 us
  other arithmetic: 0.63 us -> 1.81 us
    unnamed x9 -> x8, local copies, waits for them, and re-layouts: 3.11 us -> 0.02 us
    all_to_all x2, waiting for transfers between devices: 22.3 us -> 20 us  [transposed(): lax.all_to_all(value, 'member', split_axis=0, concat_axis=0, tiled=True)]
    ppermute x12 -> x10, starting transfers between devices: 16.3 us -> 15 us  [swap(): return lax.ppermute(value, axis, [(i, i ^ bit) for i in range(size)])]
    convert_element_type x0 -> x1, other arithmetic: none -> 1.18 us  [on_device(): (back.astype(F32) * factor).astype(BF16).reshape(1, region_rows, features)]
    slice x0 -> x2, local copies, waits for them, and re-layouts: none -> 1.02 us  [on_device(): factor = float(region_rows * regions) / (total[0, 0] + across[0, 0])]
    all_to_all x2, starting transfers between devices: 11.2 us -> 12.1 us  [transposed(): lax.all_to_all(value, 'member', split_axis=0, concat_axis=0, tiled=True)]
    ppermute x12 -> x10, waiting for transfers between devices: 14 us -> 14.7 us  [swap(): return lax.ppermute(value, axis, [(i, i ^ bit) for i in range(size)])]
  transfers between devices with their start and end apart: 14 -> 12, of which waited for: 10 -> 7; matrix products, arithmetic and copies ran while one was open for 1% -> 2% of each run, Pallas kernels for 5% -> 17%
where the time goes in v7:
time: 82.1 us; the launch traced here: 80.6 us
  waiting for transfers between devices  34.8 us (42%)
  starting transfers between devices  27.1 us (33%)
  Pallas kernels  13.9 us (17%)
  between operations  2 us (2%)
  other arithmetic  1.81 us (2%)
  local copies, waits for them, and re-layouts  1.04 us (1%)
    all_to_all x2, waiting for transfers between devices, transposed(): lax.all_to_all(value, 'member', split_axis=0, concat_axis=0, tiled=True)  20 us
    ppermute x10, starting transfers between devices, swap(): return lax.ppermute(value, axis, [(i, i ^ bit) for i in range(size)])  15 us
    ppermute x10, waiting for transfers between devices, swap(): return lax.ppermute(value, axis, [(i, i ^ bit) for i in range(size)])  14.7 us
    all_to_all x2, starting transfers between devices, transposed(): lax.all_to_all(value, 'member', split_axis=0, concat_axis=0, tiled=True)  12.1 us
    pallas_call x1, Pallas kernels, on_device(): local_call(member_kernel, [jax.ShapeDtypeStruct((members, own, features),...  10.1 us
  transfers between devices with their start and end apart: 12, of which 7 were waited for; matrix products, arithmetic and copies ran while one was open for 2% of the time, Pallas kernels for 17%

profile of v7, /device:TPU:0, one launch (start us, length us, event | category | flops | bytes accessed | tf_op | source)
XLA Modules:
  0.0 80.6 jit_solution(12740049971380029023)
XLA Ops:
  0.6 0.0 copy-start.2
  0.6 0.0 copy-start.1
  0.7 0.0 copy-start
  0.7 7.5 %all-to-all-start = ((bf16[16,32,1024]{2,1,0:T(8,128)(2,1)}), bf16[16,32,1024]{2,1,0:T(8,128)(2,1)S(1)}, u32[]{:S(2)}, u32[]{:S(2)}) async-start(bf16[16,32,1024]{2,1,0:T(8,128)(2,1)} %bitcast.6), calls=%async_computation | async-start | bytes 2097152 | tf_op jit(solution)/shard_map/all_to_all | solution.py:35
  8.2 0.0 copy-start.3
  8.2 0.0 copy-done.2
  8.2 0.0 copy-done.1
  8.2 1.5 %shard_map.95 = (bf16[32,1024]{1,0:T(8,128)(2,1)S(1)}, bf16[32,1024]{1,0:T(8,128)(2,1)S(1)}, bf16[32,1024]{1,0:T(8,128)(2,1)S(1)}, bf16[32,1024]{1,0:T(8,128)(2,1)S(1)}, f32[1,32]{1,0:T(1,128)S(1)}) custom-call(s32[4]{0:T(128)S(1)} %copy-done.1, bf16[1,512,1024]{2,1,0:T(8,128)(2,1)} %analyses.1, f32[1,32]{1,0:T(1,128)S(1)} %bitcast.4), custom_call_target="tpu_custom_call" | custom-call | tf_op jit(solution)/shard_map/pallas_call | solution.py:144
  9.8 0.5 collective-permute-start
  10.2 1.7 %collective-permute-start.1 = (bf16[32,1024]{1,0:T(8,128)(2,1)S(1)}, bf16[32,1024]{1,0:T(8,128)(2,1)S(1)}, u32[]{:S(2)}, u32[]{:S(2)}) collective-permute-start(bf16[32,1024]{1,0:T(8,128)(2,1)S(1)} %get-tuple-element.21), channel_id=1, source_target_pairs={{0,2},{1,3},{2,0},{3,1},{4,6},{5,7},{6,4},{7,5},{8,10},{9,11},{10,... | collective-permute-start | bytes 196616 | tf_op jit(solution)/shard_map/ppermute | solution.py:27
  11.9 0.0 collective-permute-start.2
  11.9 1.5 %collective-permute-start.3 = (f32[1,32]{1,0:T(1,128)S(1)}, f32[1,32]{1,0:T(1,128)S(1)}, u32[]{:S(2)}, u32[]{:S(2)}) collective-permute-start(f32[1,32]{1,0:T(1,128)S(1)} %get-tuple-element.23.refs_4_.weight), channel_id=1, source_target_pairs={{0,16},{16,0},{1,17},{17,1},{2,18},{18,2},{3,19},{19,3},{4,20},{20... | collective-permute-start | bytes 392 | tf_op jit(solution)/shard_map/ppermute | solution.py:27
  13.4 2.0 %collective-permute-done.3.refs_5_ = f32[1,32]{1,0:T(1,128)S(1)} collective-permute-done((f32[1,32]{1,0:T(1,128)S(1)}, f32[1,32]{1,0:T(1,128)S(1)}, u32[]{:S(2)}, u32[]{:S(2)}) %collective-permute-start.3) | collective-permute-done | bytes 160 | tf_op jit(solution)/shard_map/ppermute | solution.py:27
  15.5 0.0 collective-permute-done.refs_1_
  15.5 4.3 %collective-permute-done.1.refs_2_ = bf16[32,1024]{1,0:T(8,128)(2,1)S(1)} collective-permute-done((bf16[32,1024]{1,0:T(8,128)(2,1)S(1)}, bf16[32,1024]{1,0:T(8,128)(2,1)S(1)}, u32[]{:S(2)}, u32[]{:S(2)}) %collective-permute-start.1) | collective-permute-done | bytes 65568 | tf_op jit(solution)/shard_map/ppermute | solution.py:27
  19.8 0.6 collective-permute-done.2.refs_3_
  20.4 0.6 shard_map.96
  21.0 0.1 collective-permute-start.4
  21.1 1.4 %collective-permute-start.5 = (f32[1,32]{1,0:T(1,128)S(1)}, f32[1,32]{1,0:T(1,128)S(1)}, u32[]{:S(2)}, u32[]{:S(2)}) collective-permute-start(f32[1,32]{1,0:T(1,128)S(1)} %get-tuple-element.26.refs_0_), channel_id=1, source_target_pairs={{0,1},{1,0},{2,3},{3,2},{4,5},{5,4},{6,7},{7,6},{8,9},{9,8},{10,11... | collective-permute-start | bytes 392 | tf_op jit(solution)/shard_map/ppermute | solution.py:27
  22.5 0.0 collective-permute-start.6
  22.5 1.4 %collective-permute-start.7 = (f32[1,32]{1,0:T(1,128)S(1)}, f32[1,32]{1,0:T(1,128)S(1)}, u32[]{:S(2)}, u32[]{:S(2)}) collective-permute-start(f32[1,32]{1,0:T(1,128)S(1)} %get-tuple-element.26.refs_0_), channel_id=1, source_target_pairs={{0,3},{1,2},{2,1},{3,0},{4,7},{5,6},{6,5},{7,4},{8,11},{9,10},{10,... | collective-permute-start | bytes 392 | tf_op jit(solution)/shard_map/ppermute | solution.py:27
  23.9 0.0 collective-permute-done.5.refs_1_
  23.9 2.1 %collective-permute-done.6.refs_2_ = f32[1,32]{1,0:T(1,128)S(1)} collective-permute-done((f32[1,32]{1,0:T(1,128)S(1)}, f32[1,32]{1,0:T(1,128)S(1)}, u32[]{:S(2)}, u32[]{:S(2)}) %collective-permute-start.6) | collective-permute-done | bytes 160 | tf_op jit(solution)/shard_map/ppermute | solution.py:27
  26.0 0.0 collective-permute-done.7.refs_3_
  26.0 3.1 %collective-permute-done.4.got = bf16[2,32,1024]{2,1,0:T(8,128)(2,1)S(1)} collective-permute-done((bf16[2,32,1024]{2,1,0:T(8,128)(2,1)S(1)}, bf16[2,32,1024]{2,1,0:T(8,128)(2,1)S(1)}, u32[]{:S(2)}, u32[]{:S(2)}) %collective-permute-start.4) | collective-permute-done | bytes 131104 | tf_op jit(solution)/shard_map/ppermute | solution.py:27
  29.1 0.7 shard_map.97
  29.8 4.5 %collective-permute-start.8 = (bf16[48,1024]{1,0:T(8,128)(2,1)S(1)}, bf16[48,1024]{1,0:T(8,128)(2,1)S(1)}, u32[]{:S(2)}, u32[]{:S(2)}) collective-permute-start(bf16[48,1024]{1,0:T(8,128)(2,1)S(1)} %get-tuple-element.28), channel_id=1, source_target_pairs={{0,8},{1,9},{2,10},{3,11},{4,12},{5,13},{6,14},{7,15},{8,0},{9,1},... | collective-permute-start | bytes 294920 | tf_op jit(solution)/shard_map/ppermute | solution.py:27
  34.2 2.6 %collective-permute-done.8.got = bf16[48,1024]{1,0:T(8,128)(2,1)S(1)} collective-permute-done((bf16[48,1024]{1,0:T(8,128)(2,1)S(1)}, bf16[48,1024]{1,0:T(8,128)(2,1)S(1)}, u32[]{:S(2)}, u32[]{:S(2)}) %collective-permute-start.8) | collective-permute-done | bytes 98336 | tf_op jit(solution)/shard_map/ppermute | solution.py:27
  36.9 0.0 copy-done
  36.9 1.0 %shard_map.98 = (bf16[32,1024]{1,0:T(8,128)(2,1)S(1)}, f32[8,128]{1,0:T(8,128)S(1)}) custom-call(s32[4]{0:T(128)S(1)} %copy-done.1, bf16[1,32,1024]{2,1,0:T(8,128)(2,1)S(1)} %get-tuple-element.27.keep, bf16[48,1024]{1,0:T(8,128)(2,1)S(1)} %collective-permute-done.8.got, bf16[1024,1024]{1,0:T(8,128)(2,1)S(1)} %copy-done, f32[8,128]{1,0:T(8,128)S(1)} %get-tuple-element.29.total), custom_call_target="tpu_custom_call" | custom-call | flops 67108864 | tf_op jit(solution)/shard_map/pallas_call | solution.py:172
  37.9 4.0 %collective-permute-start.9 = (f32[8,128]{1,0:T(8,128)S(1)}, f32[8,128]{1,0:T(8,128)S(1)}, u32[]{:S(2)}, u32[]{:S(2)}) collective-permute-start(f32[8,128]{1,0:T(8,128)S(1)} %get-tuple-element.32), channel_id=1, source_target_pairs={{0,4},{1,5},{2,6},{3,7},{4,0},{5,1},{6,2},{7,3},{8,12},{9,13},{10,... | collective-permute-start | bytes 12296 | tf_op jit(solution)/shard_map/ppermute | solution.py:27
  41.8 0.0 all-to-all-done.noise
  41.8 0.0 copy-done.3
  41.8 10.1 %shard_map.99 = (bf16[16,32,1024]{2,1,0:T(8,128)(2,1)}, f32[32,1]{1,0:T(8,128)S(1)}) custom-call(bf16[16,32,1024]{2,1,0:T(8,128)(2,1)S(1)} %all-to-all-done.noise, bf16[32,1024]{1,0:T(8,128)(2,1)S(1)} %get-tuple-element.30.latent, f32[1,32]{1,0:T(1,128)S(1)} %get-tuple-element.23.refs_4_.weight, bf16[32,1024]{1,0:T(8,128)(2,1)S(1)} %copy-done.3, ...), custom_call_target="tpu_custom_call" | custom-call | flops 4328521728 | bytes 8388608 | tf_op jit(solution)/shard_map/pallas_call | solution.py:316
  52.0 0.0 collective-permute-done.9
  52.0 4.5 %all-to-all-start.1 = ((bf16[16,32,1024]{2,1,0:T(8,128)(2,1)}), bf16[16,32,1024]{2,1,0:T(8,128)(2,1)S(1)}, u32[]{:S(2)}, u32[]{:S(2)}) async-start(bf16[16,32,1024]{2,1,0:T(8,128)(2,1)} %get-tuple-element.33), calls=%async_computation.1 | async-start | bytes 2097152 | tf_op jit(solution)/shard_map/all_to_all | solution.py:35
  56.5 0.5 slice.6
  57.0 0.5 slice.7
  58.8 0.6 multiply_reduce_fusion
  59.4 20.0 %all-to-all-done.1 = bf16[16,32,1024]{2,1,0:T(8,128)(2,1)S(1)} async-done(((bf16[16,32,1024]{2,1,0:T(8,128)(2,1)}), bf16[16,32,1024]{2,1,0:T(8,128)(2,1)S(1)}, u32[]{:S(2)}, u32[]{:S(2)}) %all-to-all-start.1) | async-done | bytes 1048608 | tf_op jit(solution)/shard_map/all_to_all | solution.py:35
  79.5 1.2 %multiply_convert_fusion = bf16[16,32,1024]{2,1,0:T(8,128)(2,1)} fusion(bf16[16,32,1024]{2,1,0:T(8,128)(2,1)S(1)} %all-to-all-done.1, f32[]{:T(128)} %bitcast.2), kind=kLoop, calls=%fused_computation | loop fusion | flops 1572864 | bytes 2097156 | tf_op jit(solution)/shard_map/convert_element_type | solution.py:337
Async XLA Ops:
  0.6 7.6 %copy-start.2 = (f32[32]{0:T(128)S(1)}, f32[32]{0:T(128)}, u32[]{:S(2)}) copy-start(f32[32]{0:T(128)} %param.12) | copy-start | bytes 388
  0.6 7.6 %copy-start.1 = (s32[4]{0:T(128)S(1)}, s32[4]{0:T(128)}, u32[]{:S(2)}) copy-start(s32[4]{0:T(128)} %owners.7) | copy-start | bytes 52
  0.7 36.2 %copy-start = (bf16[1024,1024]{1,0:T(8,128)(2,1)S(1)}, bf16[1024,1024]{1,0:T(8,128)(2,1)}, u32[]{:S(2)}) copy-start(bf16[1024,1024]{1,0:T(8,128)(2,1)} %encoder.1) | copy-start | bytes 6291460
  0.7 41.2 %all-to-all-start = ((bf16[16,32,1024]{2,1,0:T(8,128)(2,1)}), bf16[16,32,1024]{2,1,0:T(8,128)(2,1)S(1)}, u32[]{:S(2)}, u32[]{:S(2)}) async-start(bf16[16,32,1024]{2,1,0:T(8,128)(2,1)} %bitcast.6), calls=%async_computation | async-start | bytes 2097152 | tf_op jit(solution)/shard_map/all_to_all | solution.py:35
  8.2 33.6 %copy-start.3 = (bf16[32,1024]{1,0:T(8,128)(2,1)S(1)}, bf16[32,1024]{1,0:T(8,128)(2,1)}, u32[]{:S(2)}) copy-start(bf16[32,1024]{1,0:T(8,128)(2,1)} %targets_hbm.1) | copy-start | bytes 196612
  9.8 5.7 %collective-permute-start = (bf16[32,1024]{1,0:T(8,128)(2,1)S(1)}, bf16[32,1024]{1,0:T(8,128)(2,1)S(1)}, u32[]{:S(2)}, u32[]{:S(2)}) collective-permute-start(bf16[32,1024]{1,0:T(8,128)(2,1)S(1)} %get-tuple-element.20), channel_id=1, source_target_pairs={{0,1},{1,0},{2,3},{3,2},{4,5},{5,4},{6,7},{7,6},{8,9},{9,8},{10,11... | collective-permute-start | bytes 196616 | tf_op jit(solution)/shard_map/ppermute | solution.py:27
  10.2 9.6 %collective-permute-start.1 = (bf16[32,1024]{1,0:T(8,128)(2,1)S(1)}, bf16[32,1024]{1,0:T(8,128)(2,1)S(1)}, u32[]{:S(2)}, u32[]{:S(2)}) collective-permute-start(bf16[32,1024]{1,0:T(8,128)(2,1)S(1)} %get-tuple-element.21), channel_id=1, source_target_pairs={{0,2},{1,3},{2,0},{3,1},{4,6},{5,7},{6,4},{7,5},{8,10},{9,11},{10,... | collective-permute-start | bytes 196616 | tf_op jit(solution)/shard_map/ppermute | solution.py:27
  11.9 8.4 %collective-permute-start.2 = (bf16[32,1024]{1,0:T(8,128)(2,1)S(1)}, bf16[32,1024]{1,0:T(8,128)(2,1)S(1)}, u32[]{:S(2)}, u32[]{:S(2)}) collective-permute-start(bf16[32,1024]{1,0:T(8,128)(2,1)S(1)} %get-tuple-element.22), channel_id=1, source_target_pairs={{0,3},{1,2},{2,1},{3,0},{4,7},{5,6},{6,5},{7,4},{8,11},{9,10},{10,... | collective-permute-start | bytes 196616 | tf_op jit(solution)/shard_map/ppermute | solution.py:27
  11.9 3.5 %collective-permute-start.3 = (f32[1,32]{1,0:T(1,128)S(1)}, f32[1,32]{1,0:T(1,128)S(1)}, u32[]{:S(2)}, u32[]{:S(2)}) collective-permute-start(f32[1,32]{1,0:T(1,128)S(1)} %get-tuple-element.23.refs_4_.weight), channel_id=1, source_target_pairs={{0,16},{16,0},{1,17},{17,1},{2,18},{18,2},{3,19},{19,3},{4,20},{20... | collective-permute-start | bytes 392 | tf_op jit(solution)/shard_map/ppermute | solution.py:27
  21.0 8.1 %collective-permute-start.4 = (bf16[2,32,1024]{2,1,0:T(8,128)(2,1)S(1)}, bf16[2,32,1024]{2,1,0:T(8,128)(2,1)S(1)}, u32[]{:S(2)}, u32[]{:S(2)}) collective-permute-start(bf16[2,32,1024]{2,1,0:T(8,128)(2,1)S(1)} %get-tuple-element.25), channel_id=1, source_target_pairs={{0,4},{1,5},{2,6},{3,7},{4,0},{5,1},{6,2},{7,3},{8,12},{9,13},{10,... | collective-permute-start | bytes 393224 | tf_op jit(solution)/shard_map/ppermute | solution.py:27
  21.1 2.9 %collective-permute-start.5 = (f32[1,32]{1,0:T(1,128)S(1)}, f32[1,32]{1,0:T(1,128)S(1)}, u32[]{:S(2)}, u32[]{:S(2)}) collective-permute-start(f32[1,32]{1,0:T(1,128)S(1)} %get-tuple-element.26.refs_0_), channel_id=1, source_target_pairs={{0,1},{1,0},{2,3},{3,2},{4,5},{5,4},{6,7},{7,6},{8,9},{9,8},{10,11... | collective-permute-start | bytes 392 | tf_op jit(solution)/shard_map/ppermute | solution.py:27
  22.5 3.5 %collective-permute-start.6 = (f32[1,32]{1,0:T(1,128)S(1)}, f32[1,32]{1,0:T(1,128)S(1)}, u32[]{:S(2)}, u32[]{:S(2)}) collective-permute-start(f32[1,32]{1,0:T(1,128)S(1)} %get-tuple-element.26.refs_0_), channel_id=1, source_target_pairs={{0,2},{1,3},{2,0},{3,1},{4,6},{5,7},{6,4},{7,5},{8,10},{9,11},{10,... | collective-permute-start | bytes 392 | tf_op jit(solution)/shard_map/ppermute | solution.py:27
  22.5 3.5 %collective-permute-start.7 = (f32[1,32]{1,0:T(1,128)S(1)}, f32[1,32]{1,0:T(1,128)S(1)}, u32[]{:S(2)}, u32[]{:S(2)}) collective-permute-start(f32[1,32]{1,0:T(1,128)S(1)} %get-tuple-element.26.refs_0_), channel_id=1, source_target_pairs={{0,3},{1,2},{2,1},{3,0},{4,7},{5,6},{6,5},{7,4},{8,11},{9,10},{10,... | collective-permute-start | bytes 392 | tf_op jit(solution)/shard_map/ppermute | solution.py:27
  29.8 7.1 %collective-permute-start.8 = (bf16[48,1024]{1,0:T(8,128)(2,1)S(1)}, bf16[48,1024]{1,0:T(8,128)(2,1)S(1)}, u32[]{:S(2)}, u32[]{:S(2)}) collective-permute-start(bf16[48,1024]{1,0:T(8,128)(2,1)S(1)} %get-tuple-element.28), channel_id=1, source_target_pairs={{0,8},{1,9},{2,10},{3,11},{4,12},{5,13},{6,14},{7,15},{8,0},{9,1},... | collective-permute-start | bytes 294920 | tf_op jit(solution)/shard_map/ppermute | solution.py:27
  37.9 14.1 %collective-permute-start.9 = (f32[8,128]{1,0:T(8,128)S(1)}, f32[8,128]{1,0:T(8,128)S(1)}, u32[]{:S(2)}, u32[]{:S(2)}) collective-permute-start(f32[8,128]{1,0:T(8,128)S(1)} %get-tuple-element.32), channel_id=1, source_target_pairs={{0,4},{1,5},{2,6},{3,7},{4,0},{5,1},{6,2},{7,3},{8,12},{9,13},{10,... | collective-permute-start | bytes 12296 | tf_op jit(solution)/shard_map/ppermute | solution.py:27
  52.0 27.5 %all-to-all-start.1 = ((bf16[16,32,1024]{2,1,0:T(8,128)(2,1)}), bf16[16,32,1024]{2,1,0:T(8,128)(2,1)S(1)}, u32[]{:S(2)}, u32[]{:S(2)}) async-start(bf16[16,32,1024]{2,1,0:T(8,128)(2,1)} %get-tuple-element.33), calls=%async_computation.1 | async-start | bytes 2097152 | tf_op jit(solution)/shard_map/all_to_all | solution.py:35

commit v8 on v7

--- a/solution.py
+++ b/solution.py
@@ -176,7 +176,7 @@
         flops=2 * own * features * features,
         limit=8,
     )(owners, keep, got, encoder, total)
-    return latent, own_weight, total, swap(total, "member", lanes)
+    return latent, own_weight, total
 
 
 def column(row):
@@ -312,7 +312,7 @@
     hidden = sample_inlet_matrix.shape[1]
     own = region_rows // members
     here = transposed(noise.reshape(members, own, features))
-    latent, weight, total, across = prepared(analyses, owners, enc_weight, area_weight)
+    latent, weight, total = prepared(analyses, owners, enc_weight, area_weight)
     gradient, energy = local_call(
         member_kernel,
         [
@@ -331,8 +331,9 @@
         ],
         limit=NETWORK_LIMIT,
     )(here, latent, weight, targets, sample_inlet_matrix, sample_outlet_matrix)
-    gradient, across = lax.optimization_barrier((gradient, across))
+    gradient, total = lax.optimization_barrier((gradient, total))
     back = transposed(gradient)
+    across = swap(total, "member", members // owners.shape[0])
     factor = float(region_rows * regions) / (total[0, 0] + across[0, 0])
     member_grad = (back.astype(F32) * factor).astype(BF16).reshape(1, region_rows, features)
     return member_grad, energy[:, 0] * factor

time: 82.1 us -> 81.6 us (level)
  waiting for transfers between devices: 34.8 us -> 32.7 us
  starting transfers between devices: 27.1 us -> 28.6 us
    all_to_all x2, waiting for transfers between devices: 20 us -> 2.37 us  [transposed(): lax.all_to_all(value, 'member', split_axis=0, concat_axis=0, tiled=True)]
    ppermute x10, waiting for transfers between devices: 14.7 us -> 30.3 us  [swap(): return lax.ppermute(value, axis, [(i, i ^ bit) for i in range(size)])]
    all_to_all x2, starting transfers between devices: 12.1 us -> 15.5 us  [transposed(): lax.all_to_all(value, 'member', split_axis=0, concat_axis=0, tiled=True)]
    ppermute x10, starting transfers between devices: 15 us -> 13.2 us  [swap(): return lax.ppermute(value, axis, [(i, i ^ bit) for i in range(size)])]
  transfers between devices with their start and end apart: 12 -> 12, of which waited for: 7 -> 8; matrix products, arithmetic and copies ran while one was open for 2% -> 2% of each run, Pallas kernels for 17% -> 5%
where the time goes in v8:
time: 81.6 us; the launch traced here: 80.1 us
  waiting for transfers between devices  32.7 us (40%)
  starting transfers between devices  28.6 us (35%)
  Pallas kernels  13.9 us (17%)
  between operations  2 us (2%)
  other arithmetic  1.81 us (2%)
  local copies, waits for them, and re-layouts  1.04 us (1%)
    ppermute x10, waiting for transfers between devices, swap(): return lax.ppermute(value, axis, [(i, i ^ bit) for i in range(size)])  30.3 us
    all_to_all x2, starting transfers between devices, transposed(): lax.all_to_all(value, 'member', split_axis=0, concat_axis=0, tiled=True)  15.5 us
    ppermute x10, starting transfers between devices, swap(): return lax.ppermute(value, axis, [(i, i ^ bit) for i in range(size)])  13.2 us
    pallas_call x1, Pallas kernels, on_device(): local_call(member_kernel, [jax.ShapeDtypeStruct((members, own, features),...  10.1 us
    all_to_all x2, waiting for transfers between devices, transposed(): lax.all_to_all(value, 'member', split_axis=0, concat_axis=0, tiled=True)  2.37 us
  transfers between devices with their start and end apart: 12, of which 8 were waited for; matrix products, arithmetic and copies ran while one was open for 2% of the time, Pallas kernels for 5%

profile of v8, /device:TPU:0, one launch (start us, length us, event | category | flops | bytes accessed | tf_op | source)
XLA Modules:
  0.0 80.1 jit_solution(13211728128213976039)
XLA Ops:
  0.6 0.0 copy-start.1
  0.6 0.0 copy-start.2
  0.7 0.0 copy-start
  0.7 7.5 %all-to-all-start = ((bf16[16,32,1024]{2,1,0:T(8,128)(2,1)}), bf16[16,32,1024]{2,1,0:T(8,128)(2,1)S(1)}, u32[]{:S(2)}, u32[]{:S(2)}) async-start(bf16[16,32,1024]{2,1,0:T(8,128)(2,1)} %bitcast.6), calls=%async_computation | async-start | bytes 2097152 | tf_op jit(solution)/shard_map/all_to_all | solution.py:35
  8.2 0.0 copy-start.3
  8.2 0.0 copy-done.1
  8.2 0.0 copy-done.2
  8.2 1.5 %shard_map.95 = (bf16[32,1024]{1,0:T(8,128)(2,1)S(1)}, bf16[32,1024]{1,0:T(8,128)(2,1)S(1)}, bf16[32,1024]{1,0:T(8,128)(2,1)S(1)}, bf16[32,1024]{1,0:T(8,128)(2,1)S(1)}, f32[1,32]{1,0:T(1,128)S(1)}) custom-call(s32[4]{0:T(128)S(1)} %copy-done.1, bf16[1,512,1024]{2,1,0:T(8,128)(2,1)} %analyses.1, f32[1,32]{1,0:T(1,128)S(1)} %bitcast.4), custom_call_target="tpu_custom_call" | custom-call | tf_op jit(solution)/shard_map/pallas_call | solution.py:144
  9.8 0.5 collective-permute-start
  10.2 1.7 %collective-permute-start.1 = (bf16[32,1024]{1,0:T(8,128)(2,1)S(1)}, bf16[32,1024]{1,0:T(8,128)(2,1)S(1)}, u32[]{:S(2)}, u32[]{:S(2)}) collective-permute-start(bf16[32,1024]{1,0:T(8,128)(2,1)S(1)} %get-tuple-element.21), channel_id=1, source_target_pairs={{0,2},{1,3},{2,0},{3,1},{4,6},{5,7},{6,4},{7,5},{8,10},{9,11},{10,... | collective-permute-start | bytes 196616 | tf_op jit(solution)/shard_map/ppermute | solution.py:27
  11.9 0.0 collective-permute-start.2
  11.9 1.5 %collective-permute-start.3 = (f32[1,32]{1,0:T(1,128)S(1)}, f32[1,32]{1,0:T(1,128)S(1)}, u32[]{:S(2)}, u32[]{:S(2)}) collective-permute-start(f32[1,32]{1,0:T(1,128)S(1)} %get-tuple-element.23.refs_4_.weight), channel_id=1, source_target_pairs={{0,16},{16,0},{1,17},{17,1},{2,18},{18,2},{3,19},{19,3},{4,20},{20... | collective-permute-start | bytes 392 | tf_op jit(solution)/shard_map/ppermute | solution.py:27
  13.4 2.0 %collective-permute-done.3.refs_5_ = f32[1,32]{1,0:T(1,128)S(1)} collective-permute-done((f32[1,32]{1,0:T(1,128)S(1)}, f32[1,32]{1,0:T(1,128)S(1)}, u32[]{:S(2)}, u32[]{:S(2)}) %collective-permute-start.3) | collective-permute-done | bytes 160 | tf_op jit(solution)/shard_map/ppermute | solution.py:27
  15.5 0.0 collective-permute-done.refs_1_
  15.5 4.3 %collective-permute-done.1.refs_2_ = bf16[32,1024]{1,0:T(8,128)(2,1)S(1)} collective-permute-done((bf16[32,1024]{1,0:T(8,128)(2,1)S(1)}, bf16[32,1024]{1,0:T(8,128)(2,1)S(1)}, u32[]{:S(2)}, u32[]{:S(2)}) %collective-permute-start.1) | collective-permute-done | bytes 65568 | tf_op jit(solution)/shard_map/ppermute | solution.py:27
  19.8 0.6 collective-permute-done.2.refs_3_
  20.4 0.6 shard_map.96
  21.0 0.1 collective-permute-start.4
  21.1 0.8 %collective-permute-start.7 = (f32[1,32]{1,0:T(1,128)S(1)}, f32[1,32]{1,0:T(1,128)S(1)}, u32[]{:S(2)}, u32[]{:S(2)}) collective-permute-start(f32[1,32]{1,0:T(1,128)S(1)} %get-tuple-element.26.refs_0_), channel_id=1, source_target_pairs={{0,3},{1,2},{2,1},{3,0},{4,7},{5,6},{6,5},{7,4},{8,11},{9,10},{10,... | collective-permute-start | bytes 392 | tf_op jit(solution)/shard_map/ppermute | solution.py:27
  21.9 2.2 %collective-permute-start.6 = (f32[1,32]{1,0:T(1,128)S(1)}, f32[1,32]{1,0:T(1,128)S(1)}, u32[]{:S(2)}, u32[]{:S(2)}) collective-permute-start(f32[1,32]{1,0:T(1,128)S(1)} %get-tuple-element.26.refs_0_), channel_id=1, source_target_pairs={{0,2},{1,3},{2,0},{3,1},{4,6},{5,7},{6,4},{7,5},{8,10},{9,11},{10,... | collective-permute-start | bytes 392 | tf_op jit(solution)/shard_map/ppermute | solution.py:27
  24.1 0.0 collective-permute-start.5
  24.1 0.0 collective-permute-done.7.refs_3_
  24.1 1.5 %collective-permute-done.6.refs_2_ = f32[1,32]{1,0:T(1,128)S(1)} collective-permute-done((f32[1,32]{1,0:T(1,128)S(1)}, f32[1,32]{1,0:T(1,128)S(1)}, u32[]{:S(2)}, u32[]{:S(2)}) %collective-permute-start.6) | collective-permute-done | bytes 160 | tf_op jit(solution)/shard_map/ppermute | solution.py:27
  25.6 0.0 collective-permute-done.5.refs_1_
  25.6 3.5 %collective-permute-done.4.got = bf16[2,32,1024]{2,1,0:T(8,128)(2,1)S(1)} collective-permute-done((bf16[2,32,1024]{2,1,0:T(8,128)(2,1)S(1)}, bf16[2,32,1024]{2,1,0:T(8,128)(2,1)S(1)}, u32[]{:S(2)}, u32[]{:S(2)}) %collective-permute-start.4) | collective-permute-done | bytes 131104 | tf_op jit(solution)/shard_map/ppermute | solution.py:27
  29.1 0.7 shard_map.97
  29.8 4.5 %collective-permute-start.8 = (bf16[48,1024]{1,0:T(8,128)(2,1)S(1)}, bf16[48,1024]{1,0:T(8,128)(2,1)S(1)}, u32[]{:S(2)}, u32[]{:S(2)}) collective-permute-start(bf16[48,1024]{1,0:T(8,128)(2,1)S(1)} %get-tuple-element.28), channel_id=1, source_target_pairs={{0,8},{1,9},{2,10},{3,11},{4,12},{5,13},{6,14},{7,15},{8,0},{9,1},... | collective-permute-start | bytes 294920 | tf_op jit(solution)/shard_map/ppermute | solution.py:27
  34.2 2.6 %collective-permute-done.8.got = bf16[48,1024]{1,0:T(8,128)(2,1)S(1)} collective-permute-done((bf16[48,1024]{1,0:T(8,128)(2,1)S(1)}, bf16[48,1024]{1,0:T(8,128)(2,1)S(1)}, u32[]{:S(2)}, u32[]{:S(2)}) %collective-permute-start.8) | collective-permute-done | bytes 98336 | tf_op jit(solution)/shard_map/ppermute | solution.py:27
  36.9 0.0 copy-done
  36.9 1.0 %shard_map.98 = (bf16[32,1024]{1,0:T(8,128)(2,1)S(1)}, f32[8,128]{1,0:T(8,128)S(1)}) custom-call(s32[4]{0:T(128)S(1)} %copy-done.1, bf16[1,32,1024]{2,1,0:T(8,128)(2,1)S(1)} %get-tuple-element.27.keep, bf16[48,1024]{1,0:T(8,128)(2,1)S(1)} %collective-permute-done.8.got, bf16[1024,1024]{1,0:T(8,128)(2,1)S(1)} %copy-done, f32[8,128]{1,0:T(8,128)S(1)} %get-tuple-element.29.total), custom_call_target="tpu_custom_call" | custom-call | flops 67108864 | tf_op jit(solution)/shard_map/pallas_call | solution.py:172
  37.9 0.0 all-to-all-done.noise
  37.9 0.0 copy-done.3
  37.9 10.1 %shard_map.99 = (bf16[16,32,1024]{2,1,0:T(8,128)(2,1)}, f32[32,1]{1,0:T(8,128)S(1)}) custom-call(bf16[16,32,1024]{2,1,0:T(8,128)(2,1)S(1)} %all-to-all-done.noise, bf16[32,1024]{1,0:T(8,128)(2,1)S(1)} %get-tuple-element.30.latent, f32[1,32]{1,0:T(1,128)S(1)} %get-tuple-element.23.refs_4_.weight, bf16[32,1024]{1,0:T(8,128)(2,1)S(1)} %copy-done.3, ...), custom_call_target="tpu_custom_call" | custom-call | flops 4328521728 | bytes 8388608 | tf_op jit(solution)/shard_map/pallas_call | solution.py:316
  48.0 7.9 %all-to-all-start.1 = ((bf16[16,32,1024]{2,1,0:T(8,128)(2,1)}), bf16[16,32,1024]{2,1,0:T(8,128)(2,1)S(1)}, u32[]{:S(2)}, u32[]{:S(2)}) async-start(bf16[16,32,1024]{2,1,0:T(8,128)(2,1)} %get-tuple-element.33), calls=%async_computation.1 | async-start | bytes 2097152 | tf_op jit(solution)/shard_map/all_to_all | solution.py:35
  55.9 1.9 %collective-permute-start.9 = (f32[8,128]{1,0:T(8,128)S(1)}, f32[8,128]{1,0:T(8,128)S(1)}, u32[]{:S(2)}, u32[]{:S(2)}) collective-permute-start(f32[8,128]{1,0:T(8,128)S(1)} %get-tuple-element.34), channel_id=1, source_target_pairs={{0,4},{1,5},{2,6},{3,7},{4,0},{5,1},{6,2},{7,3},{8,12},{9,13},{10,... | collective-permute-start | bytes 12296 | tf_op jit(solution)/shard_map/ppermute | solution.py:27
  57.9 0.5 slice.6
  58.4 15.8 %collective-permute-done.9 = f32[8,128]{1,0:T(8,128)S(1)} collective-permute-done((f32[8,128]{1,0:T(8,128)S(1)}, f32[8,128]{1,0:T(8,128)S(1)}, u32[]{:S(2)}, u32[]{:S(2)}) %collective-permute-start.9) | collective-permute-done | bytes 4128 | tf_op jit(solution)/shard_map/ppermute | solution.py:27
  74.1 0.5 slice.7
  75.9 0.6 multiply_reduce_fusion
  76.5 2.4 %all-to-all-done.1 = bf16[16,32,1024]{2,1,0:T(8,128)(2,1)S(1)} async-done(((bf16[16,32,1024]{2,1,0:T(8,128)(2,1)}), bf16[16,32,1024]{2,1,0:T(8,128)(2,1)S(1)}, u32[]{:S(2)}, u32[]{:S(2)}) %all-to-all-start.1) | async-done | bytes 1048608 | tf_op jit(solution)/shard_map/all_to_all | solution.py:35
  78.9 1.2 %multiply_convert_fusion = bf16[16,32,1024]{2,1,0:T(8,128)(2,1)} fusion(bf16[16,32,1024]{2,1,0:T(8,128)(2,1)S(1)} %all-to-all-done.1, f32[]{:T(128)} %bitcast.2), kind=kLoop, calls=%fused_computation | loop fusion | flops 1572864 | bytes 2097156 | tf_op jit(solution)/shard_map/convert_element_type | solution.py:338
Async XLA Ops:
  0.6 7.6 %copy-start.1 = (s32[4]{0:T(128)S(1)}, s32[4]{0:T(128)}, u32[]{:S(2)}) copy-start(s32[4]{0:T(128)} %owners.7) | copy-start | bytes 52
  0.6 7.6 %copy-start.2 = (f32[32]{0:T(128)S(1)}, f32[32]{0:T(128)}, u32[]{:S(2)}) copy-start(f32[32]{0:T(128)} %param.12) | copy-start | bytes 388
  0.7 36.2 %copy-start = (bf16[1024,1024]{1,0:T(8,128)(2,1)S(1)}, bf16[1024,1024]{1,0:T(8,128)(2,1)}, u32[]{:S(2)}) copy-start(bf16[1024,1024]{1,0:T(8,128)(2,1)} %encoder.1) | copy-start | bytes 6291460
  0.7 37.2 %all-to-all-start = ((bf16[16,32,1024]{2,1,0:T(8,128)(2,1)}), bf16[16,32,1024]{2,1,0:T(8,128)(2,1)S(1)}, u32[]{:S(2)}, u32[]{:S(2)}) async-start(bf16[16,32,1024]{2,1,0:T(8,128)(2,1)} %bitcast.6), calls=%async_computation | async-start | bytes 2097152 | tf_op jit(solution)/shard_map/all_to_all | solution.py:35
  8.2 29.7 %copy-start.3 = (bf16[32,1024]{1,0:T(8,128)(2,1)S(1)}, bf16[32,1024]{1,0:T(8,128)(2,1)}, u32[]{:S(2)}) copy-start(bf16[32,1024]{1,0:T(8,128)(2,1)} %targets_hbm.1) | copy-start | bytes 196612
  9.8 5.7 %collective-permute-start = (bf16[32,1024]{1,0:T(8,128)(2,1)S(1)}, bf16[32,1024]{1,0:T(8,128)(2,1)S(1)}, u32[]{:S(2)}, u32[]{:S(2)}) collective-permute-start(bf16[32,1024]{1,0:T(8,128)(2,1)S(1)} %get-tuple-element.20), channel_id=1, source_target_pairs={{0,1},{1,0},{2,3},{3,2},{4,5},{5,4},{6,7},{7,6},{8,9},{9,8},{10,11... | collective-permute-start | bytes 196616 | tf_op jit(solution)/shard_map/ppermute | solution.py:27
  10.2 9.6 %collective-permute-start.1 = (bf16[32,1024]{1,0:T(8,128)(2,1)S(1)}, bf16[32,1024]{1,0:T(8,128)(2,1)S(1)}, u32[]{:S(2)}, u32[]{:S(2)}) collective-permute-start(bf16[32,1024]{1,0:T(8,128)(2,1)S(1)} %get-tuple-element.21), channel_id=1, source_target_pairs={{0,2},{1,3},{2,0},{3,1},{4,6},{5,7},{6,4},{7,5},{8,10},{9,11},{10,... | collective-permute-start | bytes 196616 | tf_op jit(solution)/shard_map/ppermute | solution.py:27
  11.9 8.4 %collective-permute-start.2 = (bf16[32,1024]{1,0:T(8,128)(2,1)S(1)}, bf16[32,1024]{1,0:T(8,128)(2,1)S(1)}, u32[]{:S(2)}, u32[]{:S(2)}) collective-permute-start(bf16[32,1024]{1,0:T(8,128)(2,1)S(1)} %get-tuple-element.22), channel_id=1, source_target_pairs={{0,3},{1,2},{2,1},{3,0},{4,7},{5,6},{6,5},{7,4},{8,11},{9,10},{10,... | collective-permute-start | bytes 196616 | tf_op jit(solution)/shard_map/ppermute | solution.py:27
  11.9 3.5 %collective-permute-start.3 = (f32[1,32]{1,0:T(1,128)S(1)}, f32[1,32]{1,0:T(1,128)S(1)}, u32[]{:S(2)}, u32[]{:S(2)}) collective-permute-start(f32[1,32]{1,0:T(1,128)S(1)} %get-tuple-element.23.refs_4_.weight), channel_id=1, source_target_pairs={{0,16},{16,0},{1,17},{17,1},{2,18},{18,2},{3,19},{19,3},{4,20},{20... | collective-permute-start | bytes 392 | tf_op jit(solution)/shard_map/ppermute | solution.py:27
  21.0 8.1 %collective-permute-start.4 = (bf16[2,32,1024]{2,1,0:T(8,128)(2,1)S(1)}, bf16[2,32,1024]{2,1,0:T(8,128)(2,1)S(1)}, u32[]{:S(2)}, u32[]{:S(2)}) collective-permute-start(bf16[2,32,1024]{2,1,0:T(8,128)(2,1)S(1)} %get-tuple-element.25), channel_id=1, source_target_pairs={{0,4},{1,5},{2,6},{3,7},{4,0},{5,1},{6,2},{7,3},{8,12},{9,13},{10,... | collective-permute-start | bytes 393224 | tf_op jit(solution)/shard_map/ppermute | solution.py:27
  21.1 3.1 %collective-permute-start.7 = (f32[1,32]{1,0:T(1,128)S(1)}, f32[1,32]{1,0:T(1,128)S(1)}, u32[]{:S(2)}, u32[]{:S(2)}) collective-permute-start(f32[1,32]{1,0:T(1,128)S(1)} %get-tuple-element.26.refs_0_), channel_id=1, source_target_pairs={{0,3},{1,2},{2,1},{3,0},{4,7},{5,6},{6,5},{7,4},{8,11},{9,10},{10,... | collective-permute-start | bytes 392 | tf_op jit(solution)/shard_map/ppermute | solution.py:27
  21.9 3.7 %collective-permute-start.6 = (f32[1,32]{1,0:T(1,128)S(1)}, f32[1,32]{1,0:T(1,128)S(1)}, u32[]{:S(2)}, u32[]{:S(2)}) collective-permute-start(f32[1,32]{1,0:T(1,128)S(1)} %get-tuple-element.26.refs_0_), channel_id=1, source_target_pairs={{0,2},{1,3},{2,0},{3,1},{4,6},{5,7},{6,4},{7,5},{8,10},{9,11},{10,... | collective-permute-start | bytes 392 | tf_op jit(solution)/shard_map/ppermute | solution.py:27
  24.1 1.5 %collective-permute-start.5 = (f32[1,32]{1,0:T(1,128)S(1)}, f32[1,32]{1,0:T(1,128)S(1)}, u32[]{:S(2)}, u32[]{:S(2)}) collective-permute-start(f32[1,32]{1,0:T(1,128)S(1)} %get-tuple-element.26.refs_0_), channel_id=1, source_target_pairs={{0,1},{1,0},{2,3},{3,2},{4,5},{5,4},{6,7},{7,6},{8,9},{9,8},{10,11... | collective-permute-start | bytes 392 | tf_op jit(solution)/shard_map/ppermute | solution.py:27
  29.8 7.1 %collective-permute-start.8 = (bf16[48,1024]{1,0:T(8,128)(2,1)S(1)}, bf16[48,1024]{1,0:T(8,128)(2,1)S(1)}, u32[]{:S(2)}, u32[]{:S(2)}) collective-permute-start(bf16[48,1024]{1,0:T(8,128)(2,1)S(1)} %get-tuple-element.28), channel_id=1, source_target_pairs={{0,8},{1,9},{2,10},{3,11},{4,12},{5,13},{6,14},{7,15},{8,0},{9,1},... | collective-permute-start | bytes 294920 | tf_op jit(solution)/shard_map/ppermute | solution.py:27
  48.0 30.9 %all-to-all-start.1 = ((bf16[16,32,1024]{2,1,0:T(8,128)(2,1)}), bf16[16,32,1024]{2,1,0:T(8,128)(2,1)S(1)}, u32[]{:S(2)}, u32[]{:S(2)}) async-start(bf16[16,32,1024]{2,1,0:T(8,128)(2,1)} %get-tuple-element.33), calls=%async_computation.1 | async-start | bytes 2097152 | tf_op jit(solution)/shard_map/all_to_all | solution.py:35
  55.9 18.2 %collective-permute-start.9 = (f32[8,128]{1,0:T(8,128)S(1)}, f32[8,128]{1,0:T(8,128)S(1)}, u32[]{:S(2)}, u32[]{:S(2)}) collective-permute-start(f32[8,128]{1,0:T(8,128)S(1)} %get-tuple-element.34), channel_id=1, source_target_pairs={{0,4},{1,5},{2,6},{3,7},{4,0},{5,1},{6,2},{7,3},{8,12},{9,13},{10,... | collective-permute-start | bytes 12296 | tf_op jit(solution)/shard_map/ppermute | solution.py:27

commit v9 on v8

--- a/solution.py
+++ b/solution.py
@@ -11,9 +11,9 @@
 TOKENS_AT_ONCE = 16
 TAIL = 16
 HIDDEN_PIECES = 2
-INLET_PARTS = 2
 ROWS_LIMIT = 53
-NETWORK_LIMIT = 50
+NETWORK_LIMIT = 46
+FETCH_LIMIT = 46
 BF16 = jnp.bfloat16
 F32 = jnp.float32
 
@@ -121,6 +121,12 @@
     give[pl.ds(keep_out.shape[0] * own, TAIL), :] = weight_rows(total, features)
 
 
+def fetch_kernel(matrix, after, near, sem):
+    copy = pltpu.make_async_copy(matrix, near, sem)
+    copy.start()
+    copy.wait()
+
+
 def encode_kernel(lanes, bit, owners, keep, got, encoder, total, latent, total_out):
     own = latent.shape[0]
     plane = lax.axis_index("member") // lanes
@@ -130,7 +136,7 @@
     total_out[...] = total[...] + weight_from(got[pl.ds(own, TAIL), :])
 
 
-def prepared(analyses, owners, encoder, area_weight):
+def prepared(analyses, owners, encoder, area_weight, matrix, after):
     members, regions = lax.axis_size("member"), lax.axis_size("region")
     _, rows, features = analyses.shape
     blocks = owners.shape[0]
@@ -169,6 +175,15 @@
         limit=8,
     )(owners, keep, got, *weights)
     got = swap(give, "member", 2 * lanes)
+    (near,) = local_call(
+        fetch_kernel,
+        [jax.ShapeDtypeStruct(matrix.shape, BF16)],
+        [HBM, VMEM],
+        moved=2 * matrix.size,
+        scratch=[pltpu.SemaphoreType.DMA],
+        limit=FETCH_LIMIT,
+    )(matrix, after)
+    got, near = lax.optimization_barrier((got, near))
     latent, total = local_call(
         functools.partial(encode_kernel, lanes, 2),
         [row, small],
@@ -176,7 +191,7 @@
         flops=2 * own * features * features,
         limit=8,
     )(owners, keep, got, encoder, total)
-    return latent, own_weight, total
+    return latent, own_weight, total, near
 
 
 def column(row):
@@ -233,56 +248,38 @@
     noise,
     latent,
     weight,
+    inlet,
     targets_hbm,
-    inlet_hbm,
     outlet_hbm,
     gradient_out,
     energy_out,
     targets,
-    inlet,
     outlet,
     hidden,
     sems,
 ):
     members, own, features = noise.shape
     width = inlet.shape[1] // HIDDEN_PIECES
-    part = width // INLET_PARTS
-    copies = []
+    copies = [pltpu.make_async_copy(targets_hbm, targets, sems.at[HIDDEN_PIECES])]
     for piece in range(HIDDEN_PIECES):
-        for i in range(INLET_PARTS):
-            columns = pl.ds(piece * width + i * part, part)
-            copies.append((inlet_hbm.at[:, columns], inlet.at[:, columns]))
         rows = pl.ds(piece * width, width)
-        copies.append((outlet_hbm.at[rows, :], outlet.at[rows, :]))
-    copies = [
-        pltpu.make_async_copy(source, target, sems.at[i])
-        for i, (source, target) in enumerate(copies)
-    ]
-
-    def arrived(i):
-        copies[i].wait()
-        if i + 2 < len(copies):
-            copies[i + 2].start()
-
-    aside = pltpu.make_async_copy(targets_hbm, targets, sems.at[len(copies)])
-    for copy in (*copies[:2], aside):
+        copies.append(
+            pltpu.make_async_copy(outlet_hbm.at[rows, :], outlet.at[rows, :], sems.at[piece])
+        )
+    for copy in copies:
         copy.start()
 
     def hidden_piece(normed, piece):
-        for i in range(INLET_PARTS):
-            arrived(piece * (INLET_PARTS + 1) + i)
-            first = piece * width + i * part
-            hidden[:, i * part : (i + 1) * part] = jax.nn.gelu(
-                jnp.dot(normed, inlet[:, first : first + part], preferred_element_type=F32),
-                approximate=True,
-            ).astype(BF16)
-        arrived(piece * (INLET_PARTS + 1) + INLET_PARTS)
         rows = slice(piece * width, (piece + 1) * width)
+        hidden[...] = jax.nn.gelu(
+            jnp.dot(normed, inlet[:, rows], preferred_element_type=F32), approximate=True
+        ).astype(BF16)
+        copies[piece + 1].wait()
         return jnp.dot(hidden[...], outlet[rows, :], preferred_element_type=F32)
 
     forecast = network(noise[...], latent[...], hidden_piece, HIDDEN_PIECES)
     forecast = forecast.reshape(members, own, features)
-    aside.wait()
+    copies[0].wait()
     scales = column(weight[...])
     for first in range(0, own, TOKENS_AT_ONCE):
         here = slice(first, first + TOKENS_AT_ONCE)
@@ -312,25 +309,26 @@
     hidden = sample_inlet_matrix.shape[1]
     own = region_rows // members
     here = transposed(noise.reshape(members, own, features))
-    latent, weight, total = prepared(analyses, owners, enc_weight, area_weight)
+    latent, weight, total, inlet = prepared(
+        analyses, owners, enc_weight, area_weight, sample_inlet_matrix, here
+    )
     gradient, energy = local_call(
         member_kernel,
         [
             jax.ShapeDtypeStruct((members, own, features), BF16),
             jax.ShapeDtypeStruct((own, 1), F32),
         ],
-        [VMEM] * 3 + [HBM] * 3,
+        [VMEM] * 4 + [HBM] * 2,
         flops=4 * members * own * features * (hidden + members),
         moved=4 * features * hidden,
         scratch=[
             pltpu.VMEM((own, features), BF16),
-            pltpu.VMEM((features, hidden), BF16),
             pltpu.VMEM((hidden, features), BF16),
             pltpu.VMEM((members * own, hidden // HIDDEN_PIECES), BF16),
-            pltpu.SemaphoreType.DMA((HIDDEN_PIECES * (INLET_PARTS + 1) + 1,)),
+            pltpu.SemaphoreType.DMA((HIDDEN_PIECES + 1,)),
         ],
         limit=NETWORK_LIMIT,
-    )(here, latent, weight, targets, sample_inlet_matrix, sample_outlet_matrix)
+    )(here, latent, weight, inlet, targets, sample_outlet_matrix)
     gradient, total = lax.optimization_barrier((gradient, total))
     back = transposed(gradient)
     across = swap(total, "member", members // owners.shape[0])

time: 81.6 us -> 80.1 us (0.982)
  waiting for transfers between devices: 32.7 us -> 30.4 us
    ppermute x10, waiting for transfers between devices: 30.3 us -> 28.1 us  [swap(): return lax.ppermute(value, axis, [(i, i ^ bit) for i in range(size)])]
    pallas_call x0 -> x1, Pallas kernels: none -> 2.2 us  [prepared(): local_call(fetch_kernel, [jax.ShapeDtypeStruct(matrix.shape, BF16)], [HBM...]
    pallas_call x1, Pallas kernels: 10.1 us -> 8.67 us  [on_device(): local_call(member_kernel, [jax.ShapeDtypeStruct((members, own, features),...]
  transfers between devices with their start and end apart: 12 -> 12, of which waited for: 8 -> 8; matrix products, arithmetic and copies ran while one was open for 2% -> 2% of each run, Pallas kernels for 5% -> 6%
where the time goes in v9:
time: 80.1 us; the launch traced here: 78.6 us
  waiting for transfers between devices  30.4 us (38%)
  starting transfers between devices  28.7 us (36%)
  Pallas kernels  14.7 us (18%)
  between operations  2 us (2%)
  other arithmetic  1.8 us (2%)
  local copies, waits for them, and re-layouts  1.04 us (1%)
    ppermute x10, waiting for transfers between devices, swap(): return lax.ppermute(value, axis, [(i, i ^ bit) for i in range(size)])  28.1 us
    all_to_all x2, starting transfers between devices, transposed(): lax.all_to_all(value, 'member', split_axis=0, concat_axis=0, tiled=True)  15.5 us
    ppermute x10, starting transfers between devices, swap(): return lax.ppermute(value, axis, [(i, i ^ bit) for i in range(size)])  13.2 us
    pallas_call x1, Pallas kernels, on_device(): local_call(member_kernel, [jax.ShapeDtypeStruct((members, own, features),...  8.67 us
    all_to_all x2, waiting for transfers between devices, transposed(): lax.all_to_all(value, 'member', split_axis=0, concat_axis=0, tiled=True)  2.37 us
    pallas_call x1, Pallas kernels, prepared(): local_call(fetch_kernel, [jax.ShapeDtypeStruct(matrix.shape, BF16)], [HBM...  2.2 us
  transfers between devices with their start and end apart: 12, of which 8 were waited for; matrix products, arithmetic and copies ran while one was open for 2% of the time, Pallas kernels for 6%

profile of v9, /device:TPU:0, one launch (start us, length us, event | category | flops | bytes accessed | tf_op | source)
XLA Modules:
  0.0 78.6 jit_solution(12709047186473919678)
XLA Ops:
  0.6 0.0 copy-start.1
  0.6 0.0 copy-start.2
  0.6 7.5 %all-to-all-start = ((bf16[16,32,1024]{2,1,0:T(8,128)(2,1)}), bf16[16,32,1024]{2,1,0:T(8,128)(2,1)S(1)}, u32[]{:S(2)}, u32[]{:S(2)}) async-start(bf16[16,32,1024]{2,1,0:T(8,128)(2,1)} %bitcast.6), calls=%async_computation | async-start | bytes 2097152 | tf_op jit(solution)/shard_map/all_to_all | solution.py:35
  8.2 0.0 copy-done.1
  8.2 0.0 copy-done.2
  8.2 1.5 %shard_map.95 = (bf16[32,1024]{1,0:T(8,128)(2,1)S(1)}, bf16[32,1024]{1,0:T(8,128)(2,1)S(1)}, bf16[32,1024]{1,0:T(8,128)(2,1)S(1)}, bf16[32,1024]{1,0:T(8,128)(2,1)S(1)}, f32[1,32]{1,0:T(1,128)S(1)}) custom-call(s32[4]{0:T(128)S(1)} %copy-done.1, bf16[1,512,1024]{2,1,0:T(8,128)(2,1)} %analyses.1, f32[1,32]{1,0:T(1,128)S(1)} %bitcast.4), custom_call_target="tpu_custom_call" | custom-call | tf_op jit(solution)/shard_map/pallas_call | solution.py:150
  9.8 0.5 collective-permute-start
  10.2 1.7 %collective-permute-start.1 = (bf16[32,1024]{1,0:T(8,128)(2,1)S(1)}, bf16[32,1024]{1,0:T(8,128)(2,1)S(1)}, u32[]{:S(2)}, u32[]{:S(2)}) collective-permute-start(bf16[32,1024]{1,0:T(8,128)(2,1)S(1)} %get-tuple-element.23), channel_id=1, source_target_pairs={{0,2},{1,3},{2,0},{3,1},{4,6},{5,7},{6,4},{7,5},{8,10},{9,11},{10,... | collective-permute-start | bytes 196616 | tf_op jit(solution)/shard_map/ppermute | solution.py:27
  11.9 0.0 collective-permute-start.2
  11.9 1.5 %collective-permute-start.3 = (f32[1,32]{1,0:T(1,128)S(1)}, f32[1,32]{1,0:T(1,128)S(1)}, u32[]{:S(2)}, u32[]{:S(2)}) collective-permute-start(f32[1,32]{1,0:T(1,128)S(1)} %get-tuple-element.25.refs_4_.weight), channel_id=1, source_target_pairs={{0,16},{16,0},{1,17},{17,1},{2,18},{18,2},{3,19},{19,3},{4,20},{20... | collective-permute-start | bytes 392 | tf_op jit(solution)/shard_map/ppermute | solution.py:27
  13.4 2.0 %collective-permute-done.3.refs_5_ = f32[1,32]{1,0:T(1,128)S(1)} collective-permute-done((f32[1,32]{1,0:T(1,128)S(1)}, f32[1,32]{1,0:T(1,128)S(1)}, u32[]{:S(2)}, u32[]{:S(2)}) %collective-permute-start.3) | collective-permute-done | bytes 160 | tf_op jit(solution)/shard_map/ppermute | solution.py:27
  15.4 0.0 collective-permute-done.refs_1_
  15.5 4.3 %collective-permute-done.1.refs_2_ = bf16[32,1024]{1,0:T(8,128)(2,1)S(1)} collective-permute-done((bf16[32,1024]{1,0:T(8,128)(2,1)S(1)}, bf16[32,1024]{1,0:T(8,128)(2,1)S(1)}, u32[]{:S(2)}, u32[]{:S(2)}) %collective-permute-start.1) | collective-permute-done | bytes 65568 | tf_op jit(solution)/shard_map/ppermute | solution.py:27
  19.8 0.6 collective-permute-done.2.refs_3_
  20.4 0.6 shard_map.96
  21.0 0.1 collective-permute-start.4
  21.0 0.8 %collective-permute-start.7 = (f32[1,32]{1,0:T(1,128)S(1)}, f32[1,32]{1,0:T(1,128)S(1)}, u32[]{:S(2)}, u32[]{:S(2)}) collective-permute-start(f32[1,32]{1,0:T(1,128)S(1)} %get-tuple-element.28.refs_0_), channel_id=1, source_target_pairs={{0,3},{1,2},{2,1},{3,0},{4,7},{5,6},{6,5},{7,4},{8,11},{9,10},{10,... | collective-permute-start | bytes 392 | tf_op jit(solution)/shard_map/ppermute | solution.py:27
  21.9 2.2 %collective-permute-start.6 = (f32[1,32]{1,0:T(1,128)S(1)}, f32[1,32]{1,0:T(1,128)S(1)}, u32[]{:S(2)}, u32[]{:S(2)}) collective-permute-start(f32[1,32]{1,0:T(1,128)S(1)} %get-tuple-element.28.refs_0_), channel_id=1, source_target_pairs={{0,2},{1,3},{2,0},{3,1},{4,6},{5,7},{6,4},{7,5},{8,10},{9,11},{10,... | collective-permute-start | bytes 392 | tf_op jit(solution)/shard_map/ppermute | solution.py:27
  24.1 0.0 collective-permute-start.5
  24.1 0.0 collective-permute-done.7.refs_3_
  24.1 1.5 %collective-permute-done.6.refs_2_ = f32[1,32]{1,0:T(1,128)S(1)} collective-permute-done((f32[1,32]{1,0:T(1,128)S(1)}, f32[1,32]{1,0:T(1,128)S(1)}, u32[]{:S(2)}, u32[]{:S(2)}) %collective-permute-start.6) | collective-permute-done | bytes 160 | tf_op jit(solution)/shard_map/ppermute | solution.py:27
  25.6 0.0 collective-permute-done.5.refs_1_
  25.6 3.5 %collective-permute-done.4.got = bf16[2,32,1024]{2,1,0:T(8,128)(2,1)S(1)} collective-permute-done((bf16[2,32,1024]{2,1,0:T(8,128)(2,1)S(1)}, bf16[2,32,1024]{2,1,0:T(8,128)(2,1)S(1)}, u32[]{:S(2)}, u32[]{:S(2)}) %collective-permute-start.4) | collective-permute-done | bytes 131104 | tf_op jit(solution)/shard_map/ppermute | solution.py:27
  29.1 0.7 shard_map.97
  29.8 0.0 copy-start
  29.8 4.5 %collective-permute-start.8 = (bf16[48,1024]{1,0:T(8,128)(2,1)S(1)}, bf16[48,1024]{1,0:T(8,128)(2,1)S(1)}, u32[]{:S(2)}, u32[]{:S(2)}) collective-permute-start(bf16[48,1024]{1,0:T(8,128)(2,1)S(1)} %get-tuple-element.30), channel_id=1, source_target_pairs={{0,8},{1,9},{2,10},{3,11},{4,12},{5,13},{6,14},{7,15},{8,0},{9,1},... | collective-permute-start | bytes 294920 | tf_op jit(solution)/shard_map/ppermute | solution.py:27
  34.2 0.0 all-to-all-done.after.noise
  34.2 2.2 %shard_map.98.inlet = bf16[1024,2048]{1,0:T(8,128)(2,1)S(1)} custom-call(bf16[1024,2048]{1,0:T(8,128)(2,1)} %matrix.1, bf16[16,32,1024]{2,1,0:T(8,128)(2,1)S(1)} %all-to-all-done.after.noise), custom_call_target="tpu_custom_call" | custom-call | bytes 4194304 | tf_op jit(solution)/shard_map/pallas_call | solution.py:178
  36.4 0.0 copy-start.3
  36.5 0.4 collective-permute-done.8.got
  36.8 0.0 copy-done
  36.8 1.0 %shard_map.99 = (bf16[32,1024]{1,0:T(8,128)(2,1)S(1)}, f32[8,128]{1,0:T(8,128)S(1)}) custom-call(s32[4]{0:T(128)S(1)} %copy-done.1, bf16[1,32,1024]{2,1,0:T(8,128)(2,1)S(1)} %get-tuple-element.29.keep, bf16[48,1024]{1,0:T(8,128)(2,1)S(1)} %collective-permute-done.8.got, bf16[1024,1024]{1,0:T(8,128)(2,1)S(1)} %copy-done, f32[8,128]{1,0:T(8,128)S(1)} %get-tuple-element.32.total), custom_call_target="tpu_custom_call" | custom-call | flops 67108864 | tf_op jit(solution)/shard_map/pallas_call | solution.py:187
  37.9 0.0 copy-done.3
  37.9 8.7 %shard_map.100 = (bf16[16,32,1024]{2,1,0:T(8,128)(2,1)}, f32[32,1]{1,0:T(8,128)S(1)}) custom-call(bf16[16,32,1024]{2,1,0:T(8,128)(2,1)S(1)} %all-to-all-done.after.noise, bf16[32,1024]{1,0:T(8,128)(2,1)S(1)} %get-tuple-element.33.latent, f32[1,32]{1,0:T(1,128)S(1)} %get-tuple-element.25.refs_4_.weight, bf16[1024,2048]{1,0:T(8,128)(2,1)S(1)} %shard_map.98.inlet, ...), custom_call_target="tpu_custom_call" | custom-call | flops 4328521728 | bytes 8388608 | tf_op jit(solution)/shard_map/pallas_call | solution.py:315
  46.5 8.0 %all-to-all-start.1 = ((bf16[16,32,1024]{2,1,0:T(8,128)(2,1)}), bf16[16,32,1024]{2,1,0:T(8,128)(2,1)S(1)}, u32[]{:S(2)}, u32[]{:S(2)}) async-start(bf16[16,32,1024]{2,1,0:T(8,128)(2,1)} %get-tuple-element.37), calls=%async_computation.1 | async-start | bytes 2097152 | tf_op jit(solution)/shard_map/all_to_all | solution.py:35
  54.5 1.9 %collective-permute-start.9 = (f32[8,128]{1,0:T(8,128)S(1)}, f32[8,128]{1,0:T(8,128)S(1)}, u32[]{:S(2)}, u32[]{:S(2)}) collective-permute-start(f32[8,128]{1,0:T(8,128)S(1)} %get-tuple-element.38), channel_id=1, source_target_pairs={{0,4},{1,5},{2,6},{3,7},{4,0},{5,1},{6,2},{7,3},{8,12},{9,13},{10,... | collective-permute-start | bytes 12296 | tf_op jit(solution)/shard_map/ppermute | solution.py:27
  56.4 0.5 slice.6
  57.0 15.8 %collective-permute-done.9 = f32[8,128]{1,0:T(8,128)S(1)} collective-permute-done((f32[8,128]{1,0:T(8,128)S(1)}, f32[8,128]{1,0:T(8,128)S(1)}, u32[]{:S(2)}, u32[]{:S(2)}) %collective-permute-start.9) | collective-permute-done | bytes 4128 | tf_op jit(solution)/shard_map/ppermute | solution.py:27
  72.7 0.5 slice.7
  74.5 0.6 multiply_reduce_fusion
  75.1 2.4 %all-to-all-done.1 = bf16[16,32,1024]{2,1,0:T(8,128)(2,1)S(1)} async-done(((bf16[16,32,1024]{2,1,0:T(8,128)(2,1)}), bf16[16,32,1024]{2,1,0:T(8,128)(2,1)S(1)}, u32[]{:S(2)}, u32[]{:S(2)}) %all-to-all-start.1) | async-done | bytes 1048608 | tf_op jit(solution)/shard_map/all_to_all | solution.py:35
  77.5 1.2 %multiply_convert_fusion = bf16[16,32,1024]{2,1,0:T(8,128)(2,1)} fusion(bf16[16,32,1024]{2,1,0:T(8,128)(2,1)S(1)} %all-to-all-done.1, f32[]{:T(128)} %bitcast.2), kind=kLoop, calls=%fused_computation | loop fusion | flops 1572864 | bytes 2097156 | tf_op jit(solution)/shard_map/convert_element_type | solution.py:336
Async XLA Ops:
  0.6 7.6 %copy-start.1 = (s32[4]{0:T(128)S(1)}, s32[4]{0:T(128)}, u32[]{:S(2)}) copy-start(s32[4]{0:T(128)} %owners.7) | copy-start | bytes 52
  0.6 7.6 %copy-start.2 = (f32[32]{0:T(128)S(1)}, f32[32]{0:T(128)}, u32[]{:S(2)}) copy-start(f32[32]{0:T(128)} %param.12) | copy-start | bytes 388
  0.6 33.6 %all-to-all-start = ((bf16[16,32,1024]{2,1,0:T(8,128)(2,1)}), bf16[16,32,1024]{2,1,0:T(8,128)(2,1)S(1)}, u32[]{:S(2)}, u32[]{:S(2)}) async-start(bf16[16,32,1024]{2,1,0:T(8,128)(2,1)} %bitcast.6), calls=%async_computation | async-start | bytes 2097152 | tf_op jit(solution)/shard_map/all_to_all | solution.py:35
  9.8 5.7 %collective-permute-start = (bf16[32,1024]{1,0:T(8,128)(2,1)S(1)}, bf16[32,1024]{1,0:T(8,128)(2,1)S(1)}, u32[]{:S(2)}, u32[]{:S(2)}) collective-permute-start(bf16[32,1024]{1,0:T(8,128)(2,1)S(1)} %get-tuple-element.22), channel_id=1, source_target_pairs={{0,1},{1,0},{2,3},{3,2},{4,5},{5,4},{6,7},{7,6},{8,9},{9,8},{10,11... | collective-permute-start | bytes 196616 | tf_op jit(solution)/shard_map/ppermute | solution.py:27
  10.2 9.6 %collective-permute-start.1 = (bf16[32,1024]{1,0:T(8,128)(2,1)S(1)}, bf16[32,1024]{1,0:T(8,128)(2,1)S(1)}, u32[]{:S(2)}, u32[]{:S(2)}) collective-permute-start(bf16[32,1024]{1,0:T(8,128)(2,1)S(1)} %get-tuple-element.23), channel_id=1, source_target_pairs={{0,2},{1,3},{2,0},{3,1},{4,6},{5,7},{6,4},{7,5},{8,10},{9,11},{10,... | collective-permute-start | bytes 196616 | tf_op jit(solution)/shard_map/ppermute | solution.py:27
  11.9 8.5 %collective-permute-start.2 = (bf16[32,1024]{1,0:T(8,128)(2,1)S(1)}, bf16[32,1024]{1,0:T(8,128)(2,1)S(1)}, u32[]{:S(2)}, u32[]{:S(2)}) collective-permute-start(bf16[32,1024]{1,0:T(8,128)(2,1)S(1)} %get-tuple-element.24), channel_id=1, source_target_pairs={{0,3},{1,2},{2,1},{3,0},{4,7},{5,6},{6,5},{7,4},{8,11},{9,10},{10,... | collective-permute-start | bytes 196616 | tf_op jit(solution)/shard_map/ppermute | solution.py:27
  11.9 3.5 %collective-permute-start.3 = (f32[1,32]{1,0:T(1,128)S(1)}, f32[1,32]{1,0:T(1,128)S(1)}, u32[]{:S(2)}, u32[]{:S(2)}) collective-permute-start(f32[1,32]{1,0:T(1,128)S(1)} %get-tuple-element.25.refs_4_.weight), channel_id=1, source_target_pairs={{0,16},{16,0},{1,17},{17,1},{2,18},{18,2},{3,19},{19,3},{4,20},{20... | collective-permute-start | bytes 392 | tf_op jit(solution)/shard_map/ppermute | solution.py:27
  21.0 8.1 %collective-permute-start.4 = (bf16[2,32,1024]{2,1,0:T(8,128)(2,1)S(1)}, bf16[2,32,1024]{2,1,0:T(8,128)(2,1)S(1)}, u32[]{:S(2)}, u32[]{:S(2)}) collective-permute-start(bf16[2,32,1024]{2,1,0:T(8,128)(2,1)S(1)} %get-tuple-element.27), channel_id=1, source_target_pairs={{0,4},{1,5},{2,6},{3,7},{4,0},{5,1},{6,2},{7,3},{8,12},{9,13},{10,... | collective-permute-start | bytes 393224 | tf_op jit(solution)/shard_map/ppermute | solution.py:27
  21.0 3.1 %collective-permute-start.7 = (f32[1,32]{1,0:T(1,128)S(1)}, f32[1,32]{1,0:T(1,128)S(1)}, u32[]{:S(2)}, u32[]{:S(2)}) collective-permute-start(f32[1,32]{1,0:T(1,128)S(1)} %get-tuple-element.28.refs_0_), channel_id=1, source_target_pairs={{0,3},{1,2},{2,1},{3,0},{4,7},{5,6},{6,5},{7,4},{8,11},{9,10},{10,... | collective-permute-start | bytes 392 | tf_op jit(solution)/shard_map/ppermute | solution.py:27
  21.9 3.7 %collective-permute-start.6 = (f32[1,32]{1,0:T(1,128)S(1)}, f32[1,32]{1,0:T(1,128)S(1)}, u32[]{:S(2)}, u32[]{:S(2)}) collective-permute-start(f32[1,32]{1,0:T(1,128)S(1)} %get-tuple-element.28.refs_0_), channel_id=1, source_target_pairs={{0,2},{1,3},{2,0},{3,1},{4,6},{5,7},{6,4},{7,5},{8,10},{9,11},{10,... | collective-permute-start | bytes 392 | tf_op jit(solution)/shard_map/ppermute | solution.py:27
  24.1 1.5 %collective-permute-start.5 = (f32[1,32]{1,0:T(1,128)S(1)}, f32[1,32]{1,0:T(1,128)S(1)}, u32[]{:S(2)}, u32[]{:S(2)}) collective-permute-start(f32[1,32]{1,0:T(1,128)S(1)} %get-tuple-element.28.refs_0_), channel_id=1, source_target_pairs={{0,1},{1,0},{2,3},{3,2},{4,5},{5,4},{6,7},{7,6},{8,9},{9,8},{10,11... | collective-permute-start | bytes 392 | tf_op jit(solution)/shard_map/ppermute | solution.py:27
  29.8 7.1 %copy-start = (bf16[1024,1024]{1,0:T(8,128)(2,1)S(1)}, bf16[1024,1024]{1,0:T(8,128)(2,1)}, u32[]{:S(2)}) copy-start(bf16[1024,1024]{1,0:T(8,128)(2,1)} %encoder.1) | copy-start | bytes 6291460
  29.8 7.1 %collective-permute-start.8 = (bf16[48,1024]{1,0:T(8,128)(2,1)S(1)}, bf16[48,1024]{1,0:T(8,128)(2,1)S(1)}, u32[]{:S(2)}, u32[]{:S(2)}) collective-permute-start(bf16[48,1024]{1,0:T(8,128)(2,1)S(1)} %get-tuple-element.30), channel_id=1, source_target_pairs={{0,8},{1,9},{2,10},{3,11},{4,12},{5,13},{6,14},{7,15},{8,0},{9,1},... | collective-permute-start | bytes 294920 | tf_op jit(solution)/shard_map/ppermute | solution.py:27
  36.4 1.4 %copy-start.3 = (bf16[32,1024]{1,0:T(8,128)(2,1)S(1)}, bf16[32,1024]{1,0:T(8,128)(2,1)}, u32[]{:S(2)}) copy-start(bf16[32,1024]{1,0:T(8,128)(2,1)} %targets_hbm.1) | copy-start | bytes 196612
  46.5 30.9 %all-to-all-start.1 = ((bf16[16,32,1024]{2,1,0:T(8,128)(2,1)}), bf16[16,32,1024]{2,1,0:T(8,128)(2,1)S(1)}, u32[]{:S(2)}, u32[]{:S(2)}) async-start(bf16[16,32,1024]{2,1,0:T(8,128)(2,1)} %get-tuple-element.37), calls=%async_computation.1 | async-start | bytes 2097152 | tf_op jit(solution)/shard_map/all_to_all | solution.py:35
  54.5 18.2 %collective-permute-start.9 = (f32[8,128]{1,0:T(8,128)S(1)}, f32[8,128]{1,0:T(8,128)S(1)}, u32[]{:S(2)}, u32[]{:S(2)}) collective-permute-start(f32[8,128]{1,0:T(8,128)S(1)} %get-tuple-element.38), channel_id=1, source_target_pairs={{0,4},{1,5},{2,6},{3,7},{4,0},{5,1},{6,2},{7,3},{8,12},{9,13},{10,... | collective-permute-start | bytes 12296 | tf_op jit(solution)/shard_map/ppermute | solution.py:27

commit v10 on v9

--- a/solution.py
+++ b/solution.py
@@ -9,7 +9,6 @@
 
 EPSILON = 1e-06
 TOKENS_AT_ONCE = 16
-TAIL = 16
 HIDDEN_PIECES = 2
 ROWS_LIMIT = 53
 NETWORK_LIMIT = 46
@@ -69,56 +68,17 @@
         copy.wait()
 
 
-def blocks_kernel(lanes, owners, *refs):
-    held, (weight, across, keep, give, weight_out) = refs[:lanes], refs[lanes:]
+def planes_kernel(lanes, owners, *refs):
+    held, (weight, across, *outs, weight_out) = refs[:lanes], refs[lanes:]
     weight_out[...] = weight[...] + across[...]
     me = lax.axis_index("member")
     lane, plane = me % lanes, me // lanes
-
-    def rows_of(block):
-        place = (owners[block] % lanes) ^ lane
+    for j, out in enumerate(outs):
+        place = (owners[plane ^ j] % lanes) ^ lane
         rows = held[0][...]
         for k in range(1, lanes):
             rows = jnp.where(place == k, held[k][...], rows)
-        return rows
-
-    side = plane % 2
-    for j in range(keep.shape[0]):
-        keep[j] = rows_of(2 * j + side)
-        give[j] = rows_of(2 * j + 1 - side)
-
-
-def weight_rows(total, features):
-    high = total.astype(BF16).astype(F32)
-    middle = (total - high).astype(BF16).astype(F32)
-    low = total - high - middle
-    row = lax.broadcasted_iota(jnp.int32, (TAIL, features), 0)
-    picked = jnp.where(row == 0, high, jnp.where(row == 1, middle, jnp.where(row == 2, low, 0.0)))
-    return picked.astype(BF16)
-
-
-def weight_from(rows):
-    return jnp.sum(rows[:, 0:128].astype(F32), axis=0, keepdims=True)
-
-
-def merged(lanes, owners, plane, bit, keep, got, j):
-    block = j * (2 * bit) + plane % (2 * bit)
-    there = ((owners[block] // lanes) ^ plane) // bit % 2
-    return jnp.where(there == 1, got[j], keep[j])
-
-
-def halve_kernel(lanes, bit, owners, keep, got, *refs):
-    *weights, keep_out, give, weight_out = refs
-    own, features = keep.shape[1], keep.shape[2]
-    total = jnp.sum(sum((ref[...] for ref in weights[1:]), weights[0][...]), keepdims=True)
-    weight_out[...] = jnp.broadcast_to(total, weight_out.shape)
-    plane = lax.axis_index("member") // lanes
-    side = plane // (2 * bit) % 2
-    rows = [merged(lanes, owners, plane, bit, keep, got, j) for j in range(keep.shape[0])]
-    for j in range(keep_out.shape[0]):
-        keep_out[j] = jnp.where(side == 1, rows[2 * j + 1], rows[2 * j])
-        give[pl.ds(j * own, own), :] = jnp.where(side == 1, rows[2 * j], rows[2 * j + 1])
-    give[pl.ds(keep_out.shape[0] * own, TAIL), :] = weight_rows(total, features)
+        out[...] = rows
 
 
 def fetch_kernel(matrix, after, near, sem):
@@ -127,13 +87,16 @@
     copy.wait()
 
 
-def encode_kernel(lanes, bit, owners, keep, got, encoder, total, latent, total_out):
-    own = latent.shape[0]
+def encode_kernel(lanes, blocks, owners, encoder, *refs):
+    held, (*weights, latent, total_out) = refs[:blocks], refs[blocks:]
     plane = lax.axis_index("member") // lanes
-    rows = [got[pl.ds(0, own), :]]
-    control = merged(lanes, owners, plane, bit, keep, rows, 0)
+    place = (owners[plane] // lanes) ^ plane
+    control = held[0][...]
+    for k in range(1, blocks):
+        control = jnp.where(place == k, held[k][...], control)
     latent[...] = jnp.dot(control, encoder[...], preferred_element_type=F32).astype(BF16)
-    total_out[...] = total[...] + weight_from(got[pl.ds(own, TAIL), :])
+    total = jnp.sum(sum((ref[...] for ref in weights[1:]), weights[0][...]), keepdims=True)
+    total_out[...] = jnp.broadcast_to(total, total_out.shape)
 
 
 def prepared(analyses, owners, encoder, area_weight, matrix, after):
@@ -143,9 +106,6 @@
     lanes, own = members // blocks, rows // members
     row = jax.ShapeDtypeStruct((own, features), BF16)
     line = jax.ShapeDtypeStruct((1, own), F32)
-
-    def kept(many):
-        return jax.ShapeDtypeStruct((many, own, features), BF16)
 
     *by_lane, own_weight = local_call(
         functools.partial(rows_kernel, lanes),
@@ -159,22 +119,16 @@
     for bit in bits_of(regions)[:-1]:
         weight = weight + swap(weight, "region", bit)
     across = swap(weight, "region", regions // 2)
-    keep, give, weight = local_call(
-        functools.partial(blocks_kernel, lanes),
-        [kept(blocks // 2)] * 2 + [line],
+    *by_plane, weight = local_call(
+        functools.partial(planes_kernel, lanes),
+        [row] * blocks + [line],
         [SMEM] + [VMEM] * (lanes + 2),
         limit=8,
     )(owners, *by_lane, weight, across)
+    by_plane = [by_plane[0]] + [
+        swap(by_plane[k], "member", k * lanes) for k in range(1, blocks)
+    ]
     weights = [weight] + [swap(weight, "member", k) for k in range(1, lanes)]
-    got = swap(give, "member", lanes)
-    small = jax.ShapeDtypeStruct((8, 128), F32)
-    keep, give, total = local_call(
-        functools.partial(halve_kernel, lanes, 1),
-        [kept(1), jax.ShapeDtypeStruct((own + TAIL, features), BF16), small],
-        [SMEM] + [VMEM] * (2 + len(weights)),
-        limit=8,
-    )(owners, keep, got, *weights)
-    got = swap(give, "member", 2 * lanes)
     (near,) = local_call(
         fetch_kernel,
         [jax.ShapeDtypeStruct(matrix.shape, BF16)],
@@ -183,14 +137,14 @@
         scratch=[pltpu.SemaphoreType.DMA],
         limit=FETCH_LIMIT,
     )(matrix, after)
-    got, near = lax.optimization_barrier((got, near))
+    near, *by_plane = lax.optimization_barrier((near, *by_plane))
     latent, total = local_call(
-        functools.partial(encode_kernel, lanes, 2),
-        [row, small],
-        [SMEM] + [VMEM] * 4,
+        functools.partial(encode_kernel, lanes, blocks),
+        [row, jax.ShapeDtypeStruct((8, 128), F32)],
+        [SMEM] + [VMEM] * (1 + blocks + lanes),
         flops=2 * own * features * features,
         limit=8,
-    )(owners, keep, got, encoder, total)
+    )(owners, encoder, *by_plane, *weights)
     return latent, own_weight, total, near
 
 
@@ -331,8 +285,11 @@
     )(here, latent, weight, inlet, targets, sample_outlet_matrix)
     gradient, total = lax.optimization_barrier((gradient, total))
     back = transposed(gradient)
-    across = swap(total, "member", members // owners.shape[0])
-    factor = float(region_rows * regions) / (total[0, 0] + across[0, 0])
+    lanes = members // owners.shape[0]
+    total = sum(
+        (swap(total, "member", k * lanes) for k in range(1, owners.shape[0])), total
+    )
+    factor = float(region_rows * regions) / total[0, 0]
     member_grad = (back.astype(F32) * factor).astype(BF16).reshape(1, region_rows, features)
     return member_grad, energy[:, 0] * factor
 

time: 80.1 us -> 84.7 us (1.057); the launches traced: 78.6 us -> 84.4 us
  waiting for transfers between devices: 30.4 us -> 37.7 us
    ppermute x10 -> x13, waiting for transfers between devices: 28.1 us -> 34.8 us  [swap(): return lax.ppermute(value, axis, [(i, i ^ bit) for i in range(size)])]
    all_to_all x2, starting transfers between devices: 15.5 us -> 12.8 us  [transposed(): lax.all_to_all(value, 'member', split_axis=0, concat_axis=0, tiled=True)]
    ppermute x10 -> x13, starting transfers between devices: 13.2 us -> 15.4 us  [swap(): return lax.ppermute(value, axis, [(i, i ^ bit) for i in range(size)])]
    pallas_call x3 -> x2, Pallas kernels: 2.28 us -> 2.24 us  [the longest x1 1.22 us: prepared(): local_call(functools.partial(planes_kernel, lanes), [row] * blocks + [lin...]
  transfers between devices with their start and end apart: 12 -> 15, of which waited for: 8 -> 7; matrix products, arithmetic and copies ran while one was open for 2% -> 1% of each run, Pallas kernels for 6% -> 6%
where the time goes in v10:
time: 84.7 us; the launch traced here: 84.4 us
  waiting for transfers between devices  37.7 us (45%)
  starting transfers between devices  28.2 us (33%)
  Pallas kernels  14.6 us (17%)
  other arithmetic  1.81 us (2%)
  between operations  1.45 us (2%)
    ppermute x13, waiting for transfers between devices, swap(): return lax.ppermute(value, axis, [(i, i ^ bit) for i in range(size)])  34.8 us
    ppermute x13, starting transfers between devices, swap(): return lax.ppermute(value, axis, [(i, i ^ bit) for i in range(size)])  15.4 us
    all_to_all x2, starting transfers between devices, transposed(): lax.all_to_all(value, 'member', split_axis=0, concat_axis=0, tiled=True)  12.8 us
    pallas_call x1, Pallas kernels, on_device(): local_call(member_kernel, [jax.ShapeDtypeStruct((members, own, features),...  8.68 us
    all_to_all x2, waiting for transfers between devices, transposed(): lax.all_to_all(value, 'member', split_axis=0, concat_axis=0, tiled=True)  2.9 us
    pallas_call x1, Pallas kernels, prepared(): local_call(fetch_kernel, [jax.ShapeDtypeStruct(matrix.shape, BF16)], [HBM...  2.2 us
  transfers between devices with their start and end apart: 15, of which 7 were waited for; matrix products, arithmetic and copies ran while one was open for 1% of the time, Pallas kernels for 6%

profile of v10, /device:TPU:0, one launch (start us, length us, event | category | flops | bytes accessed | tf_op | source)
XLA Modules:
  0.0 84.4 jit_solution(17481988275723082856)
XLA Ops:
  0.6 0.0 copy-start.1
  0.6 0.0 copy-start.2
  0.6 7.5 %all-to-all-start = ((bf16[16,32,1024]{2,1,0:T(8,128)(2,1)}), bf16[16,32,1024]{2,1,0:T(8,128)(2,1)S(1)}, u32[]{:S(2)}, u32[]{:S(2)}) async-start(bf16[16,32,1024]{2,1,0:T(8,128)(2,1)} %bitcast.6), calls=%async_computation | async-start | bytes 2097152 | tf_op jit(solution)/shard_map/all_to_all | solution.py:34
  8.2 0.0 copy-done.1
  8.2 0.0 copy-done.2
  8.2 1.5 %shard_map.96 = (bf16[32,1024]{1,0:T(8,128)(2,1)S(1)}, bf16[32,1024]{1,0:T(8,128)(2,1)S(1)}, bf16[32,1024]{1,0:T(8,128)(2,1)S(1)}, bf16[32,1024]{1,0:T(8,128)(2,1)S(1)}, f32[1,32]{1,0:T(1,128)S(1)}) custom-call(s32[4]{0:T(128)S(1)} %copy-done.1, bf16[1,512,1024]{2,1,0:T(8,128)(2,1)} %analyses.1, f32[1,32]{1,0:T(1,128)S(1)} %bitcast.4), custom_call_target="tpu_custom_call" | custom-call | tf_op jit(solution)/shard_map/pallas_call | solution.py:110
  9.8 0.5 collective-permute-start
  10.2 1.7 %collective-permute-start.1 = (bf16[32,1024]{1,0:T(8,128)(2,1)S(1)}, bf16[32,1024]{1,0:T(8,128)(2,1)S(1)}, u32[]{:S(2)}, u32[]{:S(2)}) collective-permute-start(bf16[32,1024]{1,0:T(8,128)(2,1)S(1)} %get-tuple-element.25), channel_id=1, source_target_pairs={{0,2},{1,3},{2,0},{3,1},{4,6},{5,7},{6,4},{7,5},{8,10},{9,11},{10,... | collective-permute-start | bytes 196616 | tf_op jit(solution)/shard_map/ppermute | solution.py:26
  11.9 0.0 collective-permute-start.2
  11.9 1.5 %collective-permute-start.3 = (f32[1,32]{1,0:T(1,128)S(1)}, f32[1,32]{1,0:T(1,128)S(1)}, u32[]{:S(2)}, u32[]{:S(2)}) collective-permute-start(f32[1,32]{1,0:T(1,128)S(1)} %get-tuple-element.27.refs_4_.weight), channel_id=1, source_target_pairs={{0,16},{16,0},{1,17},{17,1},{2,18},{18,2},{3,19},{19,3},{4,20},{20... | collective-permute-start | bytes 392 | tf_op jit(solution)/shard_map/ppermute | solution.py:26
  13.4 2.0 %collective-permute-done.3.refs_5_ = f32[1,32]{1,0:T(1,128)S(1)} collective-permute-done((f32[1,32]{1,0:T(1,128)S(1)}, f32[1,32]{1,0:T(1,128)S(1)}, u32[]{:S(2)}, u32[]{:S(2)}) %collective-permute-start.3) | collective-permute-done | bytes 160 | tf_op jit(solution)/shard_map/ppermute | solution.py:26
  15.4 0.0 collective-permute-done.refs_1_
  15.5 4.3 %collective-permute-done.1.refs_2_ = bf16[32,1024]{1,0:T(8,128)(2,1)S(1)} collective-permute-done((bf16[32,1024]{1,0:T(8,128)(2,1)S(1)}, bf16[32,1024]{1,0:T(8,128)(2,1)S(1)}, u32[]{:S(2)}, u32[]{:S(2)}) %collective-permute-start.1) | collective-permute-done | bytes 65568 | tf_op jit(solution)/shard_map/ppermute | solution.py:26
  19.8 0.6 collective-permute-done.2.refs_3_
  20.4 1.2 %shard_map.97 = (bf16[32,1024]{1,0:T(8,128)(2,1)S(1)}, bf16[32,1024]{1,0:T(8,128)(2,1)}, bf16[32,1024]{1,0:T(8,128)(2,1)}, bf16[32,1024]{1,0:T(8,128)(2,1)S(1)}, f32[1,32]{1,0:T(1,128)S(1)}) custom-call(s32[4]{0:T(128)S(1)} %copy-done.1, bf16[32,1024]{1,0:T(8,128)(2,1)S(1)} %get-tuple-element.23.refs_0_, bf16[32,1024]{1,0:T(8,128)(2,1)S(1)} %collective-permute-done.refs_1_, ...), custom_call_target="tpu_custom_call" | custom-call | tf_op jit(solution)/shard_map/pallas_call | solution.py:122
  21.6 0.0 collective-permute-start.4
  21.6 4.5 %collective-permute-start.5 = (bf16[32,1024]{1,0:T(8,128)(2,1)}, bf16[32,1024]{1,0:T(8,128)(2,1)S(1)}, u32[]{:S(2)}, u32[]{:S(2)}) collective-permute-start(bf16[32,1024]{1,0:T(8,128)(2,1)} %get-tuple-element.30), channel_id=1, source_target_pairs={{0,8},{1,9},{2,10},{3,11},{4,12},{5,13},{6,14},{7,15},{8,0},{9,1},... | collective-permute-start | bytes 196616 | tf_op jit(solution)/shard_map/ppermute | solution.py:26
  26.1 0.0 collective-permute-start.6
  26.1 0.0 copy-start
  26.1 0.2 collective-permute-start.9
  26.3 2.3 %collective-permute-start.8 = (f32[1,32]{1,0:T(1,128)S(1)}, f32[1,32]{1,0:T(1,128)S(1)}, u32[]{:S(2)}, u32[]{:S(2)}) collective-permute-start(f32[1,32]{1,0:T(1,128)S(1)} %get-tuple-element.36.refs_4_), channel_id=1, source_target_pairs={{0,2},{1,3},{2,0},{3,1},{4,6},{5,7},{6,4},{7,5},{8,10},{9,11},{10,... | collective-permute-start | bytes 392 | tf_op jit(solution)/shard_map/ppermute | solution.py:26
  28.6 2.9 %all-to-all-done.after.noise = bf16[16,32,1024]{2,1,0:T(8,128)(2,1)S(1)} async-done(((bf16[16,32,1024]{2,1,0:T(8,128)(2,1)}), bf16[16,32,1024]{2,1,0:T(8,128)(2,1)S(1)}, u32[]{:S(2)}, u32[]{:S(2)}) %all-to-all-start) | async-done | bytes 1048608 | tf_op jit(solution)/shard_map/all_to_all | solution.py:34
  31.5 2.2 %shard_map.95.inlet = bf16[1024,2048]{1,0:T(8,128)(2,1)S(1)} custom-call(bf16[1024,2048]{1,0:T(8,128)(2,1)} %matrix.1, bf16[16,32,1024]{2,1,0:T(8,128)(2,1)S(1)} %all-to-all-done.after.noise), custom_call_target="tpu_custom_call" | custom-call | bytes 4194304 | tf_op jit(solution)/shard_map/pallas_call | solution.py:132
  33.7 0.0 copy-start.3
  33.7 0.0 collective-permute-done.4.refs_1_
  33.7 0.3 collective-permute-start.7
  34.0 5.4 %collective-permute-done.5.refs_2_ = bf16[32,1024]{1,0:T(8,128)(2,1)S(1)} collective-permute-done((bf16[32,1024]{1,0:T(8,128)(2,1)}, bf16[32,1024]{1,0:T(8,128)(2,1)S(1)}, u32[]{:S(2)}, u32[]{:S(2)}) %collective-permute-start.5) | collective-permute-done | bytes 65568 | tf_op jit(solution)/shard_map/ppermute | solution.py:26
  39.4 0.0 collective-permute-done.6.refs_3_
  39.4 0.0 collective-permute-done.9.refs_7_
  39.4 0.0 collective-permute-done.8.refs_6_
  39.4 0.0 collective-permute-done.7.refs_5_
  39.4 0.0 copy-done
  39.5 1.0 %shard_map.98 = (bf16[32,1024]{1,0:T(8,128)(2,1)S(1)}, f32[8,128]{1,0:T(8,128)S(1)}) custom-call(s32[4]{0:T(128)S(1)} %copy-done.1, bf16[1024,1024]{1,0:T(8,128)(2,1)S(1)} %copy-done, bf16[32,1024]{1,0:T(8,128)(2,1)S(1)} %get-tuple-element.32.refs_0_, bf16[32,1024]{1,0:T(8,128)(2,1)S(1)} %collective-permute-done.4.refs_1_, ...), custom_call_target="tpu_custom_call" | custom-call | flops 67108864 | tf_op jit(solution)/shard_map/pallas_call | solution.py:141
  40.5 0.0 copy-done.3
  40.5 8.7 %shard_map.99 = (bf16[16,32,1024]{2,1,0:T(8,128)(2,1)}, f32[32,1]{1,0:T(8,128)S(1)}) custom-call(bf16[16,32,1024]{2,1,0:T(8,128)(2,1)S(1)} %all-to-all-done.after.noise, bf16[32,1024]{1,0:T(8,128)(2,1)S(1)} %get-tuple-element.37.latent, f32[1,32]{1,0:T(1,128)S(1)} %get-tuple-element.27.refs_4_.weight, bf16[1024,2048]{1,0:T(8,128)(2,1)S(1)} %shard_map.95.inlet, ...), custom_call_target="tpu_custom_call" | custom-call | flops 4328521728 | bytes 8388608 | tf_op jit(solution)/shard_map/pallas_call | solution.py:269
  49.2 5.3 %all-to-all-start.1 = ((bf16[16,32,1024]{2,1,0:T(8,128)(2,1)}), bf16[16,32,1024]{2,1,0:T(8,128)(2,1)S(1)}, u32[]{:S(2)}, u32[]{:S(2)}) async-start(bf16[16,32,1024]{2,1,0:T(8,128)(2,1)} %get-tuple-element.41), calls=%async_computation.1 | async-start | bytes 2097152 | tf_op jit(solution)/shard_map/all_to_all | solution.py:34
  54.4 3.7 %collective-permute-start.12 = (f32[8,128]{1,0:T(8,128)S(1)}, f32[8,128]{1,0:T(8,128)S(1)}, u32[]{:S(2)}, u32[]{:S(2)}) collective-permute-start(f32[8,128]{1,0:T(8,128)S(1)} %get-tuple-element.42), channel_id=1, source_target_pairs={{0,12},{1,13},{2,14},{3,15},{4,8},{5,9},{6,10},{7,11},{8,4},{9,5},... | collective-permute-start | bytes 12296 | tf_op jit(solution)/shard_map/ppermute | solution.py:26
  58.2 0.0 collective-permute-start.11
  58.2 0.7 collective-permute-start.10
  58.9 17.7 %collective-permute-done.12 = f32[8,128]{1,0:T(8,128)S(1)} collective-permute-done((f32[8,128]{1,0:T(8,128)S(1)}, f32[8,128]{1,0:T(8,128)S(1)}, u32[]{:S(2)}, u32[]{:S(2)}) %collective-permute-start.12) | collective-permute-done | bytes 4128 | tf_op jit(solution)/shard_map/ppermute | solution.py:26
  76.6 4.7 %collective-permute-done.11 = f32[8,128]{1,0:T(8,128)S(1)} collective-permute-done((f32[8,128]{1,0:T(8,128)S(1)}, f32[8,128]{1,0:T(8,128)S(1)}, u32[]{:S(2)}, u32[]{:S(2)}) %collective-permute-start.11) | collective-permute-done | bytes 4128 | tf_op jit(solution)/shard_map/ppermute | solution.py:26
  81.3 0.0 collective-permute-done.10
  81.3 0.5 slice.3
  82.6 0.6 multiply_reduce_fusion
  83.2 0.0 all-to-all-done.1
  83.2 1.2 %multiply_convert_fusion = bf16[16,32,1024]{2,1,0:T(8,128)(2,1)} fusion(bf16[16,32,1024]{2,1,0:T(8,128)(2,1)S(1)} %all-to-all-done.1, f32[]{:T(128)} %bitcast.2), kind=kLoop, calls=%fused_computation | loop fusion | flops 1572864 | bytes 2097156 | tf_op jit(solution)/shard_map/convert_element_type | solution.py:293
  (1 shorter events, 0.0 us)
Async XLA Ops:
  0.6 7.6 %copy-start.1 = (s32[4]{0:T(128)S(1)}, s32[4]{0:T(128)}, u32[]{:S(2)}) copy-start(s32[4]{0:T(128)} %owners.5) | copy-start | bytes 52
  0.6 7.6 %copy-start.2 = (f32[32]{0:T(128)S(1)}, f32[32]{0:T(128)}, u32[]{:S(2)}) copy-start(f32[32]{0:T(128)} %param.12) | copy-start | bytes 388
  0.6 30.9 %all-to-all-start = ((bf16[16,32,1024]{2,1,0:T(8,128)(2,1)}), bf16[16,32,1024]{2,1,0:T(8,128)(2,1)S(1)}, u32[]{:S(2)}, u32[]{:S(2)}) async-start(bf16[16,32,1024]{2,1,0:T(8,128)(2,1)} %bitcast.6), calls=%async_computation | async-start | bytes 2097152 | tf_op jit(solution)/shard_map/all_to_all | solution.py:34
  9.8 5.7 %collective-permute-start = (bf16[32,1024]{1,0:T(8,128)(2,1)S(1)}, bf16[32,1024]{1,0:T(8,128)(2,1)S(1)}, u32[]{:S(2)}, u32[]{:S(2)}) collective-permute-start(bf16[32,1024]{1,0:T(8,128)(2,1)S(1)} %get-tuple-element.24), channel_id=1, source_target_pairs={{0,1},{1,0},{2,3},{3,2},{4,5},{5,4},{6,7},{7,6},{8,9},{9,8},{10,11... | collective-permute-start | bytes 196616 | tf_op jit(solution)/shard_map/ppermute | solution.py:26
  10.2 9.6 %collective-permute-start.1 = (bf16[32,1024]{1,0:T(8,128)(2,1)S(1)}, bf16[32,1024]{1,0:T(8,128)(2,1)S(1)}, u32[]{:S(2)}, u32[]{:S(2)}) collective-permute-start(bf16[32,1024]{1,0:T(8,128)(2,1)S(1)} %get-tuple-element.25), channel_id=1, source_target_pairs={{0,2},{1,3},{2,0},{3,1},{4,6},{5,7},{6,4},{7,5},{8,10},{9,11},{10,... | collective-permute-start | bytes 196616 | tf_op jit(solution)/shard_map/ppermute | solution.py:26
  11.9 8.5 %collective-permute-start.2 = (bf16[32,1024]{1,0:T(8,128)(2,1)S(1)}, bf16[32,1024]{1,0:T(8,128)(2,1)S(1)}, u32[]{:S(2)}, u32[]{:S(2)}) collective-permute-start(bf16[32,1024]{1,0:T(8,128)(2,1)S(1)} %get-tuple-element.26), channel_id=1, source_target_pairs={{0,3},{1,2},{2,1},{3,0},{4,7},{5,6},{6,5},{7,4},{8,11},{9,10},{10,... | collective-permute-start | bytes 196616 | tf_op jit(solution)/shard_map/ppermute | solution.py:26
  11.9 3.5 %collective-permute-start.3 = (f32[1,32]{1,0:T(1,128)S(1)}, f32[1,32]{1,0:T(1,128)S(1)}, u32[]{:S(2)}, u32[]{:S(2)}) collective-permute-start(f32[1,32]{1,0:T(1,128)S(1)} %get-tuple-element.27.refs_4_.weight), channel_id=1, source_target_pairs={{0,16},{16,0},{1,17},{17,1},{2,18},{18,2},{3,19},{19,3},{4,20},{20... | collective-permute-start | bytes 392 | tf_op jit(solution)/shard_map/ppermute | solution.py:26
  21.6 12.1 %collective-permute-start.4 = (bf16[32,1024]{1,0:T(8,128)(2,1)}, bf16[32,1024]{1,0:T(8,128)(2,1)S(1)}, u32[]{:S(2)}, u32[]{:S(2)}) collective-permute-start(bf16[32,1024]{1,0:T(8,128)(2,1)} %get-tuple-element.29), channel_id=1, source_target_pairs={{0,4},{1,5},{2,6},{3,7},{4,0},{5,1},{6,2},{7,3},{8,12},{9,13},{10,... | collective-permute-start | bytes 196616 | tf_op jit(solution)/shard_map/ppermute | solution.py:26
  21.6 17.8 %collective-permute-start.5 = (bf16[32,1024]{1,0:T(8,128)(2,1)}, bf16[32,1024]{1,0:T(8,128)(2,1)S(1)}, u32[]{:S(2)}, u32[]{:S(2)}) collective-permute-start(bf16[32,1024]{1,0:T(8,128)(2,1)} %get-tuple-element.30), channel_id=1, source_target_pairs={{0,8},{1,9},{2,10},{3,11},{4,12},{5,13},{6,14},{7,15},{8,0},{9,1},... | collective-permute-start | bytes 196616 | tf_op jit(solution)/shard_map/ppermute | solution.py:26
  26.1 13.3 %collective-permute-start.6 = (bf16[32,1024]{1,0:T(8,128)(2,1)S(1)}, bf16[32,1024]{1,0:T(8,128)(2,1)S(1)}, u32[]{:S(2)}, u32[]{:S(2)}) collective-permute-start(bf16[32,1024]{1,0:T(8,128)(2,1)S(1)} %get-tuple-element.31), channel_id=1, source_target_pairs={{0,12},{1,13},{2,14},{3,15},{4,8},{5,9},{6,10},{7,11},{8,4},{9,5},... | collective-permute-start | bytes 196616 | tf_op jit(solution)/shard_map/ppermute | solution.py:26
  26.1 13.3 %copy-start = (bf16[1024,1024]{1,0:T(8,128)(2,1)S(1)}, bf16[1024,1024]{1,0:T(8,128)(2,1)}, u32[]{:S(2)}) copy-start(bf16[1024,1024]{1,0:T(8,128)(2,1)} %encoder.1) | copy-start | bytes 6291460
  26.1 13.3 %collective-permute-start.9 = (f32[1,32]{1,0:T(1,128)S(1)}, f32[1,32]{1,0:T(1,128)S(1)}, u32[]{:S(2)}, u32[]{:S(2)}) collective-permute-start(f32[1,32]{1,0:T(1,128)S(1)} %get-tuple-element.36.refs_4_), channel_id=1, source_target_pairs={{0,3},{1,2},{2,1},{3,0},{4,7},{5,6},{6,5},{7,4},{8,11},{9,10},{10,... | collective-permute-start | bytes 392 | tf_op jit(solution)/shard_map/ppermute | solution.py:26
  26.3 13.1 %collective-permute-start.8 = (f32[1,32]{1,0:T(1,128)S(1)}, f32[1,32]{1,0:T(1,128)S(1)}, u32[]{:S(2)}, u32[]{:S(2)}) collective-permute-start(f32[1,32]{1,0:T(1,128)S(1)} %get-tuple-element.36.refs_4_), channel_id=1, source_target_pairs={{0,2},{1,3},{2,0},{3,1},{4,6},{5,7},{6,4},{7,5},{8,10},{9,11},{10,... | collective-permute-start | bytes 392 | tf_op jit(solution)/shard_map/ppermute | solution.py:26
  33.7 6.8 %copy-start.3 = (bf16[32,1024]{1,0:T(8,128)(2,1)S(1)}, bf16[32,1024]{1,0:T(8,128)(2,1)}, u32[]{:S(2)}) copy-start(bf16[32,1024]{1,0:T(8,128)(2,1)} %targets_hbm.1) | copy-start | bytes 196612
  33.7 5.7 %collective-permute-start.7 = (f32[1,32]{1,0:T(1,128)S(1)}, f32[1,32]{1,0:T(1,128)S(1)}, u32[]{:S(2)}, u32[]{:S(2)}) collective-permute-start(f32[1,32]{1,0:T(1,128)S(1)} %get-tuple-element.36.refs_4_), channel_id=1, source_target_pairs={{0,1},{1,0},{2,3},{3,2},{4,5},{5,4},{6,7},{7,6},{8,9},{9,8},{10,11... | collective-permute-start | bytes 392 | tf_op jit(solution)/shard_map/ppermute | solution.py:26
  49.2 34.0 %all-to-all-start.1 = ((bf16[16,32,1024]{2,1,0:T(8,128)(2,1)}), bf16[16,32,1024]{2,1,0:T(8,128)(2,1)S(1)}, u32[]{:S(2)}, u32[]{:S(2)}) async-start(bf16[16,32,1024]{2,1,0:T(8,128)(2,1)} %get-tuple-element.41), calls=%async_computation.1 | async-start | bytes 2097152 | tf_op jit(solution)/shard_map/all_to_all | solution.py:34
  54.4 22.2 %collective-permute-start.12 = (f32[8,128]{1,0:T(8,128)S(1)}, f32[8,128]{1,0:T(8,128)S(1)}, u32[]{:S(2)}, u32[]{:S(2)}) collective-permute-start(f32[8,128]{1,0:T(8,128)S(1)} %get-tuple-element.42), channel_id=1, source_target_pairs={{0,12},{1,13},{2,14},{3,15},{4,8},{5,9},{6,10},{7,11},{8,4},{9,5},... | collective-permute-start | bytes 12296 | tf_op jit(solution)/shard_map/ppermute | solution.py:26
  58.2 23.2 %collective-permute-start.11 = (f32[8,128]{1,0:T(8,128)S(1)}, f32[8,128]{1,0:T(8,128)S(1)}, u32[]{:S(2)}, u32[]{:S(2)}) collective-permute-start(f32[8,128]{1,0:T(8,128)S(1)} %get-tuple-element.42), channel_id=1, source_target_pairs={{0,8},{1,9},{2,10},{3,11},{4,12},{5,13},{6,14},{7,15},{8,0},{9,1},... | collective-permute-start | bytes 12296 | tf_op jit(solution)/shard_map/ppermute | solution.py:26
  58.2 23.2 %collective-permute-start.10 = (f32[8,128]{1,0:T(8,128)S(1)}, f32[8,128]{1,0:T(8,128)S(1)}, u32[]{:S(2)}, u32[]{:S(2)}) collective-permute-start(f32[8,128]{1,0:T(8,128)S(1)} %get-tuple-element.42), channel_id=1, source_target_pairs={{0,4},{1,5},{2,6},{3,7},{4,0},{5,1},{6,2},{7,3},{8,12},{9,13},{10,... | collective-permute-start | bytes 12296 | tf_op jit(solution)/shard_map/ppermute | solution.py:26

commit v11 on v9

--- a/solution.py
+++ b/solution.py
@@ -12,8 +12,8 @@
 TAIL = 16
 HIDDEN_PIECES = 2
 ROWS_LIMIT = 53
-NETWORK_LIMIT = 46
-FETCH_LIMIT = 46
+NETWORK_LIMIT = 42
+FETCH_LIMIT = 44
 BF16 = jnp.bfloat16
 F32 = jnp.float32
 
@@ -35,11 +35,13 @@
     return lax.all_to_all(value, "member", split_axis=0, concat_axis=0, tiled=True)
 
 
-def local_call(kernel, out_shape, in_specs, flops=0, moved=0, scratch=(), limit=40):
+def local_call(
+    kernel, out_shape, in_specs, flops=0, moved=0, scratch=(), limit=40, out_specs=None
+):
     return pl.pallas_call(
         kernel,
         in_specs=in_specs,
-        out_specs=[VMEM] * len(out_shape),
+        out_specs=out_specs or [VMEM] * len(out_shape),
         out_shape=out_shape,
         scratch_shapes=list(scratch),
         compiler_params=pltpu.CompilerParams(vmem_limit_bytes=limit * 2**20),
@@ -121,22 +123,19 @@
     give[pl.ds(keep_out.shape[0] * own, TAIL), :] = weight_rows(total, features)
 
 
-def fetch_kernel(matrix, after, near, sem):
-    copy = pltpu.make_async_copy(matrix, near, sem)
-    copy.start()
-    copy.wait()
-
-
-def encode_kernel(lanes, bit, owners, keep, got, encoder, total, latent, total_out):
-    own = latent.shape[0]
-    plane = lax.axis_index("member") // lanes
-    rows = [got[pl.ds(0, own), :]]
-    control = merged(lanes, owners, plane, bit, keep, rows, 0)
-    latent[...] = jnp.dot(control, encoder[...], preferred_element_type=F32).astype(BF16)
-    total_out[...] = total[...] + weight_from(got[pl.ds(own, TAIL), :])
-
-
-def prepared(analyses, owners, encoder, area_weight, matrix, after):
+def fetch_kernel(inlet, outlet, after, inlet_near, outlet_near, sems):
+    rows = pl.ds(0, outlet_near.shape[0])
+    copies = [
+        pltpu.make_async_copy(inlet, inlet_near, sems.at[0]),
+        pltpu.make_async_copy(outlet.at[rows, :], outlet_near, sems.at[1]),
+    ]
+    for copy in copies:
+        copy.start()
+    for copy in copies:
+        copy.wait()
+
+
+def prepared(analyses, owners, area_weight, inlet, outlet, after):
     members, regions = lax.axis_size("member"), lax.axis_size("region")
     _, rows, features = analyses.shape
     blocks = owners.shape[0]
@@ -175,23 +174,19 @@
         limit=8,
     )(owners, keep, got, *weights)
     got = swap(give, "member", 2 * lanes)
-    (near,) = local_call(
+    near = local_call(
         fetch_kernel,
-        [jax.ShapeDtypeStruct(matrix.shape, BF16)],
-        [HBM, VMEM],
-        moved=2 * matrix.size,
-        scratch=[pltpu.SemaphoreType.DMA],
+        [
+            jax.ShapeDtypeStruct(inlet.shape, BF16),
+            jax.ShapeDtypeStruct((outlet.shape[0] // HIDDEN_PIECES, features), BF16),
+        ],
+        [HBM, HBM, VMEM],
+        moved=3 * inlet.size,
+        scratch=[pltpu.SemaphoreType.DMA((2,))],
         limit=FETCH_LIMIT,
-    )(matrix, after)
-    got, near = lax.optimization_barrier((got, near))
-    latent, total = local_call(
-        functools.partial(encode_kernel, lanes, 2),
-        [row, small],
-        [SMEM] + [VMEM] * 4,
-        flops=2 * own * features * features,
-        limit=8,
-    )(owners, keep, got, encoder, total)
-    return latent, own_weight, total, near
+    )(inlet, outlet, after)
+    got, *near = lax.optimization_barrier((got, *near))
+    return keep, got, own_weight, total, *near
 
 
 def column(row):
@@ -245,42 +240,64 @@
 
 
 def member_kernel(
+    lanes,
+    bit,
+    owners,
+    keep,
+    got,
+    encoder,
+    weight,
+    total,
     noise,
-    latent,
-    weight,
     inlet,
+    outlet_near,
     targets_hbm,
     outlet_hbm,
-    gradient_out,
+    gradient_hbm,
     energy_out,
+    total_out,
     targets,
     outlet,
     hidden,
+    gradient_near,
     sems,
+    out_sems,
 ):
     members, own, features = noise.shape
     width = inlet.shape[1] // HIDDEN_PIECES
-    copies = [pltpu.make_async_copy(targets_hbm, targets, sems.at[HIDDEN_PIECES])]
-    for piece in range(HIDDEN_PIECES):
-        rows = pl.ds(piece * width, width)
+    copies = [pltpu.make_async_copy(targets_hbm, targets, sems.at[0])]
+    for piece in range(1, HIDDEN_PIECES):
         copies.append(
-            pltpu.make_async_copy(outlet_hbm.at[rows, :], outlet.at[rows, :], sems.at[piece])
+            pltpu.make_async_copy(
+                outlet_hbm.at[pl.ds(piece * width, width), :],
+                outlet.at[pl.ds((piece - 1) * width, width), :],
+                sems.at[piece],
+            )
         )
     for copy in copies:
         copy.start()
 
     def hidden_piece(normed, piece):
-        rows = slice(piece * width, (piece + 1) * width)
+        columns = slice(piece * width, (piece + 1) * width)
         hidden[...] = jax.nn.gelu(
-            jnp.dot(normed, inlet[:, rows], preferred_element_type=F32), approximate=True
+            jnp.dot(normed, inlet[:, columns], preferred_element_type=F32), approximate=True
         ).astype(BF16)
-        copies[piece + 1].wait()
-        return jnp.dot(hidden[...], outlet[rows, :], preferred_element_type=F32)
-
-    forecast = network(noise[...], latent[...], hidden_piece, HIDDEN_PIECES)
+        if piece == 0:
+            matrix = outlet_near[...]
+        else:
+            copies[piece].wait()
+            matrix = outlet[(piece - 1) * width : piece * width, :]
+        return jnp.dot(hidden[...], matrix, preferred_element_type=F32)
+
+    plane = lax.axis_index("member") // lanes
+    control = merged(lanes, owners, plane, bit, keep, [got[pl.ds(0, own), :]], 0)
+    latent = jnp.dot(control, encoder[...], preferred_element_type=F32).astype(BF16)
+    total_out[...] = total[...] + weight_from(got[pl.ds(own, TAIL), :])
+    forecast = network(noise[...], latent, hidden_piece, HIDDEN_PIECES)
     forecast = forecast.reshape(members, own, features)
     copies[0].wait()
     scales = column(weight[...])
+    returns = []
     for first in range(0, own, TOKENS_AT_ONCE):
         here = slice(first, first + TOKENS_AT_ONCE)
         gradient, energy = score(
@@ -290,8 +307,19 @@
             members,
             TOKENS_AT_ONCE,
         )
-        gradient_out[:, here, :] = gradient.astype(BF16)
+        gradient_near[:, here, :] = gradient.astype(BF16)
         energy_out[here, :] = energy
+        tokens = pl.ds(first, TOKENS_AT_ONCE)
+        returns.append(
+            pltpu.make_async_copy(
+                gradient_near.at[:, tokens, :],
+                gradient_hbm.at[:, tokens, :],
+                out_sems.at[len(returns)],
+            )
+        )
+        returns[-1].start()
+    for copy in returns:
+        copy.wait()
 
 
 def on_device(
@@ -309,29 +337,46 @@
     hidden = sample_inlet_matrix.shape[1]
     own = region_rows // members
     here = transposed(noise.reshape(members, own, features))
-    latent, weight, total, inlet = prepared(
-        analyses, owners, enc_weight, area_weight, sample_inlet_matrix, here
-    )
-    gradient, energy = local_call(
-        member_kernel,
+    keep, got, weight, total, inlet, outlet_near = prepared(
+        analyses, owners, area_weight, sample_inlet_matrix, sample_outlet_matrix, here
+    )
+    lanes = members // owners.shape[0]
+    gradient, energy, total = local_call(
+        functools.partial(member_kernel, lanes, owners.shape[0] // 2),
         [
             jax.ShapeDtypeStruct((members, own, features), BF16),
             jax.ShapeDtypeStruct((own, 1), F32),
+            jax.ShapeDtypeStruct((8, 128), F32),
         ],
-        [VMEM] * 4 + [HBM] * 2,
+        [SMEM] + [VMEM] * 8 + [HBM] * 2,
         flops=4 * members * own * features * (hidden + members),
         moved=4 * features * hidden,
         scratch=[
             pltpu.VMEM((own, features), BF16),
-            pltpu.VMEM((hidden, features), BF16),
+            pltpu.VMEM((hidden - hidden // HIDDEN_PIECES, features), BF16),
             pltpu.VMEM((members * own, hidden // HIDDEN_PIECES), BF16),
-            pltpu.SemaphoreType.DMA((HIDDEN_PIECES + 1,)),
+            pltpu.VMEM((members, own, features), BF16),
+            pltpu.SemaphoreType.DMA((HIDDEN_PIECES,)),
+            pltpu.SemaphoreType.DMA((own // TOKENS_AT_ONCE,)),
         ],
         limit=NETWORK_LIMIT,
-    )(here, latent, weight, inlet, targets, sample_outlet_matrix)
+        out_specs=[HBM, VMEM, VMEM],
+    )(
+        owners,
+        keep,
+        got,
+        enc_weight,
+        weight,
+        total,
+        here,
+        inlet,
+        outlet_near,
+        targets,
+        sample_outlet_matrix,
+    )
     gradient, total = lax.optimization_barrier((gradient, total))
     back = transposed(gradient)
-    across = swap(total, "member", members // owners.shape[0])
+    across = swap(total, "member", lanes)
     factor = float(region_rows * regions) / (total[0, 0] + across[0, 0])
     member_grad = (back.astype(F32) * factor).astype(BF16).reshape(1, region_rows, features)
     return member_grad, energy[:, 0] * factor

time: 80.1 us -> 80.6 us (level)
  Pallas kernels: 14.7 us -> 15.8 us
    pallas_call x3 -> x2, Pallas kernels: 11.9 us -> 13 us  [the longest x1 10.1 us: on_device(): local_call(functools.partial(member_kernel, lanes, owners.shape[0] // 2),...]
  transfers between devices with their start and end apart: 12 -> 12, of which waited for: 8 -> 7; matrix products, arithmetic and copies ran while one was open for 2% -> 2% of each run, Pallas kernels for 6% -> 7%
where the time goes in v11:
time: 80.6 us; the launch traced here: 79.1 us
  waiting for transfers between devices  30.1 us (37%)
  starting transfers between devices  28.3 us (35%)
  Pallas kernels  15.8 us (20%)
  between operations  2.02 us (3%)
  other arithmetic  1.8 us (2%)
  local copies, waits for them, and re-layouts  1.04 us (1%)
    ppermute x10, waiting for transfers between devices, swap(): return lax.ppermute(value, axis, [(i, i ^ bit) for i in range(size)])  27.7 us
    all_to_all x2, starting transfers between devices, transposed(): lax.all_to_all(value, 'member', split_axis=0, concat_axis=0, tiled=True)  15.2 us
    ppermute x10, starting transfers between devices, swap(): return lax.ppermute(value, axis, [(i, i ^ bit) for i in range(size)])  13.2 us
    pallas_call x1, Pallas kernels, on_device(): local_call(functools.partial(member_kernel, lanes, owners.shape[0] // 2),...  10.1 us
    pallas_call x1, Pallas kernels, prepared(): local_call(fetch_kernel, [jax.ShapeDtypeStruct(inlet.shape, BF16), jax.Sh...  2.88 us
    all_to_all x2, waiting for transfers between devices, transposed(): lax.all_to_all(value, 'member', split_axis=0, concat_axis=0, tiled=True)  2.37 us
  transfers between devices with their start and end apart: 12, of which 7 were waited for; matrix products, arithmetic and copies ran while one was open for 2% of the time, Pallas kernels for 7%

profile of v11, /device:TPU:0, one launch (start us, length us, event | category | flops | bytes accessed | tf_op | source)
XLA Modules:
  0.0 79.1 jit_solution(17229808068545267440)
XLA Ops:
  0.6 0.0 copy-start
  0.6 0.0 copy-start.1
  0.6 7.5 %all-to-all-start = ((bf16[16,32,1024]{2,1,0:T(8,128)(2,1)}), bf16[16,32,1024]{2,1,0:T(8,128)(2,1)S(1)}, u32[]{:S(2)}, u32[]{:S(2)}) async-start(bf16[16,32,1024]{2,1,0:T(8,128)(2,1)} %bitcast.6), calls=%async_computation | async-start | bytes 2097152 | tf_op jit(solution)/shard_map/all_to_all | solution.py:35
  8.2 0.0 copy-done
  8.2 0.0 copy-done.1
  8.2 1.5 %shard_map.95 = (bf16[32,1024]{1,0:T(8,128)(2,1)S(1)}, bf16[32,1024]{1,0:T(8,128)(2,1)S(1)}, bf16[32,1024]{1,0:T(8,128)(2,1)S(1)}, bf16[32,1024]{1,0:T(8,128)(2,1)S(1)}, f32[1,32]{1,0:T(1,128)S(1)}) custom-call(s32[4]{0:T(128)S(1)} %copy-done, bf16[1,512,1024]{2,1,0:T(8,128)(2,1)} %analyses.1, f32[1,32]{1,0:T(1,128)S(1)} %bitcast.4), custom_call_target="tpu_custom_call" | custom-call | tf_op jit(solution)/shard_map/pallas_call | solution.py:149
  9.8 0.5 collective-permute-start
  10.2 1.7 %collective-permute-start.1 = (bf16[32,1024]{1,0:T(8,128)(2,1)S(1)}, bf16[32,1024]{1,0:T(8,128)(2,1)S(1)}, u32[]{:S(2)}, u32[]{:S(2)}) collective-permute-start(bf16[32,1024]{1,0:T(8,128)(2,1)S(1)} %get-tuple-element.25), channel_id=1, source_target_pairs={{0,2},{1,3},{2,0},{3,1},{4,6},{5,7},{6,4},{7,5},{8,10},{9,11},{10,... | collective-permute-start | bytes 196616 | tf_op jit(solution)/shard_map/ppermute | solution.py:27
  11.9 0.0 collective-permute-start.2
  11.9 1.5 %collective-permute-start.3 = (f32[1,32]{1,0:T(1,128)S(1)}, f32[1,32]{1,0:T(1,128)S(1)}, u32[]{:S(2)}, u32[]{:S(2)}) collective-permute-start(f32[1,32]{1,0:T(1,128)S(1)} %get-tuple-element.27.refs_4_.weight), channel_id=1, source_target_pairs={{0,16},{16,0},{1,17},{17,1},{2,18},{18,2},{3,19},{19,3},{4,20},{20... | collective-permute-start | bytes 392 | tf_op jit(solution)/shard_map/ppermute | solution.py:27
  13.4 2.0 %collective-permute-done.3.refs_5_ = f32[1,32]{1,0:T(1,128)S(1)} collective-permute-done((f32[1,32]{1,0:T(1,128)S(1)}, f32[1,32]{1,0:T(1,128)S(1)}, u32[]{:S(2)}, u32[]{:S(2)}) %collective-permute-start.3) | collective-permute-done | bytes 160 | tf_op jit(solution)/shard_map/ppermute | solution.py:27
  15.4 0.0 collective-permute-done.refs_1_
  15.5 4.3 %collective-permute-done.1.refs_2_ = bf16[32,1024]{1,0:T(8,128)(2,1)S(1)} collective-permute-done((bf16[32,1024]{1,0:T(8,128)(2,1)S(1)}, bf16[32,1024]{1,0:T(8,128)(2,1)S(1)}, u32[]{:S(2)}, u32[]{:S(2)}) %collective-permute-start.1) | collective-permute-done | bytes 65568 | tf_op jit(solution)/shard_map/ppermute | solution.py:27
  19.8 0.6 collective-permute-done.2.refs_3_
  20.4 0.6 shard_map.96
  21.0 0.1 collective-permute-start.4
  21.0 0.8 %collective-permute-start.7 = (f32[1,32]{1,0:T(1,128)S(1)}, f32[1,32]{1,0:T(1,128)S(1)}, u32[]{:S(2)}, u32[]{:S(2)}) collective-permute-start(f32[1,32]{1,0:T(1,128)S(1)} %get-tuple-element.30.refs_0_), channel_id=1, source_target_pairs={{0,3},{1,2},{2,1},{3,0},{4,7},{5,6},{6,5},{7,4},{8,11},{9,10},{10,... | collective-permute-start | bytes 392 | tf_op jit(solution)/shard_map/ppermute | solution.py:27
  21.9 2.2 %collective-permute-start.6 = (f32[1,32]{1,0:T(1,128)S(1)}, f32[1,32]{1,0:T(1,128)S(1)}, u32[]{:S(2)}, u32[]{:S(2)}) collective-permute-start(f32[1,32]{1,0:T(1,128)S(1)} %get-tuple-element.30.refs_0_), channel_id=1, source_target_pairs={{0,2},{1,3},{2,0},{3,1},{4,6},{5,7},{6,4},{7,5},{8,10},{9,11},{10,... | collective-permute-start | bytes 392 | tf_op jit(solution)/shard_map/ppermute | solution.py:27
  24.1 0.0 collective-permute-start.5
  24.1 0.0 collective-permute-done.7.refs_3_
  24.1 1.5 %collective-permute-done.6.refs_2_ = f32[1,32]{1,0:T(1,128)S(1)} collective-permute-done((f32[1,32]{1,0:T(1,128)S(1)}, f32[1,32]{1,0:T(1,128)S(1)}, u32[]{:S(2)}, u32[]{:S(2)}) %collective-permute-start.6) | collective-permute-done | bytes 160 | tf_op jit(solution)/shard_map/ppermute | solution.py:27
  25.6 0.0 collective-permute-done.5.refs_1_
  25.6 3.5 %collective-permute-done.4.got = bf16[2,32,1024]{2,1,0:T(8,128)(2,1)S(1)} collective-permute-done((bf16[2,32,1024]{2,1,0:T(8,128)(2,1)S(1)}, bf16[2,32,1024]{2,1,0:T(8,128)(2,1)S(1)}, u32[]{:S(2)}, u32[]{:S(2)}) %collective-permute-start.4) | collective-permute-done | bytes 131104 | tf_op jit(solution)/shard_map/ppermute | solution.py:27
  29.1 0.7 shard_map.97
  29.8 0.0 copy-start.2
  29.8 0.0 copy-start.3
  29.8 4.5 %collective-permute-start.8 = (bf16[48,1024]{1,0:T(8,128)(2,1)S(1)}, bf16[48,1024]{1,0:T(8,128)(2,1)S(1)}, u32[]{:S(2)}, u32[]{:S(2)}) collective-permute-start(bf16[48,1024]{1,0:T(8,128)(2,1)S(1)} %get-tuple-element.32), channel_id=1, source_target_pairs={{0,8},{1,9},{2,10},{3,11},{4,12},{5,13},{6,14},{7,15},{8,0},{9,1},... | collective-permute-start | bytes 294920 | tf_op jit(solution)/shard_map/ppermute | solution.py:27
  34.2 0.0 all-to-all-done.after.noise
  34.3 2.9 %shard_map.98 = (bf16[1024,2048]{1,0:T(8,128)(2,1)S(1)}, bf16[1024,1024]{1,0:T(8,128)(2,1)S(1)}) custom-call(bf16[1024,2048]{1,0:T(8,128)(2,1)} %inlet.1, bf16[2048,1024]{1,0:T(8,128)(2,1)} %outlet_hbm.1, bf16[16,32,1024]{2,1,0:T(8,128)(2,1)S(1)} %all-to-all-done.after.noise), custom_call_target="tpu_custom_call" | custom-call | bytes 6291456 | tf_op jit(solution)/shard_map/pallas_call | solution.py:177
  37.1 0.0 collective-permute-done.8.got
  37.2 0.0 copy-done.2
  37.2 0.0 copy-done.3
  37.2 10.1 %shard_map.99 = (bf16[16,32,1024]{2,1,0:T(8,128)(2,1)}, f32[32,1]{1,0:T(8,128)S(1)}, f32[8,128]{1,0:T(8,128)S(1)}) custom-call(s32[4]{0:T(128)S(1)} %copy-done, bf16[1,32,1024]{2,1,0:T(8,128)(2,1)S(1)} %get-tuple-element.31.keep, bf16[48,1024]{1,0:T(8,128)(2,1)S(1)} %collective-permute-done.8.got, bf16[1024,1024]{1,0:T(8,128)(2,1)S(1)} %copy-done.2, ...), custom_call_target="tpu_custom_call" | custom-call | flops 4328521728 | bytes 8388608 | tf_op jit(solution)/shard_map/pallas_call | solution.py:344
  47.3 7.6 %all-to-all-start.1 = ((bf16[16,32,1024]{2,1,0:T(8,128)(2,1)}), bf16[16,32,1024]{2,1,0:T(8,128)(2,1)S(1)}, u32[]{:S(2)}, u32[]{:S(2)}) async-start(bf16[16,32,1024]{2,1,0:T(8,128)(2,1)} %get-tuple-element.41), calls=%async_computation.1 | async-start | bytes 2097152 | tf_op jit(solution)/shard_map/all_to_all | solution.py:35
  55.0 1.9 %collective-permute-start.9 = (f32[8,128]{1,0:T(8,128)S(1)}, f32[8,128]{1,0:T(8,128)S(1)}, u32[]{:S(2)}, u32[]{:S(2)}) collective-permute-start(f32[8,128]{1,0:T(8,128)S(1)} %get-tuple-element.42), channel_id=1, source_target_pairs={{0,4},{1,5},{2,6},{3,7},{4,0},{5,1},{6,2},{7,3},{8,12},{9,13},{10,... | collective-permute-start | bytes 12296 | tf_op jit(solution)/shard_map/ppermute | solution.py:27
  56.9 0.5 slice.6
  57.4 15.8 %collective-permute-done.9 = f32[8,128]{1,0:T(8,128)S(1)} collective-permute-done((f32[8,128]{1,0:T(8,128)S(1)}, f32[8,128]{1,0:T(8,128)S(1)}, u32[]{:S(2)}, u32[]{:S(2)}) %collective-permute-start.9) | collective-permute-done | bytes 4128 | tf_op jit(solution)/shard_map/ppermute | solution.py:27
  73.2 0.5 slice.7
  74.9 0.6 multiply_reduce_fusion
  75.5 2.4 %all-to-all-done.1 = bf16[16,32,1024]{2,1,0:T(8,128)(2,1)S(1)} async-done(((bf16[16,32,1024]{2,1,0:T(8,128)(2,1)}), bf16[16,32,1024]{2,1,0:T(8,128)(2,1)S(1)}, u32[]{:S(2)}, u32[]{:S(2)}) %all-to-all-start.1) | async-done | bytes 1048608 | tf_op jit(solution)/shard_map/all_to_all | solution.py:35
  77.9 1.2 %multiply_convert_fusion = bf16[16,32,1024]{2,1,0:T(8,128)(2,1)} fusion(bf16[16,32,1024]{2,1,0:T(8,128)(2,1)S(1)} %all-to-all-done.1, f32[]{:T(128)} %bitcast.2), kind=kLoop, calls=%fused_computation | loop fusion | flops 1572864 | bytes 2097156 | tf_op jit(solution)/shard_map/convert_element_type | solution.py:381
Async XLA Ops:
  0.6 7.6 %copy-start = (s32[4]{0:T(128)S(1)}, s32[4]{0:T(128)}, u32[]{:S(2)}) copy-start(s32[4]{0:T(128)} %owners.7) | copy-start | bytes 52
  0.6 7.6 %copy-start.1 = (f32[32]{0:T(128)S(1)}, f32[32]{0:T(128)}, u32[]{:S(2)}) copy-start(f32[32]{0:T(128)} %param.12) | copy-start | bytes 388
  0.6 33.6 %all-to-all-start = ((bf16[16,32,1024]{2,1,0:T(8,128)(2,1)}), bf16[16,32,1024]{2,1,0:T(8,128)(2,1)S(1)}, u32[]{:S(2)}, u32[]{:S(2)}) async-start(bf16[16,32,1024]{2,1,0:T(8,128)(2,1)} %bitcast.6), calls=%async_computation | async-start | bytes 2097152 | tf_op jit(solution)/shard_map/all_to_all | solution.py:35
  9.8 5.7 %collective-permute-start = (bf16[32,1024]{1,0:T(8,128)(2,1)S(1)}, bf16[32,1024]{1,0:T(8,128)(2,1)S(1)}, u32[]{:S(2)}, u32[]{:S(2)}) collective-permute-start(bf16[32,1024]{1,0:T(8,128)(2,1)S(1)} %get-tuple-element.24), channel_id=1, source_target_pairs={{0,1},{1,0},{2,3},{3,2},{4,5},{5,4},{6,7},{7,6},{8,9},{9,8},{10,11... | collective-permute-start | bytes 196616 | tf_op jit(solution)/shard_map/ppermute | solution.py:27
  10.2 9.6 %collective-permute-start.1 = (bf16[32,1024]{1,0:T(8,128)(2,1)S(1)}, bf16[32,1024]{1,0:T(8,128)(2,1)S(1)}, u32[]{:S(2)}, u32[]{:S(2)}) collective-permute-start(bf16[32,1024]{1,0:T(8,128)(2,1)S(1)} %get-tuple-element.25), channel_id=1, source_target_pairs={{0,2},{1,3},{2,0},{3,1},{4,6},{5,7},{6,4},{7,5},{8,10},{9,11},{10,... | collective-permute-start | bytes 196616 | tf_op jit(solution)/shard_map/ppermute | solution.py:27
  11.9 8.5 %collective-permute-start.2 = (bf16[32,1024]{1,0:T(8,128)(2,1)S(1)}, bf16[32,1024]{1,0:T(8,128)(2,1)S(1)}, u32[]{:S(2)}, u32[]{:S(2)}) collective-permute-start(bf16[32,1024]{1,0:T(8,128)(2,1)S(1)} %get-tuple-element.26), channel_id=1, source_target_pairs={{0,3},{1,2},{2,1},{3,0},{4,7},{5,6},{6,5},{7,4},{8,11},{9,10},{10,... | collective-permute-start | bytes 196616 | tf_op jit(solution)/shard_map/ppermute | solution.py:27
  11.9 3.5 %collective-permute-start.3 = (f32[1,32]{1,0:T(1,128)S(1)}, f32[1,32]{1,0:T(1,128)S(1)}, u32[]{:S(2)}, u32[]{:S(2)}) collective-permute-start(f32[1,32]{1,0:T(1,128)S(1)} %get-tuple-element.27.refs_4_.weight), channel_id=1, source_target_pairs={{0,16},{16,0},{1,17},{17,1},{2,18},{18,2},{3,19},{19,3},{4,20},{20... | collective-permute-start | bytes 392 | tf_op jit(solution)/shard_map/ppermute | solution.py:27
  21.0 8.1 %collective-permute-start.4 = (bf16[2,32,1024]{2,1,0:T(8,128)(2,1)S(1)}, bf16[2,32,1024]{2,1,0:T(8,128)(2,1)S(1)}, u32[]{:S(2)}, u32[]{:S(2)}) collective-permute-start(bf16[2,32,1024]{2,1,0:T(8,128)(2,1)S(1)} %get-tuple-element.29), channel_id=1, source_target_pairs={{0,4},{1,5},{2,6},{3,7},{4,0},{5,1},{6,2},{7,3},{8,12},{9,13},{10,... | collective-permute-start | bytes 393224 | tf_op jit(solution)/shard_map/ppermute | solution.py:27
  21.0 3.1 %collective-permute-start.7 = (f32[1,32]{1,0:T(1,128)S(1)}, f32[1,32]{1,0:T(1,128)S(1)}, u32[]{:S(2)}, u32[]{:S(2)}) collective-permute-start(f32[1,32]{1,0:T(1,128)S(1)} %get-tuple-element.30.refs_0_), channel_id=1, source_target_pairs={{0,3},{1,2},{2,1},{3,0},{4,7},{5,6},{6,5},{7,4},{8,11},{9,10},{10,... | collective-permute-start | bytes 392 | tf_op jit(solution)/shard_map/ppermute | solution.py:27
  21.9 3.7 %collective-permute-start.6 = (f32[1,32]{1,0:T(1,128)S(1)}, f32[1,32]{1,0:T(1,128)S(1)}, u32[]{:S(2)}, u32[]{:S(2)}) collective-permute-start(f32[1,32]{1,0:T(1,128)S(1)} %get-tuple-element.30.refs_0_), channel_id=1, source_target_pairs={{0,2},{1,3},{2,0},{3,1},{4,6},{5,7},{6,4},{7,5},{8,10},{9,11},{10,... | collective-permute-start | bytes 392 | tf_op jit(solution)/shard_map/ppermute | solution.py:27
  24.1 1.5 %collective-permute-start.5 = (f32[1,32]{1,0:T(1,128)S(1)}, f32[1,32]{1,0:T(1,128)S(1)}, u32[]{:S(2)}, u32[]{:S(2)}) collective-permute-start(f32[1,32]{1,0:T(1,128)S(1)} %get-tuple-element.30.refs_0_), channel_id=1, source_target_pairs={{0,1},{1,0},{2,3},{3,2},{4,5},{5,4},{6,7},{7,6},{8,9},{9,8},{10,11... | collective-permute-start | bytes 392 | tf_op jit(solution)/shard_map/ppermute | solution.py:27
  29.8 7.4 %copy-start.2 = (bf16[1024,1024]{1,0:T(8,128)(2,1)S(1)}, bf16[1024,1024]{1,0:T(8,128)(2,1)}, u32[]{:S(2)}) copy-start(bf16[1024,1024]{1,0:T(8,128)(2,1)} %encoder.1) | copy-start | bytes 6291460
  29.8 7.4 %copy-start.3 = (bf16[32,1024]{1,0:T(8,128)(2,1)S(1)}, bf16[32,1024]{1,0:T(8,128)(2,1)}, u32[]{:S(2)}) copy-start(bf16[32,1024]{1,0:T(8,128)(2,1)} %targets_hbm.1) | copy-start | bytes 196612
  29.8 7.4 %collective-permute-start.8 = (bf16[48,1024]{1,0:T(8,128)(2,1)S(1)}, bf16[48,1024]{1,0:T(8,128)(2,1)S(1)}, u32[]{:S(2)}, u32[]{:S(2)}) collective-permute-start(bf16[48,1024]{1,0:T(8,128)(2,1)S(1)} %get-tuple-element.32), channel_id=1, source_target_pairs={{0,8},{1,9},{2,10},{3,11},{4,12},{5,13},{6,14},{7,15},{8,0},{9,1},... | collective-permute-start | bytes 294920 | tf_op jit(solution)/shard_map/ppermute | solution.py:27
  47.3 30.6 %all-to-all-start.1 = ((bf16[16,32,1024]{2,1,0:T(8,128)(2,1)}), bf16[16,32,1024]{2,1,0:T(8,128)(2,1)S(1)}, u32[]{:S(2)}, u32[]{:S(2)}) async-start(bf16[16,32,1024]{2,1,0:T(8,128)(2,1)} %get-tuple-element.41), calls=%async_computation.1 | async-start | bytes 2097152 | tf_op jit(solution)/shard_map/all_to_all | solution.py:35
  55.0 18.2 %collective-permute-start.9 = (f32[8,128]{1,0:T(8,128)S(1)}, f32[8,128]{1,0:T(8,128)S(1)}, u32[]{:S(2)}, u32[]{:S(2)}) collective-permute-start(f32[8,128]{1,0:T(8,128)S(1)} %get-tuple-element.42), channel_id=1, source_target_pairs={{0,4},{1,5},{2,6},{3,7},{4,0},{5,1},{6,2},{7,3},{8,12},{9,13},{10,... | collective-permute-start | bytes 12296 | tf_op jit(solution)/shard_map/ppermute | solution.py:27

commit v12 on v9

--- a/solution.py
+++ b/solution.py
@@ -10,10 +10,10 @@
 EPSILON = 1e-06
 TOKENS_AT_ONCE = 16
 TAIL = 16
-HIDDEN_PIECES = 2
 ROWS_LIMIT = 53
-NETWORK_LIMIT = 46
-FETCH_LIMIT = 46
+NETWORK_LIMIT = 32
+ENCODE_LIMIT = 46
+FETCH_LIMIT = 44
 BF16 = jnp.bfloat16
 F32 = jnp.float32
 
@@ -121,22 +121,34 @@
     give[pl.ds(keep_out.shape[0] * own, TAIL), :] = weight_rows(total, features)
 
 
-def fetch_kernel(matrix, after, near, sem):
-    copy = pltpu.make_async_copy(matrix, near, sem)
+def fetch_kernel(inlet, outlet, after, inlet_near, outlet_near, sems):
+    rows = pl.ds(0, outlet_near.shape[0])
+    copies = [
+        pltpu.make_async_copy(inlet, inlet_near, sems.at[0]),
+        pltpu.make_async_copy(outlet.at[rows, :], outlet_near, sems.at[1]),
+    ]
+    for copy in copies:
+        copy.start()
+    for copy in copies:
+        copy.wait()
+
+
+def encode_kernel(
+    lanes, bit, owners, keep, got, encoder, total, outlet, latent, total_out, outlet_near, sem
+):
+    half = outlet_near.shape[0]
+    copy = pltpu.make_async_copy(outlet.at[pl.ds(half, half), :], outlet_near, sem)
     copy.start()
-    copy.wait()
-
-
-def encode_kernel(lanes, bit, owners, keep, got, encoder, total, latent, total_out):
     own = latent.shape[0]
     plane = lax.axis_index("member") // lanes
     rows = [got[pl.ds(0, own), :]]
     control = merged(lanes, owners, plane, bit, keep, rows, 0)
     latent[...] = jnp.dot(control, encoder[...], preferred_element_type=F32).astype(BF16)
     total_out[...] = total[...] + weight_from(got[pl.ds(own, TAIL), :])
-
-
-def prepared(analyses, owners, encoder, area_weight, matrix, after):
+    copy.wait()
+
+
+def prepared(analyses, owners, encoder, area_weight, inlet, outlet, after):
     members, regions = lax.axis_size("member"), lax.axis_size("region")
     _, rows, features = analyses.shape
     blocks = owners.shape[0]
@@ -175,23 +187,25 @@
         limit=8,
     )(owners, keep, got, *weights)
     got = swap(give, "member", 2 * lanes)
-    (near,) = local_call(
+    half = jax.ShapeDtypeStruct((outlet.shape[0] // 2, features), BF16)
+    inlet, first_half = local_call(
         fetch_kernel,
-        [jax.ShapeDtypeStruct(matrix.shape, BF16)],
-        [HBM, VMEM],
-        moved=2 * matrix.size,
+        [jax.ShapeDtypeStruct(inlet.shape, BF16), half],
+        [HBM, HBM, VMEM],
+        moved=3 * inlet.size,
+        scratch=[pltpu.SemaphoreType.DMA((2,))],
+        limit=FETCH_LIMIT,
+    )(inlet, outlet, after)
+    got, inlet, first_half = lax.optimization_barrier((got, inlet, first_half))
+    latent, total, second_half = local_call(
+        functools.partial(encode_kernel, lanes, 2),
+        [row, small, half],
+        [SMEM] + [VMEM] * 4 + [HBM],
+        flops=2 * own * features * features,
         scratch=[pltpu.SemaphoreType.DMA],
-        limit=FETCH_LIMIT,
-    )(matrix, after)
-    got, near = lax.optimization_barrier((got, near))
-    latent, total = local_call(
-        functools.partial(encode_kernel, lanes, 2),
-        [row, small],
-        [SMEM] + [VMEM] * 4,
-        flops=2 * own * features * features,
-        limit=8,
-    )(owners, keep, got, encoder, total)
-    return latent, own_weight, total, near
+        limit=ENCODE_LIMIT,
+    )(owners, keep, got, encoder, total, outlet)
+    return latent, own_weight, total, inlet, first_half, second_half
 
 
 def column(row):
@@ -249,37 +263,31 @@
     latent,
     weight,
     inlet,
+    first_half,
+    second_half,
     targets_hbm,
-    outlet_hbm,
     gradient_out,
     energy_out,
     targets,
-    outlet,
     hidden,
-    sems,
+    sem,
 ):
     members, own, features = noise.shape
-    width = inlet.shape[1] // HIDDEN_PIECES
-    copies = [pltpu.make_async_copy(targets_hbm, targets, sems.at[HIDDEN_PIECES])]
-    for piece in range(HIDDEN_PIECES):
-        rows = pl.ds(piece * width, width)
-        copies.append(
-            pltpu.make_async_copy(outlet_hbm.at[rows, :], outlet.at[rows, :], sems.at[piece])
-        )
-    for copy in copies:
-        copy.start()
+    aside = pltpu.make_async_copy(targets_hbm, targets, sem)
+    aside.start()
+    halves = (first_half, second_half)
+    width = first_half.shape[0]
 
     def hidden_piece(normed, piece):
-        rows = slice(piece * width, (piece + 1) * width)
+        columns = slice(piece * width, (piece + 1) * width)
         hidden[...] = jax.nn.gelu(
-            jnp.dot(normed, inlet[:, rows], preferred_element_type=F32), approximate=True
+            jnp.dot(normed, inlet[:, columns], preferred_element_type=F32), approximate=True
         ).astype(BF16)
-        copies[piece + 1].wait()
-        return jnp.dot(hidden[...], outlet[rows, :], preferred_element_type=F32)
-
-    forecast = network(noise[...], latent[...], hidden_piece, HIDDEN_PIECES)
+        return jnp.dot(hidden[...], halves[piece][...], preferred_element_type=F32)
+
+    forecast = network(noise[...], latent[...], hidden_piece, len(halves))
     forecast = forecast.reshape(members, own, features)
-    copies[0].wait()
+    aside.wait()
     scales = column(weight[...])
     for first in range(0, own, TOKENS_AT_ONCE):
         here = slice(first, first + TOKENS_AT_ONCE)
@@ -309,8 +317,14 @@
     hidden = sample_inlet_matrix.shape[1]
     own = region_rows // members
     here = transposed(noise.reshape(members, own, features))
-    latent, weight, total, inlet = prepared(
-        analyses, owners, enc_weight, area_weight, sample_inlet_matrix, here
+    latent, weight, total, *matrices = prepared(
+        analyses,
+        owners,
+        enc_weight,
+        area_weight,
+        sample_inlet_matrix,
+        sample_outlet_matrix,
+        here,
     )
     gradient, energy = local_call(
         member_kernel,
@@ -318,17 +332,16 @@
             jax.ShapeDtypeStruct((members, own, features), BF16),
             jax.ShapeDtypeStruct((own, 1), F32),
         ],
-        [VMEM] * 4 + [HBM] * 2,
+        [VMEM] * 6 + [HBM],
         flops=4 * members * own * features * (hidden + members),
         moved=4 * features * hidden,
         scratch=[
             pltpu.VMEM((own, features), BF16),
-            pltpu.VMEM((hidden, features), BF16),
-            pltpu.VMEM((members * own, hidden // HIDDEN_PIECES), BF16),
-            pltpu.SemaphoreType.DMA((HIDDEN_PIECES + 1,)),
+            pltpu.VMEM((members * own, hidden // 2), BF16),
+            pltpu.SemaphoreType.DMA,
         ],
         limit=NETWORK_LIMIT,
-    )(here, latent, weight, inlet, targets, sample_outlet_matrix)
+    )(here, latent, weight, *matrices, targets)
     gradient, total = lax.optimization_barrier((gradient, total))
     back = transposed(gradient)
     across = swap(total, "member", members // owners.shape[0])

time: 80.1 us -> 80.4 us (level)
  Pallas kernels: 14.7 us -> 15.6 us
    pallas_call x2, Pallas kernels: 3.2 us -> 5.06 us  [the longest x1 2.88 us: prepared(): local_call(fetch_kernel, [jax.ShapeDtypeStruct(inlet.shape, BF16), half],...]
    pallas_call x1, Pallas kernels: 8.67 us -> 7.73 us  [on_device(): local_call(member_kernel, [jax.ShapeDtypeStruct((members, own, features),...]
  transfers between devices with their start and end apart: 12 -> 12, of which waited for: 8 -> 7; matrix products, arithmetic and copies ran while one was open for 2% -> 2% of each run, Pallas kernels for 6% -> 7%
where the time goes in v12:
time: 80.4 us; the launch traced here: 78.8 us
  waiting for transfers between devices  30 us (37%)
  starting transfers between devices  28.3 us (35%)
  Pallas kernels  15.6 us (19%)
  between operations  2.09 us (3%)
  other arithmetic  1.8 us (2%)
  local copies, waits for them, and re-layouts  1.06 us (1%)
    ppermute x10, waiting for transfers between devices, swap(): return lax.ppermute(value, axis, [(i, i ^ bit) for i in range(size)])  27.7 us
    all_to_all x2, starting transfers between devices, transposed(): lax.all_to_all(value, 'member', split_axis=0, concat_axis=0, tiled=True)  15.2 us
    ppermute x10, starting transfers between devices, swap(): return lax.ppermute(value, axis, [(i, i ^ bit) for i in range(size)])  13.2 us
    pallas_call x1, Pallas kernels, on_device(): local_call(member_kernel, [jax.ShapeDtypeStruct((members, own, features),...  7.73 us
    pallas_call x1, Pallas kernels, prepared(): local_call(fetch_kernel, [jax.ShapeDtypeStruct(inlet.shape, BF16), half],...  2.88 us
    all_to_all x2, waiting for transfers between devices, transposed(): lax.all_to_all(value, 'member', split_axis=0, concat_axis=0, tiled=True)  2.29 us
    pallas_call x1, Pallas kernels, prepared(): local_call(functools.partial(encode_kernel, lanes, 2), [row, small, half]...  2.17 us
  transfers between devices with their start and end apart: 12, of which 7 were waited for; matrix products, arithmetic and copies ran while one was open for 2% of the time, Pallas kernels for 7%

profile of v12, /device:TPU:0, one launch (start us, length us, event | category | flops | bytes accessed | tf_op | source)
XLA Modules:
  0.0 78.8 jit_solution(2906547234138408400)
XLA Ops:
  0.6 0.0 copy-start.1
  0.6 0.0 copy-start.2
  0.6 7.5 %all-to-all-start = ((bf16[16,32,1024]{2,1,0:T(8,128)(2,1)}), bf16[16,32,1024]{2,1,0:T(8,128)(2,1)S(1)}, u32[]{:S(2)}, u32[]{:S(2)}) async-start(bf16[16,32,1024]{2,1,0:T(8,128)(2,1)} %bitcast.6), calls=%async_computation | async-start | bytes 2097152 | tf_op jit(solution)/shard_map/all_to_all | solution.py:35
  8.2 0.0 copy-done.1
  8.2 0.0 copy-done.2
  8.2 1.5 %shard_map.95 = (bf16[32,1024]{1,0:T(8,128)(2,1)S(1)}, bf16[32,1024]{1,0:T(8,128)(2,1)S(1)}, bf16[32,1024]{1,0:T(8,128)(2,1)S(1)}, bf16[32,1024]{1,0:T(8,128)(2,1)S(1)}, f32[1,32]{1,0:T(1,128)S(1)}) custom-call(s32[4]{0:T(128)S(1)} %copy-done.1, bf16[1,512,1024]{2,1,0:T(8,128)(2,1)} %analyses.1, f32[1,32]{1,0:T(1,128)S(1)} %bitcast.4), custom_call_target="tpu_custom_call" | custom-call | tf_op jit(solution)/shard_map/pallas_call | solution.py:162
  9.8 0.5 collective-permute-start
  10.2 1.7 %collective-permute-start.1 = (bf16[32,1024]{1,0:T(8,128)(2,1)S(1)}, bf16[32,1024]{1,0:T(8,128)(2,1)S(1)}, u32[]{:S(2)}, u32[]{:S(2)}) collective-permute-start(bf16[32,1024]{1,0:T(8,128)(2,1)S(1)} %get-tuple-element.27), channel_id=1, source_target_pairs={{0,2},{1,3},{2,0},{3,1},{4,6},{5,7},{6,4},{7,5},{8,10},{9,11},{10,... | collective-permute-start | bytes 196616 | tf_op jit(solution)/shard_map/ppermute | solution.py:27
  11.9 0.0 collective-permute-start.2
  11.9 1.5 %collective-permute-start.3 = (f32[1,32]{1,0:T(1,128)S(1)}, f32[1,32]{1,0:T(1,128)S(1)}, u32[]{:S(2)}, u32[]{:S(2)}) collective-permute-start(f32[1,32]{1,0:T(1,128)S(1)} %get-tuple-element.29.refs_4_.weight), channel_id=1, source_target_pairs={{0,16},{16,0},{1,17},{17,1},{2,18},{18,2},{3,19},{19,3},{4,20},{20... | collective-permute-start | bytes 392 | tf_op jit(solution)/shard_map/ppermute | solution.py:27
  13.4 2.0 %collective-permute-done.3.refs_5_ = f32[1,32]{1,0:T(1,128)S(1)} collective-permute-done((f32[1,32]{1,0:T(1,128)S(1)}, f32[1,32]{1,0:T(1,128)S(1)}, u32[]{:S(2)}, u32[]{:S(2)}) %collective-permute-start.3) | collective-permute-done | bytes 160 | tf_op jit(solution)/shard_map/ppermute | solution.py:27
  15.4 0.0 collective-permute-done.refs_1_
  15.5 4.3 %collective-permute-done.1.refs_2_ = bf16[32,1024]{1,0:T(8,128)(2,1)S(1)} collective-permute-done((bf16[32,1024]{1,0:T(8,128)(2,1)S(1)}, bf16[32,1024]{1,0:T(8,128)(2,1)S(1)}, u32[]{:S(2)}, u32[]{:S(2)}) %collective-permute-start.1) | collective-permute-done | bytes 65568 | tf_op jit(solution)/shard_map/ppermute | solution.py:27
  19.8 0.6 collective-permute-done.2.refs_3_
  20.4 0.6 shard_map.96
  21.0 0.1 collective-permute-start.4
  21.0 0.8 %collective-permute-start.7 = (f32[1,32]{1,0:T(1,128)S(1)}, f32[1,32]{1,0:T(1,128)S(1)}, u32[]{:S(2)}, u32[]{:S(2)}) collective-permute-start(f32[1,32]{1,0:T(1,128)S(1)} %get-tuple-element.32.refs_0_), channel_id=1, source_target_pairs={{0,3},{1,2},{2,1},{3,0},{4,7},{5,6},{6,5},{7,4},{8,11},{9,10},{10,... | collective-permute-start | bytes 392 | tf_op jit(solution)/shard_map/ppermute | solution.py:27
  21.9 2.2 %collective-permute-start.6 = (f32[1,32]{1,0:T(1,128)S(1)}, f32[1,32]{1,0:T(1,128)S(1)}, u32[]{:S(2)}, u32[]{:S(2)}) collective-permute-start(f32[1,32]{1,0:T(1,128)S(1)} %get-tuple-element.32.refs_0_), channel_id=1, source_target_pairs={{0,2},{1,3},{2,0},{3,1},{4,6},{5,7},{6,4},{7,5},{8,10},{9,11},{10,... | collective-permute-start | bytes 392 | tf_op jit(solution)/shard_map/ppermute | solution.py:27
  24.1 0.0 collective-permute-start.5
  24.1 0.0 collective-permute-done.7.refs_3_
  24.1 1.5 %collective-permute-done.6.refs_2_ = f32[1,32]{1,0:T(1,128)S(1)} collective-permute-done((f32[1,32]{1,0:T(1,128)S(1)}, f32[1,32]{1,0:T(1,128)S(1)}, u32[]{:S(2)}, u32[]{:S(2)}) %collective-permute-start.6) | collective-permute-done | bytes 160 | tf_op jit(solution)/shard_map/ppermute | solution.py:27
  25.6 0.0 collective-permute-done.5.refs_1_
  25.6 3.5 %collective-permute-done.4.got = bf16[2,32,1024]{2,1,0:T(8,128)(2,1)S(1)} collective-permute-done((bf16[2,32,1024]{2,1,0:T(8,128)(2,1)S(1)}, bf16[2,32,1024]{2,1,0:T(8,128)(2,1)S(1)}, u32[]{:S(2)}, u32[]{:S(2)}) %collective-permute-start.4) | collective-permute-done | bytes 131104 | tf_op jit(solution)/shard_map/ppermute | solution.py:27
  29.1 0.7 shard_map.97
  29.8 0.0 copy-start
  29.8 4.5 %collective-permute-start.8 = (bf16[48,1024]{1,0:T(8,128)(2,1)S(1)}, bf16[48,1024]{1,0:T(8,128)(2,1)S(1)}, u32[]{:S(2)}, u32[]{:S(2)}) collective-permute-start(bf16[48,1024]{1,0:T(8,128)(2,1)S(1)} %get-tuple-element.34), channel_id=1, source_target_pairs={{0,8},{1,9},{2,10},{3,11},{4,12},{5,13},{6,14},{7,15},{8,0},{9,1},... | collective-permute-start | bytes 294920 | tf_op jit(solution)/shard_map/ppermute | solution.py:27
  34.2 0.0 all-to-all-done.after.noise
  34.2 2.9 %shard_map.98 = (bf16[1024,2048]{1,0:T(8,128)(2,1)S(1)}, bf16[1024,1024]{1,0:T(8,128)(2,1)S(1)}) custom-call(bf16[1024,2048]{1,0:T(8,128)(2,1)} %inlet.1, bf16[2048,1024]{1,0:T(8,128)(2,1)} %outlet.3, bf16[16,32,1024]{2,1,0:T(8,128)(2,1)S(1)} %all-to-all-done.after.noise), custom_call_target="tpu_custom_call" | custom-call | bytes 6291456 | tf_op jit(solution)/shard_map/pallas_call | solution.py:191
  37.1 0.0 collective-permute-done.8.got
  37.1 0.0 copy-done
  37.2 0.0 copy-start.3
  37.2 2.2 %shard_map.99 = (bf16[32,1024]{1,0:T(8,128)(2,1)S(1)}, f32[8,128]{1,0:T(8,128)S(1)}, bf16[1024,1024]{1,0:T(8,128)(2,1)S(1)}) custom-call(s32[4]{0:T(128)S(1)} %copy-done.1, bf16[1,32,1024]{2,1,0:T(8,128)(2,1)S(1)} %get-tuple-element.33.keep, bf16[48,1024]{1,0:T(8,128)(2,1)S(1)} %collective-permute-done.8.got, bf16[1024,1024]{1,0:T(8,128)(2,1)S(1)} %copy-done, ...), custom_call_target="tpu_custom_call" | custom-call | flops 67108864 | tf_op jit(solution)/shard_map/pallas_call | solution.py:200
  39.3 0.0 copy-done.3
  39.4 7.7 %shard_map.100 = (bf16[16,32,1024]{2,1,0:T(8,128)(2,1)}, f32[32,1]{1,0:T(8,128)S(1)}) custom-call(bf16[16,32,1024]{2,1,0:T(8,128)(2,1)S(1)} %all-to-all-done.after.noise, bf16[32,1024]{1,0:T(8,128)(2,1)S(1)} %get-tuple-element.39.latent, f32[1,32]{1,0:T(1,128)S(1)} %get-tuple-element.29.refs_4_.weight, bf16[1024,2048]{1,0:T(8,128)(2,1)S(1)} %get-tuple-element.40.inlet, ...), custom_call_target="tpu_custom_call" | custom-call | flops 4328521728 | bytes 8388608 | tf_op jit(solution)/shard_map/pallas_call | solution.py:329
  47.1 7.6 %all-to-all-start.1 = ((bf16[16,32,1024]{2,1,0:T(8,128)(2,1)}), bf16[16,32,1024]{2,1,0:T(8,128)(2,1)S(1)}, u32[]{:S(2)}, u32[]{:S(2)}) async-start(bf16[16,32,1024]{2,1,0:T(8,128)(2,1)} %get-tuple-element.45), calls=%async_computation.1 | async-start | bytes 2097152 | tf_op jit(solution)/shard_map/all_to_all | solution.py:35
  54.7 1.9 %collective-permute-start.9 = (f32[8,128]{1,0:T(8,128)S(1)}, f32[8,128]{1,0:T(8,128)S(1)}, u32[]{:S(2)}, u32[]{:S(2)}) collective-permute-start(f32[8,128]{1,0:T(8,128)S(1)} %get-tuple-element.46), channel_id=1, source_target_pairs={{0,4},{1,5},{2,6},{3,7},{4,0},{5,1},{6,2},{7,3},{8,12},{9,13},{10,... | collective-permute-start | bytes 12296 | tf_op jit(solution)/shard_map/ppermute | solution.py:27
  56.7 0.5 slice.6
  57.2 15.8 %collective-permute-done.9 = f32[8,128]{1,0:T(8,128)S(1)} collective-permute-done((f32[8,128]{1,0:T(8,128)S(1)}, f32[8,128]{1,0:T(8,128)S(1)}, u32[]{:S(2)}, u32[]{:S(2)}) %collective-permute-start.9) | collective-permute-done | bytes 4128 | tf_op jit(solution)/shard_map/ppermute | solution.py:27
  72.9 0.5 slice.7
  74.8 0.6 multiply_reduce_fusion
  75.4 2.3 %all-to-all-done.1 = bf16[16,32,1024]{2,1,0:T(8,128)(2,1)S(1)} async-done(((bf16[16,32,1024]{2,1,0:T(8,128)(2,1)}), bf16[16,32,1024]{2,1,0:T(8,128)(2,1)S(1)}, u32[]{:S(2)}, u32[]{:S(2)}) %all-to-all-start.1) | async-done | bytes 1048608 | tf_op jit(solution)/shard_map/all_to_all | solution.py:35
  77.7 1.2 %multiply_convert_fusion = bf16[16,32,1024]{2,1,0:T(8,128)(2,1)} fusion(bf16[16,32,1024]{2,1,0:T(8,128)(2,1)S(1)} %all-to-all-done.1, f32[]{:T(128)} %bitcast.2), kind=kLoop, calls=%fused_computation | loop fusion | flops 1572864 | bytes 2097156 | tf_op jit(solution)/shard_map/convert_element_type | solution.py:349
Async XLA Ops:
  0.6 7.6 %copy-start.1 = (s32[4]{0:T(128)S(1)}, s32[4]{0:T(128)}, u32[]{:S(2)}) copy-start(s32[4]{0:T(128)} %owners.7) | copy-start | bytes 52
  0.6 7.6 %copy-start.2 = (f32[32]{0:T(128)S(1)}, f32[32]{0:T(128)}, u32[]{:S(2)}) copy-start(f32[32]{0:T(128)} %param.12) | copy-start | bytes 388
  0.6 33.6 %all-to-all-start = ((bf16[16,32,1024]{2,1,0:T(8,128)(2,1)}), bf16[16,32,1024]{2,1,0:T(8,128)(2,1)S(1)}, u32[]{:S(2)}, u32[]{:S(2)}) async-start(bf16[16,32,1024]{2,1,0:T(8,128)(2,1)} %bitcast.6), calls=%async_computation | async-start | bytes 2097152 | tf_op jit(solution)/shard_map/all_to_all | solution.py:35
  9.8 5.7 %collective-permute-start = (bf16[32,1024]{1,0:T(8,128)(2,1)S(1)}, bf16[32,1024]{1,0:T(8,128)(2,1)S(1)}, u32[]{:S(2)}, u32[]{:S(2)}) collective-permute-start(bf16[32,1024]{1,0:T(8,128)(2,1)S(1)} %get-tuple-element.26), channel_id=1, source_target_pairs={{0,1},{1,0},{2,3},{3,2},{4,5},{5,4},{6,7},{7,6},{8,9},{9,8},{10,11... | collective-permute-start | bytes 196616 | tf_op jit(solution)/shard_map/ppermute | solution.py:27
  10.2 9.6 %collective-permute-start.1 = (bf16[32,1024]{1,0:T(8,128)(2,1)S(1)}, bf16[32,1024]{1,0:T(8,128)(2,1)S(1)}, u32[]{:S(2)}, u32[]{:S(2)}) collective-permute-start(bf16[32,1024]{1,0:T(8,128)(2,1)S(1)} %get-tuple-element.27), channel_id=1, source_target_pairs={{0,2},{1,3},{2,0},{3,1},{4,6},{5,7},{6,4},{7,5},{8,10},{9,11},{10,... | collective-permute-start | bytes 196616 | tf_op jit(solution)/shard_map/ppermute | solution.py:27
  11.9 8.5 %collective-permute-start.2 = (bf16[32,1024]{1,0:T(8,128)(2,1)S(1)}, bf16[32,1024]{1,0:T(8,128)(2,1)S(1)}, u32[]{:S(2)}, u32[]{:S(2)}) collective-permute-start(bf16[32,1024]{1,0:T(8,128)(2,1)S(1)} %get-tuple-element.28), channel_id=1, source_target_pairs={{0,3},{1,2},{2,1},{3,0},{4,7},{5,6},{6,5},{7,4},{8,11},{9,10},{10,... | collective-permute-start | bytes 196616 | tf_op jit(solution)/shard_map/ppermute | solution.py:27
  11.9 3.5 %collective-permute-start.3 = (f32[1,32]{1,0:T(1,128)S(1)}, f32[1,32]{1,0:T(1,128)S(1)}, u32[]{:S(2)}, u32[]{:S(2)}) collective-permute-start(f32[1,32]{1,0:T(1,128)S(1)} %get-tuple-element.29.refs_4_.weight), channel_id=1, source_target_pairs={{0,16},{16,0},{1,17},{17,1},{2,18},{18,2},{3,19},{19,3},{4,20},{20... | collective-permute-start | bytes 392 | tf_op jit(solution)/shard_map/ppermute | solution.py:27
  21.0 8.1 %collective-permute-start.4 = (bf16[2,32,1024]{2,1,0:T(8,128)(2,1)S(1)}, bf16[2,32,1024]{2,1,0:T(8,128)(2,1)S(1)}, u32[]{:S(2)}, u32[]{:S(2)}) collective-permute-start(bf16[2,32,1024]{2,1,0:T(8,128)(2,1)S(1)} %get-tuple-element.31), channel_id=1, source_target_pairs={{0,4},{1,5},{2,6},{3,7},{4,0},{5,1},{6,2},{7,3},{8,12},{9,13},{10,... | collective-permute-start | bytes 393224 | tf_op jit(solution)/shard_map/ppermute | solution.py:27
  21.0 3.1 %collective-permute-start.7 = (f32[1,32]{1,0:T(1,128)S(1)}, f32[1,32]{1,0:T(1,128)S(1)}, u32[]{:S(2)}, u32[]{:S(2)}) collective-permute-start(f32[1,32]{1,0:T(1,128)S(1)} %get-tuple-element.32.refs_0_), channel_id=1, source_target_pairs={{0,3},{1,2},{2,1},{3,0},{4,7},{5,6},{6,5},{7,4},{8,11},{9,10},{10,... | collective-permute-start | bytes 392 | tf_op jit(solution)/shard_map/ppermute | solution.py:27
  21.9 3.7 %collective-permute-start.6 = (f32[1,32]{1,0:T(1,128)S(1)}, f32[1,32]{1,0:T(1,128)S(1)}, u32[]{:S(2)}, u32[]{:S(2)}) collective-permute-start(f32[1,32]{1,0:T(1,128)S(1)} %get-tuple-element.32.refs_0_), channel_id=1, source_target_pairs={{0,2},{1,3},{2,0},{3,1},{4,6},{5,7},{6,4},{7,5},{8,10},{9,11},{10,... | collective-permute-start | bytes 392 | tf_op jit(solution)/shard_map/ppermute | solution.py:27
  24.1 1.5 %collective-permute-start.5 = (f32[1,32]{1,0:T(1,128)S(1)}, f32[1,32]{1,0:T(1,128)S(1)}, u32[]{:S(2)}, u32[]{:S(2)}) collective-permute-start(f32[1,32]{1,0:T(1,128)S(1)} %get-tuple-element.32.refs_0_), channel_id=1, source_target_pairs={{0,1},{1,0},{2,3},{3,2},{4,5},{5,4},{6,7},{7,6},{8,9},{9,8},{10,11... | collective-permute-start | bytes 392 | tf_op jit(solution)/shard_map/ppermute | solution.py:27
  29.8 7.4 %copy-start = (bf16[1024,1024]{1,0:T(8,128)(2,1)S(1)}, bf16[1024,1024]{1,0:T(8,128)(2,1)}, u32[]{:S(2)}) copy-start(bf16[1024,1024]{1,0:T(8,128)(2,1)} %encoder.1) | copy-start | bytes 6291460
  29.8 7.4 %collective-permute-start.8 = (bf16[48,1024]{1,0:T(8,128)(2,1)S(1)}, bf16[48,1024]{1,0:T(8,128)(2,1)S(1)}, u32[]{:S(2)}, u32[]{:S(2)}) collective-permute-start(bf16[48,1024]{1,0:T(8,128)(2,1)S(1)} %get-tuple-element.34), channel_id=1, source_target_pairs={{0,8},{1,9},{2,10},{3,11},{4,12},{5,13},{6,14},{7,15},{8,0},{9,1},... | collective-permute-start | bytes 294920 | tf_op jit(solution)/shard_map/ppermute | solution.py:27
  37.2 2.2 %copy-start.3 = (bf16[32,1024]{1,0:T(8,128)(2,1)S(1)}, bf16[32,1024]{1,0:T(8,128)(2,1)}, u32[]{:S(2)}) copy-start(bf16[32,1024]{1,0:T(8,128)(2,1)} %targets_hbm.1) | copy-start | bytes 196612
  47.1 30.6 %all-to-all-start.1 = ((bf16[16,32,1024]{2,1,0:T(8,128)(2,1)}), bf16[16,32,1024]{2,1,0:T(8,128)(2,1)S(1)}, u32[]{:S(2)}, u32[]{:S(2)}) async-start(bf16[16,32,1024]{2,1,0:T(8,128)(2,1)} %get-tuple-element.45), calls=%async_computation.1 | async-start | bytes 2097152 | tf_op jit(solution)/shard_map/all_to_all | solution.py:35
  54.7 18.2 %collective-permute-start.9 = (f32[8,128]{1,0:T(8,128)S(1)}, f32[8,128]{1,0:T(8,128)S(1)}, u32[]{:S(2)}, u32[]{:S(2)}) collective-permute-start(f32[8,128]{1,0:T(8,128)S(1)} %get-tuple-element.46), channel_id=1, source_target_pairs={{0,4},{1,5},{2,6},{3,7},{4,0},{5,1},{6,2},{7,3},{8,12},{9,13},{10,... | collective-permute-start | bytes 12296 | tf_op jit(solution)/shard_map/ppermute | solution.py:27

commit v13 on v12

--- a/solution.py
+++ b/solution.py
@@ -11,8 +11,7 @@
 TOKENS_AT_ONCE = 16
 TAIL = 16
 ROWS_LIMIT = 53
-NETWORK_LIMIT = 32
-ENCODE_LIMIT = 46
+NETWORK_LIMIT = 44
 FETCH_LIMIT = 44
 BF16 = jnp.bfloat16
 F32 = jnp.float32
@@ -133,19 +132,13 @@
         copy.wait()
 
 
-def encode_kernel(
-    lanes, bit, owners, keep, got, encoder, total, outlet, latent, total_out, outlet_near, sem
-):
-    half = outlet_near.shape[0]
-    copy = pltpu.make_async_copy(outlet.at[pl.ds(half, half), :], outlet_near, sem)
-    copy.start()
+def encode_kernel(lanes, bit, owners, keep, got, encoder, total, latent, total_out):
     own = latent.shape[0]
     plane = lax.axis_index("member") // lanes
     rows = [got[pl.ds(0, own), :]]
     control = merged(lanes, owners, plane, bit, keep, rows, 0)
     latent[...] = jnp.dot(control, encoder[...], preferred_element_type=F32).astype(BF16)
     total_out[...] = total[...] + weight_from(got[pl.ds(own, TAIL), :])
-    copy.wait()
 
 
 def prepared(analyses, owners, encoder, area_weight, inlet, outlet, after):
@@ -197,15 +190,14 @@
         limit=FETCH_LIMIT,
     )(inlet, outlet, after)
     got, inlet, first_half = lax.optimization_barrier((got, inlet, first_half))
-    latent, total, second_half = local_call(
+    latent, total = local_call(
         functools.partial(encode_kernel, lanes, 2),
-        [row, small, half],
-        [SMEM] + [VMEM] * 4 + [HBM],
+        [row, small],
+        [SMEM] + [VMEM] * 4,
         flops=2 * own * features * features,
-        scratch=[pltpu.SemaphoreType.DMA],
-        limit=ENCODE_LIMIT,
-    )(owners, keep, got, encoder, total, outlet)
-    return latent, own_weight, total, inlet, first_half, second_half
+        limit=8,
+    )(owners, keep, got, encoder, total)
+    return latent, own_weight, total, inlet, first_half
 
 
 def column(row):
@@ -264,25 +256,30 @@
     weight,
     inlet,
     first_half,
-    second_half,
     targets_hbm,
+    outlet_hbm,
     gradient_out,
     energy_out,
     targets,
+    second_half,
     hidden,
-    sem,
+    sems,
 ):
     members, own, features = noise.shape
-    aside = pltpu.make_async_copy(targets_hbm, targets, sem)
+    width = first_half.shape[0]
+    rest = pltpu.make_async_copy(outlet_hbm.at[pl.ds(width, width), :], second_half, sems.at[0])
+    aside = pltpu.make_async_copy(targets_hbm, targets, sems.at[1])
+    rest.start()
     aside.start()
     halves = (first_half, second_half)
-    width = first_half.shape[0]
 
     def hidden_piece(normed, piece):
         columns = slice(piece * width, (piece + 1) * width)
         hidden[...] = jax.nn.gelu(
             jnp.dot(normed, inlet[:, columns], preferred_element_type=F32), approximate=True
         ).astype(BF16)
+        if piece == 1:
+            rest.wait()
         return jnp.dot(hidden[...], halves[piece][...], preferred_element_type=F32)
 
     forecast = network(noise[...], latent[...], hidden_piece, len(halves))
@@ -332,16 +329,17 @@
             jax.ShapeDtypeStruct((members, own, features), BF16),
             jax.ShapeDtypeStruct((own, 1), F32),
         ],
-        [VMEM] * 6 + [HBM],
+        [VMEM] * 5 + [HBM] * 2,
         flops=4 * members * own * features * (hidden + members),
         moved=4 * features * hidden,
         scratch=[
             pltpu.VMEM((own, features), BF16),
+            pltpu.VMEM((hidden // 2, features), BF16),
             pltpu.VMEM((members * own, hidden // 2), BF16),
-            pltpu.SemaphoreType.DMA,
+            pltpu.SemaphoreType.DMA((2,)),
         ],
         limit=NETWORK_LIMIT,
-    )(here, latent, weight, *matrices, targets)
+    )(here, latent, weight, *matrices, targets, sample_outlet_matrix)
     gradient, total = lax.optimization_barrier((gradient, total))
     back = transposed(gradient)
     across = swap(total, "member", members // owners.shape[0])

time: 80.4 us -> 79.7 us (level)
    pallas_call x1, Pallas kernels: 2.17 us -> 1.01 us  [prepared(): local_call(functools.partial(encode_kernel, lanes, 2), [row, small], [SME...]
where the time goes in v13:
time: 79.7 us; the launch traced here: 78.2 us
  waiting for transfers between devices  30 us (38%)
  starting transfers between devices  28.3 us (36%)
  Pallas kernels  15 us (19%)
  between operations  2.08 us (3%)
  other arithmetic  1.8 us (2%)
  local copies, waits for them, and re-layouts  1.06 us (1%)
    ppermute x10, waiting for transfers between devices, swap(): return lax.ppermute(value, axis, [(i, i ^ bit) for i in range(size)])  27.7 us
    all_to_all x2, starting transfers between devices, transposed(): lax.all_to_all(value, 'member', split_axis=0, concat_axis=0, tiled=True)  15.2 us
    ppermute x10, starting transfers between devices, swap(): return lax.ppermute(value, axis, [(i, i ^ bit) for i in range(size)])  13.2 us
    pallas_call x1, Pallas kernels, on_device(): local_call(member_kernel, [jax.ShapeDtypeStruct((members, own, features),...  8.26 us
    pallas_call x1, Pallas kernels, prepared(): local_call(fetch_kernel, [jax.ShapeDtypeStruct(inlet.shape, BF16), half],...  2.88 us
    all_to_all x2, waiting for transfers between devices, transposed(): lax.all_to_all(value, 'member', split_axis=0, concat_axis=0, tiled=True)  2.29 us
  transfers between devices with their start and end apart: 12, of which 7 were waited for; matrix products, arithmetic and copies ran while one was open for 2% of the time, Pallas kernels for 7%

profile of v13, /device:TPU:0, one launch (start us, length us, event | category | flops | bytes accessed | tf_op | source)
XLA Modules:
  0.0 78.2 jit_solution(1284237488614254402)
XLA Ops:
  0.6 0.0 copy-start.1
  0.6 0.0 copy-start.2
  0.6 7.5 %all-to-all-start = ((bf16[16,32,1024]{2,1,0:T(8,128)(2,1)}), bf16[16,32,1024]{2,1,0:T(8,128)(2,1)S(1)}, u32[]{:S(2)}, u32[]{:S(2)}) async-start(bf16[16,32,1024]{2,1,0:T(8,128)(2,1)} %bitcast.6), calls=%async_computation | async-start | bytes 2097152 | tf_op jit(solution)/shard_map/all_to_all | solution.py:34
  8.2 0.0 copy-done.1
  8.2 0.0 copy-done.2
  8.2 1.5 %shard_map.95 = (bf16[32,1024]{1,0:T(8,128)(2,1)S(1)}, bf16[32,1024]{1,0:T(8,128)(2,1)S(1)}, bf16[32,1024]{1,0:T(8,128)(2,1)S(1)}, bf16[32,1024]{1,0:T(8,128)(2,1)S(1)}, f32[1,32]{1,0:T(1,128)S(1)}) custom-call(s32[4]{0:T(128)S(1)} %copy-done.1, bf16[1,512,1024]{2,1,0:T(8,128)(2,1)} %analyses.1, f32[1,32]{1,0:T(1,128)S(1)} %bitcast.4), custom_call_target="tpu_custom_call" | custom-call | tf_op jit(solution)/shard_map/pallas_call | solution.py:155
  9.8 0.5 collective-permute-start
  10.2 1.7 %collective-permute-start.1 = (bf16[32,1024]{1,0:T(8,128)(2,1)S(1)}, bf16[32,1024]{1,0:T(8,128)(2,1)S(1)}, u32[]{:S(2)}, u32[]{:S(2)}) collective-permute-start(bf16[32,1024]{1,0:T(8,128)(2,1)S(1)} %get-tuple-element.26), channel_id=1, source_target_pairs={{0,2},{1,3},{2,0},{3,1},{4,6},{5,7},{6,4},{7,5},{8,10},{9,11},{10,... | collective-permute-start | bytes 196616 | tf_op jit(solution)/shard_map/ppermute | solution.py:26
  11.9 0.0 collective-permute-start.2
  11.9 1.5 %collective-permute-start.3 = (f32[1,32]{1,0:T(1,128)S(1)}, f32[1,32]{1,0:T(1,128)S(1)}, u32[]{:S(2)}, u32[]{:S(2)}) collective-permute-start(f32[1,32]{1,0:T(1,128)S(1)} %get-tuple-element.28.refs_4_.weight), channel_id=1, source_target_pairs={{0,16},{16,0},{1,17},{17,1},{2,18},{18,2},{3,19},{19,3},{4,20},{20... | collective-permute-start | bytes 392 | tf_op jit(solution)/shard_map/ppermute | solution.py:26
  13.4 2.0 %collective-permute-done.3.refs_5_ = f32[1,32]{1,0:T(1,128)S(1)} collective-permute-done((f32[1,32]{1,0:T(1,128)S(1)}, f32[1,32]{1,0:T(1,128)S(1)}, u32[]{:S(2)}, u32[]{:S(2)}) %collective-permute-start.3) | collective-permute-done | bytes 160 | tf_op jit(solution)/shard_map/ppermute | solution.py:26
  15.4 0.0 collective-permute-done.refs_1_
  15.5 4.3 %collective-permute-done.1.refs_2_ = bf16[32,1024]{1,0:T(8,128)(2,1)S(1)} collective-permute-done((bf16[32,1024]{1,0:T(8,128)(2,1)S(1)}, bf16[32,1024]{1,0:T(8,128)(2,1)S(1)}, u32[]{:S(2)}, u32[]{:S(2)}) %collective-permute-start.1) | collective-permute-done | bytes 65568 | tf_op jit(solution)/shard_map/ppermute | solution.py:26
  19.8 0.6 collective-permute-done.2.refs_3_
  20.4 0.6 shard_map.96
  21.0 0.1 collective-permute-start.4
  21.0 0.8 %collective-permute-start.7 = (f32[1,32]{1,0:T(1,128)S(1)}, f32[1,32]{1,0:T(1,128)S(1)}, u32[]{:S(2)}, u32[]{:S(2)}) collective-permute-start(f32[1,32]{1,0:T(1,128)S(1)} %get-tuple-element.31.refs_0_), channel_id=1, source_target_pairs={{0,3},{1,2},{2,1},{3,0},{4,7},{5,6},{6,5},{7,4},{8,11},{9,10},{10,... | collective-permute-start | bytes 392 | tf_op jit(solution)/shard_map/ppermute | solution.py:26
  21.9 2.2 %collective-permute-start.6 = (f32[1,32]{1,0:T(1,128)S(1)}, f32[1,32]{1,0:T(1,128)S(1)}, u32[]{:S(2)}, u32[]{:S(2)}) collective-permute-start(f32[1,32]{1,0:T(1,128)S(1)} %get-tuple-element.31.refs_0_), channel_id=1, source_target_pairs={{0,2},{1,3},{2,0},{3,1},{4,6},{5,7},{6,4},{7,5},{8,10},{9,11},{10,... | collective-permute-start | bytes 392 | tf_op jit(solution)/shard_map/ppermute | solution.py:26
  24.1 0.0 collective-permute-start.5
  24.1 0.0 collective-permute-done.7.refs_3_
  24.1 1.5 %collective-permute-done.6.refs_2_ = f32[1,32]{1,0:T(1,128)S(1)} collective-permute-done((f32[1,32]{1,0:T(1,128)S(1)}, f32[1,32]{1,0:T(1,128)S(1)}, u32[]{:S(2)}, u32[]{:S(2)}) %collective-permute-start.6) | collective-permute-done | bytes 160 | tf_op jit(solution)/shard_map/ppermute | solution.py:26
  25.6 0.0 collective-permute-done.5.refs_1_
  25.6 3.5 %collective-permute-done.4.got = bf16[2,32,1024]{2,1,0:T(8,128)(2,1)S(1)} collective-permute-done((bf16[2,32,1024]{2,1,0:T(8,128)(2,1)S(1)}, bf16[2,32,1024]{2,1,0:T(8,128)(2,1)S(1)}, u32[]{:S(2)}, u32[]{:S(2)}) %collective-permute-start.4) | collective-permute-done | bytes 131104 | tf_op jit(solution)/shard_map/ppermute | solution.py:26
  29.1 0.7 shard_map.97
  29.8 0.0 copy-start
  29.8 4.5 %collective-permute-start.8 = (bf16[48,1024]{1,0:T(8,128)(2,1)S(1)}, bf16[48,1024]{1,0:T(8,128)(2,1)S(1)}, u32[]{:S(2)}, u32[]{:S(2)}) collective-permute-start(bf16[48,1024]{1,0:T(8,128)(2,1)S(1)} %get-tuple-element.33), channel_id=1, source_target_pairs={{0,8},{1,9},{2,10},{3,11},{4,12},{5,13},{6,14},{7,15},{8,0},{9,1},... | collective-permute-start | bytes 294920 | tf_op jit(solution)/shard_map/ppermute | solution.py:26
  34.2 0.0 all-to-all-done.after.noise
  34.2 2.9 %shard_map.98 = (bf16[1024,2048]{1,0:T(8,128)(2,1)S(1)}, bf16[1024,1024]{1,0:T(8,128)(2,1)S(1)}) custom-call(bf16[1024,2048]{1,0:T(8,128)(2,1)} %inlet.1, bf16[2048,1024]{1,0:T(8,128)(2,1)} %outlet_hbm.1, bf16[16,32,1024]{2,1,0:T(8,128)(2,1)S(1)} %all-to-all-done.after.noise), custom_call_target="tpu_custom_call" | custom-call | bytes 6291456 | tf_op jit(solution)/shard_map/pallas_call | solution.py:184
  37.1 0.0 copy-start.3
  37.1 0.0 collective-permute-done.8.got
  37.2 0.0 copy-done
  37.2 1.0 %shard_map.99 = (bf16[32,1024]{1,0:T(8,128)(2,1)S(1)}, f32[8,128]{1,0:T(8,128)S(1)}) custom-call(s32[4]{0:T(128)S(1)} %copy-done.1, bf16[1,32,1024]{2,1,0:T(8,128)(2,1)S(1)} %get-tuple-element.32.keep, bf16[48,1024]{1,0:T(8,128)(2,1)S(1)} %collective-permute-done.8.got, bf16[1024,1024]{1,0:T(8,128)(2,1)S(1)} %copy-done, f32[8,128]{1,0:T(8,128)S(1)} %get-tuple-element.37.total), custom_call_target="tpu_custom_call" | custom-call | flops 67108864 | tf_op jit(solution)/shard_map/pallas_call | solution.py:193
  38.2 0.0 copy-done.3
  38.2 8.3 %shard_map.100 = (bf16[16,32,1024]{2,1,0:T(8,128)(2,1)}, f32[32,1]{1,0:T(8,128)S(1)}) custom-call(bf16[16,32,1024]{2,1,0:T(8,128)(2,1)S(1)} %all-to-all-done.after.noise, bf16[32,1024]{1,0:T(8,128)(2,1)S(1)} %get-tuple-element.38.latent, f32[1,32]{1,0:T(1,128)S(1)} %get-tuple-element.28.refs_4_.weight, bf16[1024,2048]{1,0:T(8,128)(2,1)S(1)} %get-tuple-element.39.inlet, ...), custom_call_target="tpu_custom_call" | custom-call | flops 4328521728 | bytes 8388608 | tf_op jit(solution)/shard_map/pallas_call | solution.py:326
  46.5 7.6 %all-to-all-start.1 = ((bf16[16,32,1024]{2,1,0:T(8,128)(2,1)}), bf16[16,32,1024]{2,1,0:T(8,128)(2,1)S(1)}, u32[]{:S(2)}, u32[]{:S(2)}) async-start(bf16[16,32,1024]{2,1,0:T(8,128)(2,1)} %get-tuple-element.43), calls=%async_computation.1 | async-start | bytes 2097152 | tf_op jit(solution)/shard_map/all_to_all | solution.py:34
  54.1 1.9 %collective-permute-start.9 = (f32[8,128]{1,0:T(8,128)S(1)}, f32[8,128]{1,0:T(8,128)S(1)}, u32[]{:S(2)}, u32[]{:S(2)}) collective-permute-start(f32[8,128]{1,0:T(8,128)S(1)} %get-tuple-element.44), channel_id=1, source_target_pairs={{0,4},{1,5},{2,6},{3,7},{4,0},{5,1},{6,2},{7,3},{8,12},{9,13},{10,... | collective-permute-start | bytes 12296 | tf_op jit(solution)/shard_map/ppermute | solution.py:26
  56.0 0.5 slice.6
  56.5 15.8 %collective-permute-done.9 = f32[8,128]{1,0:T(8,128)S(1)} collective-permute-done((f32[8,128]{1,0:T(8,128)S(1)}, f32[8,128]{1,0:T(8,128)S(1)}, u32[]{:S(2)}, u32[]{:S(2)}) %collective-permute-start.9) | collective-permute-done | bytes 4128 | tf_op jit(solution)/shard_map/ppermute | solution.py:26
  72.3 0.5 slice.7
  74.1 0.6 multiply_reduce_fusion
  74.7 2.3 %all-to-all-done.1 = bf16[16,32,1024]{2,1,0:T(8,128)(2,1)S(1)} async-done(((bf16[16,32,1024]{2,1,0:T(8,128)(2,1)}), bf16[16,32,1024]{2,1,0:T(8,128)(2,1)S(1)}, u32[]{:S(2)}, u32[]{:S(2)}) %all-to-all-start.1) | async-done | bytes 1048608 | tf_op jit(solution)/shard_map/all_to_all | solution.py:34
  77.0 1.2 %multiply_convert_fusion = bf16[16,32,1024]{2,1,0:T(8,128)(2,1)} fusion(bf16[16,32,1024]{2,1,0:T(8,128)(2,1)S(1)} %all-to-all-done.1, f32[]{:T(128)} %bitcast.2), kind=kLoop, calls=%fused_computation | loop fusion | flops 1572864 | bytes 2097156 | tf_op jit(solution)/shard_map/convert_element_type | solution.py:347
Async XLA Ops:
  0.6 7.6 %copy-start.1 = (s32[4]{0:T(128)S(1)}, s32[4]{0:T(128)}, u32[]{:S(2)}) copy-start(s32[4]{0:T(128)} %owners.7) | copy-start | bytes 52
  0.6 7.6 %copy-start.2 = (f32[32]{0:T(128)S(1)}, f32[32]{0:T(128)}, u32[]{:S(2)}) copy-start(f32[32]{0:T(128)} %param.12) | copy-start | bytes 388
  0.6 33.6 %all-to-all-start = ((bf16[16,32,1024]{2,1,0:T(8,128)(2,1)}), bf16[16,32,1024]{2,1,0:T(8,128)(2,1)S(1)}, u32[]{:S(2)}, u32[]{:S(2)}) async-start(bf16[16,32,1024]{2,1,0:T(8,128)(2,1)} %bitcast.6), calls=%async_computation | async-start | bytes 2097152 | tf_op jit(solution)/shard_map/all_to_all | solution.py:34
  9.8 5.7 %collective-permute-start = (bf16[32,1024]{1,0:T(8,128)(2,1)S(1)}, bf16[32,1024]{1,0:T(8,128)(2,1)S(1)}, u32[]{:S(2)}, u32[]{:S(2)}) collective-permute-start(bf16[32,1024]{1,0:T(8,128)(2,1)S(1)} %get-tuple-element.25), channel_id=1, source_target_pairs={{0,1},{1,0},{2,3},{3,2},{4,5},{5,4},{6,7},{7,6},{8,9},{9,8},{10,11... | collective-permute-start | bytes 196616 | tf_op jit(solution)/shard_map/ppermute | solution.py:26
  10.2 9.6 %collective-permute-start.1 = (bf16[32,1024]{1,0:T(8,128)(2,1)S(1)}, bf16[32,1024]{1,0:T(8,128)(2,1)S(1)}, u32[]{:S(2)}, u32[]{:S(2)}) collective-permute-start(bf16[32,1024]{1,0:T(8,128)(2,1)S(1)} %get-tuple-element.26), channel_id=1, source_target_pairs={{0,2},{1,3},{2,0},{3,1},{4,6},{5,7},{6,4},{7,5},{8,10},{9,11},{10,... | collective-permute-start | bytes 196616 | tf_op jit(solution)/shard_map/ppermute | solution.py:26
  11.9 8.5 %collective-permute-start.2 = (bf16[32,1024]{1,0:T(8,128)(2,1)S(1)}, bf16[32,1024]{1,0:T(8,128)(2,1)S(1)}, u32[]{:S(2)}, u32[]{:S(2)}) collective-permute-start(bf16[32,1024]{1,0:T(8,128)(2,1)S(1)} %get-tuple-element.27), channel_id=1, source_target_pairs={{0,3},{1,2},{2,1},{3,0},{4,7},{5,6},{6,5},{7,4},{8,11},{9,10},{10,... | collective-permute-start | bytes 196616 | tf_op jit(solution)/shard_map/ppermute | solution.py:26
  11.9 3.5 %collective-permute-start.3 = (f32[1,32]{1,0:T(1,128)S(1)}, f32[1,32]{1,0:T(1,128)S(1)}, u32[]{:S(2)}, u32[]{:S(2)}) collective-permute-start(f32[1,32]{1,0:T(1,128)S(1)} %get-tuple-element.28.refs_4_.weight), channel_id=1, source_target_pairs={{0,16},{16,0},{1,17},{17,1},{2,18},{18,2},{3,19},{19,3},{4,20},{20... | collective-permute-start | bytes 392 | tf_op jit(solution)/shard_map/ppermute | solution.py:26
  21.0 8.1 %collective-permute-start.4 = (bf16[2,32,1024]{2,1,0:T(8,128)(2,1)S(1)}, bf16[2,32,1024]{2,1,0:T(8,128)(2,1)S(1)}, u32[]{:S(2)}, u32[]{:S(2)}) collective-permute-start(bf16[2,32,1024]{2,1,0:T(8,128)(2,1)S(1)} %get-tuple-element.30), channel_id=1, source_target_pairs={{0,4},{1,5},{2,6},{3,7},{4,0},{5,1},{6,2},{7,3},{8,12},{9,13},{10,... | collective-permute-start | bytes 393224 | tf_op jit(solution)/shard_map/ppermute | solution.py:26
  21.0 3.1 %collective-permute-start.7 = (f32[1,32]{1,0:T(1,128)S(1)}, f32[1,32]{1,0:T(1,128)S(1)}, u32[]{:S(2)}, u32[]{:S(2)}) collective-permute-start(f32[1,32]{1,0:T(1,128)S(1)} %get-tuple-element.31.refs_0_), channel_id=1, source_target_pairs={{0,3},{1,2},{2,1},{3,0},{4,7},{5,6},{6,5},{7,4},{8,11},{9,10},{10,... | collective-permute-start | bytes 392 | tf_op jit(solution)/shard_map/ppermute | solution.py:26
  21.9 3.7 %collective-permute-start.6 = (f32[1,32]{1,0:T(1,128)S(1)}, f32[1,32]{1,0:T(1,128)S(1)}, u32[]{:S(2)}, u32[]{:S(2)}) collective-permute-start(f32[1,32]{1,0:T(1,128)S(1)} %get-tuple-element.31.refs_0_), channel_id=1, source_target_pairs={{0,2},{1,3},{2,0},{3,1},{4,6},{5,7},{6,4},{7,5},{8,10},{9,11},{10,... | collective-permute-start | bytes 392 | tf_op jit(solution)/shard_map/ppermute | solution.py:26
  24.1 1.5 %collective-permute-start.5 = (f32[1,32]{1,0:T(1,128)S(1)}, f32[1,32]{1,0:T(1,128)S(1)}, u32[]{:S(2)}, u32[]{:S(2)}) collective-permute-start(f32[1,32]{1,0:T(1,128)S(1)} %get-tuple-element.31.refs_0_), channel_id=1, source_target_pairs={{0,1},{1,0},{2,3},{3,2},{4,5},{5,4},{6,7},{7,6},{8,9},{9,8},{10,11... | collective-permute-start | bytes 392 | tf_op jit(solution)/shard_map/ppermute | solution.py:26
  29.8 7.4 %copy-start = (bf16[1024,1024]{1,0:T(8,128)(2,1)S(1)}, bf16[1024,1024]{1,0:T(8,128)(2,1)}, u32[]{:S(2)}) copy-start(bf16[1024,1024]{1,0:T(8,128)(2,1)} %encoder.1) | copy-start | bytes 6291460
  29.8 7.4 %collective-permute-start.8 = (bf16[48,1024]{1,0:T(8,128)(2,1)S(1)}, bf16[48,1024]{1,0:T(8,128)(2,1)S(1)}, u32[]{:S(2)}, u32[]{:S(2)}) collective-permute-start(bf16[48,1024]{1,0:T(8,128)(2,1)S(1)} %get-tuple-element.33), channel_id=1, source_target_pairs={{0,8},{1,9},{2,10},{3,11},{4,12},{5,13},{6,14},{7,15},{8,0},{9,1},... | collective-permute-start | bytes 294920 | tf_op jit(solution)/shard_map/ppermute | solution.py:26
  37.1 1.0 %copy-start.3 = (bf16[32,1024]{1,0:T(8,128)(2,1)S(1)}, bf16[32,1024]{1,0:T(8,128)(2,1)}, u32[]{:S(2)}) copy-start(bf16[32,1024]{1,0:T(8,128)(2,1)} %targets_hbm.1) | copy-start | bytes 196612
  46.5 30.6 %all-to-all-start.1 = ((bf16[16,32,1024]{2,1,0:T(8,128)(2,1)}), bf16[16,32,1024]{2,1,0:T(8,128)(2,1)S(1)}, u32[]{:S(2)}, u32[]{:S(2)}) async-start(bf16[16,32,1024]{2,1,0:T(8,128)(2,1)} %get-tuple-element.43), calls=%async_computation.1 | async-start | bytes 2097152 | tf_op jit(solution)/shard_map/all_to_all | solution.py:34
  54.1 18.2 %collective-permute-start.9 = (f32[8,128]{1,0:T(8,128)S(1)}, f32[8,128]{1,0:T(8,128)S(1)}, u32[]{:S(2)}, u32[]{:S(2)}) collective-permute-start(f32[8,128]{1,0:T(8,128)S(1)} %get-tuple-element.44), channel_id=1, source_target_pairs={{0,4},{1,5},{2,6},{3,7},{4,0},{5,1},{6,2},{7,3},{8,12},{9,13},{10,... | collective-permute-start | bytes 12296 | tf_op jit(solution)/shard_map/ppermute | solution.py:26
